TPU v7x, 512 devices: a whole 4x8x8 slice. The times are simulated.
512 devices in a mesh: row: 64 (over y_lo, z, core), col: 8 (over x, y_hi).
Axes of the slice: x: 4, y: 8 (y_hi: 2, y_lo: 4; y = y_hi * 4 + y_lo), z: 8, core: 2. Of those that a mesh axis runs over, the one named last changes fastest.
Arguments:
- tokens: bfloat16 [1024, 6144], P('row', 'col'), may hold values from -6 to 6
- in_weight: bfloat16 [96, 384], replicated, may hold values from -0.625 to 0.625
- conv_weight: float32 [3, 3, 192], replicated, may hold values from -2 to 2
- conv_bias: float32 [192], replicated, may hold values from -3 to 3
- scan_weight: bfloat16 [4, 192, 35], replicated, may hold values from -0.4375 to 0.4375
- step_bias: float32 [4, 3], replicated, may hold values from -5 to -1.5
- log_decay: float32 [4, 3], replicated, may hold values from -1.5 to 1
- skip_gain: float32 [4, 192], replicated, may hold values from 0.5 to 1.5
- norm_gain: float32 [192], replicated, may hold values from 0.5 to 1.5
- norm_bias: float32 [192], replicated, may hold values from -2 to 2
- out_weight: bfloat16 [192, 96], replicated, may hold values from -0.4375 to 0.4375
- cotangent: bfloat16 [1024, 6144], P('row', 'col'), may hold values from -6 to 6
Outputs:
- output: bfloat16 [1024, 6144], P('row', 'col')
- grad_tokens: bfloat16 [1024, 6144], P('row', 'col')
- grad_in_weight: float32 [96, 384], replicated
- grad_conv_weight: float32 [3, 3, 192], replicated
- grad_conv_bias: float32 [192], replicated
- grad_scan_weight: float32 [4, 192, 35], replicated
- grad_step_bias: float32 [4, 3], replicated
- grad_log_decay: float32 [4, 3], replicated
- grad_skip_gain: float32 [4, 192], replicated
- grad_norm_gain: float32 [192], replicated
- grad_norm_bias: float32 [192], replicated
- grad_out_weight: float32 [192, 96], replicated
All inputs are finite; a program needn't handle non-finite values.
Results may differ from a plain program's by a relative error of at most 0.022.
Values may be sent and summed in bfloat16 or wider, within the bound.
No kernel may reach another device: no remote copies, remote signals or barrier semaphores. Data moves between devices by JAX's collectives and lax.ppermute only.
A program may use at most 128 MiB of HBM per device.

v0:
```python
from functools import partial

import jax
import jax.numpy as jnp
from jax import lax
from jax.sharding import PartitionSpec as P

D = 96
QC = 64


highest = lax.Precision.HIGHEST


def with_halo(value, sides, width):
    for axis, dim in sides:
        size, length = (lax.axis_size(axis), value.shape[dim])
        up = [(i, (i + 1) % size) for i in range(size - 1)]
        down = [(j, i) for i, j in up]
        last = lax.slice_in_dim(value, length - width, length, axis=dim)
        leading = lax.slice_in_dim(value, 0, width, axis=dim)
        before = lax.ppermute(last, axis, up)
        after = lax.ppermute(leading, axis, down)
        value = jnp.concatenate([before, value, after], axis=dim)
    return value


def carried_in(value, axis, join, neutral, backward):
    count = lax.axis_size(axis)
    place = lax.axis_index(axis)
    ahead = count - 1 - place if backward else place
    gathered = jax.tree.map(
        lambda a, kind: lax.all_gather(a.astype(kind), axis),
        value,
        jax.tree.map(lambda a: jnp.bfloat16 if a.dtype == jnp.float32 else a.dtype, value),
    )
    state = jax.tree.map(lambda a, e: jnp.zeros_like(a) + jnp.asarray(e, a.dtype), value, neutral)

    def one(step, state):
        source = count - 1 - step if backward else step
        return join(
            state,
            jax.tree.map(
                lambda a, own: lax.dynamic_index_in_dim(a, source, 0, False).astype(own.dtype),
                gathered,
                value,
            ),
        )

    return lax.fori_loop(0, ahead, one, state)


def prefix(value, axis, combine, identity, reverse):
    length, mine = (lax.axis_size(axis), lax.axis_index(axis))
    everything = jax.tree.map(lambda part: lax.all_gather(part, axis), value)
    start = jax.tree.map(
        lambda part, zero: jnp.broadcast_to(jnp.asarray(zero, part.dtype), part.shape),
        value,
        identity,
    )

    def step(k, before):
        at = length - 1 - k if reverse else k
        reached = at > mine if reverse else at < mine
        new = combine(before, jax.tree.map(lambda part: part[at], everything))
        return jax.tree.map(lambda a, b: jnp.where(reached, a, b), new, before)

    return lax.fori_loop(0, length, step, start)


def to_lines(planes, direction):
    if direction == 1:
        return jnp.flip(planes, 1)
    if direction == 2:
        return jnp.swapaxes(planes, 0, 1)
    if direction == 3:
        return jnp.flip(jnp.swapaxes(planes, 0, 1), 1)
    return planes


def from_lines(planes, direction):
    if direction == 1:
        return jnp.flip(planes, 1)
    if direction == 2:
        return jnp.swapaxes(planes, 0, 1)
    if direction == 3:
        return jnp.swapaxes(jnp.flip(planes, 1), 0, 1)
    return planes


def segment(values, step_size, in_gate, out_gate, decay_rate, window_cap):
    line_count, length, inner_width = values.shape
    head_count = step_size.shape[-1]
    head_dim = inner_width // head_count
    states = in_gate.shape[-1]
    window = min(window_cap, length)
    pieces = length // window
    log_step = step_size * decay_rate
    scaled = (
        values.reshape(line_count, length, head_count, head_dim) * step_size[..., None]
    ).reshape(line_count, pieces, window, head_count, head_dim)
    log_inner = jnp.cumsum(log_step.reshape(line_count, pieces, window, head_count), axis=2)
    keys_block = in_gate.reshape(line_count, pieces, window, states)
    query_block = out_gate.reshape(line_count, pieces, window, states)
    scores = jnp.einsum("mkqn,mksn->mkqs", query_block, keys_block, precision=highest)
    spread = log_inner[:, :, :, None, :] - log_inner[:, :, None, :, :]
    causal = (jnp.arange(window)[:, None] >= jnp.arange(window)[None, :])[None, None, :, :, None]
    decay_table = jnp.where(causal, jnp.exp(jnp.where(causal, spread, 0.0)), 0.0)
    weights = scores[..., None] * decay_table
    inside = jnp.einsum("mkqsh,mkshp->mkqhp", weights, scaled, precision=highest)
    to_end = jnp.exp(log_inner[:, :, -1:, :] - log_inner)
    block_state = jnp.einsum(
        "mksh,mkshp,mksn->mkhpn", to_end, scaled, keys_block, precision=highest
    )
    block_log = log_inner[:, :, -1, :]

    def advance(carry_state, step_items):
        contrib, piece_log = step_items
        return (jnp.exp(piece_log)[..., None, None] * carry_state + contrib, carry_state)

    zero_state = jnp.zeros((line_count, head_count, head_dim, states), jnp.float32)
    end_state, incoming = lax.scan(
        advance, zero_state, (jnp.moveaxis(block_state, 1, 0), jnp.moveaxis(block_log, 1, 0))
    )
    incoming = jnp.moveaxis(incoming, 0, 1)
    across = jnp.einsum(
        "mkqn,mkqh,mkhpn->mkqhp", query_block, jnp.exp(log_inner), incoming, precision=highest
    )
    output = (inside + across).reshape(line_count, length, inner_width)
    log_full = jnp.cumsum(log_step, axis=1)
    return (output, end_state, log_full)


def direction_terms(values, raw_proj, step_shift, log_rate, skip_part, direction):
    head_count = step_shift.shape[0]
    line_values = to_lines(values, direction)
    line_raw = to_lines(raw_proj, direction)
    states = (line_raw.shape[-1] - head_count) // 2
    step_size = jax.nn.softplus(line_raw[..., :head_count] + step_shift)
    out_gate = line_raw[..., head_count + states :]
    output, end_state, log_full = segment(
        line_values,
        step_size,
        line_raw[..., head_count : head_count + states],
        out_gate,
        -jnp.exp(log_rate),
        QC,
    )
    result = from_lines(output, direction) + skip_part * values
    return (result, end_state, log_full[:, -1, :], out_gate, log_full)


def carried(out_gate, log_full, state_in, direction):
    line_count, length, head_count = log_full.shape
    term = jnp.einsum(
        "mln,mlh,mhpn->mlhp", out_gate, jnp.exp(log_full), state_in, precision=highest
    )
    return from_lines(term.reshape(line_count, length, -1), direction)


def depthwise(padded, kernel, height, width):
    accumulated = jnp.zeros((height, width, kernel.shape[-1]), jnp.float32)
    for offset_row in range(3):
        for offset_col in range(3):
            accumulated = (
                accumulated
                + kernel[offset_row, offset_col]
                * padded[offset_row : offset_row + height, offset_col : offset_col + width]
            )
    return accumulated


def flipped(padded_grad, kernel, height, width):
    accumulated = jnp.zeros((height, width, kernel.shape[-1]), jnp.float32)
    for offset_row in range(3):
        for offset_col in range(3):
            accumulated = (
                accumulated
                + kernel[offset_row, offset_col]
                * padded_grad[
                    2 - offset_row : 2 - offset_row + height,
                    2 - offset_col : 2 - offset_col + width,
                ]
            )
    return accumulated


def kernel_grads(grad_wide, padded, height, width):
    kernel_rows = []
    for offset_row in range(3):
        for offset_col in range(3):
            kernel_rows.append(
                jnp.sum(
                    grad_wide
                    * padded[offset_row : offset_row + height, offset_col : offset_col + width],
                    axis=(0, 1),
                )
            )
    return (jnp.stack(kernel_rows).reshape(3, 3, -1), jnp.sum(grad_wide, axis=(0, 1)))


def post_norm(summed, gate_wide, norm_gain, norm_bias):
    center = summed - jnp.mean(summed, axis=-1, keepdims=True)
    spread = jnp.mean(center * center, axis=-1, keepdims=True)
    normed = center * lax.rsqrt(spread + 1e-05) * norm_gain + norm_bias
    return normed * gate_wide * jax.nn.sigmoid(gate_wide)


def add_rims(planes):
    return with_halo(planes, (("row", 0), ("col", 1)), 1)


def combine(earlier, latter):
    return (earlier[0] + latter[0], latter[1] + jnp.exp(latter[0])[..., None, None] * earlier[1])


def chain_cols(paired, backward):
    neutral = (jnp.zeros_like(paired[0]), jnp.zeros_like(paired[1]))
    return carried_in(paired, "col", combine, neutral, backward)[1]


def chain_rows(paired, backward):
    neutral = (jnp.zeros_like(paired[0]), jnp.zeros_like(paired[1]))
    return prefix(paired, "row", combine, neutral, backward)[1]


def vertical_carry(paired, backward):
    return chain_rows(paired, backward)


def local(
    tokens,
    in_weight,
    conv_weight,
    conv_bias,
    scan_weight,
    step_bias,
    log_decay,
    skip_gain,
    norm_gain,
    norm_bias,
    out_weight,
    cotangent,
):
    grid_rows = tokens.shape[0]
    grid_cols = tokens.shape[1] // D
    inner_width = in_weight.shape[1] // 2
    block_in = tokens.reshape(grid_rows, grid_cols, D)
    projected = jnp.einsum("rcd,de->rce", block_in, in_weight, preferred_element_type=jnp.float32)
    branch = projected[..., :inner_width].astype(jnp.bfloat16)
    gate_in = projected[..., inner_width:].astype(jnp.bfloat16)
    padded = add_rims(branch)
    before = depthwise(padded, conv_weight, grid_rows, grid_cols) + conv_bias
    sigmoid_pre = jax.nn.sigmoid(before)
    activated = (before * sigmoid_pre).astype(jnp.bfloat16)
    wide_act = lax.optimization_barrier(activated).astype(jnp.float32)
    raw_all = jnp.einsum(
        "rci,kij->krcj", activated, scan_weight, preferred_element_type=jnp.float32
    )
    summed = jnp.zeros((grid_rows, grid_cols, inner_width), jnp.float32)
    stored = []
    for direction in range(4):
        outcome, pull_local = jax.vjp(
            partial(direction_terms, direction=direction),
            wide_act,
            raw_all[direction],
            step_bias[direction],
            log_decay[direction],
            skip_gain[direction],
        )
        result, end_state, total_log, out_gate, log_full = outcome
        if direction < 2:
            state_in = chain_cols((total_log, end_state), direction == 1)
        else:
            state_in = vertical_carry((total_log, end_state), direction == 3)
        carried_part, pull_carry = jax.vjp(
            partial(carried, direction=direction), out_gate, log_full, state_in
        )
        summed = summed + result + carried_part
        stored.append((direction, pull_local, pull_carry, total_log, state_in))
    gate_wide = lax.optimization_barrier(gate_in).astype(jnp.float32)
    gated_out, pull_post = jax.vjp(post_norm, summed, gate_wide, norm_gain, norm_bias)
    gated_low = gated_out.astype(jnp.bfloat16)
    output = jnp.einsum(
        "rci,id->rcd", gated_low, out_weight, preferred_element_type=jnp.float32
    ).astype(jnp.bfloat16)
    back_in = cotangent.reshape(grid_rows, grid_cols, D)
    grad_gated = jnp.einsum("rcd,id->rci", back_in, out_weight, preferred_element_type=jnp.float32)
    grad_out = jnp.einsum("rci,rcd->id", gated_low, back_in, preferred_element_type=jnp.float32)
    grad_sum, grad_gate, grad_gain, grad_shift = pull_post(grad_gated)
    grad_low = grad_sum.astype(jnp.bfloat16)
    grad_wide = lax.optimization_barrier(grad_low).astype(jnp.float32)
    grad_act = jnp.zeros_like(summed)
    weight_grads = []
    bias_grads = []
    rate_grads = []
    skip_grads = []
    for direction, pull_local, pull_carry, total_log, state_in in stored:
        grad_gate_out, grad_log_full, grad_state = pull_carry(grad_wide)
        if direction < 2:
            state_after = chain_cols((total_log, grad_state), direction != 1)
        else:
            state_after = vertical_carry((total_log, grad_state), direction != 3)
        grad_span = jnp.sum(state_after * state_in, axis=(2, 3)) * jnp.exp(total_log)
        pieces = pull_local((grad_wide, state_after, grad_span, grad_gate_out, grad_log_full))
        raw_low = pieces[1].astype(jnp.bfloat16)
        grad_act = (
            grad_act
            + pieces[0]
            + jnp.einsum(
                "rcj,ij->rci", raw_low, scan_weight[direction], preferred_element_type=jnp.float32
            )
        )
        weight_grads.append(
            jnp.einsum("rci,rcj->ij", activated, raw_low, preferred_element_type=jnp.float32)
        )
        bias_grads.append(pieces[2])
        rate_grads.append(pieces[3])
        skip_grads.append(pieces[4])
    grad_before = (grad_act * sigmoid_pre * (1.0 + before * (1.0 - sigmoid_pre))).astype(
        jnp.bfloat16
    )
    before_wide = lax.optimization_barrier(grad_before).astype(jnp.float32)
    grad_padded = add_rims(grad_before)
    grad_branch = flipped(grad_padded, conv_weight, grid_rows, grid_cols)
    grad_kernel, grad_cbias = kernel_grads(before_wide, padded, grid_rows, grid_cols)
    grad_mixed = jnp.concatenate([grad_branch, grad_gate], axis=-1).astype(jnp.bfloat16)
    grad_tokens = jnp.einsum(
        "rce,de->rcd", grad_mixed, in_weight, preferred_element_type=jnp.float32
    ).astype(jnp.bfloat16)
    grad_in = jnp.einsum("rcd,rce->de", block_in, grad_mixed, preferred_element_type=jnp.float32)
    scale = float(grid_rows * grid_cols * lax.axis_size("row") * lax.axis_size("col")) ** (-0.5)
    totals = lax.psum(
        (
            grad_in,
            grad_kernel,
            grad_cbias,
            jnp.stack(weight_grads),
            jnp.stack(bias_grads),
            jnp.stack(rate_grads),
            jnp.stack(skip_grads),
            grad_gain,
            grad_shift,
            grad_out,
        ),
        ("row", "col"),
    )
    return (
        output.reshape(grid_rows, grid_cols * D),
        grad_tokens.reshape(grid_rows, grid_cols * D),
        totals[0] * scale,
        totals[1] * scale,
        totals[2] * scale,
        totals[3] * scale,
        totals[4] * scale,
        totals[5] * scale,
        totals[6] * scale,
        totals[7] * scale,
        totals[8] * scale,
        totals[9] * scale,
    )


def solution(mesh):
    in_specs = (P("row", "col"), P(), P(), P(), P(), P(), P(), P(), P(), P(), P(), P("row", "col"))
    out_specs = (P("row", "col"), P("row", "col"), P(), P(), P(), P(), P(), P(), P(), P(), P(), P())
    return jax.shard_map(local, mesh=mesh, in_specs=in_specs, out_specs=out_specs, check_vma=False)
```

profile of v0, /device:TPU:56, one launch (start us, length us, event | category | flops | bytes accessed | tf_op | source)
XLA Modules:
  0.0 1689.7 jit_solution(1555374045098096227)
XLA Ops:
  8.3 11.2 collective-permute-start.1
  26.5 4.7 collective-permute-start.2
  31.3 5.0 collective-permute-start.3
  37.7 4.0 collective-permute-done.3
  64.1 60.0 %all-gather.7 = f32[512,1,3]{2,0,1:T(8,128)S(1)} all-gather(f32[8,1,3]{2,0,1:T(8,128)S(1)} %slice.397), channel_id=9, replica_groups=mesh['row'=64,'col'=8] {'row'}, dimensions={0}, use_global_device_ids=true | all-gather | bytes 6240 | tf_op jit(solution)/shard_map/all_gather | solution.py:55
  133.4 76.6 %all-gather.5 = f32[512,1,3]{2,0,1:T(8,128)S(1)} all-gather(f32[8,1,3]{2,0,1:T(8,128)S(1)} %slice.391), channel_id=7, replica_groups=mesh['row'=64,'col'=8] {'row'}, dimensions={0}, use_global_device_ids=true | all-gather | bytes 6240 | tf_op jit(solution)/shard_map/all_gather | solution.py:55
  217.2 41.9 %all-gather.3 = bf16[128,1,3]{2,1,0:T(2,128)(2,1)S(1)} all-gather(bf16[16,1,3]{2,1,0:T(2,128)(2,1)S(1)} %copy.639), channel_id=5, replica_groups=mesh['row'=64,'col'=8] {'col'}, dimensions={0}, use_global_device_ids=true | all-gather | bytes 864 | tf_op jit(solution)/shard_map/all_gather | solution.py:33
  262.6 65.2 %all-gather.2 = bf16[128,3,64,16]{2,3,1,0:T(8,128)(2,1)S(1)} all-gather(bf16[16,3,64,16]{2,3,1,0:T(8,128)(2,1)S(1)} %fusion.5), channel_id=4, replica_groups=mesh['row'=64,'col'=8] {'col'}, dimensions={0}, use_global_device_ids=true | all-gather | bytes 884736 | tf_op jit(solution)/shard_map/all_gather | solution.py:33
  327.9 6.0 while.73
  342.8 41.8 %all-gather.1 = bf16[128,1,3]{2,1,0:T(2,128)(2,1)S(1)} all-gather(bf16[16,1,3]{2,1,0:T(2,128)(2,1)S(1)} %copy.620), channel_id=3, replica_groups=mesh['row'=64,'col'=8] {'col'}, dimensions={0}, use_global_device_ids=true | all-gather | bytes 864 | tf_op jit(solution)/shard_map/all_gather | solution.py:33
  389.5 66.3 %all-gather = bf16[128,3,64,16]{2,3,1,0:T(8,128)(2,1)S(1)} all-gather(bf16[16,3,64,16]{2,3,1,0:T(8,128)(2,1)S(1)} %fusion.4), channel_id=2, replica_groups=mesh['row'=64,'col'=8] {'col'}, dimensions={0}, use_global_device_ids=true | all-gather | bytes 884736 | tf_op jit(solution)/shard_map/all_gather | solution.py:33
  476.9 116.8 %while.77 = (s32[]{:T(128)}, f32[8,3,64,16]{2,3,1,0:T(8,128)S(1)}, s32[]{:T(128)}, f32[64,8,3,64,16]{3,4,2,1,0:T(8,128)}, f32[64,8,3]{1,2,0:T(4,128)}, /*index=5*/s32[]{:T(128)}, s32[]{:T(128)}, s32[]{:T(128)}, s32[]{:T(128)}) while((s32[]{:T(128)}, f32[8,3,64,16]{2,3,1,0:T(8,128)S(1)}, s32[]{:T(128)}, ...), condition=%wide.region_15.18_spmd.clone, body=%wide.region_14.17_spmd.clone.sunk | while | flops 98312 | bytes 295567 | solution.py:68
  594.6 17.7 %all-gather.17.cloned.1.call-done = f32[512,3,64,16]{2,3,1,0:T(8,128)} async-done(((f32[8,3,64,16]{2,3,1,0:T(8,128)}), f32[512,3,64,16]{2,3,1,0:T(8,128)}) %all-gather.17.cloned.1.call-update) | async-done | bytes 6291472 | tf_op jit(solution)/shard_map/all_gather | solution.py:55
  612.3 116.2 %while.76 = (s32[]{:T(128)}, f32[8,3,64,16]{2,3,1,0:T(8,128)S(1)}, s32[]{:T(128)}, f32[64,8,3,64,16]{3,4,2,1,0:T(8,128)}, f32[64,8,3]{1,2,0:T(4,128)}, /*index=5*/s32[]{:T(128)}, s32[]{:T(128)}) while((s32[]{:T(128)}, f32[8,3,64,16]{2,3,1,0:T(8,128)S(1)}, s32[]{:T(128)}, f32[64,8,3,64,16]{3,4,2,1,0:T(8,128)}, ...), condition=%wide.region_11.14_spmd.clone, body=%wide.region_10.13_spmd.clone.sunk | while | flops 98308 | bytes 295505 | solution.py:68
  736.1 70.9 %all-gather.8 = bf16[128,3,64,16]{2,3,1,0:T(8,128)(2,1)} all-gather(bf16[16,3,64,16]{2,3,1,0:T(8,128)(2,1)S(1)} %convolution_convert_fusion.1), channel_id=10, replica_groups=mesh['row'=64,'col'=8] {'col'}, dimensions={0}, use_global_device_ids=true | all-gather | bytes 884736 | tf_op jit(solution)/shard_map/all_gather | solution.py:33
  807.0 11.4 while.74
  821.3 2.6 fusion.71
  824.0 2.8 fusion.73
  855.2 66.7 %all-gather.9 = bf16[128,3,64,16]{2,3,1,0:T(8,128)(2,1)S(1)} all-gather(bf16[16,3,64,16]{2,3,1,0:T(8,128)(2,1)S(1)} %convolution_convert_fusion), channel_id=11, replica_groups=mesh['row'=64,'col'=8] {'col'}, dimensions={0}, use_global_device_ids=true | all-gather | bytes 884736 | tf_op jit(solution)/shard_map/all_gather | solution.py:33
  979.5 2.6 fusion.46
  982.1 2.6 fusion.42
  984.7 2.6 fusion.38
  994.0 22.3 %all-gather.21.cloned.1.call-done = f32[512,3,64,16]{2,3,1,0:T(8,128)} async-done(((f32[8,3,64,16]{2,3,1,0:T(8,128)}), f32[512,3,64,16]{2,3,1,0:T(8,128)}) %all-gather.21.cloned.1.call-update) | async-done | bytes 6291472 | tf_op jit(solution)/shard_map/all_gather | solution.py:55
  1016.3 116.9 %while.78 = (s32[]{:T(128)}, f32[8,3,64,16]{2,3,1,0:T(8,128)S(1)}, s32[]{:T(128)}, f32[64,8,3,64,16]{3,4,2,1,0:T(8,128)}, f32[64,8,3]{1,2,0:T(4,128)}, /*index=5*/s32[]{:T(128)}, s32[]{:T(128)}, s32[]{:T(128)}, s32[]{:T(128)}) while((s32[]{:T(128)}, f32[8,3,64,16]{2,3,1,0:T(8,128)S(1)}, s32[]{:T(128)}, ...), condition=%wide.region_43.46_spmd.clone, body=%wide.region_42.45_spmd.clone.sunk | while | flops 98312 | bytes 295567 | solution.py:68
  1135.3 12.6 all-gather.23.cloned.1.call-done
  1147.9 116.0 %while.79 = (s32[]{:T(128)}, f32[8,3,64,16]{2,3,1,0:T(8,128)S(1)}, s32[]{:T(128)}, f32[64,8,3,64,16]{3,4,2,1,0:T(8,128)}, f32[64,8,3]{1,2,0:T(4,128)}, /*index=5*/s32[]{:T(128)}, s32[]{:T(128)}) while((s32[]{:T(128)}, f32[8,3,64,16]{2,3,1,0:T(8,128)S(1)}, s32[]{:T(128)}, f32[64,8,3,64,16]{3,4,2,1,0:T(8,128)}, ...), condition=%wide.region_54.57_spmd.clone, body=%wide.region_53.56_spmd.clone.sunk | while | flops 98308 | bytes 295505 | solution.py:68
  1289.4 4.4 collective-permute-start.5
  1299.0 97.7 %all-reduce.24 = (f32[3,3,192]{2,1,0:T(4,128)S(1)}, f32[192]{0:T(256)S(1)}, f32[4,3]{1,0:T(4,128)S(1)}, f32[4,3]{1,0:T(4,128)S(1)}, f32[4,192]{1,0:T(4,128)S(1)}, /*index=5*/f32[192]{0:T(256)S(1)}, f32[192]{0:T(256)S(1)}) all-reduce(f32[3,3,192]{2,1,0:T(4,128)S(1)} %reshape.1239, ...), channel_id=1, replica_groups=mesh['row'=64,'col'=8] {'row','col'}, use_global_device_ids=true, to_apply=%region_74.77 | all-reduce | flops 3096 | bytes 24768 | tf_op jit(solution)/shard_map/psum | solution.py:333
  1400.8 5.6 collective-permute-start.6
  1406.3 5.1 collective-permute-start.7
  1412.9 3.0 collective-permute-done.7
  1418.7 259.3 %all-reduce.28.cloned.1.call-done = (f32[96,384]{1,0:T(8,128)}, f32[4,192,35]{1,2,0:T(8,128)}, f32[192,96]{1,0:T(8,128)}) async-done(((f32[96,384]{1,0:T(8,128)}, f32[4,192,35]{1,2,0:T(8,128)}, f32[192,96]{1,0:T(8,128)}), (f32[96,384]{1,0:T(8,128)}, f32[4,192,35]{1,2,0:T(8,128)}, f32[192,96]{1,0:T(8,128)})) %all-reduce.28.cloned.1.call-update) | async-done | bytes 328720 | tf_op jit(solution)/shard_map/psum | solution.py:333
  (1483 shorter events, 711.6 us)
Async XLA Ops:
  7.2 469.7 %all-gather.19.cloned.1.call-start = ((), (), s32[]{:S(2)}) async-start(), calls=%async_computation.1 | async-start | bytes 12779520 | tf_op jit(solution)/shard_map/all_gather | solution.py:55
  8.3 15.6 collective-permute-start.1
  19.5 7.0 collective-permute-start
  26.5 11.2 collective-permute-start.2
  31.3 10.5 collective-permute-start.3
  49.6 562.7 %all-gather.17.cloned.1.call-start = ((), (), s32[]{:S(2)}) async-start(), calls=%async_computation | async-start | bytes 12779520 | tf_op jit(solution)/shard_map/all_gather | solution.py:55
  456.8 277.9 %copy-start.21 = (f32[16,8,16]{2,1,0:T(8,128)S(1)}, f32[16,8,16]{2,1,0:T(8,128)}, u32[]{:S(2)}) copy-start(f32[16,8,16]{2,1,0:T(8,128)} %copy.606) | copy-start | bytes 24580
  466.6 351.9 %copy-start.50 = (f32[16,8,16]{2,1,0:T(8,128)S(1)}, f32[16,8,16]{2,1,0:T(8,128)}, u32[]{:S(2)}) copy-start(f32[16,8,16]{2,1,0:T(8,128)} %copy-done.49) | copy-start | bytes 24580
  476.9 539.5 %all-gather.21.cloned.1.call-start = ((), (), s32[]{:S(2)}) async-start(), calls=%async_computation.2 | async-start | bytes 12779520 | tf_op jit(solution)/shard_map/all_gather | solution.py:55
  847.7 300.2 %all-gather.23.cloned.1.call-start = ((), (), s32[]{:S(2)}) async-start(), calls=%async_computation.3 | async-start | bytes 12779520 | tf_op jit(solution)/shard_map/all_gather | solution.py:55
  938.5 327.9 %copy-start.2 = (f32[8,16,3,64]{3,2,0,1:T(4,128)S(1)}, f32[8,16,3,64]{3,2,0,1:T(4,128)}, u32[]{:S(2)}) copy-start(f32[8,16,3,64]{3,2,0,1:T(4,128)} %copy-done.1) | copy-start | bytes 294916
  943.0 325.0 %copy-start.41 = (f32[8,16,3]{2,0,1:T(8,128)S(1)}, f32[8,16,3]{2,0,1:T(8,128)}, u32[]{:S(2)}) copy-start(f32[8,16,3]{2,0,1:T(8,128)} %copy-done.40) | copy-start | bytes 4612
  948.2 321.6 %copy-start.25 = (f32[8,16,3]{2,0,1:T(8,128)S(1)}, f32[8,16,3]{2,0,1:T(8,128)}, u32[]{:S(2)}) copy-start(f32[8,16,3]{2,0,1:T(8,128)} %copy-done.24) | copy-start | bytes 4612
  948.2 321.6 %copy-start.18 = (f32[8,1,16,3]{3,0,1,2:T(8,128)S(1)}, f32[8,1,16,3]{3,0,1,2:T(8,128)}, u32[]{:S(2)}) copy-start(f32[8,1,16,3]{3,0,1,2:T(8,128)} %copy-done.17) | copy-start | bytes 4612
  949.9 323.4 %copy-start.72 = (f32[8,16,3]{1,0,2:T(8,128)S(1)}, f32[8,16,3]{1,0,2:T(8,128)}, u32[]{:S(2)}) copy-start(f32[8,16,3]{1,0,2:T(8,128)} %copy-done.71) | copy-start | bytes 4612
  949.9 325.3 %copy-start.6 = (f32[8,16,3,64]{3,2,0,1:T(4,128)S(1)}, f32[8,16,3,64]{3,2,0,1:T(4,128)}, u32[]{:S(2)}) copy-start(f32[8,16,3,64]{3,2,0,1:T(4,128)} %copy-done.5) | copy-start | bytes 294916
  949.9 325.3 %copy-start.82 = (f32[8,16,3]{1,2,0:T(4,128)S(1)}, f32[8,16,3]{1,2,0:T(4,128)}, u32[]{:S(2)}) copy-start(f32[8,16,3]{1,2,0:T(4,128)} %copy-done.81) | copy-start | bytes 4612
  949.9 325.3 %copy-start.107 = (pred[16,16]{0,1:T(8,128)(4,1)S(1)}, pred[16,16]{0,1:T(8,128)(4,1)}, u32[]{:S(2)}) copy-start(pred[16,16]{0,1:T(8,128)(4,1)} %copy-done.106) | copy-start | bytes 772
  954.5 323.5 %copy-start.39 = (f32[8,16,3]{2,0,1:T(8,128)S(1)}, f32[8,16,3]{2,0,1:T(8,128)}, u32[]{:S(2)}) copy-start(f32[8,16,3]{2,0,1:T(8,128)} %copy-done.38) | copy-start | bytes 4612
  958.0 322.5 %copy-start.23 = (f32[8,16,3]{2,0,1:T(8,128)S(1)}, f32[8,16,3]{2,0,1:T(8,128)}, u32[]{:S(2)}) copy-start(f32[8,16,3]{2,0,1:T(8,128)} %copy-done.22) | copy-start | bytes 4612
  958.0 322.6 %copy-start.16 = (f32[8,1,16,3]{3,0,1,2:T(8,128)S(1)}, f32[8,1,16,3]{3,0,1,2:T(8,128)}, u32[]{:S(2)}) copy-start(f32[8,1,16,3]{3,0,1,2:T(8,128)} %copy-done.15) | copy-start | bytes 4612
  970.7 325.1 %copy-start.4 = (bf16[18,9,192]{2,1,0:T(8,128)(2,1)S(1)}, bf16[18,9,192]{2,1,0:T(8,128)(2,1)}, u32[]{:S(2)}) copy-start(bf16[18,9,192]{2,1,0:T(8,128)(2,1)} %copy-done.3) | copy-start | bytes 186628
  970.7 325.1 %copy-start.13 = (bf16[16,8,192]{2,1,0:T(8,128)(2,1)S(1)}, bf16[16,8,192]{2,1,0:T(8,128)(2,1)}, u32[]{:S(2)}) copy-start(bf16[16,8,192]{2,1,0:T(8,128)(2,1)} %copy-done.12) | copy-start | bytes 147460
  970.7 325.1 %copy-start.34 = (bf16[16,8,384]{2,1,0:T(8,128)(2,1)S(1)}, bf16[16,8,384]{2,1,0:T(8,128)(2,1)}, u32[]{:S(2)}) copy-start(bf16[16,8,384]{2,1,0:T(8,128)(2,1)} %copy-done.33) | copy-start | bytes 294916
  970.7 325.1 %copy-start.98 = (bf16[1,8,192]{2,1,0:T(8,128)(2,1)S(1)}, bf16[1,8,192]{2,1,0:T(8,128)(2,1)}, u32[]{:S(2)}) copy-start(bf16[1,8,192]{2,1,0:T(8,128)(2,1)} %copy-done.97) | copy-start | bytes 9220
  982.1 434.7 %copy-start.51 = (bf16[16,8,192]{2,1,0:T(8,128)(2,1)S(1)}, bf16[16,8,192]{2,1,0:T(8,128)(2,1)}, u32[]{:S(2)}) copy-start(bf16[16,8,192]{2,1,0:T(8,128)(2,1)} %get-tuple-element.1368) | copy-start | bytes 147460
  989.0 292.3 %copy-start.59 = (f32[8,16,3]{2,0,1:T(8,128)S(1)}, f32[8,16,3]{2,0,1:T(8,128)}, u32[]{:S(2)}) copy-start(f32[8,16,3]{2,0,1:T(8,128)} %copy.815) | copy-start | bytes 4612
  989.0 688.9 %all-reduce.28.cloned.1.call-start = ((), (), s32[]{:S(2)}) async-start(), calls=%async_computation.4 | async-start | bytes 819200 | tf_op jit(solution)/shard_map/psum | solution.py:333
  1289.4 111.3 %collective-permute-start.5 = (bf16[1,8,192]{2,1,0:T(8,128)(2,1)S(1)}, bf16[1,8,192]{2,1,0:T(8,128)(2,1)S(1)}, u32[]{:S(2)}, u32[]{:S(2)}) collective-permute-start(bf16[1,8,192]{2,1,0:T(8,128)(2,1)S(1)} %get-tuple-element.1393), channel_id=1, source_target_pairs={{8,0},{16,8},{24,16},{32,24},{40,32},{48,40},{56,48},{64,56},{72,6... | collective-permute-start | bytes 9224 | tf_op jit(solution)/shard_map/ppermute | solution.py:23
  1293.9 106.9 %collective-permute-start.4 = (bf16[1,8,192]{2,1,0:T(8,128)(2,1)S(1)}, bf16[1,8,192]{2,1,0:T(8,128)(2,1)S(1)}, u32[]{:S(2)}, u32[]{:S(2)}) collective-permute-start(bf16[1,8,192]{2,1,0:T(8,128)(2,1)S(1)} %get-tuple-element.1392), channel_id=1, source_target_pairs={{0,8},{8,16},{16,24},{24,32},{32,40},{40,48},{48,56},{56,64},{64,7... | collective-permute-start | bytes 9224 | tf_op jit(solution)/shard_map/ppermute | solution.py:22
  1400.8 12.1 collective-permute-start.6
  1406.3 9.6 collective-permute-start.7
  (108 other events, 8091.1 us)
Sparse Core Ops, SparseCore 0:
  49.7 124.5 all-gather.18
  477.0 135.2 all-gather.16
  847.8 168.4 all-gather.20
  1018.4 129.4 all-gather.22
  1417.9 260.0 all-reduce.27
where the time goes:
time: 1720 us; the launch traced here: 1690 us
  blocking collectives  587 us (34%)
  other arithmetic  342 us (20%)
  waiting for transfers between devices  322 us (19%)
  local copies, waits for them, and re-layouts  274 us (16%)
  matrix products  100 us (6%)
  starting transfers between devices  40 us (2%)
    all_gather x6, blocking collectives, carried_in(): lax.all_gather(a.astype(kind), axis)  353 us
    select_n x256, other arithmetic, step(): return jax.tree.map(lambda a, b: jnp.where(reached, a, b), new, before)  266 us
    psum x1, waiting for transfers between devices, local(): lax.psum((grad_in, grad_kernel, grad_cbias, jnp.stack(weight_grads), jnp....  259 us
    exp x526, local copies, waits for them, and re-layouts, combine(): jnp.exp(latter[0])[..., None, None] * earlier[1]  194 us
    all_gather x2, blocking collectives, prefix(): everything = jax.tree.map(lambda part: lax.all_gather(part, axis), value)  137 us
    psum x1, blocking collectives, local(): lax.psum((grad_in, grad_kernel, grad_cbias, jnp.stack(weight_grads), jnp....  97.7 us
    all_gather x4, waiting for transfers between devices, prefix(): everything = jax.tree.map(lambda part: lax.all_gather(part, axis), value)  52.7 us
  transfers between devices with their start and end apart: 13, of which 7 were waited for; matrix products, arithmetic and copies ran while one was open for 23% of the time, Pallas kernels for 0%

commit v1 on v0

v1 whole, which is shorter than its diff:
```python
from functools import partial

import jax
import jax.numpy as jnp
from jax import lax
from jax.experimental import pallas as pl
from jax.experimental.pallas import tpu as pltpu
from jax.sharding import PartitionSpec as P

D = 96
DI = 192
NS = 16
HEADS = 3
R = 16
C = 8
T = R * C
PITCH = 16

F32 = jnp.float32
BF = jnp.bfloat16
HI = lax.Precision.HIGHEST
FAR = -1e30


def dot(a, b, ca=1, cb=0, precision=None):
    return lax.dot_general(
        a, b, (((ca,), (cb,)), ((), ())), precision=precision, preferred_element_type=F32
    )


def iota(shape, dim):
    return lax.broadcasted_iota(jnp.int32, shape, dim)


def mask(k):
    t, s = (iota((T, T), 0), iota((T, T), 1))
    rt, ct, rs, cs = (t >> 3, t & 7, s >> 3, s & 7)
    if k == 0:
        return (rt == rs) & (cs <= ct)
    if k == 1:
        return (rt == rs) & (cs >= ct)
    if k == 2:
        return (ct == cs) & (rs <= rt)
    return (ct == cs) & (rs >= rt)


def same_line(vertical):
    t, s = (iota((T, T), 0), iota((T, T), 1))
    return (t & 7) == (s & 7) if vertical else (t >> 3) == (s >> 3)


def pick_lanes(parts):
    lane = iota((T, T), 1) // 3
    out = parts[3]
    for k in range(3):
        out = jnp.where(lane == k, parts[k], out)
    return out


def as_f32(m):
    return jnp.where(m, 1.0, 0.0).astype(F32)


def lines_of(k):
    return R if k < 2 else C


def half_of(k):
    return lines_of(k) * 8


def spread_states(bc, k):
    lines, half = (lines_of(k), half_of(k))
    i, j = (iota((T, 2 * half), 0), iota((T, 2 * half), 1))
    n = 2 * (j & 7) + j // half
    wide = dot(bc, as_f32(i == 16 * k + n), precision=HI)
    return jnp.where(on_line(k), wide, 0.0)


def on_line(k):
    lines, half = (lines_of(k), half_of(k))
    t, j = (iota((T, 2 * half), 0), iota((T, 2 * half), 1))
    line = t >> 3 if k < 2 else t & 7
    return ((j >> 3) & (lines - 1)) == line


def gather_states(wide, k):
    half = half_of(k)
    j, i = (iota((2 * half, T), 0), iota((2 * half, T), 1))
    n = 2 * (j & 7) + j // half
    return dot(jnp.where(on_line(k), wide, 0.0), as_f32(i == 16 * k + n), precision=HI)


def by_head(values, k):
    lane = iota((T, DI), 1)
    a, b, c = (values[:, 3 * k + h : 3 * k + h + 1] for h in range(HEADS))
    return jnp.where(lane < 64, a, jnp.where(lane < 128, b, c))


def head_sum(wide, k):
    c, j = (iota((DI, T), 0), iota((DI, T), 1))
    return dot(wide, as_f32(j == 3 * k + c // 64), precision=HI)


def per_head(f):
    lane = iota((T, DI), 1)
    a, b, c = (f(h) for h in range(HEADS))
    return jnp.where(lane < 64, a, jnp.where(lane < 128, b, c))


def write_message(ref, states, totals, k_first):
    half = half_of(k_first)
    for d in range(2):
        s = states[d]
        for h in range(HEADS):
            ref[:, d * 3 + h, :] = jnp.concatenate(
                [s[:half, 64 * h : 64 * h + 64], s[half:, 64 * h : 64 * h + 64]], axis=1
            )
    j, t = (iota((half, T), 0), iota((half, T), 1))
    sel = as_f32(t == ((j >> 3) if k_first == 2 else (j >> 3) * 8))
    if k_first == 2:
        i, o = (iota((T, T), 0), iota((T, T), 1))
        totals = dot(totals, as_f32(i == o + 6), precision=HI)
    ref[:, 6, :] = dot(sel, totals, precision=HI)
    ref[:, 7, :] = jnp.zeros((half, T), F32)


def read_message(ref, d):
    x = [ref[:, d * 3 + h, :] for h in range(HEADS)]
    top = jnp.concatenate([v[:, :64] for v in x], axis=1)
    bottom = jnp.concatenate([v[:, 64:] for v in x], axis=1)
    return jnp.concatenate([top, bottom], axis=0)


def chain_kernel(backward, got_ref, out_ref):
    n, m = (got_ref.shape[0], got_ref.shape[1])
    sub = iota((m, 8, 128), 1)
    lane = iota((m, 8, 128), 2)
    ahead = sub < 3 if not backward else sub >= 3

    def factor(i):
        row = jnp.broadcast_to(got_ref[i, :, 6:7, :], (m, 8, 128))
        return jnp.sum(jnp.where(lane == sub, row, 0.0), axis=2, keepdims=True)

    up = jnp.zeros((m, 8, 128), F32)
    for i in range(n):
        out_ref[i] = up
        if i < n - 1:
            up = factor(i) * up + got_ref[i]
    down = jnp.zeros((m, 8, 128), F32)
    for i in range(n - 1, -1, -1):
        out_ref[i] = jnp.where(ahead, out_ref[i], down)
        if i > 0:
            down = factor(i) * down + got_ref[i]


def sigmoid(x):
    return jax.nn.sigmoid(x)


def softplus(x):
    return jnp.maximum(x, 0.0) + jnp.log1p(jnp.exp(-jnp.abs(x)))


def conv_in(tok_ref, wbr_ref):
    branch = dot(tok_ref[...], wbr_ref[...]).astype(BF).astype(F32)
    return branch.reshape(R + 2, PITCH, DI)


def first_kernel(
    tok_ref, wbr_ref, cw_ref, cb_ref, wd_ref, wbc_ref, sb_ref, ld_ref,
    before_ref, act_ref, rawd_ref, bc_ref, step_ref, log_ref, tot_ref, mv_ref, mh_ref,
):
    padded = conv_in(tok_ref, wbr_ref)
    total = jnp.zeros((R, C, DI), F32)
    for b in range(3):
        shifted = padded[:, b : b + C, :]
        for a in range(3):
            total = total + cw_ref[3 * a + b : 3 * a + b + 1, :] * shifted[a : a + R]
    before = total.reshape(T, DI) + cb_ref[...]
    act = (before * sigmoid(before)).astype(BF)
    before_ref[...] = before
    act_ref[...] = act
    raw_d = dot(act, wd_ref[...])
    bc = dot(act, wbc_ref[...])
    step = softplus(raw_d + sb_ref[...])
    log_step = step * -jnp.exp(ld_ref[...])
    log = pick_lanes([dot(as_f32(mask(k)), log_step, precision=HI) for k in range(4)])
    rows, cols = (dot(as_f32(same_line(v)), log_step, precision=HI) for v in (False, True))
    tot = pick_lanes([rows, rows, cols, cols])
    rawd_ref[...] = raw_d
    bc_ref[...] = bc
    step_ref[...] = step
    log_ref[...] = log
    tot_ref[...] = tot
    weight = jnp.exp(tot - log) * step
    wide = act.astype(F32)
    states = [
        dot(spread_states(bc, k), by_head(weight, k) * wide, 0, 0, HI) for k in range(4)
    ]
    factor = jnp.exp(tot)
    write_message(mv_ref, states[2:], factor, 2)
    write_message(mh_ref, states[:2], factor, 0)


def tables(k, bc, out_gate):
    lane = iota((T, T), 1) >> 4
    return dot(jnp.where(lane == k, out_gate, 0.0), bc, 1, 1, HI)


def decay(k, h, log, log_t):
    i = 3 * k + h
    return jnp.exp(jnp.where(mask(k), log[:, i : i + 1] - log_t[i : i + 1, :], FAR))


def shifted_gate(bc):
    return pltpu.roll(bc, 64, 1)


def local_kernel(act_ref, bc_ref, step_ref, log_ref, y_ref):
    bc = bc_ref[...]
    out_gate = shifted_gate(bc)
    log = log_ref[...]
    log_t, step_t = (log.T, step_ref[...].T)
    weights = [jnp.zeros((T, T), F32)] * HEADS
    for k in range(4):
        scores = tables(k, bc, out_gate)
        for h in range(HEADS):
            i = 3 * k + h
            weights[h] = weights[h] + scores * (
                decay(k, h, log, log_t) * step_t[i : i + 1, :]
            )
    wide = act_ref[...].astype(F32)
    y_ref[...] = per_head(lambda h: dot(weights[h], wide, precision=HI))


def carry(k, out_gate, exp_log, state):
    return by_head(exp_log, k) * dot(spread_states(out_gate, k), state, precision=HI)


def norm_kernel(
    y_ref, act_ref, bc_ref, log_ref, tot_ref, sv_ref, sh_ref, skip_ref, tok_ref, wg_ref, gain_ref,
    nb_ref, ow_ref, cot_ref,
    out_ref, g_ref, dgate_ref, gated_ref, norms_ref, mv_ref, mh_ref,
):
    bc = bc_ref[...]
    out_gate = shifted_gate(bc)
    exp_log = jnp.exp(log_ref[...])
    summed = y_ref[...] + skip_ref[...] * act_ref[...].astype(F32)
    for k in range(4):
        state = read_message(sh_ref if k < 2 else sv_ref, k % 2)
        summed = summed + carry(k, out_gate, exp_log, state)
    gate = dot(tok_ref[...], wg_ref[...]).astype(BF).astype(F32)
    sig = sigmoid(gate)
    center = summed - jnp.mean(summed, axis=1, keepdims=True)
    inv = lax.rsqrt(jnp.mean(center * center, axis=1, keepdims=True) + 1e-5)
    unit = center * inv
    normed = unit * gain_ref[...] + nb_ref[...]
    gated = (normed * gate * sig).astype(BF)
    gated_ref[...] = gated
    out_ref[...] = dot(gated, ow_ref[...]).astype(BF)
    grad = dot(cot_ref[...], ow_ref[...], 1, 1)
    dnormed = grad * gate * sig
    dgate_ref[...] = (grad * normed * (sig * (1.0 + gate * (1.0 - sig)))).astype(BF)
    norms_ref[0:1, :] = jnp.sum(dnormed * unit, axis=0, keepdims=True)
    norms_ref[1:2, :] = jnp.sum(dnormed, axis=0, keepdims=True)
    dunit = dnormed * gain_ref[...]
    g = inv * (
        dunit
        - jnp.mean(dunit, axis=1, keepdims=True)
        - unit * jnp.mean(dunit * unit, axis=1, keepdims=True)
    )
    g = g.astype(BF)
    g_ref[...] = g
    g = g.astype(F32)
    states = [
        dot(spread_states(out_gate, k), by_head(exp_log, k) * g, 0, 0, HI) for k in range(4)
    ]
    factor = jnp.exp(tot_ref[...])
    write_message(mv_ref, states[2:], factor, 2)
    write_message(mh_ref, states[:2], factor, 0)


def back_kernel(
    act_ref, bc_ref, step_ref, log_ref, g_ref, sv_ref, sh_ref,
    dact_ref, dbc_ref, dstep_ref, dlog_ref,
):
    bc = bc_ref[...]
    out_gate = shifted_gate(bc)
    log = log_ref[...]
    step = step_ref[...]
    log_t, step_t = (log.T, step.T)
    exp_log = jnp.exp(log)
    act = act_ref[...]
    g = g_ref[...]
    gw = g.astype(F32)
    lane = iota((T, DI), 1) // 64
    lane16 = iota((T, T), 1) >> 4
    lane1 = iota((T, T), 1)
    pair = [dot(jnp.where(lane == h, g, jnp.zeros_like(g)), act, 1, 1) for h in range(HEADS)]
    weights = [jnp.zeros((T, T), F32)] * HEADS
    d_in = jnp.zeros((T, T), F32)
    d_out = jnp.zeros((T, T), F32)
    row_sums = jnp.zeros((T, T), F32)
    step_rows = []
    for k in range(4):
        scores = tables(k, bc, out_gate)
        d_scores = jnp.zeros((T, T), F32)
        for h in range(HEADS):
            i = 3 * k + h
            dec = decay(k, h, log, log_t)
            dec_step = dec * step_t[i : i + 1, :]
            weights[h] = weights[h] + scores * dec_step
            d_scores = d_scores + pair[h] * dec_step
            d_step = pair[h] * dec * scores
            step_rows.append(jnp.sum(d_step, axis=0, keepdims=True))
            rows = jnp.sum(d_step * step_t[i : i + 1, :], axis=1, keepdims=True)
            row_sums = jnp.where(lane1 == i, rows, row_sums)
        d_out = d_out + dot(d_scores, jnp.where(lane16 == k, bc, 0.0), precision=HI)
        d_in = d_in + dot(d_scores, jnp.where(lane16 == k, out_gate, 0.0), 0, 0, HI)
        state = read_message(sh_ref if k < 2 else sv_ref, k % 2)
        expg = by_head(exp_log, k) * gw
        carried = dot(spread_states(out_gate, k), state, precision=HI)
        row_sums = row_sums + head_sum(carried * expg, k)
        d_out = d_out + gather_states(dot(expg, state, 1, 1, HI), k)
    d_step = jnp.concatenate(step_rows + [jnp.zeros((T - 12, T), F32)], axis=0).T
    dact_ref[...] = per_head(lambda h: dot(weights[h], gw, 0, 0, HI))
    dbc_ref[...] = d_in + pltpu.roll(d_out, 64, 1)
    dstep_ref[...] = d_step
    dlog_ref[...] = row_sums - step * d_step


def gate_grads_kernel(tok_ref, dgate_ref, gated_ref, cot_ref, gin_ref, gout_ref):
    gin_ref[...] = dot(tok_ref[...], dgate_ref[...], 0, 0)
    gout_ref[...] = dot(cot_ref[...], gated_ref[...], 0, 0)


def last_kernel(
    tok_ref, wbr_ref, cw_ref, before_ref, act_ref, rawd_ref, bc_ref, step_ref, log_ref, tot_ref, g_ref,
    sv_ref, sh_ref, lv_ref, lh_ref, dact_ref, dbc_ref, dstep_ref, dlog_ref, skip_ref, wd_ref, wbc_ref,
    sb_ref, ld_ref, gin_gate_ref, gout_ref, norms_ref,
    gb_ref, pack_ref,
):
    step, log, tot, bc = (step_ref[...], log_ref[...], tot_ref[...], bc_ref[...])
    act = act_ref[...]
    wide = act.astype(F32)
    g = g_ref[...].astype(F32)
    d_act = dact_ref[...] + skip_ref[...] * g
    d_bc = dbc_ref[...]
    to_end = jnp.exp(tot - log)
    weight = to_end * step
    through = jnp.exp(tot)
    inner = jnp.zeros((T, T), F32)
    cross = jnp.zeros((T, T), F32)
    for k in range(4):
        later = read_message(lh_ref if k < 2 else lv_ref, k % 2)
        earlier = read_message(sh_ref if k < 2 else sv_ref, k % 2)
        reach = dot(spread_states(bc, k), later, precision=HI)
        wk = by_head(weight, k)
        d_act = d_act + wk * reach
        inner = inner + head_sum(wide * reach, k)
        d_bc = d_bc + gather_states(dot(wk * wide, later, 1, 1, HI), k)
        cross = cross + dot(as_f32(on_line(k)), head_sum(later * earlier, k), precision=HI)
    d_step = dstep_ref[...] + to_end * inner
    left = weight * inner
    d_log = dlog_ref[...]
    parts = []
    for k in range(4):
        m = as_f32(mask(k))
        rest = as_f32(same_line(k >= 2)) - m.T
        parts.append(dot(m, d_log, 0, 0, HI) + dot(rest, left, precision=HI))
    d_log_step = pick_lanes(parts) + cross * through
    rate = -jnp.exp(ld_ref[...])
    d_rate = jnp.sum(d_log_step * step, axis=0, keepdims=True) * rate
    d_raw = (d_step + rate * d_log_step) * sigmoid(rawd_ref[...] + sb_ref[...])
    live = iota((T, T), 1) < 12
    d_raw = jnp.where(live, d_raw, 0.0)
    d_bias = jnp.sum(d_raw, axis=0, keepdims=True)
    d_raw = d_raw.astype(BF)
    d_bc = d_bc.astype(BF)
    d_act = d_act + dot(d_raw, wd_ref[...], 1, 1) + dot(d_bc, wbc_ref[...], 1, 1)
    before = before_ref[...]
    sig = sigmoid(before)
    gb = (d_act * sig * (1.0 + before * (1.0 - sig))).astype(BF)
    gb_ref[...] = gb
    gbw = gb.astype(F32)
    padded = conv_in(tok_ref, wbr_ref)
    tok = tok_ref[...].astype(F32).reshape(R + 2, PITCH, D)
    gin = jnp.zeros((D, DI), F32)
    conv_rows = [None] * 9
    for b in range(3):
        near = padded[:, b : b + C, :]
        near_tok = tok[:, b : b + C, :]
        for a in range(3):
            i = 3 * a + b
            conv_rows[i] = jnp.sum(gbw * near[a : a + R].reshape(T, DI), axis=0, keepdims=True)
            gin = gin + cw_ref[i : i + 1, :] * dot(
                near_tok[a : a + R].reshape(T, D).astype(BF), gb, 0, 0
            )
    wide_row = lambda x: jnp.concatenate([x, jnp.zeros((1, DI - T), F32)], axis=1)
    small = jnp.concatenate(
        conv_rows
        + [
            jnp.sum(gbw, axis=0, keepdims=True),
            jnp.sum(g * wide, axis=0, keepdims=True),
            norms_ref[0:1, :],
            norms_ref[1:2, :],
            wide_row(d_bias),
            wide_row(jnp.where(live[:1], d_rate, 0.0)),
            jnp.zeros((1, DI), F32),
        ],
        axis=0,
    )
    both = [
        gin, gin_gate_ref[...], gout_ref[...], small, dot(d_bc, act, 0, 0),
        dot(d_raw, act, 0, 0)[:16],
    ]
    full = jnp.concatenate(both, axis=0)
    pack_ref[0:448, :] = full[:, :128]
    pack_ref[448:672, :] = jnp.concatenate([full[:224, 128:], full[224:, 128:]], axis=1)


def out_kernel(gb_ref, cw_ref, dgate_ref, wbr_ref, wg_ref, out_ref):
    padded = gb_ref[...].astype(F32).reshape(R + 2, PITCH, DI)
    total = jnp.zeros((R, C, DI), F32)
    for b in range(3):
        shifted = padded[:, 2 - b : 2 - b + C, :]
        for a in range(3):
            total = total + cw_ref[3 * a + b : 3 * a + b + 1, :] * shifted[2 - a : 2 - a + R]
    d_branch = total.reshape(T, DI).astype(BF)
    out_ref[...] = (
        dot(d_branch, wbr_ref[...], 1, 1) + dot(dgate_ref[...], wg_ref[...], 1, 1)
    ).astype(BF)


def call(kernel, outs, *args, flops=10**8):
    whole = pl.BlockSpec(memory_space=pltpu.VMEM)
    return pl.pallas_call(
        kernel,
        out_shape=[jax.ShapeDtypeStruct(s, t) for s, t in outs],
        in_specs=[whole] * len(args),
        out_specs=[whole] * len(outs),
        compiler_params=pltpu.CompilerParams(vmem_limit_bytes=40 * 2**20),
        cost_estimate=pl.CostEstimate(flops=flops, bytes_accessed=10**6, transcendentals=0),
    )(*args)


def shift_over(x, axes, steps):
    sizes = [lax.axis_size(a) for a in axes]
    pairs = []
    if len(axes) == 1:
        for i in range(sizes[0]):
            if 0 <= i + steps[0] < sizes[0]:
                pairs.append((i + steps[0], i))
        return lax.ppermute(x, axes[0], pairs)
    for i in range(sizes[0]):
        for j in range(sizes[1]):
            a, b = (i + steps[0], j + steps[1])
            if 0 <= a < sizes[0] and 0 <= b < sizes[1]:
                pairs.append((a * sizes[1] + b, i * sizes[1] + j))
    return lax.ppermute(x, axes, pairs)


def with_rim(x):
    both = ("row", "col")
    up = shift_over(x[-1:], ("row",), (-1,))
    down = shift_over(x[:1], ("row",), (1,))
    left = shift_over(x[:, -1:], ("col",), (-1,))
    right = shift_over(x[:, :1], ("col",), (1,))
    corner = {
        (i, j): shift_over(
            x[-1:, -1:] if (i, j) == (-1, -1)
            else x[-1:, :1] if (i, j) == (-1, 1)
            else x[:1, -1:] if (i, j) == (1, -1)
            else x[:1, :1],
            both,
            (i, j),
        )
        for i in (-1, 1)
        for j in (-1, 1)
    }
    top = jnp.concatenate([corner[-1, -1], up, corner[-1, 1]], axis=1)
    mid = jnp.concatenate([left, x, right], axis=1)
    low = jnp.concatenate([corner[1, -1], down, corner[1, 1]], axis=1)
    full = jnp.concatenate([top, mid, low], axis=0)
    full = jnp.pad(full, ((0, 0), (0, PITCH - C - 2), (0, 0)))
    return full.reshape((R + 2) * PITCH, x.shape[-1])


def exchange(message, axis, backward):
    size = lax.axis_size(axis)
    got = lax.all_to_all(message, axis, 0, 0, tiled=True)
    shape = (size, message.shape[0] // size, 8, 128)
    (states,) = call(partial(chain_kernel, backward), [(shape, F32)], got.reshape(shape), flops=10**7)
    return lax.all_to_all(states.reshape(message.shape), axis, 0, 0, tiled=True)


def local(
    tokens, in_weight, conv_weight, conv_bias, scan_weight, step_bias, log_decay, skip_gain, norm_gain,
    norm_bias, out_weight, cotangent,
):
    own = tokens.reshape(T, D)
    halo = with_rim(tokens.reshape(R, C, D))
    cot = cotangent.reshape(T, D)
    w_branch, w_gate = (in_weight[:, :DI], in_weight[:, DI:])
    taps = jnp.pad(conv_weight.reshape(9, DI), ((0, 7), (0, 0)))
    by_channel = jnp.moveaxis(scan_weight, 1, 0)
    w_step = jnp.pad(by_channel[:, :, :HEADS].reshape(DI, 12), ((0, 0), (0, 116)))
    w_bc = jnp.concatenate(
        [
            by_channel[:, :, HEADS : HEADS + NS].reshape(DI, 64),
            by_channel[:, :, HEADS + NS :].reshape(DI, 64),
        ],
        axis=1,
    )
    row = lambda x: x.reshape(1, -1)
    bias = jnp.pad(row(step_bias), ((0, 0), (0, 116)))
    rate = jnp.pad(row(log_decay), ((0, 0), (0, 116)))
    skip = row(jnp.sum(skip_gain, axis=0))
    square = ((T, T), F32)
    wide = ((T, DI), F32)
    low = ((T, DI), BF)
    msg_v, msg_h = (((64, 8, 128), F32), ((128, 8, 128), F32))

    before, act, raw_d, bc, step, log, tot, mv, mh = call(
        first_kernel, [wide, low, square, square, square, square, square, msg_v, msg_h],
        halo, w_branch, taps, row(conv_bias), w_step, w_bc, bias, rate,
    )
    sv = exchange(mv, "row", False)
    sh = exchange(mh, "col", False)
    (y,) = call(local_kernel, [wide], act, bc, step, log)
    out, g, d_gate, gated, norms, mv, mh = call(
        norm_kernel, [((T, D), BF), low, low, low, ((8, DI), F32), msg_v, msg_h],
        y, act, bc, log, tot, sv, sh, skip, own, w_gate, row(norm_gain), row(norm_bias), out_weight, cot,
    )
    lv = exchange(mv, "row", True)
    lh = exchange(mh, "col", True)
    d_act, d_bc, d_step, d_log = call(
        back_kernel, [wide, square, square, square], act, bc, step, log, g, sv, sh
    )
    gin_gate, gout = call(
        gate_grads_kernel, [((D, DI), F32), ((D, DI), F32)], own, d_gate, gated, cot, flops=10**7
    )
    gb, pack = call(
        last_kernel, [low, ((672, 128), F32)],
        halo, w_branch, taps, before, act, raw_d, bc, step, log, tot, g, sv, sh, lv, lh, d_act, d_bc, d_step,
        d_log, skip, w_step, w_bc, bias, rate, gin_gate, gout, norms,
    )
    total = lax.psum(pack, ("row", "col"))
    gb_halo = with_rim(gb.reshape(R, C, DI))
    (d_tokens,) = call(out_kernel, [((T, D), BF)], gb_halo, taps, d_gate, w_branch, w_gate)
    scale = float(T * lax.axis_size("row") * lax.axis_size("col")) ** (-0.5)
    total = total * scale
    full = jnp.concatenate(
        [total[:448], jnp.concatenate([total[448:, :64], total[448:, 64:]], axis=0)], axis=1
    )
    small = full[288:304]
    g_bc = full[304:432].reshape(2, 4, NS, DI)
    g_step = full[432:444].reshape(4, HEADS, DI)
    g_scan = jnp.concatenate([g_step, g_bc[0], g_bc[1]], axis=1)
    return (
        out.reshape(R, C * D),
        d_tokens.reshape(R, C * D),
        jnp.concatenate([full[:96], full[96:192]], axis=1),
        small[:9].reshape(3, 3, DI),
        small[9],
        jnp.swapaxes(g_scan, 1, 2),
        small[13, :12].reshape(4, HEADS),
        small[14, :12].reshape(4, HEADS),
        jnp.broadcast_to(small[10], (4, DI)),
        small[11],
        small[12],
        full[192:288].T,
    )


def solution(mesh):
    in_specs = (P("row", "col"), P(), P(), P(), P(), P(), P(), P(), P(), P(), P(), P("row", "col"))
    out_specs = (P("row", "col"), P("row", "col"), P(), P(), P(), P(), P(), P(), P(), P(), P(), P())
    return jax.shard_map(local, mesh=mesh, in_specs=in_specs, out_specs=out_specs, check_vma=False)
```

time: 1720 us -> 525 us (0.31); the launches traced: 1690 us -> 519 us
  blocking collectives: 587 us -> 40.2 us
  other arithmetic: 342 us -> 3.36 us
  local copies, waits for them, and re-layouts: 274 us -> 11.6 us
  matrix products: 100 us -> 0 us
  starting transfers between devices: 40 us -> 131 us
  waiting for transfers between devices: 322 us -> 292 us
  Pallas kernels: 0 us -> 26.2 us
    all_gather x8 -> x0, blocking collectives: 489 us -> none  [the longest x6 353 us: carried_in(): lax.all_gather(a.astype(kind), axis)]
    select_n x258 -> x0, other arithmetic: 267 us -> none  [the longest x256 266 us: step(): return jax.tree.map(lambda a, b: jnp.where(reached, a, b), new, before)]
    exp x542 -> x0, local copies, waits for them, and re-layouts: 202 us -> none  [the longest x526 194 us: combine(): jnp.exp(latter[0])[..., None, None] * earlier[1]]
    dot_general x79 -> x0, matrix products: 100 us -> none  [the longest x16 23.8 us: carried(): jnp.einsum('mln,mlh,mhpn->mlhp', out_gate, jnp.exp(log_full), state_in, p...]
    psum x1 -> x0, blocking collectives: 97.7 us -> none  [local(): lax.psum((grad_in, grad_kernel, grad_cbias, jnp.stack(weight_grads), jnp....]
    psum x1, waiting for transfers between devices: 259 us -> 202 us  [local(): total = lax.psum(pack, ('row', 'col'))]
    all_to_all x0 -> x6, starting transfers between devices: none -> 55.4 us  [the longest x4 36.8 us: exchange(): return lax.all_to_all(states.reshape(message.shape), axis, 0, 0, tiled=True)]
    all_gather x4 -> x0, waiting for transfers between devices: 52.7 us -> none  [prefix(): everything = jax.tree.map(lambda part: lax.all_gather(part, axis), value)]
  transfers between devices with their start and end apart: 13 -> 23, of which waited for: 7 -> 14; matrix products, arithmetic and copies ran while one was open for 23% -> 1% of each run, Pallas kernels for 0% -> 2%
where the time goes in v1:
time: 525 us; the launch traced here: 519 us
  waiting for transfers between devices  292 us (56%)
  starting transfers between devices  131 us (25%)
  blocking collectives  40.2 us (8%)
  Pallas kernels  26.2 us (5%)
  between operations  14.5 us (3%)
  local copies, waits for them, and re-layouts  11.6 us (2%)
    psum x1, waiting for transfers between devices, local(): total = lax.psum(pack, ('row', 'col'))  202 us
    ppermute x8, starting transfers between devices, shift_over(): return lax.ppermute(x, axes[0], pairs)  41.4 us
    all_to_all x2, blocking collectives, exchange(): got = lax.all_to_all(message, axis, 0, 0, tiled=True)  40.2 us
    ppermute x8, waiting for transfers between devices, shift_over(): return lax.ppermute(x, axes, pairs)  37.9 us
    all_to_all x4, starting transfers between devices, exchange(): return lax.all_to_all(states.reshape(message.shape), axis, 0, 0, tiled=True)  36.8 us
    ppermute x8, starting transfers between devices, shift_over(): return lax.ppermute(x, axes, pairs)  34.6 us
    all_to_all x4, waiting for transfers between devices, exchange(): return lax.all_to_all(states.reshape(message.shape), axis, 0, 0, tiled=True)  33.7 us
    pallas_call x11, Pallas kernels, call(): pl.pallas_call(kernel, out_shape=[jax.ShapeDtypeStruct(s, t) for s, t in...  26.2 us
  transfers between devices with their start and end apart: 23, of which 14 were waited for; matrix products, arithmetic and copies ran while one was open for 1% of the time, Pallas kernels for 2%

profile of v1, /device:TPU:56, one launch (start us, length us, event | category | flops | bytes accessed | tf_op | source)
XLA Modules:
  0.0 519.3 jit_solution(4175898569791676650)
XLA Ops:
  8.1 11.2 %collective-permute-start.6 = (bf16[1,8,96]{2,1,0:T(8,128)(2,1)S(1)}, bf16[1,8,96]{2,1,0:T(8,128)(2,1)S(1)}, u32[]{:S(2)}, u32[]{:S(2)}) collective-permute-start(bf16[1,8,96]{2,1,0:T(8,128)(2,1)S(1)} %slice.148), channel_id=1, source_target_pairs={{8,0},{16,8},{24,16},{32,24},{40,32},{48,40},{56,48},{64,56},{72,6... | collective-permute-start | bytes 4616 | tf_op jit(solution)/shard_map/ppermute | solution.py:455
  24.0 4.7 collective-permute-start.3
  28.8 5.0 collective-permute-start.4
  36.4 4.8 collective-permute-start.7
  41.2 4.9 collective-permute-done.7
  46.0 10.3 %collective-permute-start.5 = (bf16[1,1,96]{2,1,0:T(2,128)(2,1)S(1)}, bf16[1,1,96]{2,1,0:T(2,128)(2,1)S(1)}, u32[]{:S(2)}, u32[]{:S(2)}) collective-permute-start(bf16[1,1,96]{2,1,0:T(2,128)(2,1)S(1)} %get-tuple-element.113), channel_id=1, source_target_pairs={{8,1},{9,2},{10,3},{11,4},{12,5},{13,6},{14,7},{16,9},{17,10},{18,... | collective-permute-start | bytes 584 | tf_op jit(solution)/shard_map/ppermute | solution.py:461
  59.7 8.8 %collective-permute-done.2 = bf16[1,1,96]{2,1,0:T(2,128)(2,1)S(1)} collective-permute-done((bf16[1,1,96]{2,1,0:T(2,128)(2,1)S(1)}, bf16[1,1,96]{2,1,0:T(2,128)(2,1)S(1)}, u32[]{:S(2)}, u32[]{:S(2)}) %collective-permute-start.2) | collective-permute-done | bytes 224 | tf_op jit(solution)/shard_map/ppermute | solution.py:461
  73.0 19.8 %all_to_all.40 = f32[64,8,128]{2,1,0:T(8,128)S(1)} all-to-all(f32[64,8,128]{2,1,0:T(8,128)S(1)} %get-tuple-element.41), channel_id=1, replica_groups=mesh['row'=64,'col'=8] {'row'}, dimensions={0} | all-to-all | bytes 524288 | tf_op jit(solution)/shard_map/all_to_all | solution.py:492
  92.9 9.4 %all-to-all-start.2 = ((f32[128,8,128]{2,1,0:T(8,128)}), f32[128,8,128]{2,1,0:T(8,128)S(1)}, u32[]{:S(2)}, u32[]{:S(2)}) async-start(f32[128,8,128]{2,1,0:T(8,128)} %get-tuple-element.42), calls=%async_computation.2 | async-start | bytes 1048576 | tf_op jit(solution)/shard_map/all_to_all | solution.py:492
  103.1 9.3 %all-to-all-done.2 = f32[128,8,128]{2,1,0:T(8,128)S(1)} async-done(((f32[128,8,128]{2,1,0:T(8,128)}), f32[128,8,128]{2,1,0:T(8,128)S(1)}, u32[]{:S(2)}, u32[]{:S(2)}) %all-to-all-start.2) | async-done | bytes 524320 | tf_op jit(solution)/shard_map/all_to_all | solution.py:492
  112.4 9.2 %all-to-all-start.1 = ((f32[64,8,128]{2,1,0:T(8,128)}), f32[64,8,128]{2,1,0:T(8,128)S(1)}, u32[]{:S(2)}, u32[]{:S(2)}) async-start(f32[64,8,128]{2,1,0:T(8,128)} %bitcast.6), calls=%async_computation.1 | async-start | bytes 524288 | tf_op jit(solution)/shard_map/all_to_all | solution.py:495
  122.7 10.4 %all-to-all-done.1.sv_ref = f32[64,8,128]{2,1,0:T(8,128)S(1)} async-done(((f32[64,8,128]{2,1,0:T(8,128)}), f32[64,8,128]{2,1,0:T(8,128)S(1)}, u32[]{:S(2)}, u32[]{:S(2)}) %all-to-all-start.1) | async-done | bytes 262176 | tf_op jit(solution)/shard_map/all_to_all | solution.py:495
  133.1 9.3 %all-to-all-start.3 = ((f32[128,8,128]{2,1,0:T(8,128)}), f32[128,8,128]{2,1,0:T(8,128)S(1)}, u32[]{:S(2)}, u32[]{:S(2)}) async-start(f32[128,8,128]{2,1,0:T(8,128)} %bitcast.8), calls=%async_computation.3 | async-start | bytes 1048576 | tf_op jit(solution)/shard_map/all_to_all | solution.py:495
  144.6 8.2 %all-to-all-done.3.sh_ref = f32[128,8,128]{2,1,0:T(8,128)S(1)} async-done(((f32[128,8,128]{2,1,0:T(8,128)}), f32[128,8,128]{2,1,0:T(8,128)S(1)}, u32[]{:S(2)}, u32[]{:S(2)}) %all-to-all-start.3) | async-done | bytes 524320 | tf_op jit(solution)/shard_map/all_to_all | solution.py:495
  153.5 3.9 shard_map.215
  157.4 20.4 %all_to_all.41 = f32[64,8,128]{2,1,0:T(8,128)S(1)} all-to-all(f32[64,8,128]{2,1,0:T(8,128)S(1)} %get-tuple-element.47), channel_id=1, replica_groups=mesh['row'=64,'col'=8] {'row'}, dimensions={0} | all-to-all | bytes 524288 | tf_op jit(solution)/shard_map/all_to_all | solution.py:492
  177.7 9.2 %all-to-all-start.6 = ((f32[128,8,128]{2,1,0:T(8,128)}), f32[128,8,128]{2,1,0:T(8,128)S(1)}, u32[]{:S(2)}, u32[]{:S(2)}) async-start(f32[128,8,128]{2,1,0:T(8,128)} %get-tuple-element.48), calls=%async_computation.6 | async-start | bytes 1048576 | tf_op jit(solution)/shard_map/all_to_all | solution.py:492
  187.9 9.6 %all-to-all-done.6 = f32[128,8,128]{2,1,0:T(8,128)S(1)} async-done(((f32[128,8,128]{2,1,0:T(8,128)}), f32[128,8,128]{2,1,0:T(8,128)S(1)}, u32[]{:S(2)}, u32[]{:S(2)}) %all-to-all-start.6) | async-done | bytes 524320 | tf_op jit(solution)/shard_map/all_to_all | solution.py:492
  197.4 9.2 %all-to-all-start.5 = ((f32[64,8,128]{2,1,0:T(8,128)}), f32[64,8,128]{2,1,0:T(8,128)S(1)}, u32[]{:S(2)}, u32[]{:S(2)}) async-start(f32[64,8,128]{2,1,0:T(8,128)} %bitcast.13), calls=%async_computation.5 | async-start | bytes 524288 | tf_op jit(solution)/shard_map/all_to_all | solution.py:495
  207.7 10.4 %all-to-all-done.5.lv_ref = f32[64,8,128]{2,1,0:T(8,128)S(1)} async-done(((f32[64,8,128]{2,1,0:T(8,128)}), f32[64,8,128]{2,1,0:T(8,128)S(1)}, u32[]{:S(2)}, u32[]{:S(2)}) %all-to-all-start.5) | async-done | bytes 262176 | tf_op jit(solution)/shard_map/all_to_all | solution.py:495
  218.1 9.2 %all-to-all-start.7 = ((f32[128,8,128]{2,1,0:T(8,128)}), f32[128,8,128]{2,1,0:T(8,128)S(1)}, u32[]{:S(2)}, u32[]{:S(2)}) async-start(f32[128,8,128]{2,1,0:T(8,128)} %bitcast.15), calls=%async_computation.7 | async-start | bytes 1048576 | tf_op jit(solution)/shard_map/all_to_all | solution.py:495
  227.4 5.6 %shard_map.218 = (f32[128,192]{1,0:T(8,128)S(1)}, f32[128,128]{1,0:T(8,128)S(1)}, f32[128,128]{1,0:T(8,128)S(1)}, f32[128,128]{1,0:T(8,128)S(1)}) custom-call(bf16[128,192]{1,0:T(8,128)(2,1)S(1)} %get-tuple-element.36.act_ref, f32[128,128]{1,0:T(8,128)S(1)} %get-tuple-element.37.bc_ref, f32[128,128]{1,0:T(8,128)S(1)} %get-tuple-element.38.step_ref, ...), custom_call_target="tpu_custom_call" | custom-call | flops 100000000 | bytes 1000000 | tf_op jit(solution)/shard_map/pallas_call | solution.py:438
  233.0 4.7 all-to-all-done.7.lh_ref
  237.7 7.1 %shard_map.220 = (bf16[128,192]{1,0:T(8,128)(2,1)S(1)}, f32[672,128]{1,0:T(8,128)}) custom-call(bf16[288,96]{1,0:T(8,128)(2,1)S(1)} %bitcast.41, bf16[96,192]{1,0:T(8,128)(2,1)S(1)} %get-tuple-element.102.wbr_ref, f32[16,192]{1,0:T(8,128)S(1)} %pad.24.cw_ref, f32[128,192]{1,0:T(8,128)S(1)} %get-tuple-element.44.before_ref, ...), custom_call_target="tpu_custom_call" | custom-call | flops 100000000 | bytes 1000000 | tf_op jit(solution)/shard_map/pallas_call | solution.py:438
  246.8 5.8 %collective-permute-start.14 = (bf16[1,8,192]{2,1,0:T(8,128)(2,1)S(1)}, bf16[1,8,192]{2,1,0:T(8,128)(2,1)S(1)}, u32[]{:S(2)}, u32[]{:S(2)}) collective-permute-start(bf16[1,8,192]{2,1,0:T(8,128)(2,1)S(1)} %get-tuple-element.108), channel_id=1, source_target_pairs={{8,0},{16,8},{24,16},{32,24},{40,32},{48,40},{56,48},{64,56},{72,6... | collective-permute-start | bytes 9224 | tf_op jit(solution)/shard_map/ppermute | solution.py:455
  252.6 9.0 %collective-permute-start.11 = (bf16[16,1,192]{2,1,0:T(2,128)(2,1)S(1)}, bf16[16,1,192]{2,1,0:T(2,128)(2,1)S(1)}, u32[]{:S(2)}, u32[]{:S(2)}) collective-permute-start(bf16[16,1,192]{2,1,0:T(2,128)(2,1)S(1)} %get-tuple-element.109), channel_id=1, source_target_pairs={{0,1},{1,2},{2,3},{3,4},{4,5},{5,6},{6,7},{8,9},{9,10},{10,11},{11... | collective-permute-start | bytes 18440 | tf_op jit(solution)/shard_map/ppermute | solution.py:455
  263.6 5.1 collective-permute-start.8
  268.7 4.9 collective-permute-done.8
  275.5 7.8 %collective-permute-done.15 = bf16[1,1,192]{2,1,0:T(2,128)(2,1)S(1)} collective-permute-done((bf16[1,1,192]{2,1,0:T(2,128)(2,1)S(1)}, bf16[1,1,192]{2,1,0:T(2,128)(2,1)S(1)}, u32[]{:S(2)}, u32[]{:S(2)}) %collective-permute-start.15) | collective-permute-done | bytes 416 | tf_op jit(solution)/shard_map/ppermute | solution.py:461
  283.3 6.7 %collective-permute-start.13 = (bf16[1,1,192]{2,1,0:T(2,128)(2,1)S(1)}, bf16[1,1,192]{2,1,0:T(2,128)(2,1)S(1)}, u32[]{:S(2)}, u32[]{:S(2)}) collective-permute-start(bf16[1,1,192]{2,1,0:T(2,128)(2,1)S(1)} %get-tuple-element.105), channel_id=1, source_target_pairs={{8,1},{9,2},{10,3},{11,4},{12,5},{13,6},{14,7},{16,9},{17,10},{18,... | collective-permute-start | bytes 1160 | tf_op jit(solution)/shard_map/ppermute | solution.py:461
  294.7 8.3 %collective-permute-done.10 = bf16[1,1,192]{2,1,0:T(2,128)(2,1)S(1)} collective-permute-done((bf16[1,1,192]{2,1,0:T(2,128)(2,1)S(1)}, bf16[1,1,192]{2,1,0:T(2,128)(2,1)S(1)}, u32[]{:S(2)}, u32[]{:S(2)}) %collective-permute-start.10) | collective-permute-done | bytes 416 | tf_op jit(solution)/shard_map/ppermute | solution.py:461
  304.1 201.6 %all-reduce.8.cloned.1.call-done = f32[672,128]{1,0:T(8,128)} async-done(((f32[672,128]{1,0:T(8,128)}), f32[672,128]{1,0:T(8,128)}) %all-reduce.8.cloned.1.call-update) | async-done | bytes 344080 | tf_op jit(solution)/shard_map/psum | solution.py:549
  (105 shorter events, 41.3 us)
Async XLA Ops:
  7.2 26.6 %copy-start.6 = (bf16[4,192,35]{1,0,2:T(4,128)(2,1)S(1)}, bf16[4,192,35]{1,0,2:T(4,128)(2,1)}, u32[]{:S(2)}) copy-start(bf16[4,192,35]{1,0,2:T(4,128)(2,1)} %param.16) | copy-start | bytes 161284
  8.1 60.5 %collective-permute-start.6 = (bf16[1,8,96]{2,1,0:T(8,128)(2,1)S(1)}, bf16[1,8,96]{2,1,0:T(8,128)(2,1)S(1)}, u32[]{:S(2)}, u32[]{:S(2)}) collective-permute-start(bf16[1,8,96]{2,1,0:T(8,128)(2,1)S(1)} %slice.148), channel_id=1, source_target_pairs={{8,0},{16,8},{24,16},{32,24},{40,32},{48,40},{56,48},{64,56},{72,6... | collective-permute-start | bytes 4616 | tf_op jit(solution)/shard_map/ppermute | solution.py:455
  19.3 49.2 %collective-permute-start.1 = (bf16[1,8,96]{2,1,0:T(8,128)(2,1)S(1)}, bf16[1,8,96]{2,1,0:T(8,128)(2,1)S(1)}, u32[]{:S(2)}, u32[]{:S(2)}) collective-permute-start(bf16[1,8,96]{2,1,0:T(8,128)(2,1)S(1)} %slice.142), channel_id=1, source_target_pairs={{0,8},{8,16},{16,24},{24,32},{32,40},{40,48},{48,56},{56,64},{64,7... | collective-permute-start | bytes 4616 | tf_op jit(solution)/shard_map/ppermute | solution.py:455
  22.1 14.3 %collective-permute-start = (bf16[1,1,96]{2,1,0:T(2,128)(2,1)S(1)}, bf16[1,1,96]{2,1,0:T(2,128)(2,1)S(1)}, u32[]{:S(2)}, u32[]{:S(2)}) collective-permute-start(bf16[1,1,96]{2,1,0:T(2,128)(2,1)S(1)} %get-tuple-element.111), channel_id=1, source_target_pairs={{0,9},{1,10},{2,11},{3,12},{4,13},{5,14},{6,15},{8,17},{9,18},{10,... | collective-permute-start | bytes 584 | tf_op jit(solution)/shard_map/ppermute | solution.py:461
  24.0 44.5 %collective-permute-start.3 = (bf16[16,1,96]{2,1,0:T(2,128)(2,1)S(1)}, bf16[16,1,96]{2,1,0:T(2,128)(2,1)S(1)}, u32[]{:S(2)}, u32[]{:S(2)}) collective-permute-start(bf16[16,1,96]{2,1,0:T(2,128)(2,1)S(1)} %get-tuple-element.115), channel_id=1, source_target_pairs={{0,1},{1,2},{2,3},{3,4},{4,5},{5,6},{6,7},{8,9},{9,10},{10,11},{11... | collective-permute-start | bytes 9224 | tf_op jit(solution)/shard_map/ppermute | solution.py:455
  28.8 39.7 %collective-permute-start.4 = (bf16[16,1,96]{2,1,0:T(2,128)(2,1)S(1)}, bf16[16,1,96]{2,1,0:T(2,128)(2,1)S(1)}, u32[]{:S(2)}, u32[]{:S(2)}) collective-permute-start(bf16[16,1,96]{2,1,0:T(2,128)(2,1)S(1)} %get-tuple-element.116), channel_id=1, source_target_pairs={{1,0},{2,1},{3,2},{4,3},{5,4},{6,5},{7,6},{9,8},{10,9},{11,10},{12... | collective-permute-start | bytes 9224 | tf_op jit(solution)/shard_map/ppermute | solution.py:455
  33.9 0.9 copy-start.4
  34.9 0.7 copy-start.10
  34.9 21.4 %copy-start.8 = (f32[3,3,192]{2,1,0:T(4,128)S(1)}, f32[3,3,192]{2,1,0:T(4,128)}, u32[]{:S(2)}) copy-start(f32[3,3,192]{2,1,0:T(4,128)} %param.14) | copy-start | bytes 20740
  36.4 9.7 %collective-permute-start.7 = (bf16[1,1,96]{2,1,0:T(2,128)(2,1)S(1)}, bf16[1,1,96]{2,1,0:T(2,128)(2,1)S(1)}, u32[]{:S(2)}, u32[]{:S(2)}) collective-permute-start(bf16[1,1,96]{2,1,0:T(2,128)(2,1)S(1)} %get-tuple-element.112), channel_id=1, source_target_pairs={{9,0},{10,1},{11,2},{12,3},{13,4},{14,5},{15,6},{17,8},{18,9},{19,... | collective-permute-start | bytes 584 | tf_op jit(solution)/shard_map/ppermute | solution.py:461
  46.0 11.6 %collective-permute-start.5 = (bf16[1,1,96]{2,1,0:T(2,128)(2,1)S(1)}, bf16[1,1,96]{2,1,0:T(2,128)(2,1)S(1)}, u32[]{:S(2)}, u32[]{:S(2)}) collective-permute-start(bf16[1,1,96]{2,1,0:T(2,128)(2,1)S(1)} %get-tuple-element.113), channel_id=1, source_target_pairs={{8,1},{9,2},{10,3},{11,4},{12,5},{13,6},{14,7},{16,9},{17,10},{18,... | collective-permute-start | bytes 584 | tf_op jit(solution)/shard_map/ppermute | solution.py:461
  57.7 10.9 %collective-permute-start.2 = (bf16[1,1,96]{2,1,0:T(2,128)(2,1)S(1)}, bf16[1,1,96]{2,1,0:T(2,128)(2,1)S(1)}, u32[]{:S(2)}, u32[]{:S(2)}) collective-permute-start(bf16[1,1,96]{2,1,0:T(2,128)(2,1)S(1)} %get-tuple-element.114), channel_id=1, source_target_pairs={{1,8},{2,9},{3,10},{4,11},{5,12},{6,13},{7,14},{9,16},{10,17},{11,... | collective-permute-start | bytes 584 | tf_op jit(solution)/shard_map/ppermute | solution.py:461
  92.9 19.6 %all-to-all-start.2 = ((f32[128,8,128]{2,1,0:T(8,128)}), f32[128,8,128]{2,1,0:T(8,128)S(1)}, u32[]{:S(2)}, u32[]{:S(2)}) async-start(f32[128,8,128]{2,1,0:T(8,128)} %get-tuple-element.42), calls=%async_computation.2 | async-start | bytes 1048576 | tf_op jit(solution)/shard_map/all_to_all | solution.py:492
  112.4 20.6 %all-to-all-start.1 = ((f32[64,8,128]{2,1,0:T(8,128)}), f32[64,8,128]{2,1,0:T(8,128)S(1)}, u32[]{:S(2)}, u32[]{:S(2)}) async-start(f32[64,8,128]{2,1,0:T(8,128)} %bitcast.6), calls=%async_computation.1 | async-start | bytes 524288 | tf_op jit(solution)/shard_map/all_to_all | solution.py:495
  133.0 9.3 %copy-start.5 = (bf16[16,768]{1,0:T(8,128)(2,1)S(1)}, bf16[16,768]{1,0:T(8,128)(2,1)}, u32[]{:S(2)}) copy-start(bf16[16,768]{1,0:T(8,128)(2,1)} %param.12) | copy-start | bytes 73732
  133.1 19.7 %all-to-all-start.3 = ((f32[128,8,128]{2,1,0:T(8,128)}), f32[128,8,128]{2,1,0:T(8,128)S(1)}, u32[]{:S(2)}, u32[]{:S(2)}) async-start(f32[128,8,128]{2,1,0:T(8,128)} %bitcast.8), calls=%async_computation.3 | async-start | bytes 1048576 | tf_op jit(solution)/shard_map/all_to_all | solution.py:495
  142.3 0.7 copy-start.9
  142.3 0.8 copy-start.7
  143.2 9.6 %copy-start = (bf16[192,96]{1,0:T(8,128)(2,1)S(1)}, bf16[192,96]{1,0:T(8,128)(2,1)}, u32[]{:S(2)}) copy-start(bf16[192,96]{1,0:T(8,128)(2,1)} %ow_ref.1) | copy-start | bytes 110596
  143.2 9.6 %copy-start.2 = (f32[192]{0:T(256)S(1)}, f32[192]{0:T(256)}, u32[]{:S(2)}) copy-start(f32[192]{0:T(256)} %param.21) | copy-start | bytes 2308
  177.7 19.7 %all-to-all-start.6 = ((f32[128,8,128]{2,1,0:T(8,128)}), f32[128,8,128]{2,1,0:T(8,128)S(1)}, u32[]{:S(2)}, u32[]{:S(2)}) async-start(f32[128,8,128]{2,1,0:T(8,128)} %get-tuple-element.48), calls=%async_computation.6 | async-start | bytes 1048576 | tf_op jit(solution)/shard_map/all_to_all | solution.py:492
  197.4 20.6 %all-to-all-start.5 = ((f32[64,8,128]{2,1,0:T(8,128)}), f32[64,8,128]{2,1,0:T(8,128)S(1)}, u32[]{:S(2)}, u32[]{:S(2)}) async-start(f32[64,8,128]{2,1,0:T(8,128)} %bitcast.13), calls=%async_computation.5 | async-start | bytes 524288 | tf_op jit(solution)/shard_map/all_to_all | solution.py:495
  218.1 19.6 %all-to-all-start.7 = ((f32[128,8,128]{2,1,0:T(8,128)}), f32[128,8,128]{2,1,0:T(8,128)S(1)}, u32[]{:S(2)}, u32[]{:S(2)}) async-start(f32[128,8,128]{2,1,0:T(8,128)} %bitcast.15), calls=%async_computation.7 | async-start | bytes 1048576 | tf_op jit(solution)/shard_map/all_to_all | solution.py:495
  227.2 278.5 %all-reduce.8.cloned.1.call-start = ((), (), s32[]{:S(2)}) async-start(), calls=%async_computation.8 | async-start | bytes 688128 | tf_op jit(solution)/shard_map/psum | solution.py:549
  244.9 58.1 %collective-permute-start.9 = (bf16[1,8,192]{2,1,0:T(8,128)(2,1)S(1)}, bf16[1,8,192]{2,1,0:T(8,128)(2,1)S(1)}, u32[]{:S(2)}, u32[]{:S(2)}) collective-permute-start(bf16[1,8,192]{2,1,0:T(8,128)(2,1)S(1)} %get-tuple-element.107), channel_id=1, source_target_pairs={{0,8},{8,16},{16,24},{24,32},{32,40},{40,48},{48,56},{56,64},{64,7... | collective-permute-start | bytes 9224 | tf_op jit(solution)/shard_map/ppermute | solution.py:455
  246.8 56.2 %collective-permute-start.14 = (bf16[1,8,192]{2,1,0:T(8,128)(2,1)S(1)}, bf16[1,8,192]{2,1,0:T(8,128)(2,1)S(1)}, u32[]{:S(2)}, u32[]{:S(2)}) collective-permute-start(bf16[1,8,192]{2,1,0:T(8,128)(2,1)S(1)} %get-tuple-element.108), channel_id=1, source_target_pairs={{8,0},{16,8},{24,16},{32,24},{40,32},{48,40},{56,48},{64,56},{72,6... | collective-permute-start | bytes 9224 | tf_op jit(solution)/shard_map/ppermute | solution.py:455
  252.6 50.4 %collective-permute-start.11 = (bf16[16,1,192]{2,1,0:T(2,128)(2,1)S(1)}, bf16[16,1,192]{2,1,0:T(2,128)(2,1)S(1)}, u32[]{:S(2)}, u32[]{:S(2)}) collective-permute-start(bf16[16,1,192]{2,1,0:T(2,128)(2,1)S(1)} %get-tuple-element.109), channel_id=1, source_target_pairs={{0,1},{1,2},{2,3},{3,4},{4,5},{5,6},{6,7},{8,9},{9,10},{10,11},{11... | collective-permute-start | bytes 18440 | tf_op jit(solution)/shard_map/ppermute | solution.py:455
  261.6 41.3 %collective-permute-start.12 = (bf16[16,1,192]{2,1,0:T(2,128)(2,1)S(1)}, bf16[16,1,192]{2,1,0:T(2,128)(2,1)S(1)}, u32[]{:S(2)}, u32[]{:S(2)}) collective-permute-start(bf16[16,1,192]{2,1,0:T(2,128)(2,1)S(1)} %get-tuple-element.110), channel_id=1, source_target_pairs={{1,0},{2,1},{3,2},{4,3},{5,4},{6,5},{7,6},{9,8},{10,9},{11,10},{12... | collective-permute-start | bytes 18440 | tf_op jit(solution)/shard_map/ppermute | solution.py:455
  263.6 10.0 %collective-permute-start.8 = (bf16[1,1,192]{2,1,0:T(2,128)(2,1)S(1)}, bf16[1,1,192]{2,1,0:T(2,128)(2,1)S(1)}, u32[]{:S(2)}, u32[]{:S(2)}) collective-permute-start(bf16[1,1,192]{2,1,0:T(2,128)(2,1)S(1)} %get-tuple-element.103), channel_id=1, source_target_pairs={{0,9},{1,10},{2,11},{3,12},{4,13},{5,14},{6,15},{8,17},{9,18},{10,... | collective-permute-start | bytes 1160 | tf_op jit(solution)/shard_map/ppermute | solution.py:461
  273.6 9.7 %collective-permute-start.15 = (bf16[1,1,192]{2,1,0:T(2,128)(2,1)S(1)}, bf16[1,1,192]{2,1,0:T(2,128)(2,1)S(1)}, u32[]{:S(2)}, u32[]{:S(2)}) collective-permute-start(bf16[1,1,192]{2,1,0:T(2,128)(2,1)S(1)} %get-tuple-element.104), channel_id=1, source_target_pairs={{9,0},{10,1},{11,2},{12,3},{13,4},{14,5},{15,6},{17,8},{18,9},{19,... | collective-permute-start | bytes 1160 | tf_op jit(solution)/shard_map/ppermute | solution.py:461
  283.3 8.8 %collective-permute-start.13 = (bf16[1,1,192]{2,1,0:T(2,128)(2,1)S(1)}, bf16[1,1,192]{2,1,0:T(2,128)(2,1)S(1)}, u32[]{:S(2)}, u32[]{:S(2)}) collective-permute-start(bf16[1,1,192]{2,1,0:T(2,128)(2,1)S(1)} %get-tuple-element.105), channel_id=1, source_target_pairs={{8,1},{9,2},{10,3},{11,4},{12,5},{13,6},{14,7},{16,9},{17,10},{18,... | collective-permute-start | bytes 1160 | tf_op jit(solution)/shard_map/ppermute | solution.py:461
  292.0 10.9 %collective-permute-start.10 = (bf16[1,1,192]{2,1,0:T(2,128)(2,1)S(1)}, bf16[1,1,192]{2,1,0:T(2,128)(2,1)S(1)}, u32[]{:S(2)}, u32[]{:S(2)}) collective-permute-start(bf16[1,1,192]{2,1,0:T(2,128)(2,1)S(1)} %get-tuple-element.106), channel_id=1, source_target_pairs={{1,8},{2,9},{3,10},{4,11},{5,12},{6,13},{7,14},{9,16},{10,17},{11,... | collective-permute-start | bytes 1160 | tf_op jit(solution)/shard_map/ppermute | solution.py:461
  (3 other events, 2.0 us)
Sparse Core Ops, SparseCore 0:
  245.0 260.7 all-reduce.7

commit v2 on v1

--- a/solution.py
+++ b/solution.py
@@ -15,6 +15,7 @@
 C = 8
 T = R * C
 PITCH = 16
+SPAN = 80
 
 F32 = jnp.float32
 BF = jnp.bfloat16
@@ -61,34 +62,31 @@
     return jnp.where(m, 1.0, 0.0).astype(F32)
 
 
-def lines_of(k):
-    return R if k < 2 else C
-
-
-def half_of(k):
-    return lines_of(k) * 8
+def states_of(k):
+    return 256 if k < 2 else 128
+
+
+def line_and_entry(j, k):
+    if k < 2:
+        return (j >> 4, j & 15)
+    return ((j >> 3) & 7, 2 * (j & 7) + (j >> 6))
+
+
+def on_line(k):
+    t, j = (iota((T, states_of(k)), 0), iota((T, states_of(k)), 1))
+    return line_and_entry(j, k)[0] == (t >> 3 if k < 2 else t & 7)
 
 
 def spread_states(bc, k):
-    lines, half = (lines_of(k), half_of(k))
-    i, j = (iota((T, 2 * half), 0), iota((T, 2 * half), 1))
-    n = 2 * (j & 7) + j // half
-    wide = dot(bc, as_f32(i == 16 * k + n), precision=HI)
+    i, j = (iota((T, states_of(k)), 0), iota((T, states_of(k)), 1))
+    wide = dot(bc, as_f32(i == 16 * k + line_and_entry(j, k)[1]), precision=HI)
     return jnp.where(on_line(k), wide, 0.0)
 
 
-def on_line(k):
-    lines, half = (lines_of(k), half_of(k))
-    t, j = (iota((T, 2 * half), 0), iota((T, 2 * half), 1))
-    line = t >> 3 if k < 2 else t & 7
-    return ((j >> 3) & (lines - 1)) == line
-
-
 def gather_states(wide, k):
-    half = half_of(k)
-    j, i = (iota((2 * half, T), 0), iota((2 * half, T), 1))
-    n = 2 * (j & 7) + j // half
-    return dot(jnp.where(on_line(k), wide, 0.0), as_f32(i == 16 * k + n), precision=HI)
+    j, i = (iota((states_of(k), T), 0), iota((states_of(k), T), 1))
+    entry = line_and_entry(j, k)[1]
+    return dot(jnp.where(on_line(k), wide, 0.0), as_f32(i == 16 * k + entry), precision=HI)
 
 
 def by_head(values, k):
@@ -108,21 +106,18 @@
     return jnp.where(lane < 64, a, jnp.where(lane < 128, b, c))
 
 
-def write_message(ref, states, totals, k_first):
-    half = half_of(k_first)
+def write_message(ref, states, totals):
     for d in range(2):
         s = states[d]
         for h in range(HEADS):
             ref[:, d * 3 + h, :] = jnp.concatenate(
-                [s[:half, 64 * h : 64 * h + 64], s[half:, 64 * h : 64 * h + 64]], axis=1
+                [s[:64, 64 * h : 64 * h + 64], s[64:, 64 * h : 64 * h + 64]], axis=1
             )
-    j, t = (iota((half, T), 0), iota((half, T), 1))
-    sel = as_f32(t == ((j >> 3) if k_first == 2 else (j >> 3) * 8))
-    if k_first == 2:
-        i, o = (iota((T, T), 0), iota((T, T), 1))
-        totals = dot(totals, as_f32(i == o + 6), precision=HI)
-    ref[:, 6, :] = dot(sel, totals, precision=HI)
-    ref[:, 7, :] = jnp.zeros((half, T), F32)
+    j, t = (iota((64, T), 0), iota((64, T), 1))
+    i, o = (iota((T, T), 0), iota((T, T), 1))
+    totals = dot(totals, as_f32(i == o + 6), precision=HI)
+    ref[:, 6, :] = dot(as_f32(t == (j >> 3)), totals, precision=HI)
+    ref[:, 7, :] = jnp.zeros((64, T), F32)
 
 
 def read_message(ref, d):
@@ -154,6 +149,10 @@
             down = factor(i) * down + got_ref[i]
 
 
+def state_in(k, rows, columns):
+    return rows[k][...] if k < 2 else read_message(columns, k - 2)
+
+
 def sigmoid(x):
     return jax.nn.sigmoid(x)
 
@@ -169,7 +168,7 @@
 
 def first_kernel(
     tok_ref, wbr_ref, cw_ref, cb_ref, wd_ref, wbc_ref, sb_ref, ld_ref,
-    before_ref, act_ref, rawd_ref, bc_ref, step_ref, log_ref, tot_ref, mv_ref, mh_ref,
+    before_ref, act_ref, rawd_ref, bc_ref, step_ref, log_ref, tot_ref, mv_ref,
 ):
     padded = conv_in(tok_ref, wbr_ref)
     total = jnp.zeros((R, C, DI), F32)
@@ -196,11 +195,72 @@
     weight = jnp.exp(tot - log) * step
     wide = act.astype(F32)
     states = [
-        dot(spread_states(bc, k), by_head(weight, k) * wide, 0, 0, HI) for k in range(4)
+        dot(spread_states(bc, k), by_head(weight, k) * wide, 0, 0, HI) for k in (2, 3)
     ]
-    factor = jnp.exp(tot)
-    write_message(mv_ref, states[2:], factor, 2)
-    write_message(mh_ref, states[:2], factor, 0)
+    write_message(mv_ref, states, jnp.exp(tot))
+
+
+def row_scan_kernel(
+    me_ref, tok_ref, wbr_ref, cw_ref, cb_ref, wd_ref, wbc_ref, sb_ref, ld_ref,
+    s0_ref, s1_ref, later_ref, gate_ref, pad_ref,
+):
+    branch = dot(tok_ref[...], wbr_ref[...]).astype(BF).astype(F32)
+    pad_ref[...] = branch.reshape(R + 2, SPAN, DI)
+    low = me_ref[0] * C
+    high = low + C
+    t, u = (iota((T, T), 0), iota((T, T), 1))
+    same = (t >> 6) == (u >> 6)
+    t, u = (t & 63, u & 63)
+    reach = [
+        same & (u > t) & (u < low),
+        same & (u < t) & (u >= high),
+        same & (u <= t) & (u >= high),
+        same & (u >= t) & (u < low),
+    ]
+    reach = jnp.concatenate([as_f32(m) for m in reach], axis=0)
+    before, after = (t < low, t >= high)
+    first = iota((T, T), 1) < 3
+    valid_in = jnp.where(first, as_f32(before), as_f32(after))
+    valid_out = jnp.where(first, as_f32(after), as_f32(before))
+    tj, j = (iota((T, 32), 0), iota((T, 32), 1))
+    line = (tj >> 6) == (j >> 4)
+    i, ji = (iota((T, 32), 0), iota((T, 32), 1))
+    rate = -jnp.exp(ld_ref[...])
+    for group in range(R // 2):
+        total = jnp.zeros((2, 64, DI), F32)
+        for b in range(3):
+            shifted = pad_ref[2 * group : 2 * group + 4, b : b + 64, :]
+            for a in range(3):
+                total = total + cw_ref[3 * a + b : 3 * a + b + 1, :] * shifted[a : a + 2]
+        wide = total.reshape(T, DI) + cb_ref[...]
+        act = (wide * sigmoid(wide)).astype(BF)
+        wide = act.astype(F32)
+        step = softplus(dot(act, wd_ref[...]) + sb_ref[...])
+        bc = dot(act, wbc_ref[...])
+        x = dot(reach, step * rate, precision=HI)
+        w_in = jnp.exp(jnp.where(first, x[:T], x[T : 2 * T])) * step * valid_in
+        later_ref[group * T : group * T + T, :] = (
+            jnp.exp(jnp.where(first, x[2 * T : 3 * T], x[3 * T :])) * valid_out
+        )
+        gate_ref[group * T : group * T + T, :] = shifted_gate(bc)
+        for k, ref in enumerate((s0_ref, s1_ref)):
+            entry = as_f32(i == 16 * k + (ji & 15))
+            spread = jnp.where(line, dot(bc, entry, precision=HI), 0.0)
+            ref[32 * group : 32 * group + 32, :] = dot(spread, by_head(w_in, k) * wide, 0, 0, HI)
+
+
+def row_back_kernel(g_ref, later_ref, gate_ref, l0_ref, l1_ref):
+    tj, j = (iota((T, 32), 0), iota((T, 32), 1))
+    line = (tj >> 6) == (j >> 4)
+    for group in range(R // 2):
+        part = slice(group * T, group * T + T)
+        g = g_ref[part, :].astype(F32)
+        later = later_ref[part, :]
+        gate = gate_ref[part, :]
+        for k, ref in enumerate((l0_ref, l1_ref)):
+            entry = as_f32(tj == 16 * k + (j & 15))
+            spread = jnp.where(line, dot(gate, entry, precision=HI), 0.0)
+            ref[32 * group : 32 * group + 32, :] = dot(spread, by_head(later, k) * g, 0, 0, HI)
 
 
 def tables(k, bc, out_gate):
@@ -239,16 +299,16 @@
 
 
 def norm_kernel(
-    y_ref, act_ref, bc_ref, log_ref, tot_ref, sv_ref, sh_ref, skip_ref, tok_ref, wg_ref, gain_ref,
+    y_ref, act_ref, bc_ref, log_ref, tot_ref, sv_ref, s0_ref, s1_ref, skip_ref, tok_ref, wg_ref, gain_ref,
     nb_ref, ow_ref, cot_ref,
-    out_ref, g_ref, dgate_ref, gated_ref, norms_ref, mv_ref, mh_ref,
+    out_ref, g_ref, dgate_ref, gated_ref, norms_ref, mv_ref,
 ):
     bc = bc_ref[...]
     out_gate = shifted_gate(bc)
     exp_log = jnp.exp(log_ref[...])
     summed = y_ref[...] + skip_ref[...] * act_ref[...].astype(F32)
     for k in range(4):
-        state = read_message(sh_ref if k < 2 else sv_ref, k % 2)
+        state = state_in(k, (s0_ref, s1_ref), sv_ref)
         summed = summed + carry(k, out_gate, exp_log, state)
     gate = dot(tok_ref[...], wg_ref[...]).astype(BF).astype(F32)
     sig = sigmoid(gate)
@@ -274,15 +334,13 @@
     g_ref[...] = g
     g = g.astype(F32)
     states = [
-        dot(spread_states(out_gate, k), by_head(exp_log, k) * g, 0, 0, HI) for k in range(4)
+        dot(spread_states(out_gate, k), by_head(exp_log, k) * g, 0, 0, HI) for k in (2, 3)
     ]
-    factor = jnp.exp(tot_ref[...])
-    write_message(mv_ref, states[2:], factor, 2)
-    write_message(mh_ref, states[:2], factor, 0)
+    write_message(mv_ref, states, jnp.exp(tot_ref[...]))
 
 
 def back_kernel(
-    act_ref, bc_ref, step_ref, log_ref, g_ref, sv_ref, sh_ref,
+    act_ref, bc_ref, step_ref, log_ref, g_ref, sv_ref, s0_ref, s1_ref,
     dact_ref, dbc_ref, dstep_ref, dlog_ref,
 ):
     bc = bc_ref[...]
@@ -318,7 +376,7 @@
             row_sums = jnp.where(lane1 == i, rows, row_sums)
         d_out = d_out + dot(d_scores, jnp.where(lane16 == k, bc, 0.0), precision=HI)
         d_in = d_in + dot(d_scores, jnp.where(lane16 == k, out_gate, 0.0), 0, 0, HI)
-        state = read_message(sh_ref if k < 2 else sv_ref, k % 2)
+        state = state_in(k, (s0_ref, s1_ref), sv_ref)
         expg = by_head(exp_log, k) * gw
         carried = dot(spread_states(out_gate, k), state, precision=HI)
         row_sums = row_sums + head_sum(carried * expg, k)
@@ -337,7 +395,7 @@
 
 def last_kernel(
     tok_ref, wbr_ref, cw_ref, before_ref, act_ref, rawd_ref, bc_ref, step_ref, log_ref, tot_ref, g_ref,
-    sv_ref, sh_ref, lv_ref, lh_ref, dact_ref, dbc_ref, dstep_ref, dlog_ref, skip_ref, wd_ref, wbc_ref,
+    sv_ref, s0_ref, s1_ref, lv_ref, l0_ref, l1_ref, dact_ref, dbc_ref, dstep_ref, dlog_ref, skip_ref, wd_ref, wbc_ref,
     sb_ref, ld_ref, gin_gate_ref, gout_ref, norms_ref,
     gb_ref, pack_ref,
 ):
@@ -353,8 +411,8 @@
     inner = jnp.zeros((T, T), F32)
     cross = jnp.zeros((T, T), F32)
     for k in range(4):
-        later = read_message(lh_ref if k < 2 else lv_ref, k % 2)
-        earlier = read_message(sh_ref if k < 2 else sv_ref, k % 2)
+        later = state_in(k, (l0_ref, l1_ref), lv_ref)
+        earlier = state_in(k, (s0_ref, s1_ref), sv_ref)
         reach = dot(spread_states(bc, k), later, precision=HI)
         wk = by_head(weight, k)
         d_act = d_act + wk * reach
@@ -416,8 +474,14 @@
         dot(d_raw, act, 0, 0)[:16],
     ]
     full = jnp.concatenate(both, axis=0)
-    pack_ref[0:448, :] = full[:, :128]
-    pack_ref[448:672, :] = jnp.concatenate([full[:224, 128:], full[224:, 128:]], axis=1)
+    rest = small - small.astype(BF).astype(F32)
+    pack_ref[0:448, :] = full[:, :128].astype(BF)
+    pack_ref[448:672, :] = jnp.concatenate([full[:224, 128:], full[224:, 128:]], axis=1).astype(BF)
+    pack_ref[672:688, :] = rest[:, :128].astype(BF)
+    pack_ref[688:704, :] = jnp.concatenate(
+        [rest[:, 128:], jnp.zeros((16, 64), F32)], axis=1
+    ).astype(BF)
+    pack_ref[704:1024, :] = jnp.zeros((320, T), BF)
 
 
 def out_kernel(gb_ref, cw_ref, dgate_ref, wbr_ref, wg_ref, out_ref):
@@ -433,66 +497,104 @@
     ).astype(BF)
 
 
-def call(kernel, outs, *args, flops=10**8):
+def sum_kernel(scale, x_ref, out_ref):
+    total = x_ref[0].astype(F32)
+    for i in range(1, x_ref.shape[0]):
+        total = total + x_ref[i].astype(F32)
+    out_ref[...] = jnp.broadcast_to(total * scale, out_ref.shape)
+
+
+def unpack_kernel(
+    x_ref, gin_ref, conv_ref, cb_ref, scan_ref, sb_ref, ld_ref, skip_ref, gain_ref, nb_ref, gout_ref
+):
+    low, high = (x_ref[0:448, :], x_ref[448:672, :])
+    full = jnp.concatenate(
+        [low, jnp.concatenate([high[:, :64], high[:, 64:]], axis=0)], axis=1
+    )
+    rest = jnp.concatenate([x_ref[672:688, :], x_ref[688:704, :64]], axis=1)
+    gin_ref[...] = jnp.concatenate([full[:96], full[96:192]], axis=1)
+    gout_ref[...] = full[192:288].T
+    small = full[288:304] + rest
+    for a in range(3):
+        conv_ref[a] = small[3 * a : 3 * a + 3]
+    cb_ref[...] = small[9:10]
+    skip_ref[...] = jnp.broadcast_to(small[10:11], (4, DI))
+    gain_ref[...] = small[11:12]
+    nb_ref[...] = small[12:13]
+    for k in range(4):
+        sb_ref[k : k + 1, :] = small[13:14, 3 * k : 3 * k + 3]
+        ld_ref[k : k + 1, :] = small[14:15, 3 * k : 3 * k + 3]
+    scan = jnp.concatenate([full[304:448], jnp.zeros((112, DI), F32)], axis=0).T
+    for k in range(4):
+        scan_ref[k] = jnp.concatenate(
+            [
+                scan[:, 128 + 3 * k : 131 + 3 * k],
+                scan[:, 16 * k : 16 * k + 16],
+                scan[:, 64 + 16 * k : 80 + 16 * k],
+            ],
+            axis=1,
+        )
+
+
+def call(kernel, outs, *args, flops=10**8, scratch=(), scalars=0):
     whole = pl.BlockSpec(memory_space=pltpu.VMEM)
+    small = pl.BlockSpec(memory_space=pltpu.SMEM)
     return pl.pallas_call(
         kernel,
         out_shape=[jax.ShapeDtypeStruct(s, t) for s, t in outs],
-        in_specs=[whole] * len(args),
+        in_specs=[small] * scalars + [whole] * (len(args) - scalars),
         out_specs=[whole] * len(outs),
+        scratch_shapes=list(scratch),
         compiler_params=pltpu.CompilerParams(vmem_limit_bytes=40 * 2**20),
         cost_estimate=pl.CostEstimate(flops=flops, bytes_accessed=10**6, transcendentals=0),
     )(*args)
 
 
-def shift_over(x, axes, steps):
-    sizes = [lax.axis_size(a) for a in axes]
-    pairs = []
-    if len(axes) == 1:
-        for i in range(sizes[0]):
-            if 0 <= i + steps[0] < sizes[0]:
-                pairs.append((i + steps[0], i))
-        return lax.ppermute(x, axes[0], pairs)
-    for i in range(sizes[0]):
-        for j in range(sizes[1]):
-            a, b = (i + steps[0], j + steps[1])
-            if 0 <= a < sizes[0] and 0 <= b < sizes[1]:
-                pairs.append((a * sizes[1] + b, i * sizes[1] + j))
-    return lax.ppermute(x, axes, pairs)
+def edges(x, axis, dim):
+    size, length = (lax.axis_size(axis), x.shape[dim])
+    up = [(i, i + 1) for i in range(size - 1)]
+    down = [(j, i) for i, j in up]
+    before = lax.ppermute(lax.slice_in_dim(x, length - 1, length, axis=dim), axis, up)
+    after = lax.ppermute(lax.slice_in_dim(x, 0, 1, axis=dim), axis, down)
+    return before, after
 
 
 def with_rim(x):
-    both = ("row", "col")
-    up = shift_over(x[-1:], ("row",), (-1,))
-    down = shift_over(x[:1], ("row",), (1,))
-    left = shift_over(x[:, -1:], ("col",), (-1,))
-    right = shift_over(x[:, :1], ("col",), (1,))
-    corner = {
-        (i, j): shift_over(
-            x[-1:, -1:] if (i, j) == (-1, -1)
-            else x[-1:, :1] if (i, j) == (-1, 1)
-            else x[:1, -1:] if (i, j) == (1, -1)
-            else x[:1, :1],
-            both,
-            (i, j),
-        )
-        for i in (-1, 1)
-        for j in (-1, 1)
-    }
-    top = jnp.concatenate([corner[-1, -1], up, corner[-1, 1]], axis=1)
-    mid = jnp.concatenate([left, x, right], axis=1)
-    low = jnp.concatenate([corner[1, -1], down, corner[1, 1]], axis=1)
-    full = jnp.concatenate([top, mid, low], axis=0)
+    before, after = edges(x, "row", 0)
+    x = jnp.concatenate([before, x, after], axis=0)
+    before, after = edges(x, "col", 1)
+    full = jnp.concatenate([before, x, after], axis=1)
     full = jnp.pad(full, ((0, 0), (0, PITCH - C - 2), (0, 0)))
     return full.reshape((R + 2) * PITCH, x.shape[-1])
 
 
+def all_to_all(x, axis):
+    return lax.all_to_all(x, axis, 0, 0, tiled=True)
+
+
+def whole_rows(x):
+    count = lax.axis_size("col")
+    everything = all_to_all(jnp.broadcast_to(x, (count,) + x.shape), "col")
+    everything = everything.reshape(count, x.shape[0], C, -1)
+    return jnp.swapaxes(everything, 0, 1).reshape(x.shape[0], count * C, -1)
+
+
 def exchange(message, axis, backward):
     size = lax.axis_size(axis)
-    got = lax.all_to_all(message, axis, 0, 0, tiled=True)
+    got = all_to_all(message, axis)
     shape = (size, message.shape[0] // size, 8, 128)
     (states,) = call(partial(chain_kernel, backward), [(shape, F32)], got.reshape(shape), flops=10**7)
-    return lax.all_to_all(states.reshape(message.shape), axis, 0, 0, tiled=True)
+    return all_to_all(states.reshape(message.shape), axis)
+
+
+def reduced(pack, scale):
+    rows, cols = (lax.axis_size("row"), lax.axis_size("col"))
+    chunk = pack.shape[0] // rows
+    got = all_to_all(pack.reshape(rows, chunk, 128), "row")
+    (part,) = call(partial(sum_kernel, 1.0), [((cols, chunk, 128), F32)], got, flops=10**7)
+    got = all_to_all(part, "col")
+    (part,) = call(partial(sum_kernel, scale), [((rows, chunk, 128), F32)], got, flops=10**7)
+    return all_to_all(part, "row").reshape(pack.shape)
 
 
 def local(
@@ -500,7 +602,12 @@
     norm_bias, out_weight, cotangent,
 ):
     own = tokens.reshape(T, D)
-    halo = with_rim(tokens.reshape(R, C, D))
+    place = lax.axis_index("col")
+    before, after = edges(tokens, "row", 0)
+    band = whole_rows(jnp.concatenate([before, tokens, after], axis=0))
+    band = jnp.pad(band, ((0, 0), (1, SPAN - 1 - band.shape[1]), (0, 0)))
+    halo = lax.dynamic_slice_in_dim(band, place * C, PITCH, axis=1).reshape((R + 2) * PITCH, D)
+    band = band.reshape((R + 2) * SPAN, D)
     cot = cotangent.reshape(T, D)
     w_branch, w_gate = (in_weight[:, :DI], in_weight[:, DI:])
     taps = jnp.pad(conv_weight.reshape(9, DI), ((0, 7), (0, 0)))
@@ -520,57 +627,54 @@
     square = ((T, T), F32)
     wide = ((T, DI), F32)
     low = ((T, DI), BF)
-    msg_v, msg_h = (((64, 8, 128), F32), ((128, 8, 128), F32))
-
-    before, act, raw_d, bc, step, log, tot, mv, mh = call(
-        first_kernel, [wide, low, square, square, square, square, square, msg_v, msg_h],
+    message = ((64, 8, 128), F32)
+    states = ((256, DI), F32)
+    long = ((8 * T, T), F32)
+
+    before, act, raw_d, bc, step, log, tot, mv = call(
+        first_kernel, [wide, low, square, square, square, square, square, message],
         halo, w_branch, taps, row(conv_bias), w_step, w_bc, bias, rate,
     )
     sv = exchange(mv, "row", False)
-    sh = exchange(mh, "col", False)
+    s0, s1, later, gate_c = call(
+        row_scan_kernel, [states, states, long, long],
+        place.reshape(1), band, w_branch, taps, row(conv_bias), w_step, w_bc, bias, rate,
+        scratch=[pltpu.VMEM((R + 2, SPAN, DI), F32)], scalars=1, flops=10**9,
+    )
     (y,) = call(local_kernel, [wide], act, bc, step, log)
-    out, g, d_gate, gated, norms, mv, mh = call(
-        norm_kernel, [((T, D), BF), low, low, low, ((8, DI), F32), msg_v, msg_h],
-        y, act, bc, log, tot, sv, sh, skip, own, w_gate, row(norm_gain), row(norm_bias), out_weight, cot,
+    out, g, d_gate, gated, norms, mv = call(
+        norm_kernel, [((T, D), BF), low, low, low, ((8, DI), F32), message],
+        y, act, bc, log, tot, sv, s0, s1, skip, own, w_gate, row(norm_gain), row(norm_bias), out_weight, cot,
     )
     lv = exchange(mv, "row", True)
-    lh = exchange(mh, "col", True)
+    band_g = whole_rows(g.reshape(R, C * DI)).reshape(8 * T, DI)
+    l0, l1 = call(row_back_kernel, [states, states], band_g, later, gate_c, flops=10**9)
     d_act, d_bc, d_step, d_log = call(
-        back_kernel, [wide, square, square, square], act, bc, step, log, g, sv, sh
+        back_kernel, [wide, square, square, square], act, bc, step, log, g, sv, s0, s1
     )
     gin_gate, gout = call(
         gate_grads_kernel, [((D, DI), F32), ((D, DI), F32)], own, d_gate, gated, cot, flops=10**7
     )
     gb, pack = call(
-        last_kernel, [low, ((672, 128), F32)],
-        halo, w_branch, taps, before, act, raw_d, bc, step, log, tot, g, sv, sh, lv, lh, d_act, d_bc, d_step,
-        d_log, skip, w_step, w_bc, bias, rate, gin_gate, gout, norms,
-    )
-    total = lax.psum(pack, ("row", "col"))
+        last_kernel, [low, ((1024, 128), BF)],
+        halo, w_branch, taps, before, act, raw_d, bc, step, log, tot, g, sv, s0, s1, lv, l0, l1, d_act, d_bc,
+        d_step, d_log, skip, w_step, w_bc, bias, rate, gin_gate, gout, norms,
+    )
     gb_halo = with_rim(gb.reshape(R, C, DI))
     (d_tokens,) = call(out_kernel, [((T, D), BF)], gb_halo, taps, d_gate, w_branch, w_gate)
     scale = float(T * lax.axis_size("row") * lax.axis_size("col")) ** (-0.5)
-    total = total * scale
-    full = jnp.concatenate(
-        [total[:448], jnp.concatenate([total[448:, :64], total[448:, 64:]], axis=0)], axis=1
-    )
-    small = full[288:304]
-    g_bc = full[304:432].reshape(2, 4, NS, DI)
-    g_step = full[432:444].reshape(4, HEADS, DI)
-    g_scan = jnp.concatenate([g_step, g_bc[0], g_bc[1]], axis=1)
+    row_shape = ((1, DI), F32)
+    gin, g_conv, g_cb, g_scan, g_bias, g_rate, g_skip, g_gain, g_shift, gout = call(
+        unpack_kernel,
+        [
+            ((D, 2 * DI), F32), ((3, 3, DI), F32), row_shape, ((4, DI, HEADS + 2 * NS), F32),
+            ((4, HEADS), F32), ((4, HEADS), F32), ((4, DI), F32), row_shape, row_shape, ((DI, D), F32),
+        ],
+        reduced(pack, scale), flops=10**7,
+    )
     return (
-        out.reshape(R, C * D),
-        d_tokens.reshape(R, C * D),
-        jnp.concatenate([full[:96], full[96:192]], axis=1),
-        small[:9].reshape(3, 3, DI),
-        small[9],
-        jnp.swapaxes(g_scan, 1, 2),
-        small[13, :12].reshape(4, HEADS),
-        small[14, :12].reshape(4, HEADS),
-        jnp.broadcast_to(small[10], (4, DI)),
-        small[11],
-        small[12],
-        full[192:288].T,
+        out.reshape(R, C * D), d_tokens.reshape(R, C * D), gin, g_conv, g_cb.reshape(DI), g_scan, g_bias,
+        g_rate, g_skip, g_gain.reshape(DI), g_shift.reshape(DI), gout,
     )
 
 

time: 525 us -> 221 us (0.42)
  waiting for transfers between devices: 292 us -> 39.7 us
  starting transfers between devices: 131 us -> 79.3 us
  between operations: 14.5 us -> 1 us
  blocking collectives: 40.2 us -> 51.1 us
  Pallas kernels: 26.2 us -> 32 us
    psum x1 -> x0, waiting for transfers between devices: 202 us -> none  [local(): total = lax.psum(pack, ('row', 'col'))]
    ppermute x16 -> x6, starting transfers between devices: 76 us -> 30 us  [the longest x3 22.6 us: edges(): after = lax.ppermute(lax.slice_in_dim(x, 0, 1, axis=dim), axis, down)]
    all_to_all x6, waiting for transfers between devices: 52.5 us -> 24.7 us  [all_to_all(): return lax.all_to_all(x, axis, 0, 0, tiled=True)]
    ppermute x16 -> x6, waiting for transfers between devices: 37.9 us -> 15 us  [the longest x3 12.4 us: edges(): lax.ppermute(lax.slice_in_dim(x, length - 1, length, axis=dim), axis, up)]
    all_to_all x2 -> x3, blocking collectives: 40.2 us -> 51.1 us  [all_to_all(): return lax.all_to_all(x, axis, 0, 0, tiled=True)]
    all_to_all x6, starting transfers between devices: 55.4 us -> 49.4 us  [all_to_all(): return lax.all_to_all(x, axis, 0, 0, tiled=True)]
    pallas_call x11 -> x14, Pallas kernels: 26.2 us -> 32 us  [call(): pl.pallas_call(kernel, out_shape=[jax.ShapeDtypeStruct(s, t) for s, t in...]
  transfers between devices with their start and end apart: 23 -> 12, of which waited for: 14 -> 9; matrix products, arithmetic and copies ran while one was open for 1% -> 2% of each run, Pallas kernels for 2% -> 8%
where the time goes in v2:
time: 221 us; the launch traced here: 218 us
  starting transfers between devices  79.3 us (36%)
  blocking collectives  51.1 us (23%)
  waiting for transfers between devices  39.7 us (18%)
  Pallas kernels  32 us (14%)
  local copies, waits for them, and re-layouts  14 us (6%)
    all_to_all x3, blocking collectives, all_to_all(): return lax.all_to_all(x, axis, 0, 0, tiled=True)  51.1 us
    all_to_all x6, starting transfers between devices, all_to_all(): return lax.all_to_all(x, axis, 0, 0, tiled=True)  49.4 us
    pallas_call x14, Pallas kernels, call(): pl.pallas_call(kernel, out_shape=[jax.ShapeDtypeStruct(s, t) for s, t in...  32 us
    all_to_all x6, waiting for transfers between devices, all_to_all(): return lax.all_to_all(x, axis, 0, 0, tiled=True)  24.7 us
    ppermute x3, starting transfers between devices, edges(): after = lax.ppermute(lax.slice_in_dim(x, 0, 1, axis=dim), axis, down)  22.6 us
    ppermute x3, waiting for transfers between devices, edges(): lax.ppermute(lax.slice_in_dim(x, length - 1, length, axis=dim), axis, up)  12.4 us
    unnamed x32, local copies, waits for them, and re-layouts  8.37 us
    ppermute x3, starting transfers between devices, edges(): lax.ppermute(lax.slice_in_dim(x, length - 1, length, axis=dim), axis, up)  7.39 us
  transfers between devices with their start and end apart: 12, of which 9 were waited for; matrix products, arithmetic and copies ran while one was open for 2% of the time, Pallas kernels for 8%

profile of v2, /device:TPU:56, one launch (start us, length us, event | category | flops | bytes accessed | tf_op | source)
XLA Modules:
  0.0 217.5 jit_solution(15819229431314820800)
XLA Ops:
  1.4 11.2 %collective-permute-start.1 = (bf16[1,768]{1,0:T(2,128)(2,1)S(1)}, bf16[1,768]{1,0:T(2,128)(2,1)S(1)}, u32[]{:S(2)}, u32[]{:S(2)}) collective-permute-start(bf16[1,768]{1,0:T(2,128)(2,1)S(1)} %get-tuple-element.145), channel_id=1, source_target_pairs={{8,0},{16,8},{24,16},{32,24},{40,32},{48,40},{56,48},{64,56},{72,6... | collective-permute-start | bytes 4616 | tf_op jit(solution)/shard_map/ppermute | solution.py:558
  12.6 1.9 collective-permute-start
  15.4 4.2 %collective-permute-done = bf16[1,768]{1,0:T(2,128)(2,1)S(1)} collective-permute-done((bf16[1,768]{1,0:T(2,128)(2,1)S(1)}, bf16[1,768]{1,0:T(2,128)(2,1)S(1)}, u32[]{:S(2)}, u32[]{:S(2)}) %collective-permute-start) | collective-permute-done | bytes 1568 | tf_op jit(solution)/shard_map/ppermute | solution.py:557
  20.4 9.7 %all-to-all-start = ((bf16[8,18,768]{2,1,0:T(8,128)(2,1)}), bf16[8,18,768]{2,1,0:T(8,128)(2,1)S(1)}, u32[]{:S(2)}, u32[]{:S(2)}) async-start(bf16[8,18,768]{2,1,0:T(8,128)(2,1)} %broadcast_in_dim.6), calls=%async_computation | async-start | bytes 589824 | tf_op jit(solution)/shard_map/all_to_all | solution.py:572
  33.6 2.7 %all-to-all-done = bf16[8,18,768]{2,1,0:T(8,128)(2,1)S(1)} async-done(((bf16[8,18,768]{2,1,0:T(8,128)(2,1)}), bf16[8,18,768]{2,1,0:T(8,128)(2,1)S(1)}, u32[]{:S(2)}, u32[]{:S(2)}) %all-to-all-start) | async-done | bytes 221216 | tf_op jit(solution)/shard_map/all_to_all | solution.py:572
  37.4 1.8 shard_map.211
  39.2 18.0 %all_to_all.45 = f32[64,8,128]{2,1,0:T(8,128)S(1)} all-to-all(f32[64,8,128]{2,1,0:T(8,128)S(1)} %get-tuple-element.55), channel_id=1, replica_groups=mesh['row'=64,'col'=8] {'row'}, dimensions={0} | all-to-all | bytes 524288 | tf_op jit(solution)/shard_map/all_to_all | solution.py:572
  58.1 6.2 %all-to-all-start.2 = ((f32[64,8,128]{2,1,0:T(8,128)}), f32[64,8,128]{2,1,0:T(8,128)S(1)}, u32[]{:S(2)}, u32[]{:S(2)}) async-start(f32[64,8,128]{2,1,0:T(8,128)} %bitcast.8), calls=%async_computation.2 | async-start | bytes 524288 | tf_op jit(solution)/shard_map/all_to_all | solution.py:572
  65.3 1.3 shard_map.212.y_ref
  66.7 7.9 %shard_map.214 = (f32[256,192]{1,0:T(8,128)S(1)}, f32[256,192]{1,0:T(8,128)S(1)}, f32[1024,128]{1,0:T(8,128)S(1)}, f32[1024,128]{1,0:T(8,128)S(1)}) custom-call(s32[1]{0:T(128)} %bitcast.9.me_ref, bf16[1440,96]{1,0:T(8,128)(2,1)S(1)} %bitcast.41, bf16[96,192]{1,0:T(8,128)(2,1)S(1)} %get-tuple-element.141.wbr_ref, f32[16,192]{1,0:T(8,128)S(1)} %pad.24.cw_ref, ...), custom_call_target="tpu_custom_call" | custom-call | flops 1000000000 | bytes 1000000 | tf_op jit(solution)/shard_map/pallas_call | solution.py:542
  76.5 3.1 %shard_map.215 = (bf16[128,96]{1,0:T(8,128)(2,1)S(1)}, bf16[128,192]{1,0:T(8,128)(2,1)S(1)}, bf16[128,192]{1,0:T(8,128)(2,1)S(1)}, bf16[128,192]{1,0:T(8,128)(2,...) custom-call(f32[128,192]{1,0:T(8,128)S(1)} %shard_map.212.y_ref, bf16[128,192]{1,0:T(8,128)(2,1)S(1)} %get-tuple-element.50.act_ref, ...), custom_call_target="tpu_custom_call" | custom-call | flops 100000000 | bytes 1000000 | tf_op jit(solution)/shard_map/pallas_call | solution.py:542
  79.6 10.4 %all-to-all-start.3 = ((f32[64,8,128]{2,1,0:T(8,128)}), f32[64,8,128]{2,1,0:T(8,128)S(1)}, u32[]{:S(2)}, u32[]{:S(2)}) async-start(f32[64,8,128]{2,1,0:T(8,128)} %get-tuple-element.62), calls=%async_computation.3 | async-start | bytes 524288 | tf_op jit(solution)/shard_map/all_to_all | solution.py:572
  90.0 11.4 %all-to-all-done.3 = f32[64,8,128]{2,1,0:T(8,128)S(1)} async-done(((f32[64,8,128]{2,1,0:T(8,128)}), f32[64,8,128]{2,1,0:T(8,128)S(1)}, u32[]{:S(2)}, u32[]{:S(2)}) %all-to-all-start.3) | async-done | bytes 262176 | tf_op jit(solution)/shard_map/all_to_all | solution.py:572
  102.2 9.0 %all-to-all-start.5 = ((bf16[8,16,1536]{2,1,0:T(8,128)(2,1)}), bf16[8,16,1536]{2,1,0:T(8,128)(2,1)S(1)}, u32[]{:S(2)}, u32[]{:S(2)}) async-start(bf16[8,16,1536]{2,1,0:T(8,128)(2,1)} %broadcast_in_dim.7), calls=%async_computation.5 | async-start | bytes 786432 | tf_op jit(solution)/shard_map/all_to_all | solution.py:572
  112.2 8.3 %all-to-all-done.5 = bf16[8,16,1536]{2,1,0:T(8,128)(2,1)S(1)} async-done(((bf16[8,16,1536]{2,1,0:T(8,128)(2,1)}), bf16[8,16,1536]{2,1,0:T(8,128)(2,1)S(1)}, u32[]{:S(2)}, u32[]{:S(2)}) %all-to-all-start.5) | async-done | bytes 393248 | tf_op jit(solution)/shard_map/all_to_all | solution.py:572
  120.5 8.0 %all-to-all-start.4 = ((f32[64,8,128]{2,1,0:T(8,128)}), f32[64,8,128]{2,1,0:T(8,128)S(1)}, u32[]{:S(2)}, u32[]{:S(2)}) async-start(f32[64,8,128]{2,1,0:T(8,128)} %bitcast.15), calls=%async_computation.4 | async-start | bytes 524288 | tf_op jit(solution)/shard_map/all_to_all | solution.py:572
  128.6 5.4 %shard_map.218 = (f32[128,192]{1,0:T(8,128)S(1)}, f32[128,128]{1,0:T(8,128)S(1)}, f32[128,128]{1,0:T(8,128)S(1)}, f32[128,128]{1,0:T(8,128)S(1)}) custom-call(bf16[128,192]{1,0:T(8,128)(2,1)S(1)} %get-tuple-element.50.act_ref, f32[128,128]{1,0:T(8,128)S(1)} %get-tuple-element.51.bc_ref, f32[128,128]{1,0:T(8,128)S(1)} %get-tuple-element.52.step_ref, ...), custom_call_target="tpu_custom_call" | custom-call | flops 100000000 | bytes 1000000 | tf_op jit(solution)/shard_map/pallas_call | solution.py:542
  134.5 1.0 copy-done.5
  135.6 2.1 shard_map.217
  137.7 1.9 all-to-all-done.4.lv_ref
  139.7 5.9 %shard_map.220 = (bf16[128,192]{1,0:T(8,128)(2,1)S(1)}, bf16[1024,128]{1,0:T(8,128)(2,1)S(1)}) custom-call(bf16[288,96]{1,0:T(8,128)(2,1)S(1)} %bitcast.45, bf16[96,192]{1,0:T(8,128)(2,1)S(1)} %get-tuple-element.141.wbr_ref, f32[16,192]{1,0:T(8,128)S(1)} %pad.24.cw_ref, f32[128,192]{1,0:T(8,128)S(1)} %get-tuple-element.59.before_ref, ...), custom_call_target="tpu_custom_call" | custom-call | flops 100000000 | bytes 1000000 | tf_op jit(solution)/shard_map/pallas_call | solution.py:542
  145.6 20.1 %all_to_all.46.x_ref = bf16[64,16,128]{2,1,0:T(8,128)(2,1)S(1)} all-to-all(bf16[64,16,128]{2,1,0:T(8,128)(2,1)S(1)} %bitcast.46), channel_id=1, replica_groups=mesh['row'=64,'col'=8] {'row'}, dimensions={0} | all-to-all | bytes 524288 | tf_op jit(solution)/shard_map/all_to_all | solution.py:572
  165.7 13.1 %all_to_all.47.x_ref = f32[8,16,128]{2,1,0:T(8,128)S(1)} all-to-all(f32[8,16,128]{2,1,0:T(8,128)S(1)} %shard_map.222), channel_id=1, replica_groups=mesh['row'=64,'col'=8] {'col'}, dimensions={0} | all-to-all | bytes 131072 | tf_op jit(solution)/shard_map/all_to_all | solution.py:572
  179.6 6.2 %all-to-all-start.8 = ((f32[64,16,128]{2,1,0:T(8,128)}), f32[64,16,128]{2,1,0:T(8,128)S(1)}, u32[]{:S(2)}, u32[]{:S(2)}) async-start(f32[64,16,128]{2,1,0:T(8,128)} %shard_map.223), calls=%async_computation.8 | async-start | bytes 1048576 | tf_op jit(solution)/shard_map/all_to_all | solution.py:572
  185.8 4.3 %collective-permute-start.3 = (bf16[1,8,192]{2,1,0:T(8,128)(2,1)S(1)}, bf16[1,8,192]{2,1,0:T(8,128)(2,1)S(1)}, u32[]{:S(2)}, u32[]{:S(2)}) collective-permute-start(bf16[1,8,192]{2,1,0:T(8,128)(2,1)S(1)} %get-tuple-element.143), channel_id=1, source_target_pairs={{8,0},{16,8},{24,16},{32,24},{40,32},{48,40},{56,48},{64,56},{72,6... | collective-permute-start | bytes 9224 | tf_op jit(solution)/shard_map/ppermute | solution.py:558
  190.1 1.9 collective-permute-start.2
  192.1 2.6 %collective-permute-done.3 = bf16[1,8,192]{2,1,0:T(8,128)(2,1)S(1)} collective-permute-done((bf16[1,8,192]{2,1,0:T(8,128)(2,1)S(1)}, bf16[1,8,192]{2,1,0:T(8,128)(2,1)S(1)}, u32[]{:S(2)}, u32[]{:S(2)}) %collective-permute-start.3) | collective-permute-done | bytes 3104 | tf_op jit(solution)/shard_map/ppermute | solution.py:558
  194.7 2.9 %collective-permute-done.2 = bf16[1,8,192]{2,1,0:T(8,128)(2,1)S(1)} collective-permute-done((bf16[1,8,192]{2,1,0:T(8,128)(2,1)S(1)}, bf16[1,8,192]{2,1,0:T(8,128)(2,1)S(1)}, u32[]{:S(2)}, u32[]{:S(2)}) %collective-permute-start.2) | collective-permute-done | bytes 3104 | tf_op jit(solution)/shard_map/ppermute | solution.py:557
  197.6 7.1 %collective-permute-start.5 = (bf16[18,1,192]{2,1,0:T(2,128)(2,1)S(1)}, bf16[18,1,192]{2,1,0:T(2,128)(2,1)S(1)}, u32[]{:S(2)}, u32[]{:S(2)}) collective-permute-start(bf16[18,1,192]{2,1,0:T(2,128)(2,1)S(1)} %get-tuple-element.139), channel_id=1, source_target_pairs={{1,0},{2,1},{3,2},{4,3},{5,4},{6,5},{7,6},{9,8},{10,9},{11,10},{12... | collective-permute-start | bytes 20744 | tf_op jit(solution)/shard_map/ppermute | solution.py:558
  204.7 3.5 %collective-permute-start.4 = (bf16[18,1,192]{2,1,0:T(2,128)(2,1)S(1)}, bf16[18,1,192]{2,1,0:T(2,128)(2,1)S(1)}, u32[]{:S(2)}, u32[]{:S(2)}) collective-permute-start(bf16[18,1,192]{2,1,0:T(2,128)(2,1)S(1)} %get-tuple-element.138), channel_id=1, source_target_pairs={{0,1},{1,2},{2,3},{3,4},{4,5},{5,6},{6,7},{8,9},{9,10},{10,11},{11... | collective-permute-start | bytes 20744 | tf_op jit(solution)/shard_map/ppermute | solution.py:557
  209.0 5.3 %collective-permute-done.4 = bf16[18,1,192]{2,1,0:T(2,128)(2,1)S(1)} collective-permute-done((bf16[18,1,192]{2,1,0:T(2,128)(2,1)S(1)}, bf16[18,1,192]{2,1,0:T(2,128)(2,1)S(1)}, u32[]{:S(2)}, u32[]{:S(2)}) %collective-permute-start.4) | collective-permute-done | bytes 6944 | tf_op jit(solution)/shard_map/ppermute | solution.py:557
  215.4 1.2 shard_map.224
  (75 shorter events, 17.0 us)
Async XLA Ops:
  1.4 14.0 %collective-permute-start.1 = (bf16[1,768]{1,0:T(2,128)(2,1)S(1)}, bf16[1,768]{1,0:T(2,128)(2,1)S(1)}, u32[]{:S(2)}, u32[]{:S(2)}) collective-permute-start(bf16[1,768]{1,0:T(2,128)(2,1)S(1)} %get-tuple-element.145), channel_id=1, source_target_pairs={{8,0},{16,8},{24,16},{32,24},{40,32},{48,40},{56,48},{64,56},{72,6... | collective-permute-start | bytes 4616 | tf_op jit(solution)/shard_map/ppermute | solution.py:558
  12.6 7.0 %copy-start.9 = (bf16[16,768]{1,0:T(8,128)(2,1)S(1)}, bf16[16,768]{1,0:T(8,128)(2,1)}, u32[]{:S(2)}) copy-start(bf16[16,768]{1,0:T(8,128)(2,1)} %param.12) | copy-start | bytes 73732
  12.6 7.0 %collective-permute-start = (bf16[1,768]{1,0:T(2,128)(2,1)S(1)}, bf16[1,768]{1,0:T(2,128)(2,1)S(1)}, u32[]{:S(2)}, u32[]{:S(2)}) collective-permute-start(bf16[1,768]{1,0:T(2,128)(2,1)S(1)} %get-tuple-element.144), channel_id=1, source_target_pairs={{0,8},{8,16},{16,24},{24,32},{32,40},{40,48},{48,56},{56,64},{64,7... | collective-permute-start | bytes 4616 | tf_op jit(solution)/shard_map/ppermute | solution.py:557
  20.4 16.0 %all-to-all-start = ((bf16[8,18,768]{2,1,0:T(8,128)(2,1)}), bf16[8,18,768]{2,1,0:T(8,128)(2,1)S(1)}, u32[]{:S(2)}, u32[]{:S(2)}) async-start(bf16[8,18,768]{2,1,0:T(8,128)(2,1)} %broadcast_in_dim.6), calls=%async_computation | async-start | bytes 589824 | tf_op jit(solution)/shard_map/all_to_all | solution.py:572
  30.0 0.7 copy-start.11
  31.0 0.7 copy-start.13
  31.8 0.7 copy-start.14
  32.6 0.9 copy-start.8
  36.8 0.7 copy-start.3
  58.1 17.7 %all-to-all-start.2 = ((f32[64,8,128]{2,1,0:T(8,128)}), f32[64,8,128]{2,1,0:T(8,128)S(1)}, u32[]{:S(2)}, u32[]{:S(2)}) async-start(f32[64,8,128]{2,1,0:T(8,128)} %bitcast.8), calls=%async_computation.2 | async-start | bytes 524288 | tf_op jit(solution)/shard_map/all_to_all | solution.py:572
  64.3 0.7 copy-start.12
  64.3 0.7 copy-start.10
  66.6 9.2 %copy-start = (bf16[192,96]{1,0:T(8,128)(2,1)S(1)}, bf16[192,96]{1,0:T(8,128)(2,1)}, u32[]{:S(2)}) copy-start(bf16[192,96]{1,0:T(8,128)(2,1)} %ow_ref.1) | copy-start | bytes 110596
  66.7 9.1 %copy-start.2 = (f32[192]{0:T(256)S(1)}, f32[192]{0:T(256)}, u32[]{:S(2)}) copy-start(f32[192]{0:T(256)} %param.21) | copy-start | bytes 2308
  74.6 0.8 copy-start.6
  75.4 4.2 %copy-start.4 = (f32[1024,128]{1,0:T(8,128)}, f32[1024,128]{1,0:T(8,128)S(1)}, u32[]{:S(2)}) copy-start(f32[1024,128]{1,0:T(8,128)S(1)} %get-tuple-element.63.later_ref) | copy-start | bytes 1572868
  75.8 0.7 copy-start.1
  79.6 21.8 %all-to-all-start.3 = ((f32[64,8,128]{2,1,0:T(8,128)}), f32[64,8,128]{2,1,0:T(8,128)S(1)}, u32[]{:S(2)}, u32[]{:S(2)}) async-start(f32[64,8,128]{2,1,0:T(8,128)} %get-tuple-element.62), calls=%async_computation.3 | async-start | bytes 524288 | tf_op jit(solution)/shard_map/all_to_all | solution.py:572
  102.2 18.3 %all-to-all-start.5 = ((bf16[8,16,1536]{2,1,0:T(8,128)(2,1)}), bf16[8,16,1536]{2,1,0:T(8,128)(2,1)S(1)}, u32[]{:S(2)}, u32[]{:S(2)}) async-start(bf16[8,16,1536]{2,1,0:T(8,128)(2,1)} %broadcast_in_dim.7), calls=%async_computation.5 | async-start | bytes 786432 | tf_op jit(solution)/shard_map/all_to_all | solution.py:572
  120.5 19.2 %all-to-all-start.4 = ((f32[64,8,128]{2,1,0:T(8,128)}), f32[64,8,128]{2,1,0:T(8,128)S(1)}, u32[]{:S(2)}, u32[]{:S(2)}) async-start(f32[64,8,128]{2,1,0:T(8,128)} %bitcast.15), calls=%async_computation.4 | async-start | bytes 524288 | tf_op jit(solution)/shard_map/all_to_all | solution.py:572
  134.4 1.0 copy-start.5
  134.4 1.2 copy-start.7
  179.6 35.8 %all-to-all-start.8 = ((f32[64,16,128]{2,1,0:T(8,128)}), f32[64,16,128]{2,1,0:T(8,128)S(1)}, u32[]{:S(2)}, u32[]{:S(2)}) async-start(f32[64,16,128]{2,1,0:T(8,128)} %shard_map.223), calls=%async_computation.8 | async-start | bytes 1048576 | tf_op jit(solution)/shard_map/all_to_all | solution.py:572
  185.8 8.8 %collective-permute-start.3 = (bf16[1,8,192]{2,1,0:T(8,128)(2,1)S(1)}, bf16[1,8,192]{2,1,0:T(8,128)(2,1)S(1)}, u32[]{:S(2)}, u32[]{:S(2)}) collective-permute-start(bf16[1,8,192]{2,1,0:T(8,128)(2,1)S(1)} %get-tuple-element.143), channel_id=1, source_target_pairs={{8,0},{16,8},{24,16},{32,24},{40,32},{48,40},{56,48},{64,56},{72,6... | collective-permute-start | bytes 9224 | tf_op jit(solution)/shard_map/ppermute | solution.py:558
  190.1 7.4 %collective-permute-start.2 = (bf16[1,8,192]{2,1,0:T(8,128)(2,1)S(1)}, bf16[1,8,192]{2,1,0:T(8,128)(2,1)S(1)}, u32[]{:S(2)}, u32[]{:S(2)}) collective-permute-start(bf16[1,8,192]{2,1,0:T(8,128)(2,1)S(1)} %get-tuple-element.142), channel_id=1, source_target_pairs={{0,8},{8,16},{16,24},{24,32},{32,40},{40,48},{48,56},{56,64},{64,7... | collective-permute-start | bytes 9224 | tf_op jit(solution)/shard_map/ppermute | solution.py:557
  197.6 11.4 %collective-permute-start.5 = (bf16[18,1,192]{2,1,0:T(2,128)(2,1)S(1)}, bf16[18,1,192]{2,1,0:T(2,128)(2,1)S(1)}, u32[]{:S(2)}, u32[]{:S(2)}) collective-permute-start(bf16[18,1,192]{2,1,0:T(2,128)(2,1)S(1)} %get-tuple-element.139), channel_id=1, source_target_pairs={{1,0},{2,1},{3,2},{4,3},{5,4},{6,5},{7,6},{9,8},{10,9},{11,10},{12... | collective-permute-start | bytes 20744 | tf_op jit(solution)/shard_map/ppermute | solution.py:558
  204.7 9.6 %collective-permute-start.4 = (bf16[18,1,192]{2,1,0:T(2,128)(2,1)S(1)}, bf16[18,1,192]{2,1,0:T(2,128)(2,1)S(1)}, u32[]{:S(2)}, u32[]{:S(2)}) collective-permute-start(bf16[18,1,192]{2,1,0:T(2,128)(2,1)S(1)} %get-tuple-element.138), channel_id=1, source_target_pairs={{0,1},{1,2},{2,3},{3,4},{4,5},{5,6},{6,7},{8,9},{9,10},{10,11},{11... | collective-permute-start | bytes 20744 | tf_op jit(solution)/shard_map/ppermute | solution.py:557

commit v3 on v2

--- a/solution.py
+++ b/solution.py
@@ -14,19 +14,31 @@
 R = 16
 C = 8
 T = R * C
-PITCH = 16
-SPAN = 80
+PITCH = 24
 
 F32 = jnp.float32
 BF = jnp.bfloat16
-HI = lax.Precision.HIGHEST
 FAR = -1e30
 
 
-def dot(a, b, ca=1, cb=0, precision=None):
-    return lax.dot_general(
-        a, b, (((ca,), (cb,)), ((), ())), precision=precision, preferred_element_type=F32
-    )
+def dot(a, b, ca=1, cb=0):
+    return lax.dot_general(a, b, (((ca,), (cb,)), ((), ())), preferred_element_type=F32)
+
+
+def halves(x):
+    if x.dtype == BF:
+        return [x]
+    high = x.astype(BF)
+    return [high, (x - high.astype(F32)).astype(BF)]
+
+
+def fine(a, b, ca=1, cb=0):
+    a, b = (halves(a), halves(b))
+    out = dot(a[0], b[0], ca, cb)
+    for i, j in ((0, 1), (1, 0)):
+        if i < len(a) and j < len(b):
+            out = out + dot(a[i], b[j], ca, cb)
+    return out
 
 
 def iota(shape, dim):
@@ -62,6 +74,10 @@
     return jnp.where(m, 1.0, 0.0).astype(F32)
 
 
+def ones(m):
+    return as_f32(m).astype(BF)
+
+
 def states_of(k):
     return 256 if k < 2 else 128
 
@@ -79,14 +95,14 @@
 
 def spread_states(bc, k):
     i, j = (iota((T, states_of(k)), 0), iota((T, states_of(k)), 1))
-    wide = dot(bc, as_f32(i == 16 * k + line_and_entry(j, k)[1]), precision=HI)
+    wide = fine(bc, ones(i == 16 * k + line_and_entry(j, k)[1]))
     return jnp.where(on_line(k), wide, 0.0)
 
 
 def gather_states(wide, k):
     j, i = (iota((states_of(k), T), 0), iota((states_of(k), T), 1))
     entry = line_and_entry(j, k)[1]
-    return dot(jnp.where(on_line(k), wide, 0.0), as_f32(i == 16 * k + entry), precision=HI)
+    return fine(jnp.where(on_line(k), wide, 0.0), ones(i == 16 * k + entry))
 
 
 def by_head(values, k):
@@ -97,7 +113,7 @@
 
 def head_sum(wide, k):
     c, j = (iota((DI, T), 0), iota((DI, T), 1))
-    return dot(wide, as_f32(j == 3 * k + c // 64), precision=HI)
+    return fine(wide, ones(j == 3 * k + c // 64))
 
 
 def per_head(f):
@@ -106,18 +122,24 @@
     return jnp.where(lane < 64, a, jnp.where(lane < 128, b, c))
 
 
-def write_message(ref, states, totals):
+def write_message(ref, wide_ref, states, totals):
     for d in range(2):
         s = states[d]
         for h in range(HEADS):
-            ref[:, d * 3 + h, :] = jnp.concatenate(
+            wide_ref[:, d * 3 + h, :] = jnp.concatenate(
                 [s[:64, 64 * h : 64 * h + 64], s[64:, 64 * h : 64 * h + 64]], axis=1
             )
     j, t = (iota((64, T), 0), iota((64, T), 1))
     i, o = (iota((T, T), 0), iota((T, T), 1))
-    totals = dot(totals, as_f32(i == o + 6), precision=HI)
-    ref[:, 6, :] = dot(as_f32(t == (j >> 3)), totals, precision=HI)
-    ref[:, 7, :] = jnp.zeros((64, T), F32)
+    totals = fine(ones(t == (j >> 3)), fine(totals, ones(i == o + 6)))
+    high = totals.astype(BF).astype(F32)
+    wide_ref[:, 6, :] = high
+    wide_ref[:, 7, :] = totals - high
+    ref[...] = wide_ref[...].reshape(512, 128).astype(BF)
+
+
+def open_message(ref, wide_ref):
+    wide_ref[...] = ref[...].astype(F32).reshape(64, 8, 128)
 
 
 def read_message(ref, d):
@@ -128,25 +150,27 @@
 
 
 def chain_kernel(backward, got_ref, out_ref):
-    n, m = (got_ref.shape[0], got_ref.shape[1])
-    sub = iota((m, 8, 128), 1)
-    lane = iota((m, 8, 128), 2)
+    m = 512 // lax.axis_size("row")
+    n = 512 // m
+    got = got_ref[...].astype(F32).reshape(n, m // 8, 8, 128)
+    shape = (m // 8, 8, 128)
+    sub, lane = (iota(shape, 1), iota(shape, 2))
     ahead = sub < 3 if not backward else sub >= 3
 
     def factor(i):
-        row = jnp.broadcast_to(got_ref[i, :, 6:7, :], (m, 8, 128))
+        row = jnp.broadcast_to(got[i, :, 6:7, :] + got[i, :, 7:8, :], shape)
         return jnp.sum(jnp.where(lane == sub, row, 0.0), axis=2, keepdims=True)
 
-    up = jnp.zeros((m, 8, 128), F32)
-    for i in range(n):
-        out_ref[i] = up
-        if i < n - 1:
-            up = factor(i) * up + got_ref[i]
-    down = jnp.zeros((m, 8, 128), F32)
-    for i in range(n - 1, -1, -1):
-        out_ref[i] = jnp.where(ahead, out_ref[i], down)
-        if i > 0:
-            down = factor(i) * down + got_ref[i]
+    factors = [factor(i) for i in range(n)]
+    up = [jnp.zeros(shape, F32)]
+    for i in range(n - 1):
+        up.append(factors[i] * up[i] + got[i])
+    down = [jnp.zeros(shape, F32)]
+    for i in range(n - 1, 0, -1):
+        down.append(factors[i] * down[-1] + got[i])
+    down = down[::-1]
+    full = jnp.concatenate([jnp.where(ahead, u, v) for u, v in zip(up, down)], axis=0)
+    out_ref[...] = full.reshape(512, 128).astype(BF)
 
 
 def state_in(k, rows, columns):
@@ -161,19 +185,37 @@
     return jnp.maximum(x, 0.0) + jnp.log1p(jnp.exp(-jnp.abs(x)))
 
 
-def conv_in(tok_ref, wbr_ref):
-    branch = dot(tok_ref[...], wbr_ref[...]).astype(BF).astype(F32)
-    return branch.reshape(R + 2, PITCH, DI)
+def fill_rim(pad_ref, above, own, below, left, right):
+    pad_ref[0:1, 8:16, :] = above.reshape(1, C, -1)
+    pad_ref[1 : R + 1, 8:16, :] = own.reshape(R, C, -1)
+    pad_ref[R + 1 : R + 2, 8:16, :] = below.reshape(1, C, -1)
+    for r in range(R + 2):
+        pad_ref[r, 7:8, :] = left[r : r + 1]
+        pad_ref[r, 16:17, :] = right[r : r + 1]
+
+
+def edge_factor(me, blocks, j):
+    return jnp.clip(j, 0, blocks - 1), jnp.where((j >= 0) & (j < blocks), 1.0, 0.0)
+
+
+def fill_blocks(me, got_ref, pad_ref, f):
+    for i in range(3):
+        at, inside = edge_factor(me, got_ref.shape[0], me + i - 1)
+        pad_ref[:, 8 * i : 8 * i + 8, :] = f(got_ref[at]).reshape(R + 2, C, -1) * inside
+
+
+def as_branch(wbr_ref):
+    return lambda x: dot(x, wbr_ref[...]).astype(BF).astype(F32)
 
 
 def first_kernel(
-    tok_ref, wbr_ref, cw_ref, cb_ref, wd_ref, wbc_ref, sb_ref, ld_ref,
-    before_ref, act_ref, rawd_ref, bc_ref, step_ref, log_ref, tot_ref, mv_ref,
+    me_ref, got_ref, wbr_ref, cw_ref, cb_ref, wd_ref, wbc_ref, sb_ref, ld_ref,
+    before_ref, act_ref, rawd_ref, bc_ref, step_ref, log_ref, tot_ref, mv_ref, pad_ref, wide_ref,
 ):
-    padded = conv_in(tok_ref, wbr_ref)
+    fill_blocks(me_ref[0], got_ref, pad_ref, as_branch(wbr_ref))
     total = jnp.zeros((R, C, DI), F32)
     for b in range(3):
-        shifted = padded[:, b : b + C, :]
+        shifted = pad_ref[:, 7 + b : 7 + b + C, :]
         for a in range(3):
             total = total + cw_ref[3 * a + b : 3 * a + b + 1, :] * shifted[a : a + R]
     before = total.reshape(T, DI) + cb_ref[...]
@@ -184,8 +226,8 @@
     bc = dot(act, wbc_ref[...])
     step = softplus(raw_d + sb_ref[...])
     log_step = step * -jnp.exp(ld_ref[...])
-    log = pick_lanes([dot(as_f32(mask(k)), log_step, precision=HI) for k in range(4)])
-    rows, cols = (dot(as_f32(same_line(v)), log_step, precision=HI) for v in (False, True))
+    log = pick_lanes([fine(ones(mask(k)), log_step) for k in range(4)])
+    rows, cols = (fine(ones(same_line(v)), log_step) for v in (False, True))
     tot = pick_lanes([rows, rows, cols, cols])
     rawd_ref[...] = raw_d
     bc_ref[...] = bc
@@ -195,17 +237,29 @@
     weight = jnp.exp(tot - log) * step
     wide = act.astype(F32)
     states = [
-        dot(spread_states(bc, k), by_head(weight, k) * wide, 0, 0, HI) for k in (2, 3)
+        fine(spread_states(bc, k), by_head(weight, k) * wide, 0, 0) for k in (2, 3)
     ]
-    write_message(mv_ref, states, jnp.exp(tot))
+    write_message(mv_ref, wide_ref, states, jnp.exp(tot))
+
+
+def row_pair(me, blocks_ref, group):
+    lines = []
+    for r in range(2):
+        at = pl.ds(16 * group, 16)
+        for j in range(8):
+            lines.append(blocks_ref[me ^ j, at, :].astype(F32)[8 * r : 8 * r + 8])
+    return jnp.concatenate(lines, axis=0)
 
 
 def row_scan_kernel(
-    me_ref, tok_ref, wbr_ref, cw_ref, cb_ref, wd_ref, wbc_ref, sb_ref, ld_ref,
+    me_ref, got_ref, wbr_ref, cw_ref, cb_ref, wd_ref, wbc_ref, sb_ref, ld_ref,
     s0_ref, s1_ref, later_ref, gate_ref, pad_ref,
 ):
-    branch = dot(tok_ref[...], wbr_ref[...]).astype(BF).astype(F32)
-    pad_ref[...] = branch.reshape(R + 2, SPAN, DI)
+    nothing = jnp.zeros((R + 2, 8, DI), F32)
+    pad_ref[:, 0:8, :] = nothing
+    pad_ref[:, 72:80, :] = nothing
+    for j in range(8):
+        pad_ref[:, 8 + 8 * j : 16 + 8 * j, :] = as_branch(wbr_ref)(got_ref[j]).reshape(R + 2, C, DI)
     low = me_ref[0] * C
     high = low + C
     t, u = (iota((T, T), 0), iota((T, T), 1))
@@ -217,7 +271,7 @@
         same & (u <= t) & (u >= high),
         same & (u >= t) & (u < low),
     ]
-    reach = jnp.concatenate([as_f32(m) for m in reach], axis=0)
+    reach = jnp.concatenate([ones(m) for m in reach], axis=0)
     before, after = (t < low, t >= high)
     first = iota((T, T), 1) < 3
     valid_in = jnp.where(first, as_f32(before), as_f32(after))
@@ -229,7 +283,7 @@
     for group in range(R // 2):
         total = jnp.zeros((2, 64, DI), F32)
         for b in range(3):
-            shifted = pad_ref[2 * group : 2 * group + 4, b : b + 64, :]
+            shifted = pad_ref[2 * group : 2 * group + 4, 7 + b : 71 + b, :]
             for a in range(3):
                 total = total + cw_ref[3 * a + b : 3 * a + b + 1, :] * shifted[a : a + 2]
         wide = total.reshape(T, DI) + cb_ref[...]
@@ -237,35 +291,35 @@
         wide = act.astype(F32)
         step = softplus(dot(act, wd_ref[...]) + sb_ref[...])
         bc = dot(act, wbc_ref[...])
-        x = dot(reach, step * rate, precision=HI)
+        x = fine(reach, step * rate)
         w_in = jnp.exp(jnp.where(first, x[:T], x[T : 2 * T])) * step * valid_in
         later_ref[group * T : group * T + T, :] = (
             jnp.exp(jnp.where(first, x[2 * T : 3 * T], x[3 * T :])) * valid_out
         )
         gate_ref[group * T : group * T + T, :] = shifted_gate(bc)
         for k, ref in enumerate((s0_ref, s1_ref)):
-            entry = as_f32(i == 16 * k + (ji & 15))
-            spread = jnp.where(line, dot(bc, entry, precision=HI), 0.0)
-            ref[32 * group : 32 * group + 32, :] = dot(spread, by_head(w_in, k) * wide, 0, 0, HI)
-
-
-def row_back_kernel(g_ref, later_ref, gate_ref, l0_ref, l1_ref):
+            entry = ones(i == 16 * k + (ji & 15))
+            spread = jnp.where(line, fine(bc, entry), 0.0)
+            ref[32 * group : 32 * group + 32, :] = fine(spread, by_head(w_in, k) * wide, 0, 0)
+
+
+def row_back_kernel(me_ref, blocks_ref, later_ref, gate_ref, l0_ref, l1_ref):
     tj, j = (iota((T, 32), 0), iota((T, 32), 1))
     line = (tj >> 6) == (j >> 4)
     for group in range(R // 2):
         part = slice(group * T, group * T + T)
-        g = g_ref[part, :].astype(F32)
+        g = row_pair(me_ref[0], blocks_ref, group)
         later = later_ref[part, :]
         gate = gate_ref[part, :]
         for k, ref in enumerate((l0_ref, l1_ref)):
-            entry = as_f32(tj == 16 * k + (j & 15))
-            spread = jnp.where(line, dot(gate, entry, precision=HI), 0.0)
-            ref[32 * group : 32 * group + 32, :] = dot(spread, by_head(later, k) * g, 0, 0, HI)
+            entry = ones(tj == 16 * k + (j & 15))
+            spread = jnp.where(line, fine(gate, entry), 0.0)
+            ref[32 * group : 32 * group + 32, :] = fine(spread, by_head(later, k) * g, 0, 0)
 
 
 def tables(k, bc, out_gate):
     lane = iota((T, T), 1) >> 4
-    return dot(jnp.where(lane == k, out_gate, 0.0), bc, 1, 1, HI)
+    return fine(jnp.where(lane == k, out_gate, 0.0), bc, 1, 1)
 
 
 def decay(k, h, log, log_t):
@@ -290,25 +344,26 @@
             weights[h] = weights[h] + scores * (
                 decay(k, h, log, log_t) * step_t[i : i + 1, :]
             )
-    wide = act_ref[...].astype(F32)
-    y_ref[...] = per_head(lambda h: dot(weights[h], wide, precision=HI))
+    act = act_ref[...]
+    y_ref[...] = per_head(lambda h: fine(weights[h], act))
 
 
 def carry(k, out_gate, exp_log, state):
-    return by_head(exp_log, k) * dot(spread_states(out_gate, k), state, precision=HI)
+    return by_head(exp_log, k) * fine(spread_states(out_gate, k), state)
 
 
 def norm_kernel(
     y_ref, act_ref, bc_ref, log_ref, tot_ref, sv_ref, s0_ref, s1_ref, skip_ref, tok_ref, wg_ref, gain_ref,
     nb_ref, ow_ref, cot_ref,
-    out_ref, g_ref, dgate_ref, gated_ref, norms_ref, mv_ref,
+    out_ref, g_ref, dgate_ref, gated_ref, norms_ref, mv_ref, wide_ref,
 ):
+    open_message(sv_ref, wide_ref)
     bc = bc_ref[...]
     out_gate = shifted_gate(bc)
     exp_log = jnp.exp(log_ref[...])
     summed = y_ref[...] + skip_ref[...] * act_ref[...].astype(F32)
     for k in range(4):
-        state = state_in(k, (s0_ref, s1_ref), sv_ref)
+        state = state_in(k, (s0_ref, s1_ref), wide_ref)
         summed = summed + carry(k, out_gate, exp_log, state)
     gate = dot(tok_ref[...], wg_ref[...]).astype(BF).astype(F32)
     sig = sigmoid(gate)
@@ -334,15 +389,16 @@
     g_ref[...] = g
     g = g.astype(F32)
     states = [
-        dot(spread_states(out_gate, k), by_head(exp_log, k) * g, 0, 0, HI) for k in (2, 3)
+        fine(spread_states(out_gate, k), by_head(exp_log, k) * g, 0, 0) for k in (2, 3)
     ]
-    write_message(mv_ref, states, jnp.exp(tot_ref[...]))
+    write_message(mv_ref, wide_ref, states, jnp.exp(tot_ref[...]))
 
 
 def back_kernel(
     act_ref, bc_ref, step_ref, log_ref, g_ref, sv_ref, s0_ref, s1_ref,
-    dact_ref, dbc_ref, dstep_ref, dlog_ref,
+    dact_ref, dbc_ref, dstep_ref, dlog_ref, wide_ref,
 ):
+    open_message(sv_ref, wide_ref)
     bc = bc_ref[...]
     out_gate = shifted_gate(bc)
     log = log_ref[...]
@@ -374,15 +430,15 @@
             step_rows.append(jnp.sum(d_step, axis=0, keepdims=True))
             rows = jnp.sum(d_step * step_t[i : i + 1, :], axis=1, keepdims=True)
             row_sums = jnp.where(lane1 == i, rows, row_sums)
-        d_out = d_out + dot(d_scores, jnp.where(lane16 == k, bc, 0.0), precision=HI)
-        d_in = d_in + dot(d_scores, jnp.where(lane16 == k, out_gate, 0.0), 0, 0, HI)
-        state = state_in(k, (s0_ref, s1_ref), sv_ref)
+        d_out = d_out + fine(d_scores, jnp.where(lane16 == k, bc, 0.0))
+        d_in = d_in + fine(d_scores, jnp.where(lane16 == k, out_gate, 0.0), 0, 0)
+        state = state_in(k, (s0_ref, s1_ref), wide_ref)
         expg = by_head(exp_log, k) * gw
-        carried = dot(spread_states(out_gate, k), state, precision=HI)
+        carried = fine(spread_states(out_gate, k), state)
         row_sums = row_sums + head_sum(carried * expg, k)
-        d_out = d_out + gather_states(dot(expg, state, 1, 1, HI), k)
+        d_out = d_out + gather_states(fine(expg, state, 1, 1), k)
     d_step = jnp.concatenate(step_rows + [jnp.zeros((T - 12, T), F32)], axis=0).T
-    dact_ref[...] = per_head(lambda h: dot(weights[h], gw, 0, 0, HI))
+    dact_ref[...] = per_head(lambda h: fine(weights[h], g, 0, 0))
     dbc_ref[...] = d_in + pltpu.roll(d_out, 64, 1)
     dstep_ref[...] = d_step
     dlog_ref[...] = row_sums - step * d_step
@@ -394,11 +450,13 @@
 
 
 def last_kernel(
-    tok_ref, wbr_ref, cw_ref, before_ref, act_ref, rawd_ref, bc_ref, step_ref, log_ref, tot_ref, g_ref,
+    me_ref, got_ref, wbr_ref, cw_ref, before_ref, act_ref, rawd_ref, bc_ref, step_ref, log_ref, tot_ref, g_ref,
     sv_ref, s0_ref, s1_ref, lv_ref, l0_ref, l1_ref, dact_ref, dbc_ref, dstep_ref, dlog_ref, skip_ref, wd_ref, wbc_ref,
     sb_ref, ld_ref, gin_gate_ref, gout_ref, norms_ref,
-    gb_ref, pack_ref,
+    gb_ref, pack_ref, pad_ref, tok_ref, early_ref, late_ref,
 ):
+    open_message(sv_ref, early_ref)
+    open_message(lv_ref, late_ref)
     step, log, tot, bc = (step_ref[...], log_ref[...], tot_ref[...], bc_ref[...])
     act = act_ref[...]
     wide = act.astype(F32)
@@ -411,22 +469,22 @@
     inner = jnp.zeros((T, T), F32)
     cross = jnp.zeros((T, T), F32)
     for k in range(4):
-        later = state_in(k, (l0_ref, l1_ref), lv_ref)
-        earlier = state_in(k, (s0_ref, s1_ref), sv_ref)
-        reach = dot(spread_states(bc, k), later, precision=HI)
+        later = state_in(k, (l0_ref, l1_ref), late_ref)
+        earlier = state_in(k, (s0_ref, s1_ref), early_ref)
+        reach = fine(spread_states(bc, k), later)
         wk = by_head(weight, k)
         d_act = d_act + wk * reach
         inner = inner + head_sum(wide * reach, k)
-        d_bc = d_bc + gather_states(dot(wk * wide, later, 1, 1, HI), k)
-        cross = cross + dot(as_f32(on_line(k)), head_sum(later * earlier, k), precision=HI)
+        d_bc = d_bc + gather_states(fine(wk * wide, later, 1, 1), k)
+        cross = cross + fine(ones(on_line(k)), head_sum(later * earlier, k))
     d_step = dstep_ref[...] + to_end * inner
     left = weight * inner
     d_log = dlog_ref[...]
     parts = []
     for k in range(4):
-        m = as_f32(mask(k))
-        rest = as_f32(same_line(k >= 2)) - m.T
-        parts.append(dot(m, d_log, 0, 0, HI) + dot(rest, left, precision=HI))
+        after = mask(k ^ 1)
+        rest = same_line(k >= 2) & jnp.logical_not(after)
+        parts.append(fine(ones(after), d_log) + fine(ones(rest), left))
     d_log_step = pick_lanes(parts) + cross * through
     rate = -jnp.exp(ld_ref[...])
     d_rate = jnp.sum(d_log_step * step, axis=0, keepdims=True) * rate
@@ -442,13 +500,13 @@
     gb = (d_act * sig * (1.0 + before * (1.0 - sig))).astype(BF)
     gb_ref[...] = gb
     gbw = gb.astype(F32)
-    padded = conv_in(tok_ref, wbr_ref)
-    tok = tok_ref[...].astype(F32).reshape(R + 2, PITCH, D)
+    fill_blocks(me_ref[0], got_ref, pad_ref, as_branch(wbr_ref))
+    fill_blocks(me_ref[0], got_ref, tok_ref, lambda x: x.astype(F32))
     gin = jnp.zeros((D, DI), F32)
     conv_rows = [None] * 9
     for b in range(3):
-        near = padded[:, b : b + C, :]
-        near_tok = tok[:, b : b + C, :]
+        near = pad_ref[:, 7 + b : 7 + b + C, :]
+        near_tok = tok_ref[:, 7 + b : 7 + b + C, :]
         for a in range(3):
             i = 3 * a + b
             conv_rows[i] = jnp.sum(gbw * near[a : a + R].reshape(T, DI), axis=0, keepdims=True)
@@ -484,11 +542,15 @@
     pack_ref[704:1024, :] = jnp.zeros((320, T), BF)
 
 
-def out_kernel(gb_ref, cw_ref, dgate_ref, wbr_ref, wg_ref, out_ref):
-    padded = gb_ref[...].astype(F32).reshape(R + 2, PITCH, DI)
+def out_kernel(
+    above_ref, own_ref, below_ref, left_ref, right_ref, cw_ref, dgate_ref, wbr_ref, wg_ref,
+    out_ref, pad_ref,
+):
+    around = (above_ref, own_ref, below_ref, left_ref, right_ref)
+    fill_rim(pad_ref, *(ref[...].astype(F32) for ref in around))
     total = jnp.zeros((R, C, DI), F32)
     for b in range(3):
-        shifted = padded[:, 2 - b : 2 - b + C, :]
+        shifted = pad_ref[:, 9 - b : 9 - b + C, :]
         for a in range(3):
             total = total + cw_ref[3 * a + b : 3 * a + b + 1, :] * shifted[2 - a : 2 - a + R]
     d_branch = total.reshape(T, DI).astype(BF)
@@ -550,41 +612,41 @@
     )(*args)
 
 
-def edges(x, axis, dim):
-    size, length = (lax.axis_size(axis), x.shape[dim])
+def neighbours(last, first, axis):
+    size = lax.axis_size(axis)
     up = [(i, i + 1) for i in range(size - 1)]
     down = [(j, i) for i, j in up]
-    before = lax.ppermute(lax.slice_in_dim(x, length - 1, length, axis=dim), axis, up)
-    after = lax.ppermute(lax.slice_in_dim(x, 0, 1, axis=dim), axis, down)
-    return before, after
+    return lax.ppermute(last, axis, up), lax.ppermute(first, axis, down)
 
 
 def with_rim(x):
-    before, after = edges(x, "row", 0)
-    x = jnp.concatenate([before, x, after], axis=0)
-    before, after = edges(x, "col", 1)
-    full = jnp.concatenate([before, x, after], axis=1)
-    full = jnp.pad(full, ((0, 0), (0, PITCH - C - 2), (0, 0)))
-    return full.reshape((R + 2) * PITCH, x.shape[-1])
+    above, below = neighbours(x[T - C :], x[:C], "row")
+    grid = x.reshape(R, C, -1)
+    side = lambda c: jnp.concatenate([above[c : c + 1], grid[:, c], below[c : c + 1]], axis=0)
+    left, right = neighbours(side(C - 1), side(0), "col")
+    return above, x, below, left, right
 
 
 def all_to_all(x, axis):
     return lax.all_to_all(x, axis, 0, 0, tiled=True)
 
 
-def whole_rows(x):
+def along_col(x):
     count = lax.axis_size("col")
-    everything = all_to_all(jnp.broadcast_to(x, (count,) + x.shape), "col")
-    everything = everything.reshape(count, x.shape[0], C, -1)
-    return jnp.swapaxes(everything, 0, 1).reshape(x.shape[0], count * C, -1)
+    blocks = x[None]
+    step = 1
+    while step < count:
+        pairs = [(i, i ^ step) for i in range(count)]
+        blocks = jnp.concatenate([blocks, lax.ppermute(blocks, "col", pairs)], axis=0)
+        step *= 2
+    return blocks
 
 
 def exchange(message, axis, backward):
-    size = lax.axis_size(axis)
-    got = all_to_all(message, axis)
-    shape = (size, message.shape[0] // size, 8, 128)
-    (states,) = call(partial(chain_kernel, backward), [(shape, F32)], got.reshape(shape), flops=10**7)
-    return all_to_all(states.reshape(message.shape), axis)
+    chunks = (64, 8, 128)
+    got = all_to_all(message.reshape(chunks), axis).reshape(512, 128)
+    (states,) = call(partial(chain_kernel, backward), [((512, 128), BF)], got, flops=10**7)
+    return all_to_all(states.reshape(chunks), axis).reshape(512, 128)
 
 
 def reduced(pack, scale):
@@ -602,12 +664,10 @@
     norm_bias, out_weight, cotangent,
 ):
     own = tokens.reshape(T, D)
-    place = lax.axis_index("col")
-    before, after = edges(tokens, "row", 0)
-    band = whole_rows(jnp.concatenate([before, tokens, after], axis=0))
-    band = jnp.pad(band, ((0, 0), (1, SPAN - 1 - band.shape[1]), (0, 0)))
-    halo = lax.dynamic_slice_in_dim(band, place * C, PITCH, axis=1).reshape((R + 2) * PITCH, D)
-    band = band.reshape((R + 2) * SPAN, D)
+    above, below = neighbours(own[T - C :], own[:C], "row")
+    band = jnp.concatenate([above, own, below], axis=0)
+    got = all_to_all(jnp.broadcast_to(band, (lax.axis_size("col"),) + band.shape), "col")
+    place = lax.axis_index("col").reshape(1)
     cot = cotangent.reshape(T, D)
     w_branch, w_gate = (in_weight[:, :DI], in_weight[:, DI:])
     taps = jnp.pad(conv_weight.reshape(9, DI), ((0, 7), (0, 0)))
@@ -627,41 +687,50 @@
     square = ((T, T), F32)
     wide = ((T, DI), F32)
     low = ((T, DI), BF)
-    message = ((64, 8, 128), F32)
+    message = ((512, 128), BF)
+    opened = pltpu.VMEM((64, 8, 128), F32)
     states = ((256, DI), F32)
     long = ((8 * T, T), F32)
 
     before, act, raw_d, bc, step, log, tot, mv = call(
         first_kernel, [wide, low, square, square, square, square, square, message],
-        halo, w_branch, taps, row(conv_bias), w_step, w_bc, bias, rate,
+        place, got, w_branch, taps, row(conv_bias), w_step, w_bc, bias, rate,
+        scratch=[pltpu.VMEM((R + 2, PITCH, DI), F32), opened], scalars=1,
     )
     sv = exchange(mv, "row", False)
     s0, s1, later, gate_c = call(
         row_scan_kernel, [states, states, long, long],
-        place.reshape(1), band, w_branch, taps, row(conv_bias), w_step, w_bc, bias, rate,
-        scratch=[pltpu.VMEM((R + 2, SPAN, DI), F32)], scalars=1, flops=10**9,
+        place, got, w_branch, taps, row(conv_bias), w_step, w_bc, bias, rate,
+        scratch=[pltpu.VMEM((R + 2, 80, DI), F32)], scalars=1, flops=10**9,
     )
     (y,) = call(local_kernel, [wide], act, bc, step, log)
     out, g, d_gate, gated, norms, mv = call(
         norm_kernel, [((T, D), BF), low, low, low, ((8, DI), F32), message],
         y, act, bc, log, tot, sv, s0, s1, skip, own, w_gate, row(norm_gain), row(norm_bias), out_weight, cot,
+        scratch=[opened],
     )
     lv = exchange(mv, "row", True)
-    band_g = whole_rows(g.reshape(R, C * DI)).reshape(8 * T, DI)
-    l0, l1 = call(row_back_kernel, [states, states], band_g, later, gate_c, flops=10**9)
+    l0, l1 = call(
+        row_back_kernel, [states, states], place, along_col(g), later, gate_c, scalars=1, flops=10**9
+    )
     d_act, d_bc, d_step, d_log = call(
-        back_kernel, [wide, square, square, square], act, bc, step, log, g, sv, s0, s1
+        back_kernel, [wide, square, square, square], act, bc, step, log, g, sv, s0, s1,
+        scratch=[opened],
     )
     gin_gate, gout = call(
         gate_grads_kernel, [((D, DI), F32), ((D, DI), F32)], own, d_gate, gated, cot, flops=10**7
     )
     gb, pack = call(
         last_kernel, [low, ((1024, 128), BF)],
-        halo, w_branch, taps, before, act, raw_d, bc, step, log, tot, g, sv, s0, s1, lv, l0, l1, d_act, d_bc,
+        place, got, w_branch, taps, before, act, raw_d, bc, step, log, tot, g, sv, s0, s1, lv, l0, l1, d_act, d_bc,
         d_step, d_log, skip, w_step, w_bc, bias, rate, gin_gate, gout, norms,
-    )
-    gb_halo = with_rim(gb.reshape(R, C, DI))
-    (d_tokens,) = call(out_kernel, [((T, D), BF)], gb_halo, taps, d_gate, w_branch, w_gate)
+        scratch=[pltpu.VMEM((R + 2, PITCH, DI), F32), pltpu.VMEM((R + 2, PITCH, D), F32), opened, opened],
+        scalars=1,
+    )
+    (d_tokens,) = call(
+        out_kernel, [((T, D), BF)], *with_rim(gb), taps, d_gate, w_branch, w_gate,
+        scratch=[pltpu.VMEM((R + 2, PITCH, DI), F32)],
+    )
     scale = float(T * lax.axis_size("row") * lax.axis_size("col")) ** (-0.5)
     row_shape = ((1, DI), F32)
     gin, g_conv, g_cb, g_scan, g_bias, g_rate, g_skip, g_gain, g_shift, gout = call(

time: 221 us -> 201 us (0.910)
  the two profiles are of different devices: /device:TPU:56 before, /device:TPU:48 now
where the time goes in v3:
time: 201 us; the launch traced here: 200 us
  starting transfers between devices  81.4 us (40%)
  blocking collectives  48.4 us (24%)
  waiting for transfers between devices  32.2 us (16%)
  Pallas kernels  25 us (12%)
  local copies, waits for them, and re-layouts  11.6 us (6%)
    all_to_all x3, blocking collectives, all_to_all(): return lax.all_to_all(x, axis, 0, 0, tiled=True)  48.4 us
    all_to_all x5, starting transfers between devices, all_to_all(): return lax.all_to_all(x, axis, 0, 0, tiled=True)  37 us
    ppermute x6, starting transfers between devices, neighbours(): return (lax.ppermute(last, axis, up), lax.ppermute(first, axis, down))  30.5 us
    pallas_call x14, Pallas kernels, call(): pl.pallas_call(kernel, out_shape=[jax.ShapeDtypeStruct(s, t) for s, t in...  25 us
    ppermute x6, waiting for transfers between devices, neighbours(): return (lax.ppermute(last, axis, up), lax.ppermute(first, axis, down))  18.1 us
    ppermute x3, starting transfers between devices, along_col(): lax.ppermute(blocks, 'col', pairs)  13.9 us
    all_to_all x5, waiting for transfers between devices, all_to_all(): return lax.all_to_all(x, axis, 0, 0, tiled=True)  10.9 us
    unnamed x34, local copies, waits for them, and re-layouts  6.83 us
  transfers between devices with their start and end apart: 14, of which 9 were waited for; matrix products, arithmetic and copies ran while one was open for 2% of the time, Pallas kernels for 7%

profile of v3, /device:TPU:48, one launch (start us, length us, event | category | flops | bytes accessed | tf_op | source)
XLA Modules:
  0.0 200.0 jit_solution(8946473463126727387)
XLA Ops:
  1.5 11.2 %collective-permute-start.1 = (bf16[8,96]{1,0:T(8,128)(2,1)S(1)}, bf16[8,96]{1,0:T(8,128)(2,1)S(1)}, u32[]{:S(2)}, u32[]{:S(2)}) collective-permute-start(bf16[8,96]{1,0:T(8,128)(2,1)S(1)} %slice.54), channel_id=1, source_target_pairs={{8,0},{16,8},{24,16},{32,24},{40,32},{48,40},{56,48},{64,56},{72,6... | collective-permute-start | bytes 4616 | tf_op jit(solution)/shard_map/ppermute | solution.py:619
  12.8 1.9 collective-permute-start
  15.6 4.2 %collective-permute-done = bf16[8,96]{1,0:T(8,128)(2,1)S(1)} collective-permute-done((bf16[8,96]{1,0:T(8,128)(2,1)S(1)}, bf16[8,96]{1,0:T(8,128)(2,1)S(1)}, u32[]{:S(2)}, u32[]{:S(2)}) %collective-permute-start) | collective-permute-done | bytes 1568 | tf_op jit(solution)/shard_map/ppermute | solution.py:619
  20.5 9.7 %all-to-all-start = ((bf16[8,144,96]{2,1,0:T(8,128)(2,1)}), bf16[8,144,96]{2,1,0:T(8,128)(2,1)S(1)}, u32[]{:S(2)}, u32[]{:S(2)}) async-start(bf16[8,144,96]{2,1,0:T(8,128)(2,1)} %broadcast_in_dim.6), calls=%async_computation | async-start | bytes 589824 | tf_op jit(solution)/shard_map/all_to_all | solution.py:631
  33.8 2.7 %all-to-all-done.got_ref = bf16[8,144,96]{2,1,0:T(8,128)(2,1)S(1)} async-done(((bf16[8,144,96]{2,1,0:T(8,128)(2,1)}), bf16[8,144,96]{2,1,0:T(8,128)(2,1)S(1)}, u32[]{:S(2)}, u32[]{:S(2)}) %all-to-all-start) | async-done | bytes 221216 | tf_op jit(solution)/shard_map/all_to_all | solution.py:631
  37.2 1.5 shard_map.211
  38.7 14.6 %all_to_all.40 = bf16[64,8,128]{2,1,0:T(8,128)(2,1)S(1)} all-to-all(bf16[64,8,128]{2,1,0:T(8,128)(2,1)S(1)} %bitcast.45), channel_id=1, replica_groups=mesh['row'=64,'col'=8] {'row'}, dimensions={0} | all-to-all | bytes 262144 | tf_op jit(solution)/shard_map/all_to_all | solution.py:631
  54.2 6.2 %all-to-all-start.2 = ((bf16[64,8,128]{2,1,0:T(8,128)(2,1)}), bf16[64,8,128]{2,1,0:T(8,128)(2,1)S(1)}, u32[]{:S(2)}, u32[]{:S(2)}) async-start(bf16[64,8,128]{2,1,0:T(8,128)(2,1)} %bitcast.7), calls=%async_computation.2 | async-start | bytes 262144 | tf_op jit(solution)/shard_map/all_to_all | solution.py:631
  61.3 6.1 %shard_map.214 = (f32[256,192]{1,0:T(8,128)S(1)}, f32[256,192]{1,0:T(8,128)S(1)}, f32[1024,128]{1,0:T(8,128)S(1)}, f32[1024,128]{1,0:T(8,128)S(1)}) custom-call(s32[1]{0:T(128)} %bitcast.me_ref, bf16[8,144,96]{2,1,0:T(8,128)(2,1)S(1)} %all-to-all-done.got_ref, bf16[96,192]{1,0:T(8,128)(2,1)S(1)} %get-tuple-element.117.wbr_ref, f32[16,192]{1,0:T(8,128)S(1)} %pad.15.cw_ref, ...), custom_call_target="tpu_custom_call" | custom-call | flops 1000000000 | bytes 1000000 | tf_op jit(solution)/shard_map/pallas_call | solution.py:604
  70.1 2.5 %shard_map.215 = (bf16[128,96]{1,0:T(8,128)(2,1)S(1)}, bf16[128,192]{1,0:T(8,128)(2,1)S(1)}, bf16[128,192]{1,0:T(8,128)(2,1)S(1)}, bf16[128,192]{1,0:T(8,128)(2,...) custom-call(f32[128,192]{1,0:T(8,128)S(1)} %shard_map.212.y_ref, bf16[128,192]{1,0:T(8,128)(2,1)S(1)} %get-tuple-element.50.act_ref, ...), custom_call_target="tpu_custom_call" | custom-call | flops 100000000 | bytes 1000000 | tf_op jit(solution)/shard_map/pallas_call | solution.py:604
  72.5 7.5 %collective-permute-start.2 = (bf16[1,128,192]{2,1,0:T(8,128)(2,1)S(1)}, bf16[1,128,192]{2,1,0:T(8,128)(2,1)S(1)}, u32[]{:S(2)}, u32[]{:S(2)}) collective-permute-start(bf16[1,128,192]{2,1,0:T(8,128)(2,1)S(1)} %bitcast.37), channel_id=1, source_target_pairs={{0,1},{1,0},{2,3},{3,2},{4,5},{5,4},{6,7},{7,6},{8,9},{9,8},{10,11... | collective-permute-start | bytes 147464 | tf_op jit(solution)/shard_map/ppermute | solution.py:640
  80.1 3.2 %collective-permute-done.2 = bf16[1,128,192]{2,1,0:T(8,128)(2,1)S(1)} collective-permute-done((bf16[1,128,192]{2,1,0:T(8,128)(2,1)S(1)}, bf16[1,128,192]{2,1,0:T(8,128)(2,1)S(1)}, u32[]{:S(2)}, u32[]{:S(2)}) %collective-permute-start.2) | collective-permute-done | bytes 49184 | tf_op jit(solution)/shard_map/ppermute | solution.py:640
  83.3 2.4 %collective-permute-start.3 = (bf16[2,128,192]{2,1,0:T(8,128)(2,1)S(1)}, bf16[2,128,192]{2,1,0:T(8,128)(2,1)S(1)}, u32[]{:S(2)}, u32[]{:S(2)}) collective-permute-start(bf16[2,128,192]{2,1,0:T(8,128)(2,1)S(1)} %pad_maximum_fusion.2), channel_id=1, source_target_pairs={{0,2},{1,3},{2,0},{3,1},{4,6},{5,7},{6,4},{7,5},{8,10},{9,11},{10,... | collective-permute-start | bytes 294920 | tf_op jit(solution)/shard_map/ppermute | solution.py:640
  85.7 9.1 %all-to-all-start.3 = ((bf16[64,8,128]{2,1,0:T(8,128)(2,1)}), bf16[64,8,128]{2,1,0:T(8,128)(2,1)S(1)}, u32[]{:S(2)}, u32[]{:S(2)}) async-start(bf16[64,8,128]{2,1,0:T(8,128)(2,1)} %bitcast.12), calls=%async_computation.3 | async-start | bytes 262144 | tf_op jit(solution)/shard_map/all_to_all | solution.py:631
  94.8 4.0 %collective-permute-start.4 = (bf16[4,128,192]{2,1,0:T(8,128)(2,1)S(1)}, bf16[4,128,192]{2,1,0:T(8,128)(2,1)S(1)}, u32[]{:S(2)}, u32[]{:S(2)}) collective-permute-start(bf16[4,128,192]{2,1,0:T(8,128)(2,1)S(1)} %pad_maximum_fusion.1), channel_id=1, source_target_pairs={{0,4},{1,5},{2,6},{3,7},{4,0},{5,1},{6,2},{7,3},{8,12},{9,13},{10,... | collective-permute-start | bytes 589832 | tf_op jit(solution)/shard_map/ppermute | solution.py:640
  98.8 5.0 %all-to-all-done.3 = bf16[64,8,128]{2,1,0:T(8,128)(2,1)S(1)} async-done(((bf16[64,8,128]{2,1,0:T(8,128)(2,1)}), bf16[64,8,128]{2,1,0:T(8,128)(2,1)S(1)}, u32[]{:S(2)}, u32[]{:S(2)}) %all-to-all-start.3) | async-done | bytes 131104 | tf_op jit(solution)/shard_map/all_to_all | solution.py:631
  104.6 6.0 %all-to-all-start.4 = ((bf16[64,8,128]{2,1,0:T(8,128)(2,1)}), bf16[64,8,128]{2,1,0:T(8,128)(2,1)S(1)}, u32[]{:S(2)}, u32[]{:S(2)}) async-start(bf16[64,8,128]{2,1,0:T(8,128)(2,1)} %bitcast.14), calls=%async_computation.4 | async-start | bytes 262144 | tf_op jit(solution)/shard_map/all_to_all | solution.py:631
  110.9 3.3 %shard_map.218 = (f32[128,192]{1,0:T(8,128)S(1)}, f32[128,128]{1,0:T(8,128)S(1)}, f32[128,128]{1,0:T(8,128)S(1)}, f32[128,128]{1,0:T(8,128)S(1)}) custom-call(bf16[128,192]{1,0:T(8,128)(2,1)S(1)} %get-tuple-element.50.act_ref, f32[128,128]{1,0:T(8,128)S(1)} %get-tuple-element.51.bc_ref, f32[128,128]{1,0:T(8,128)S(1)} %get-tuple-element.52.step_ref, ...), custom_call_target="tpu_custom_call" | custom-call | flops 100000000 | bytes 1000000 | tf_op jit(solution)/shard_map/pallas_call | solution.py:604
  115.3 2.4 %shard_map.217 = (f32[256,192]{1,0:T(8,128)S(1)}, f32[256,192]{1,0:T(8,128)S(1)}) custom-call(s32[1]{0:T(128)} %bitcast.me_ref, bf16[8,128,192]{2,1,0:T(8,128)(2,1)S(1)} %pad_maximum_fusion.blocks_ref, f32[1024,128]{1,0:T(8,128)S(1)} %copy-done.5, f32[1024,128]{1,0:T(8,128)S(1)} %copy-done.7), custom_call_target="tpu_custom_call" | custom-call | flops 1000000000 | bytes 1000000 | tf_op jit(solution)/shard_map/pallas_call | solution.py:604
  117.7 2.0 all-to-all-done.4
  119.7 4.2 %shard_map.220 = (bf16[128,192]{1,0:T(8,128)(2,1)S(1)}, bf16[1024,128]{1,0:T(8,128)(2,1)S(1)}) custom-call(s32[1]{0:T(128)} %bitcast.me_ref, bf16[8,144,96]{2,1,0:T(8,128)(2,1)S(1)} %all-to-all-done.got_ref, bf16[96,192]{1,0:T(8,128)(2,1)S(1)} %get-tuple-element.117.wbr_ref, f32[16,192]{1,0:T(8,128)S(1)} %pad.15.cw_ref, ...), custom_call_target="tpu_custom_call" | custom-call | flops 100000000 | bytes 1000000 | tf_op jit(solution)/shard_map/pallas_call | solution.py:604
  123.9 20.1 %all_to_all.41.x_ref = bf16[64,16,128]{2,1,0:T(8,128)(2,1)S(1)} all-to-all(bf16[64,16,128]{2,1,0:T(8,128)(2,1)S(1)} %bitcast.44), channel_id=1, replica_groups=mesh['row'=64,'col'=8] {'row'}, dimensions={0} | all-to-all | bytes 524288 | tf_op jit(solution)/shard_map/all_to_all | solution.py:631
  144.1 13.6 %all_to_all.42.x_ref = f32[8,16,128]{2,1,0:T(8,128)S(1)} all-to-all(f32[8,16,128]{2,1,0:T(8,128)S(1)} %shard_map.222), channel_id=1, replica_groups=mesh['row'=64,'col'=8] {'col'}, dimensions={0} | all-to-all | bytes 131072 | tf_op jit(solution)/shard_map/all_to_all | solution.py:631
  158.5 6.1 %all-to-all-start.7 = ((f32[64,16,128]{2,1,0:T(8,128)}), f32[64,16,128]{2,1,0:T(8,128)S(1)}, u32[]{:S(2)}, u32[]{:S(2)}) async-start(f32[64,16,128]{2,1,0:T(8,128)} %shard_map.223), calls=%async_computation.7 | async-start | bytes 1048576 | tf_op jit(solution)/shard_map/all_to_all | solution.py:631
  164.6 2.1 %collective-permute-start.5 = (bf16[8,192]{1,0:T(8,128)(2,1)S(1)}, bf16[8,192]{1,0:T(8,128)(2,1)S(1)}, u32[]{:S(2)}, u32[]{:S(2)}) collective-permute-start(bf16[8,192]{1,0:T(8,128)(2,1)S(1)} %get-tuple-element.121), channel_id=1, source_target_pairs={{0,8},{8,16},{16,24},{24,32},{32,40},{40,48},{48,56},{56,64},{64,7... | collective-permute-start | bytes 9224 | tf_op jit(solution)/shard_map/ppermute | solution.py:619
  166.7 5.6 %collective-permute-start.6 = (bf16[8,192]{1,0:T(8,128)(2,1)S(1)}, bf16[8,192]{1,0:T(8,128)(2,1)S(1)}, u32[]{:S(2)}, u32[]{:S(2)}) collective-permute-start(bf16[8,192]{1,0:T(8,128)(2,1)S(1)} %get-tuple-element.120), channel_id=1, source_target_pairs={{8,0},{16,8},{24,16},{32,24},{40,32},{48,40},{56,48},{64,56},{72,6... | collective-permute-start | bytes 9224 | tf_op jit(solution)/shard_map/ppermute | solution.py:619
  172.3 3.9 %collective-permute-done.6.below_ref = bf16[8,192]{1,0:T(8,128)(2,1)S(1)} collective-permute-done((bf16[8,192]{1,0:T(8,128)(2,1)S(1)}, bf16[8,192]{1,0:T(8,128)(2,1)S(1)}, u32[]{:S(2)}, u32[]{:S(2)}) %collective-permute-start.6) | collective-permute-done | bytes 3104 | tf_op jit(solution)/shard_map/ppermute | solution.py:619
  176.3 3.0 %collective-permute-done.5.above_ref = bf16[8,192]{1,0:T(8,128)(2,1)S(1)} collective-permute-done((bf16[8,192]{1,0:T(8,128)(2,1)S(1)}, bf16[8,192]{1,0:T(8,128)(2,1)S(1)}, u32[]{:S(2)}, u32[]{:S(2)}) %collective-permute-start.5) | collective-permute-done | bytes 3104 | tf_op jit(solution)/shard_map/ppermute | solution.py:619
  179.3 7.1 %collective-permute-start.7 = (bf16[18,192]{1,0:T(8,128)(2,1)S(1)}, bf16[18,192]{1,0:T(8,128)(2,1)S(1)}, u32[]{:S(2)}, u32[]{:S(2)}) collective-permute-start(bf16[18,192]{1,0:T(8,128)(2,1)S(1)} %pad_maximum_fusion.5), channel_id=1, source_target_pairs={{0,1},{1,2},{2,3},{3,4},{4,5},{5,6},{6,7},{8,9},{9,10},{10,11},{11... | collective-permute-start | bytes 20744 | tf_op jit(solution)/shard_map/ppermute | solution.py:619
  186.4 2.6 %collective-permute-start.8 = (bf16[18,192]{1,0:T(8,128)(2,1)S(1)}, bf16[18,192]{1,0:T(8,128)(2,1)S(1)}, u32[]{:S(2)}, u32[]{:S(2)}) collective-permute-start(bf16[18,192]{1,0:T(8,128)(2,1)S(1)} %pad_maximum_fusion.6), channel_id=1, source_target_pairs={{1,0},{2,1},{3,2},{4,3},{5,4},{6,5},{7,6},{9,8},{10,9},{11,10},{12... | collective-permute-start | bytes 20744 | tf_op jit(solution)/shard_map/ppermute | solution.py:619
  189.8 7.0 %collective-permute-done.8.right_ref = bf16[18,192]{1,0:T(8,128)(2,1)S(1)} collective-permute-done((bf16[18,192]{1,0:T(8,128)(2,1)S(1)}, bf16[18,192]{1,0:T(8,128)(2,1)S(1)}, u32[]{:S(2)}, u32[]{:S(2)}) %collective-permute-start.8) | collective-permute-done | bytes 6944 | tf_op jit(solution)/shard_map/ppermute | solution.py:619
  197.9 1.2 shard_map.224
  (81 shorter events, 17.1 us)
Async XLA Ops:
  0.6 14.9 %copy-start.9 = (bf16[4,192,35]{1,0,2:T(4,128)(2,1)S(1)}, bf16[4,192,35]{1,0,2:T(4,128)(2,1)}, u32[]{:S(2)}) copy-start(bf16[4,192,35]{1,0,2:T(4,128)(2,1)} %param.16) | copy-start | bytes 161284
  1.5 14.0 %collective-permute-start.1 = (bf16[8,96]{1,0:T(8,128)(2,1)S(1)}, bf16[8,96]{1,0:T(8,128)(2,1)S(1)}, u32[]{:S(2)}, u32[]{:S(2)}) collective-permute-start(bf16[8,96]{1,0:T(8,128)(2,1)S(1)} %slice.54), channel_id=1, source_target_pairs={{8,0},{16,8},{24,16},{32,24},{40,32},{48,40},{56,48},{64,56},{72,6... | collective-permute-start | bytes 4616 | tf_op jit(solution)/shard_map/ppermute | solution.py:619
  12.8 7.0 %collective-permute-start = (bf16[8,96]{1,0:T(8,128)(2,1)S(1)}, bf16[8,96]{1,0:T(8,128)(2,1)S(1)}, u32[]{:S(2)}, u32[]{:S(2)}) collective-permute-start(bf16[8,96]{1,0:T(8,128)(2,1)S(1)} %slice.52), channel_id=1, source_target_pairs={{0,8},{8,16},{16,24},{24,32},{32,40},{40,48},{48,56},{56,64},{64,7... | collective-permute-start | bytes 4616 | tf_op jit(solution)/shard_map/ppermute | solution.py:619
  20.5 16.0 %all-to-all-start = ((bf16[8,144,96]{2,1,0:T(8,128)(2,1)}), bf16[8,144,96]{2,1,0:T(8,128)(2,1)S(1)}, u32[]{:S(2)}, u32[]{:S(2)}) async-start(bf16[8,144,96]{2,1,0:T(8,128)(2,1)} %broadcast_in_dim.6), calls=%async_computation | async-start | bytes 589824 | tf_op jit(solution)/shard_map/all_to_all | solution.py:631
  30.2 0.7 copy-start.11
  31.2 0.7 copy-start.13
  32.0 0.7 copy-start.14
  32.8 0.9 copy-start.8
  36.5 0.7 copy-start.1
  54.2 6.2 %copy-start.12 = (f32[4,192]{1,0:T(4,128)S(1)}, f32[4,192]{1,0:T(4,128)}, u32[]{:S(2)}) copy-start(f32[4,192]{1,0:T(4,128)} %param.19) | copy-start | bytes 9220
  54.2 6.2 %copy-start.10 = (bf16[16,768]{1,0:T(8,128)(2,1)S(1)}, bf16[16,768]{1,0:T(8,128)(2,1)}, u32[]{:S(2)}) copy-start(bf16[16,768]{1,0:T(8,128)(2,1)} %param.23) | copy-start | bytes 73732
  54.2 15.2 %all-to-all-start.2 = ((bf16[64,8,128]{2,1,0:T(8,128)(2,1)}), bf16[64,8,128]{2,1,0:T(8,128)(2,1)S(1)}, u32[]{:S(2)}, u32[]{:S(2)}) async-start(bf16[64,8,128]{2,1,0:T(8,128)(2,1)} %bitcast.7), calls=%async_computation.2 | async-start | bytes 262144 | tf_op jit(solution)/shard_map/all_to_all | solution.py:631
  61.3 8.1 %copy-start = (bf16[192,96]{1,0:T(8,128)(2,1)S(1)}, bf16[192,96]{1,0:T(8,128)(2,1)}, u32[]{:S(2)}) copy-start(bf16[192,96]{1,0:T(8,128)(2,1)} %ow_ref.1) | copy-start | bytes 110596
  61.3 8.1 %copy-start.3 = (f32[192]{0:T(256)S(1)}, f32[192]{0:T(256)}, u32[]{:S(2)}) copy-start(f32[192]{0:T(256)} %param.21) | copy-start | bytes 2308
  67.4 0.8 copy-start.6
  68.2 4.4 %copy-start.4 = (f32[1024,128]{1,0:T(8,128)}, f32[1024,128]{1,0:T(8,128)S(1)}, u32[]{:S(2)}) copy-start(f32[1024,128]{1,0:T(8,128)S(1)} %get-tuple-element.63.later_ref) | copy-start | bytes 1572868
  69.4 0.7 copy-start.2
  72.5 10.7 %collective-permute-start.2 = (bf16[1,128,192]{2,1,0:T(8,128)(2,1)S(1)}, bf16[1,128,192]{2,1,0:T(8,128)(2,1)S(1)}, u32[]{:S(2)}, u32[]{:S(2)}) collective-permute-start(bf16[1,128,192]{2,1,0:T(8,128)(2,1)S(1)} %bitcast.37), channel_id=1, source_target_pairs={{0,1},{1,0},{2,3},{3,2},{4,5},{5,4},{6,7},{7,6},{8,9},{9,8},{10,11... | collective-permute-start | bytes 147464 | tf_op jit(solution)/shard_map/ppermute | solution.py:640
  83.3 11.5 %collective-permute-start.3 = (bf16[2,128,192]{2,1,0:T(8,128)(2,1)S(1)}, bf16[2,128,192]{2,1,0:T(8,128)(2,1)S(1)}, u32[]{:S(2)}, u32[]{:S(2)}) collective-permute-start(bf16[2,128,192]{2,1,0:T(8,128)(2,1)S(1)} %pad_maximum_fusion.2), channel_id=1, source_target_pairs={{0,2},{1,3},{2,0},{3,1},{4,6},{5,7},{6,4},{7,5},{8,10},{9,11},{10,... | collective-permute-start | bytes 294920 | tf_op jit(solution)/shard_map/ppermute | solution.py:640
  85.7 18.1 %all-to-all-start.3 = ((bf16[64,8,128]{2,1,0:T(8,128)(2,1)}), bf16[64,8,128]{2,1,0:T(8,128)(2,1)S(1)}, u32[]{:S(2)}, u32[]{:S(2)}) async-start(bf16[64,8,128]{2,1,0:T(8,128)(2,1)} %bitcast.12), calls=%async_computation.3 | async-start | bytes 262144 | tf_op jit(solution)/shard_map/all_to_all | solution.py:631
  94.8 19.4 %collective-permute-start.4 = (bf16[4,128,192]{2,1,0:T(8,128)(2,1)S(1)}, bf16[4,128,192]{2,1,0:T(8,128)(2,1)S(1)}, u32[]{:S(2)}, u32[]{:S(2)}) collective-permute-start(bf16[4,128,192]{2,1,0:T(8,128)(2,1)S(1)} %pad_maximum_fusion.1), channel_id=1, source_target_pairs={{0,4},{1,5},{2,6},{3,7},{4,0},{5,1},{6,2},{7,3},{8,12},{9,13},{10,... | collective-permute-start | bytes 589832 | tf_op jit(solution)/shard_map/ppermute | solution.py:640
  104.6 15.1 %all-to-all-start.4 = ((bf16[64,8,128]{2,1,0:T(8,128)(2,1)}), bf16[64,8,128]{2,1,0:T(8,128)(2,1)S(1)}, u32[]{:S(2)}, u32[]{:S(2)}) async-start(bf16[64,8,128]{2,1,0:T(8,128)(2,1)} %bitcast.14), calls=%async_computation.4 | async-start | bytes 262144 | tf_op jit(solution)/shard_map/all_to_all | solution.py:631
  114.1 1.0 copy-start.5
  114.2 1.2 copy-start.7
  158.5 39.4 %all-to-all-start.7 = ((f32[64,16,128]{2,1,0:T(8,128)}), f32[64,16,128]{2,1,0:T(8,128)S(1)}, u32[]{:S(2)}, u32[]{:S(2)}) async-start(f32[64,16,128]{2,1,0:T(8,128)} %shard_map.223), calls=%async_computation.7 | async-start | bytes 1048576 | tf_op jit(solution)/shard_map/all_to_all | solution.py:631
  164.6 14.6 %collective-permute-start.5 = (bf16[8,192]{1,0:T(8,128)(2,1)S(1)}, bf16[8,192]{1,0:T(8,128)(2,1)S(1)}, u32[]{:S(2)}, u32[]{:S(2)}) collective-permute-start(bf16[8,192]{1,0:T(8,128)(2,1)S(1)} %get-tuple-element.121), channel_id=1, source_target_pairs={{0,8},{8,16},{16,24},{24,32},{32,40},{40,48},{48,56},{56,64},{64,7... | collective-permute-start | bytes 9224 | tf_op jit(solution)/shard_map/ppermute | solution.py:619
  166.7 9.6 %collective-permute-start.6 = (bf16[8,192]{1,0:T(8,128)(2,1)S(1)}, bf16[8,192]{1,0:T(8,128)(2,1)S(1)}, u32[]{:S(2)}, u32[]{:S(2)}) collective-permute-start(bf16[8,192]{1,0:T(8,128)(2,1)S(1)} %get-tuple-element.120), channel_id=1, source_target_pairs={{8,0},{16,8},{24,16},{32,24},{40,32},{48,40},{56,48},{64,56},{72,6... | collective-permute-start | bytes 9224 | tf_op jit(solution)/shard_map/ppermute | solution.py:619
  179.3 10.5 %collective-permute-start.7 = (bf16[18,192]{1,0:T(8,128)(2,1)S(1)}, bf16[18,192]{1,0:T(8,128)(2,1)S(1)}, u32[]{:S(2)}, u32[]{:S(2)}) collective-permute-start(bf16[18,192]{1,0:T(8,128)(2,1)S(1)} %pad_maximum_fusion.5), channel_id=1, source_target_pairs={{0,1},{1,2},{2,3},{3,4},{4,5},{5,6},{6,7},{8,9},{9,10},{10,11},{11... | collective-permute-start | bytes 20744 | tf_op jit(solution)/shard_map/ppermute | solution.py:619
  186.4 10.4 %collective-permute-start.8 = (bf16[18,192]{1,0:T(8,128)(2,1)S(1)}, bf16[18,192]{1,0:T(8,128)(2,1)S(1)}, u32[]{:S(2)}, u32[]{:S(2)}) collective-permute-start(bf16[18,192]{1,0:T(8,128)(2,1)S(1)} %pad_maximum_fusion.6), channel_id=1, source_target_pairs={{1,0},{2,1},{3,2},{4,3},{5,4},{6,5},{7,6},{9,8},{10,9},{11,10},{12... | collective-permute-start | bytes 20744 | tf_op jit(solution)/shard_map/ppermute | solution.py:619

commit v4 on v3

--- a/solution.py
+++ b/solution.py
@@ -198,10 +198,14 @@
     return jnp.clip(j, 0, blocks - 1), jnp.where((j >= 0) & (j < blocks), 1.0, 0.0)
 
 
-def fill_blocks(me, got_ref, pad_ref, f):
-    for i in range(3):
+def fill_blocks(me, got_ref, edge_refs, pad_ref, f):
+    for i, edge_ref in enumerate(edge_refs):
         at, inside = edge_factor(me, got_ref.shape[0], me + i - 1)
-        pad_ref[:, 8 * i : 8 * i + 8, :] = f(got_ref[at]).reshape(R + 2, C, -1) * inside
+        place = slice(8 * i, 8 * i + 8)
+        edge = f(edge_ref[...])
+        pad_ref[0:1, place, :] = edge[:C].reshape(1, C, -1)
+        pad_ref[1 : R + 1, place, :] = f(got_ref[at]).reshape(R, C, -1) * inside
+        pad_ref[R + 1 : R + 2, place, :] = edge[C:].reshape(1, C, -1)
 
 
 def as_branch(wbr_ref):
@@ -209,10 +213,11 @@
 
 
 def first_kernel(
-    me_ref, got_ref, wbr_ref, cw_ref, cb_ref, wd_ref, wbc_ref, sb_ref, ld_ref,
+    me_ref, got_ref, left_ref, edge_ref, right_ref, wbr_ref, cw_ref, cb_ref, wd_ref, wbc_ref, sb_ref, ld_ref,
     before_ref, act_ref, rawd_ref, bc_ref, step_ref, log_ref, tot_ref, mv_ref, pad_ref, wide_ref,
 ):
-    fill_blocks(me_ref[0], got_ref, pad_ref, as_branch(wbr_ref))
+    edges = (left_ref, edge_ref, right_ref)
+    fill_blocks(me_ref[0], got_ref, edges, pad_ref, as_branch(wbr_ref))
     total = jnp.zeros((R, C, DI), F32)
     for b in range(3):
         shifted = pad_ref[:, 7 + b : 7 + b + C, :]
@@ -252,14 +257,18 @@
 
 
 def row_scan_kernel(
-    me_ref, got_ref, wbr_ref, cw_ref, cb_ref, wd_ref, wbc_ref, sb_ref, ld_ref,
+    me_ref, got_ref, edges_ref, wbr_ref, cw_ref, cb_ref, wd_ref, wbc_ref, sb_ref, ld_ref,
     s0_ref, s1_ref, later_ref, gate_ref, pad_ref,
 ):
     nothing = jnp.zeros((R + 2, 8, DI), F32)
     pad_ref[:, 0:8, :] = nothing
     pad_ref[:, 72:80, :] = nothing
     for j in range(8):
-        pad_ref[:, 8 + 8 * j : 16 + 8 * j, :] = as_branch(wbr_ref)(got_ref[j]).reshape(R + 2, C, DI)
+        place = slice(8 + 8 * j, 16 + 8 * j)
+        edge = as_branch(wbr_ref)(edges_ref[me_ref[0] ^ j])
+        pad_ref[0:1, place, :] = edge[:C].reshape(1, C, DI)
+        pad_ref[1 : R + 1, place, :] = as_branch(wbr_ref)(got_ref[j]).reshape(R, C, DI)
+        pad_ref[R + 1 : R + 2, place, :] = edge[C:].reshape(1, C, DI)
     low = me_ref[0] * C
     high = low + C
     t, u = (iota((T, T), 0), iota((T, T), 1))
@@ -450,7 +459,7 @@
 
 
 def last_kernel(
-    me_ref, got_ref, wbr_ref, cw_ref, before_ref, act_ref, rawd_ref, bc_ref, step_ref, log_ref, tot_ref, g_ref,
+    me_ref, got_ref, left_ref, edge_ref, right_ref, wbr_ref, cw_ref, before_ref, act_ref, rawd_ref, bc_ref, step_ref, log_ref, tot_ref, g_ref,
     sv_ref, s0_ref, s1_ref, lv_ref, l0_ref, l1_ref, dact_ref, dbc_ref, dstep_ref, dlog_ref, skip_ref, wd_ref, wbc_ref,
     sb_ref, ld_ref, gin_gate_ref, gout_ref, norms_ref,
     gb_ref, pack_ref, pad_ref, tok_ref, early_ref, late_ref,
@@ -500,8 +509,9 @@
     gb = (d_act * sig * (1.0 + before * (1.0 - sig))).astype(BF)
     gb_ref[...] = gb
     gbw = gb.astype(F32)
-    fill_blocks(me_ref[0], got_ref, pad_ref, as_branch(wbr_ref))
-    fill_blocks(me_ref[0], got_ref, tok_ref, lambda x: x.astype(F32))
+    edges = (left_ref, edge_ref, right_ref)
+    fill_blocks(me_ref[0], got_ref, edges, pad_ref, as_branch(wbr_ref))
+    fill_blocks(me_ref[0], got_ref, edges, tok_ref, lambda x: x.astype(F32))
     gin = jnp.zeros((D, DI), F32)
     conv_rows = [None] * 9
     for b in range(3):
@@ -563,17 +573,17 @@
     total = x_ref[0].astype(F32)
     for i in range(1, x_ref.shape[0]):
         total = total + x_ref[i].astype(F32)
-    out_ref[...] = jnp.broadcast_to(total * scale, out_ref.shape)
+    out_ref[...] = jnp.broadcast_to((total * scale).astype(out_ref.dtype), out_ref.shape)
 
 
 def unpack_kernel(
     x_ref, gin_ref, conv_ref, cb_ref, scan_ref, sb_ref, ld_ref, skip_ref, gain_ref, nb_ref, gout_ref
 ):
-    low, high = (x_ref[0:448, :], x_ref[448:672, :])
+    low, high = (x_ref[0:448, :].astype(F32), x_ref[448:672, :].astype(F32))
     full = jnp.concatenate(
         [low, jnp.concatenate([high[:, :64], high[:, 64:]], axis=0)], axis=1
     )
-    rest = jnp.concatenate([x_ref[672:688, :], x_ref[688:704, :64]], axis=1)
+    rest = jnp.concatenate([x_ref[672:688, :], x_ref[688:704, :64]], axis=1).astype(F32)
     gin_ref[...] = jnp.concatenate([full[:96], full[96:192]], axis=1)
     gout_ref[...] = full[192:288].T
     small = full[288:304] + rest
@@ -586,16 +596,10 @@
     for k in range(4):
         sb_ref[k : k + 1, :] = small[13:14, 3 * k : 3 * k + 3]
         ld_ref[k : k + 1, :] = small[14:15, 3 * k : 3 * k + 3]
-    scan = jnp.concatenate([full[304:448], jnp.zeros((112, DI), F32)], axis=0).T
     for k in range(4):
-        scan_ref[k] = jnp.concatenate(
-            [
-                scan[:, 128 + 3 * k : 131 + 3 * k],
-                scan[:, 16 * k : 16 * k + 16],
-                scan[:, 64 + 16 * k : 80 + 16 * k],
-            ],
-            axis=1,
-        )
+        scan_ref[0:3, k, :] = full[432 + 3 * k : 435 + 3 * k]
+        scan_ref[3:19, k, :] = full[304 + 16 * k : 320 + 16 * k]
+        scan_ref[19:35, k, :] = full[368 + 16 * k : 384 + 16 * k]
 
 
 def call(kernel, outs, *args, flops=10**8, scratch=(), scalars=0):
@@ -631,32 +635,37 @@
     return lax.all_to_all(x, axis, 0, 0, tiled=True)
 
 
-def along_col(x):
-    count = lax.axis_size("col")
-    blocks = x[None]
-    step = 1
-    while step < count:
-        pairs = [(i, i ^ step) for i in range(count)]
-        blocks = jnp.concatenate([blocks, lax.ppermute(blocks, "col", pairs)], axis=0)
-        step *= 2
-    return blocks
-
-
-def exchange(message, axis, backward):
+def swapped(x, step):
+    return lax.ppermute(x, "col", [(i, i ^ step) for i in range(lax.axis_size("col"))])
+
+
+def in_pairs(x):
+    return jnp.stack([x, swapped(x, 1)])
+
+
+def along_col(pair):
+    others = [swapped(pair, step) for step in range(2, lax.axis_size("col"), 2)]
+    return jnp.concatenate([pair] + others, axis=0)
+
+
+def exchange(message, axis, backward, meanwhile=()):
     chunks = (64, 8, 128)
-    got = all_to_all(message.reshape(chunks), axis).reshape(512, 128)
+    got, meanwhile = lax.optimization_barrier(
+        (all_to_all(message.reshape(chunks), axis).reshape(512, 128), meanwhile)
+    )
     (states,) = call(partial(chain_kernel, backward), [((512, 128), BF)], got, flops=10**7)
-    return all_to_all(states.reshape(chunks), axis).reshape(512, 128)
-
-
-def reduced(pack, scale):
+    return all_to_all(states.reshape(chunks), axis).reshape(512, 128), meanwhile
+
+
+def reduced(pack, scale, meanwhile):
     rows, cols = (lax.axis_size("row"), lax.axis_size("col"))
     chunk = pack.shape[0] // rows
     got = all_to_all(pack.reshape(rows, chunk, 128), "row")
     (part,) = call(partial(sum_kernel, 1.0), [((cols, chunk, 128), F32)], got, flops=10**7)
+    part, meanwhile = lax.optimization_barrier((part, meanwhile))
     got = all_to_all(part, "col")
-    (part,) = call(partial(sum_kernel, scale), [((rows, chunk, 128), F32)], got, flops=10**7)
-    return all_to_all(part, "row").reshape(pack.shape)
+    (part,) = call(partial(sum_kernel, scale), [((rows, chunk, 128), BF)], got, flops=10**7)
+    return all_to_all(part, "row").reshape(pack.shape), meanwhile
 
 
 def local(
@@ -664,9 +673,10 @@
     norm_bias, out_weight, cotangent,
 ):
     own = tokens.reshape(T, D)
-    above, below = neighbours(own[T - C :], own[:C], "row")
-    band = jnp.concatenate([above, own, below], axis=0)
-    got = all_to_all(jnp.broadcast_to(band, (lax.axis_size("col"),) + band.shape), "col")
+    count = lax.axis_size("col")
+    got = all_to_all(jnp.broadcast_to(tokens, (count,) + tokens.shape), "col").reshape(count, T, D)
+    edge = jnp.concatenate(neighbours(own[T - C :], own[:C], "row"), axis=0)
+    left, right = neighbours(edge, edge, "col")
     place = lax.axis_index("col").reshape(1)
     cot = cotangent.reshape(T, D)
     w_branch, w_gate = (in_weight[:, :DI], in_weight[:, DI:])
@@ -694,13 +704,14 @@
 
     before, act, raw_d, bc, step, log, tot, mv = call(
         first_kernel, [wide, low, square, square, square, square, square, message],
-        place, got, w_branch, taps, row(conv_bias), w_step, w_bc, bias, rate,
+        place, got, left, edge, right, w_branch, taps, row(conv_bias), w_step, w_bc, bias, rate,
         scratch=[pltpu.VMEM((R + 2, PITCH, DI), F32), opened], scalars=1,
     )
-    sv = exchange(mv, "row", False)
+    mv, edge_pair = lax.optimization_barrier((mv, in_pairs(edge)))
+    sv, edges = exchange(mv, "row", False, along_col(edge_pair))
     s0, s1, later, gate_c = call(
         row_scan_kernel, [states, states, long, long],
-        place, got, w_branch, taps, row(conv_bias), w_step, w_bc, bias, rate,
+        place, got, edges, w_branch, taps, row(conv_bias), w_step, w_bc, bias, rate,
         scratch=[pltpu.VMEM((R + 2, 80, DI), F32)], scalars=1, flops=10**9,
     )
     (y,) = call(local_kernel, [wide], act, bc, step, log)
@@ -709,40 +720,42 @@
         y, act, bc, log, tot, sv, s0, s1, skip, own, w_gate, row(norm_gain), row(norm_bias), out_weight, cot,
         scratch=[opened],
     )
-    lv = exchange(mv, "row", True)
-    l0, l1 = call(
-        row_back_kernel, [states, states], place, along_col(g), later, gate_c, scalars=1, flops=10**9
-    )
+    lv, pair = exchange(mv, "row", True, in_pairs(g))
     d_act, d_bc, d_step, d_log = call(
         back_kernel, [wide, square, square, square], act, bc, step, log, g, sv, s0, s1,
         scratch=[opened],
     )
+    l0, l1 = call(
+        row_back_kernel, [states, states], place, along_col(pair), later, gate_c, scalars=1, flops=10**9
+    )
     gin_gate, gout = call(
         gate_grads_kernel, [((D, DI), F32), ((D, DI), F32)], own, d_gate, gated, cot, flops=10**7
     )
     gb, pack = call(
         last_kernel, [low, ((1024, 128), BF)],
-        place, got, w_branch, taps, before, act, raw_d, bc, step, log, tot, g, sv, s0, s1, lv, l0, l1, d_act, d_bc,
+        place, got, left, edge, right, w_branch, taps, before, act, raw_d, bc, step, log, tot, g, sv, s0, s1, lv, l0, l1, d_act, d_bc,
         d_step, d_log, skip, w_step, w_bc, bias, rate, gin_gate, gout, norms,
         scratch=[pltpu.VMEM((R + 2, PITCH, DI), F32), pltpu.VMEM((R + 2, PITCH, D), F32), opened, opened],
         scalars=1,
     )
+    scale = float(T * lax.axis_size("row") * lax.axis_size("col")) ** (-0.5)
+    total, rim = reduced(pack, scale, with_rim(gb))
     (d_tokens,) = call(
-        out_kernel, [((T, D), BF)], *with_rim(gb), taps, d_gate, w_branch, w_gate,
+        out_kernel, [((T, D), BF)], *rim, taps, d_gate, w_branch, w_gate,
         scratch=[pltpu.VMEM((R + 2, PITCH, DI), F32)],
     )
-    scale = float(T * lax.axis_size("row") * lax.axis_size("col")) ** (-0.5)
     row_shape = ((1, DI), F32)
     gin, g_conv, g_cb, g_scan, g_bias, g_rate, g_skip, g_gain, g_shift, gout = call(
         unpack_kernel,
         [
-            ((D, 2 * DI), F32), ((3, 3, DI), F32), row_shape, ((4, DI, HEADS + 2 * NS), F32),
+            ((D, 2 * DI), F32), ((3, 3, DI), F32), row_shape, ((HEADS + 2 * NS, 4, DI), F32),
             ((4, HEADS), F32), ((4, HEADS), F32), ((4, DI), F32), row_shape, row_shape, ((DI, D), F32),
         ],
-        reduced(pack, scale), flops=10**7,
+        total, flops=10**7,
     )
     return (
-        out.reshape(R, C * D), d_tokens.reshape(R, C * D), gin, g_conv, g_cb.reshape(DI), g_scan, g_bias,
+        out.reshape(R, C * D), d_tokens.reshape(R, C * D), gin, g_conv, g_cb.reshape(DI),
+        jnp.transpose(g_scan, (1, 2, 0)), g_bias,
         g_rate, g_skip, g_gain.reshape(DI), g_shift.reshape(DI), gout,
     )
 

time: 201 us -> 226 us (1.12)
  the two profiles are of different devices: /device:TPU:48 before, /device:TPU:1 now
where the time goes in v4:
time: 226 us; the launch traced here: 225 us
  starting transfers between devices  134 us (59%)
  waiting for transfers between devices  39.4 us (17%)
  Pallas kernels  25.8 us (11%)
  blocking collectives  14.1 us (6%)
  local copies, waits for them, and re-layouts  10.1 us (4%)
    all_to_all x7, starting transfers between devices, all_to_all(): return lax.all_to_all(x, axis, 0, 0, tiled=True)  76.5 us
    ppermute x8, starting transfers between devices, swapped(): lax.ppermute(x, 'col', [(i, i ^ step) for i in range(lax.axis_size('col'))])  33.6 us
    pallas_call x14, Pallas kernels, call(): pl.pallas_call(kernel, out_shape=[jax.ShapeDtypeStruct(s, t) for s, t in...  25.8 us
    ppermute x8, starting transfers between devices, neighbours(): return (lax.ppermute(last, axis, up), lax.ppermute(first, axis, down))  23.7 us
    ppermute x8, waiting for transfers between devices, neighbours(): return (lax.ppermute(last, axis, up), lax.ppermute(first, axis, down))  20.5 us
    all_to_all x7, waiting for transfers between devices, all_to_all(): return lax.all_to_all(x, axis, 0, 0, tiled=True)  14.3 us
    all_to_all x1, blocking collectives, all_to_all(): return lax.all_to_all(x, axis, 0, 0, tiled=True)  14.1 us
    unnamed x36, local copies, waits for them, and re-layouts  5.75 us
  transfers between devices with their start and end apart: 23, of which 10 were waited for; matrix products, arithmetic and copies ran while one was open for 1% of the time, Pallas kernels for 6%

profile of v4, /device:TPU:1, one launch (start us, length us, event | category | flops | bytes accessed | tf_op | source)
XLA Modules:
  0.0 224.9 jit_solution(16597426333324118779)
XLA Ops:
  2.1 10.2 %all-to-all-start = ((bf16[8,16,768]{2,1,0:T(8,128)(2,1)}), bf16[8,16,768]{2,1,0:T(8,128)(2,1)S(1)}, u32[]{:S(2)}, u32[]{:S(2)}) async-start(bf16[8,16,768]{2,1,0:T(8,128)(2,1)} %broadcast_in_dim.3), calls=%async_computation | async-start | bytes 393216 | tf_op jit(solution)/shard_map/all_to_all | solution.py:635
  12.4 4.8 %collective-permute-start = (bf16[8,96]{1,0:T(8,128)(2,1)S(1)}, bf16[8,96]{1,0:T(8,128)(2,1)S(1)}, u32[]{:S(2)}, u32[]{:S(2)}) collective-permute-start(bf16[8,96]{1,0:T(8,128)(2,1)S(1)} %slice.52), channel_id=1, source_target_pairs={{0,8},{8,16},{16,24},{24,32},{32,40},{40,48},{48,56},{56,64},{64,7... | collective-permute-start | bytes 4616 | tf_op jit(solution)/shard_map/ppermute | solution.py:623
  19.8 2.9 %collective-permute-done.1 = bf16[8,96]{1,0:T(8,128)(2,1)S(1)} collective-permute-done((bf16[8,96]{1,0:T(8,128)(2,1)S(1)}, bf16[8,96]{1,0:T(8,128)(2,1)S(1)}, u32[]{:S(2)}, u32[]{:S(2)}) %collective-permute-start.1) | collective-permute-done | bytes 1568 | tf_op jit(solution)/shard_map/ppermute | solution.py:623
  22.7 7.2 %collective-permute-start.4 = (bf16[16,96]{1,0:T(8,128)(2,1)S(1)}, bf16[16,96]{1,0:T(8,128)(2,1)S(1)}, u32[]{:S(2)}, u32[]{:S(2)}) collective-permute-start(bf16[16,96]{1,0:T(8,128)(2,1)S(1)} %constant_dynamic-update-slice_fusion.edge_ref), channel_id=1, source_target_pairs={{0,1},{1,0},{2,3},{3,2},{4,5},{5,4},{6,7},{7,6},{8,9},{9,8},{10,11... | collective-permute-start | bytes 9224 | tf_op jit(solution)/shard_map/ppermute | solution.py:639
  35.9 7.5 %collective-permute-done.3.right_ref = bf16[16,96]{1,0:T(8,128)(2,1)S(1)} collective-permute-done((bf16[16,96]{1,0:T(8,128)(2,1)S(1)}, bf16[16,96]{1,0:T(8,128)(2,1)S(1)}, u32[]{:S(2)}, u32[]{:S(2)}) %collective-permute-start.3) | collective-permute-done | bytes 3104 | tf_op jit(solution)/shard_map/ppermute | solution.py:623
  44.1 2.1 shard_map.211
  46.2 11.9 %all-to-all-start.1 = ((bf16[64,8,128]{2,1,0:T(8,128)(2,1)}), bf16[64,8,128]{2,1,0:T(8,128)(2,1)S(1)}, u32[]{:S(2)}, u32[]{:S(2)}) async-start(bf16[64,8,128]{2,1,0:T(8,128)(2,1)} %bitcast.7), calls=%async_computation.1 | async-start | bytes 262144 | tf_op jit(solution)/shard_map/all_to_all | solution.py:635
  58.1 4.0 %collective-permute-start.7 = (bf16[2,16,96]{2,1,0:T(8,128)(2,1)S(1)}, bf16[2,16,96]{2,1,0:T(8,128)(2,1)S(1)}, u32[]{:S(2)}, u32[]{:S(2)}) collective-permute-start(bf16[2,16,96]{2,1,0:T(8,128)(2,1)S(1)} %pad_maximum_fusion.6), channel_id=1, source_target_pairs={{0,6},{1,7},{2,4},{3,5},{4,2},{5,3},{6,0},{7,1},{8,14},{9,15},{10,... | collective-permute-start | bytes 18440 | tf_op jit(solution)/shard_map/ppermute | solution.py:639
  62.2 2.8 %collective-permute-start.6 = (bf16[2,16,96]{2,1,0:T(8,128)(2,1)S(1)}, bf16[2,16,96]{2,1,0:T(8,128)(2,1)S(1)}, u32[]{:S(2)}, u32[]{:S(2)}) collective-permute-start(bf16[2,16,96]{2,1,0:T(8,128)(2,1)S(1)} %pad_maximum_fusion.6), channel_id=1, source_target_pairs={{0,4},{1,5},{2,6},{3,7},{4,0},{5,1},{6,2},{7,3},{8,12},{9,13},{10,... | collective-permute-start | bytes 18440 | tf_op jit(solution)/shard_map/ppermute | solution.py:639
  64.9 2.2 collective-permute-start.5
  70.5 12.2 %all-to-all-start.2 = ((bf16[64,8,128]{2,1,0:T(8,128)(2,1)}), bf16[64,8,128]{2,1,0:T(8,128)(2,1)S(1)}, u32[]{:S(2)}, u32[]{:S(2)}) async-start(bf16[64,8,128]{2,1,0:T(8,128)(2,1)} %bitcast.9), calls=%async_computation.2 | async-start | bytes 262144 | tf_op jit(solution)/shard_map/all_to_all | solution.py:635
  84.3 6.0 %shard_map.214 = (f32[256,192]{1,0:T(8,128)S(1)}, f32[256,192]{1,0:T(8,128)S(1)}, f32[1024,128]{1,0:T(8,128)S(1)}, f32[1024,128]{1,0:T(8,128)S(1)}) custom-call(s32[1]{0:T(128)} %bitcast.me_ref, bf16[8,128,96]{2,1,0:T(8,128)(2,1)S(1)} %reshape.118.got_ref, bf16[8,16,96]{2,1,0:T(8,128)(2,1)S(1)} %pad_maximum_fusion.3.edges_ref, ...), custom_call_target="tpu_custom_call" | custom-call | flops 1000000000 | bytes 1000000 | tf_op jit(solution)/shard_map/pallas_call | solution.py:608
  93.3 2.5 %shard_map.215 = (bf16[128,96]{1,0:T(8,128)(2,1)S(1)}, bf16[128,192]{1,0:T(8,128)(2,1)S(1)}, bf16[128,192]{1,0:T(8,128)(2,1)S(1)}, bf16[128,192]{1,0:T(8,128)(2,...) custom-call(f32[128,192]{1,0:T(8,128)S(1)} %shard_map.212.y_ref, bf16[128,192]{1,0:T(8,128)(2,1)S(1)} %get-tuple-element.62.act_ref, ...), custom_call_target="tpu_custom_call" | custom-call | flops 100000000 | bytes 1000000 | tf_op jit(solution)/shard_map/pallas_call | solution.py:608
  95.8 9.2 %all-to-all-start.3 = ((bf16[64,8,128]{2,1,0:T(8,128)(2,1)}), bf16[64,8,128]{2,1,0:T(8,128)(2,1)S(1)}, u32[]{:S(2)}, u32[]{:S(2)}) async-start(bf16[64,8,128]{2,1,0:T(8,128)(2,1)} %bitcast.14), calls=%async_computation.3 | async-start | bytes 262144 | tf_op jit(solution)/shard_map/all_to_all | solution.py:635
  105.0 8.4 %collective-permute-start.8 = (bf16[128,192]{1,0:T(8,128)(2,1)S(1)}, bf16[128,192]{1,0:T(8,128)(2,1)S(1)}, u32[]{:S(2)}, u32[]{:S(2)}) collective-permute-start(bf16[128,192]{1,0:T(8,128)(2,1)S(1)} %get-tuple-element.77.g_ref), channel_id=1, source_target_pairs={{0,1},{1,0},{2,3},{3,2},{4,5},{5,4},{6,7},{7,6},{8,9},{9,8},{10,11... | collective-permute-start | bytes 147464 | tf_op jit(solution)/shard_map/ppermute | solution.py:639
  113.5 2.1 collective-permute-done.8
  115.7 3.4 %collective-permute-start.11 = (bf16[2,128,192]{2,1,0:T(8,128)(2,1)S(1)}, bf16[2,128,192]{2,1,0:T(8,128)(2,1)S(1)}, u32[]{:S(2)}, u32[]{:S(2)}) collective-permute-start(bf16[2,128,192]{2,1,0:T(8,128)(2,1)S(1)} %pad_maximum_fusion.1), channel_id=1, source_target_pairs={{0,6},{1,7},{2,4},{3,5},{4,2},{5,3},{6,0},{7,1},{8,14},{9,15},{10,... | collective-permute-start | bytes 294920 | tf_op jit(solution)/shard_map/ppermute | solution.py:639
  119.1 2.5 %collective-permute-start.10 = (bf16[2,128,192]{2,1,0:T(8,128)(2,1)S(1)}, bf16[2,128,192]{2,1,0:T(8,128)(2,1)S(1)}, u32[]{:S(2)}, u32[]{:S(2)}) collective-permute-start(bf16[2,128,192]{2,1,0:T(8,128)(2,1)S(1)} %pad_maximum_fusion.1), channel_id=1, source_target_pairs={{0,4},{1,5},{2,6},{3,7},{4,0},{5,1},{6,2},{7,3},{8,12},{9,13},{10,... | collective-permute-start | bytes 294920 | tf_op jit(solution)/shard_map/ppermute | solution.py:639
  121.6 3.1 %collective-permute-start.9 = (bf16[2,128,192]{2,1,0:T(8,128)(2,1)S(1)}, bf16[2,128,192]{2,1,0:T(8,128)(2,1)S(1)}, u32[]{:S(2)}, u32[]{:S(2)}) collective-permute-start(bf16[2,128,192]{2,1,0:T(8,128)(2,1)S(1)} %pad_maximum_fusion.1), channel_id=1, source_target_pairs={{0,2},{1,3},{2,0},{3,1},{4,6},{5,7},{6,4},{7,5},{8,10},{9,11},{10,... | collective-permute-start | bytes 294920 | tf_op jit(solution)/shard_map/ppermute | solution.py:639
  125.5 12.8 %all-to-all-start.4 = ((bf16[64,8,128]{2,1,0:T(8,128)(2,1)}), bf16[64,8,128]{2,1,0:T(8,128)(2,1)S(1)}, u32[]{:S(2)}, u32[]{:S(2)}) async-start(bf16[64,8,128]{2,1,0:T(8,128)(2,1)} %bitcast.18), calls=%async_computation.4 | async-start | bytes 262144 | tf_op jit(solution)/shard_map/all_to_all | solution.py:635
  138.5 3.3 %shard_map.218 = (f32[128,192]{1,0:T(8,128)S(1)}, f32[128,128]{1,0:T(8,128)S(1)}, f32[128,128]{1,0:T(8,128)S(1)}, f32[128,128]{1,0:T(8,128)S(1)}) custom-call(bf16[128,192]{1,0:T(8,128)(2,1)S(1)} %get-tuple-element.62.act_ref, f32[128,128]{1,0:T(8,128)S(1)} %get-tuple-element.63.bc_ref, f32[128,128]{1,0:T(8,128)S(1)} %get-tuple-element.64.step_ref, ...), custom_call_target="tpu_custom_call" | custom-call | flops 100000000 | bytes 1000000 | tf_op jit(solution)/shard_map/pallas_call | solution.py:608
  143.0 2.4 %shard_map.217 = (f32[256,192]{1,0:T(8,128)S(1)}, f32[256,192]{1,0:T(8,128)S(1)}) custom-call(s32[1]{0:T(128)} %bitcast.me_ref, bf16[8,128,192]{2,1,0:T(8,128)(2,1)S(1)} %pad_maximum_fusion.blocks_ref, f32[1024,128]{1,0:T(8,128)S(1)} %copy-done.5, f32[1024,128]{1,0:T(8,128)S(1)} %copy-done.7), custom_call_target="tpu_custom_call" | custom-call | flops 1000000000 | bytes 1000000 | tf_op jit(solution)/shard_map/pallas_call | solution.py:608
  145.4 2.9 %all-to-all-done.4 = bf16[64,8,128]{2,1,0:T(8,128)(2,1)S(1)} async-done(((bf16[64,8,128]{2,1,0:T(8,128)(2,1)}), bf16[64,8,128]{2,1,0:T(8,128)(2,1)S(1)}, u32[]{:S(2)}, u32[]{:S(2)}) %all-to-all-start.4) | async-done | bytes 131104 | tf_op jit(solution)/shard_map/all_to_all | solution.py:635
  148.3 4.9 %shard_map.220 = (bf16[128,192]{1,0:T(8,128)(2,1)S(1)}, bf16[1024,128]{1,0:T(8,128)(2,1)}) custom-call(s32[1]{0:T(128)} %bitcast.me_ref, bf16[8,128,96]{2,1,0:T(8,128)(2,1)S(1)} %reshape.118.got_ref, bf16[16,96]{1,0:T(8,128)(2,1)S(1)} %collective-permute-done.2.left_ref, bf16[16,96]{1,0:T(8,128)(2,1)S(1)} %constant_dynamic-update-slice_fusion.edge_ref, ...), custom_call_target="tpu_custom_call" | custom-call | flops 100000000 | bytes 1000000 | tf_op jit(solution)/shard_map/pallas_call | solution.py:608
  153.2 7.8 %all-to-all-start.5 = ((bf16[64,16,128]{2,1,0:T(8,128)(2,1)}), bf16[64,16,128]{2,1,0:T(8,128)(2,1)S(1)}, u32[]{:S(2)}, u32[]{:S(2)}) async-start(bf16[64,16,128]{2,1,0:T(8,128)(2,1)} %bitcast.20), calls=%async_computation.5 | async-start | bytes 524288 | tf_op jit(solution)/shard_map/all_to_all | solution.py:635
  161.1 3.5 %collective-permute-start.12 = (bf16[8,192]{1,0:T(8,128)(2,1)S(1)}, bf16[8,192]{1,0:T(8,128)(2,1)S(1)}, u32[]{:S(2)}, u32[]{:S(2)}) collective-permute-start(bf16[8,192]{1,0:T(8,128)(2,1)S(1)} %get-tuple-element.121), channel_id=1, source_target_pairs={{0,8},{8,16},{16,24},{24,32},{32,40},{40,48},{48,56},{56,64},{64,7... | collective-permute-start | bytes 9224 | tf_op jit(solution)/shard_map/ppermute | solution.py:623
  166.6 3.2 %collective-permute-done.13.below_ref = bf16[8,192]{1,0:T(8,128)(2,1)S(1)} collective-permute-done((bf16[8,192]{1,0:T(8,128)(2,1)S(1)}, bf16[8,192]{1,0:T(8,128)(2,1)S(1)}, u32[]{:S(2)}, u32[]{:S(2)}) %collective-permute-start.13) | collective-permute-done | bytes 3104 | tf_op jit(solution)/shard_map/ppermute | solution.py:623
  169.9 6.9 %collective-permute-start.14 = (bf16[18,192]{1,0:T(8,128)(2,1)S(1)}, bf16[18,192]{1,0:T(8,128)(2,1)S(1)}, u32[]{:S(2)}, u32[]{:S(2)}) collective-permute-start(bf16[18,192]{1,0:T(8,128)(2,1)S(1)} %pad_maximum_fusion.4), channel_id=1, source_target_pairs={{0,1},{1,2},{2,3},{3,4},{4,5},{5,6},{6,7},{8,9},{9,10},{10,11},{11... | collective-permute-start | bytes 20744 | tf_op jit(solution)/shard_map/ppermute | solution.py:623
  178.2 6.9 %collective-permute-done.15.right_ref = bf16[18,192]{1,0:T(8,128)(2,1)S(1)} collective-permute-done((bf16[18,192]{1,0:T(8,128)(2,1)S(1)}, bf16[18,192]{1,0:T(8,128)(2,1)S(1)}, u32[]{:S(2)}, u32[]{:S(2)}) %collective-permute-start.15) | collective-permute-done | bytes 6944 | tf_op jit(solution)/shard_map/ppermute | solution.py:623
  185.1 14.1 %all_to_all.40.x_ref = f32[8,16,128]{2,1,0:T(8,128)S(1)} all-to-all(f32[8,16,128]{2,1,0:T(8,128)S(1)} %shard_map.221), channel_id=1, replica_groups=mesh['row'=64,'col'=8] {'col'}, dimensions={0} | all-to-all | bytes 131072 | tf_op jit(solution)/shard_map/all_to_all | solution.py:635
  200.0 12.3 %all-to-all-start.7 = ((bf16[64,16,128]{2,1,0:T(8,128)(2,1)}), bf16[64,16,128]{2,1,0:T(8,128)(2,1)S(1)}, u32[]{:S(2)}, u32[]{:S(2)}) async-start(bf16[64,16,128]{2,1,0:T(8,128)(2,1)} %shard_map.223), calls=%async_computation.7 | async-start | bytes 524288 | tf_op jit(solution)/shard_map/all_to_all | solution.py:635
  214.2 9.8 %all-to-all-done.7 = bf16[64,16,128]{2,1,0:T(8,128)(2,1)S(1)} async-done(((bf16[64,16,128]{2,1,0:T(8,128)(2,1)}), bf16[64,16,128]{2,1,0:T(8,128)(2,1)S(1)}, u32[]{:S(2)}, u32[]{:S(2)}) %all-to-all-start.7) | async-done | bytes 262176 | tf_op jit(solution)/shard_map/all_to_all | solution.py:635
  (101 shorter events, 27.5 us)
Async XLA Ops:
  2.1 10.2 %copy-start.9 = (bf16[16,768]{1,0:T(8,128)(2,1)S(1)}, bf16[16,768]{1,0:T(8,128)(2,1)}, u32[]{:S(2)}) copy-start(bf16[16,768]{1,0:T(8,128)(2,1)} %param.12) | copy-start | bytes 73732
  2.1 17.4 %copy-start.8 = (bf16[96,384]{1,0:T(8,128)(2,1)S(1)}, bf16[96,384]{1,0:T(8,128)(2,1)}, u32[]{:S(2)}) copy-start(bf16[96,384]{1,0:T(8,128)(2,1)} %param.13) | copy-start | bytes 221188
  2.1 33.5 %all-to-all-start = ((bf16[8,16,768]{2,1,0:T(8,128)(2,1)}), bf16[8,16,768]{2,1,0:T(8,128)(2,1)S(1)}, u32[]{:S(2)}, u32[]{:S(2)}) async-start(bf16[8,16,768]{2,1,0:T(8,128)(2,1)} %broadcast_in_dim.3), calls=%async_computation | async-start | bytes 393216 | tf_op jit(solution)/shard_map/all_to_all | solution.py:635
  12.4 7.4 %collective-permute-start = (bf16[8,96]{1,0:T(8,128)(2,1)S(1)}, bf16[8,96]{1,0:T(8,128)(2,1)S(1)}, u32[]{:S(2)}, u32[]{:S(2)}) collective-permute-start(bf16[8,96]{1,0:T(8,128)(2,1)S(1)} %slice.52), channel_id=1, source_target_pairs={{0,8},{8,16},{16,24},{24,32},{32,40},{40,48},{48,56},{56,64},{64,7... | collective-permute-start | bytes 4616 | tf_op jit(solution)/shard_map/ppermute | solution.py:623
  17.4 2.2 copy-start.10
  17.4 5.3 %collective-permute-start.1 = (bf16[8,96]{1,0:T(8,128)(2,1)S(1)}, bf16[8,96]{1,0:T(8,128)(2,1)S(1)}, u32[]{:S(2)}, u32[]{:S(2)}) collective-permute-start(bf16[8,96]{1,0:T(8,128)(2,1)S(1)} %slice.54), channel_id=1, source_target_pairs={{8,0},{16,8},{24,16},{32,24},{40,32},{48,40},{56,48},{64,56},{72,6... | collective-permute-start | bytes 4616 | tf_op jit(solution)/shard_map/ppermute | solution.py:623
  22.7 12.9 %collective-permute-start.4 = (bf16[16,96]{1,0:T(8,128)(2,1)S(1)}, bf16[16,96]{1,0:T(8,128)(2,1)S(1)}, u32[]{:S(2)}, u32[]{:S(2)}) collective-permute-start(bf16[16,96]{1,0:T(8,128)(2,1)S(1)} %constant_dynamic-update-slice_fusion.edge_ref), channel_id=1, source_target_pairs={{0,1},{1,0},{2,3},{3,2},{4,5},{5,4},{6,7},{7,6},{8,9},{9,8},{10,11... | collective-permute-start | bytes 9224 | tf_op jit(solution)/shard_map/ppermute | solution.py:639
  32.3 3.6 %collective-permute-start.2 = (bf16[16,96]{1,0:T(8,128)(2,1)S(1)}, bf16[16,96]{1,0:T(8,128)(2,1)S(1)}, u32[]{:S(2)}, u32[]{:S(2)}) collective-permute-start(bf16[16,96]{1,0:T(8,128)(2,1)S(1)} %constant_dynamic-update-slice_fusion.edge_ref), channel_id=1, source_target_pairs={{0,1},{1,2},{2,3},{3,4},{4,5},{5,6},{6,7},{8,9},{9,10},{10,11},{11... | collective-permute-start | bytes 9224 | tf_op jit(solution)/shard_map/ppermute | solution.py:623
  34.3 9.2 %collective-permute-start.3 = (bf16[16,96]{1,0:T(8,128)(2,1)S(1)}, bf16[16,96]{1,0:T(8,128)(2,1)S(1)}, u32[]{:S(2)}, u32[]{:S(2)}) collective-permute-start(bf16[16,96]{1,0:T(8,128)(2,1)S(1)} %constant_dynamic-update-slice_fusion.edge_ref), channel_id=1, source_target_pairs={{1,0},{2,1},{3,2},{4,3},{5,4},{6,5},{7,6},{9,8},{10,9},{11,10},{12... | collective-permute-start | bytes 9224 | tf_op jit(solution)/shard_map/ppermute | solution.py:623
  46.2 23.3 %all-to-all-start.1 = ((bf16[64,8,128]{2,1,0:T(8,128)(2,1)}), bf16[64,8,128]{2,1,0:T(8,128)(2,1)S(1)}, u32[]{:S(2)}, u32[]{:S(2)}) async-start(bf16[64,8,128]{2,1,0:T(8,128)(2,1)} %bitcast.7), calls=%async_computation.1 | async-start | bytes 262144 | tf_op jit(solution)/shard_map/all_to_all | solution.py:635
  58.1 9.0 %collective-permute-start.7 = (bf16[2,16,96]{2,1,0:T(8,128)(2,1)S(1)}, bf16[2,16,96]{2,1,0:T(8,128)(2,1)S(1)}, u32[]{:S(2)}, u32[]{:S(2)}) collective-permute-start(bf16[2,16,96]{2,1,0:T(8,128)(2,1)S(1)} %pad_maximum_fusion.6), channel_id=1, source_target_pairs={{0,6},{1,7},{2,4},{3,5},{4,2},{5,3},{6,0},{7,1},{8,14},{9,15},{10,... | collective-permute-start | bytes 18440 | tf_op jit(solution)/shard_map/ppermute | solution.py:639
  62.2 6.2 %collective-permute-start.6 = (bf16[2,16,96]{2,1,0:T(8,128)(2,1)S(1)}, bf16[2,16,96]{2,1,0:T(8,128)(2,1)S(1)}, u32[]{:S(2)}, u32[]{:S(2)}) collective-permute-start(bf16[2,16,96]{2,1,0:T(8,128)(2,1)S(1)} %pad_maximum_fusion.6), channel_id=1, source_target_pairs={{0,4},{1,5},{2,6},{3,7},{4,0},{5,1},{6,2},{7,3},{8,12},{9,13},{10,... | collective-permute-start | bytes 18440 | tf_op jit(solution)/shard_map/ppermute | solution.py:639
  64.9 4.6 %collective-permute-start.5 = (bf16[2,16,96]{2,1,0:T(8,128)(2,1)S(1)}, bf16[2,16,96]{2,1,0:T(8,128)(2,1)S(1)}, u32[]{:S(2)}, u32[]{:S(2)}) collective-permute-start(bf16[2,16,96]{2,1,0:T(8,128)(2,1)S(1)} %pad_maximum_fusion.6), channel_id=1, source_target_pairs={{0,2},{1,3},{2,0},{3,1},{4,6},{5,7},{6,4},{7,5},{8,10},{9,11},{10,... | collective-permute-start | bytes 18440 | tf_op jit(solution)/shard_map/ppermute | solution.py:639
  70.5 22.2 %all-to-all-start.2 = ((bf16[64,8,128]{2,1,0:T(8,128)(2,1)}), bf16[64,8,128]{2,1,0:T(8,128)(2,1)S(1)}, u32[]{:S(2)}, u32[]{:S(2)}) async-start(bf16[64,8,128]{2,1,0:T(8,128)(2,1)} %bitcast.9), calls=%async_computation.2 | async-start | bytes 262144 | tf_op jit(solution)/shard_map/all_to_all | solution.py:635
  84.3 8.4 %copy-start = (bf16[192,96]{1,0:T(8,128)(2,1)S(1)}, bf16[192,96]{1,0:T(8,128)(2,1)}, u32[]{:S(2)}) copy-start(bf16[192,96]{1,0:T(8,128)(2,1)} %ow_ref.1) | copy-start | bytes 110596
  84.3 8.4 %copy-start.3 = (f32[192]{0:T(256)S(1)}, f32[192]{0:T(256)}, u32[]{:S(2)}) copy-start(f32[192]{0:T(256)} %param.21) | copy-start | bytes 2308
  90.3 0.8 copy-start.6
  91.1 4.7 %copy-start.4 = (f32[1024,128]{1,0:T(8,128)}, f32[1024,128]{1,0:T(8,128)S(1)}, u32[]{:S(2)}) copy-start(f32[1024,128]{1,0:T(8,128)S(1)} %get-tuple-element.81.later_ref) | copy-start | bytes 1572868
  95.8 19.8 %all-to-all-start.3 = ((bf16[64,8,128]{2,1,0:T(8,128)(2,1)}), bf16[64,8,128]{2,1,0:T(8,128)(2,1)S(1)}, u32[]{:S(2)}, u32[]{:S(2)}) async-start(bf16[64,8,128]{2,1,0:T(8,128)(2,1)} %bitcast.14), calls=%async_computation.3 | async-start | bytes 262144 | tf_op jit(solution)/shard_map/all_to_all | solution.py:635
  105.0 10.6 %collective-permute-start.8 = (bf16[128,192]{1,0:T(8,128)(2,1)S(1)}, bf16[128,192]{1,0:T(8,128)(2,1)S(1)}, u32[]{:S(2)}, u32[]{:S(2)}) collective-permute-start(bf16[128,192]{1,0:T(8,128)(2,1)S(1)} %get-tuple-element.77.g_ref), channel_id=1, source_target_pairs={{0,1},{1,0},{2,3},{3,2},{4,5},{5,4},{6,7},{7,6},{8,9},{9,8},{10,11... | collective-permute-start | bytes 147464 | tf_op jit(solution)/shard_map/ppermute | solution.py:639
  115.7 26.2 %collective-permute-start.11 = (bf16[2,128,192]{2,1,0:T(8,128)(2,1)S(1)}, bf16[2,128,192]{2,1,0:T(8,128)(2,1)S(1)}, u32[]{:S(2)}, u32[]{:S(2)}) collective-permute-start(bf16[2,128,192]{2,1,0:T(8,128)(2,1)S(1)} %pad_maximum_fusion.1), channel_id=1, source_target_pairs={{0,6},{1,7},{2,4},{3,5},{4,2},{5,3},{6,0},{7,1},{8,14},{9,15},{10,... | collective-permute-start | bytes 294920 | tf_op jit(solution)/shard_map/ppermute | solution.py:639
  119.1 22.8 %collective-permute-start.10 = (bf16[2,128,192]{2,1,0:T(8,128)(2,1)S(1)}, bf16[2,128,192]{2,1,0:T(8,128)(2,1)S(1)}, u32[]{:S(2)}, u32[]{:S(2)}) collective-permute-start(bf16[2,128,192]{2,1,0:T(8,128)(2,1)S(1)} %pad_maximum_fusion.1), channel_id=1, source_target_pairs={{0,4},{1,5},{2,6},{3,7},{4,0},{5,1},{6,2},{7,3},{8,12},{9,13},{10,... | collective-permute-start | bytes 294920 | tf_op jit(solution)/shard_map/ppermute | solution.py:639
  121.6 20.3 %collective-permute-start.9 = (bf16[2,128,192]{2,1,0:T(8,128)(2,1)S(1)}, bf16[2,128,192]{2,1,0:T(8,128)(2,1)S(1)}, u32[]{:S(2)}, u32[]{:S(2)}) collective-permute-start(bf16[2,128,192]{2,1,0:T(8,128)(2,1)S(1)} %pad_maximum_fusion.1), channel_id=1, source_target_pairs={{0,2},{1,3},{2,0},{3,1},{4,6},{5,7},{6,4},{7,5},{8,10},{9,11},{10,... | collective-permute-start | bytes 294920 | tf_op jit(solution)/shard_map/ppermute | solution.py:639
  125.5 22.8 %all-to-all-start.4 = ((bf16[64,8,128]{2,1,0:T(8,128)(2,1)}), bf16[64,8,128]{2,1,0:T(8,128)(2,1)S(1)}, u32[]{:S(2)}, u32[]{:S(2)}) async-start(bf16[64,8,128]{2,1,0:T(8,128)(2,1)} %bitcast.18), calls=%async_computation.4 | async-start | bytes 262144 | tf_op jit(solution)/shard_map/all_to_all | solution.py:635
  141.8 1.0 copy-start.5
  141.8 1.2 copy-start.7
  153.2 24.9 %all-to-all-start.5 = ((bf16[64,16,128]{2,1,0:T(8,128)(2,1)}), bf16[64,16,128]{2,1,0:T(8,128)(2,1)S(1)}, u32[]{:S(2)}, u32[]{:S(2)}) async-start(bf16[64,16,128]{2,1,0:T(8,128)(2,1)} %bitcast.20), calls=%async_computation.5 | async-start | bytes 524288 | tf_op jit(solution)/shard_map/all_to_all | solution.py:635
  161.1 8.8 %collective-permute-start.12 = (bf16[8,192]{1,0:T(8,128)(2,1)S(1)}, bf16[8,192]{1,0:T(8,128)(2,1)S(1)}, u32[]{:S(2)}, u32[]{:S(2)}) collective-permute-start(bf16[8,192]{1,0:T(8,128)(2,1)S(1)} %get-tuple-element.121), channel_id=1, source_target_pairs={{0,8},{8,16},{16,24},{24,32},{32,40},{40,48},{48,56},{56,64},{64,7... | collective-permute-start | bytes 9224 | tf_op jit(solution)/shard_map/ppermute | solution.py:623
  164.6 5.2 %collective-permute-start.13 = (bf16[8,192]{1,0:T(8,128)(2,1)S(1)}, bf16[8,192]{1,0:T(8,128)(2,1)S(1)}, u32[]{:S(2)}, u32[]{:S(2)}) collective-permute-start(bf16[8,192]{1,0:T(8,128)(2,1)S(1)} %get-tuple-element.120), channel_id=1, source_target_pairs={{8,0},{16,8},{24,16},{32,24},{40,32},{48,40},{56,48},{64,56},{72,6... | collective-permute-start | bytes 9224 | tf_op jit(solution)/shard_map/ppermute | solution.py:623
  169.9 8.3 %collective-permute-start.14 = (bf16[18,192]{1,0:T(8,128)(2,1)S(1)}, bf16[18,192]{1,0:T(8,128)(2,1)S(1)}, u32[]{:S(2)}, u32[]{:S(2)}) collective-permute-start(bf16[18,192]{1,0:T(8,128)(2,1)S(1)} %pad_maximum_fusion.4), channel_id=1, source_target_pairs={{0,1},{1,2},{2,3},{3,4},{4,5},{5,6},{6,7},{8,9},{9,10},{10,11},{11... | collective-permute-start | bytes 20744 | tf_op jit(solution)/shard_map/ppermute | solution.py:623
  176.8 8.3 %collective-permute-start.15 = (bf16[18,192]{1,0:T(8,128)(2,1)S(1)}, bf16[18,192]{1,0:T(8,128)(2,1)S(1)}, u32[]{:S(2)}, u32[]{:S(2)}) collective-permute-start(bf16[18,192]{1,0:T(8,128)(2,1)S(1)} %pad_maximum_fusion.5), channel_id=1, source_target_pairs={{1,0},{2,1},{3,2},{4,3},{5,4},{6,5},{7,6},{9,8},{10,9},{11,10},{12... | collective-permute-start | bytes 20744 | tf_op jit(solution)/shard_map/ppermute | solution.py:623
  200.0 24.0 %all-to-all-start.7 = ((bf16[64,16,128]{2,1,0:T(8,128)(2,1)}), bf16[64,16,128]{2,1,0:T(8,128)(2,1)S(1)}, u32[]{:S(2)}, u32[]{:S(2)}) async-start(bf16[64,16,128]{2,1,0:T(8,128)(2,1)} %shard_map.223), calls=%async_computation.7 | async-start | bytes 524288 | tf_op jit(solution)/shard_map/all_to_all | solution.py:635
  (7 other events, 4.9 us)

commit v5 on v4

--- a/solution.py
+++ b/solution.py
@@ -198,14 +198,10 @@
     return jnp.clip(j, 0, blocks - 1), jnp.where((j >= 0) & (j < blocks), 1.0, 0.0)
 
 
-def fill_blocks(me, got_ref, edge_refs, pad_ref, f):
-    for i, edge_ref in enumerate(edge_refs):
+def fill_blocks(me, got_ref, pad_ref, f):
+    for i in range(3):
         at, inside = edge_factor(me, got_ref.shape[0], me + i - 1)
-        place = slice(8 * i, 8 * i + 8)
-        edge = f(edge_ref[...])
-        pad_ref[0:1, place, :] = edge[:C].reshape(1, C, -1)
-        pad_ref[1 : R + 1, place, :] = f(got_ref[at]).reshape(R, C, -1) * inside
-        pad_ref[R + 1 : R + 2, place, :] = edge[C:].reshape(1, C, -1)
+        pad_ref[:, 8 * i : 8 * i + 8, :] = f(got_ref[at]).reshape(R + 2, C, -1) * inside
 
 
 def as_branch(wbr_ref):
@@ -213,11 +209,10 @@
 
 
 def first_kernel(
-    me_ref, got_ref, left_ref, edge_ref, right_ref, wbr_ref, cw_ref, cb_ref, wd_ref, wbc_ref, sb_ref, ld_ref,
+    me_ref, got_ref, wbr_ref, cw_ref, cb_ref, wd_ref, wbc_ref, sb_ref, ld_ref,
     before_ref, act_ref, rawd_ref, bc_ref, step_ref, log_ref, tot_ref, mv_ref, pad_ref, wide_ref,
 ):
-    edges = (left_ref, edge_ref, right_ref)
-    fill_blocks(me_ref[0], got_ref, edges, pad_ref, as_branch(wbr_ref))
+    fill_blocks(me_ref[0], got_ref, pad_ref, as_branch(wbr_ref))
     total = jnp.zeros((R, C, DI), F32)
     for b in range(3):
         shifted = pad_ref[:, 7 + b : 7 + b + C, :]
@@ -257,18 +252,14 @@
 
 
 def row_scan_kernel(
-    me_ref, got_ref, edges_ref, wbr_ref, cw_ref, cb_ref, wd_ref, wbc_ref, sb_ref, ld_ref,
+    me_ref, got_ref, wbr_ref, cw_ref, cb_ref, wd_ref, wbc_ref, sb_ref, ld_ref,
     s0_ref, s1_ref, later_ref, gate_ref, pad_ref,
 ):
     nothing = jnp.zeros((R + 2, 8, DI), F32)
     pad_ref[:, 0:8, :] = nothing
     pad_ref[:, 72:80, :] = nothing
     for j in range(8):
-        place = slice(8 + 8 * j, 16 + 8 * j)
-        edge = as_branch(wbr_ref)(edges_ref[me_ref[0] ^ j])
-        pad_ref[0:1, place, :] = edge[:C].reshape(1, C, DI)
-        pad_ref[1 : R + 1, place, :] = as_branch(wbr_ref)(got_ref[j]).reshape(R, C, DI)
-        pad_ref[R + 1 : R + 2, place, :] = edge[C:].reshape(1, C, DI)
+        pad_ref[:, 8 + 8 * j : 16 + 8 * j, :] = as_branch(wbr_ref)(got_ref[j]).reshape(R + 2, C, DI)
     low = me_ref[0] * C
     high = low + C
     t, u = (iota((T, T), 0), iota((T, T), 1))
@@ -459,7 +450,7 @@
 
 
 def last_kernel(
-    me_ref, got_ref, left_ref, edge_ref, right_ref, wbr_ref, cw_ref, before_ref, act_ref, rawd_ref, bc_ref, step_ref, log_ref, tot_ref, g_ref,
+    me_ref, got_ref, wbr_ref, cw_ref, before_ref, act_ref, rawd_ref, bc_ref, step_ref, log_ref, tot_ref, g_ref,
     sv_ref, s0_ref, s1_ref, lv_ref, l0_ref, l1_ref, dact_ref, dbc_ref, dstep_ref, dlog_ref, skip_ref, wd_ref, wbc_ref,
     sb_ref, ld_ref, gin_gate_ref, gout_ref, norms_ref,
     gb_ref, pack_ref, pad_ref, tok_ref, early_ref, late_ref,
@@ -509,9 +500,8 @@
     gb = (d_act * sig * (1.0 + before * (1.0 - sig))).astype(BF)
     gb_ref[...] = gb
     gbw = gb.astype(F32)
-    edges = (left_ref, edge_ref, right_ref)
-    fill_blocks(me_ref[0], got_ref, edges, pad_ref, as_branch(wbr_ref))
-    fill_blocks(me_ref[0], got_ref, edges, tok_ref, lambda x: x.astype(F32))
+    fill_blocks(me_ref[0], got_ref, pad_ref, as_branch(wbr_ref))
+    fill_blocks(me_ref[0], got_ref, tok_ref, lambda x: x.astype(F32))
     gin = jnp.zeros((D, DI), F32)
     conv_rows = [None] * 9
     for b in range(3):
@@ -657,15 +647,14 @@
     return all_to_all(states.reshape(chunks), axis).reshape(512, 128), meanwhile
 
 
-def reduced(pack, scale, meanwhile):
+def reduced(pack, scale):
     rows, cols = (lax.axis_size("row"), lax.axis_size("col"))
     chunk = pack.shape[0] // rows
     got = all_to_all(pack.reshape(rows, chunk, 128), "row")
     (part,) = call(partial(sum_kernel, 1.0), [((cols, chunk, 128), F32)], got, flops=10**7)
-    part, meanwhile = lax.optimization_barrier((part, meanwhile))
     got = all_to_all(part, "col")
     (part,) = call(partial(sum_kernel, scale), [((rows, chunk, 128), BF)], got, flops=10**7)
-    return all_to_all(part, "row").reshape(pack.shape), meanwhile
+    return all_to_all(part, "row").reshape(pack.shape)
 
 
 def local(
@@ -673,10 +662,9 @@
     norm_bias, out_weight, cotangent,
 ):
     own = tokens.reshape(T, D)
-    count = lax.axis_size("col")
-    got = all_to_all(jnp.broadcast_to(tokens, (count,) + tokens.shape), "col").reshape(count, T, D)
-    edge = jnp.concatenate(neighbours(own[T - C :], own[:C], "row"), axis=0)
-    left, right = neighbours(edge, edge, "col")
+    above, below = neighbours(own[T - C :], own[:C], "row")
+    band = jnp.concatenate([above, own, below], axis=0)
+    got = all_to_all(jnp.broadcast_to(band, (lax.axis_size("col"),) + band.shape), "col")
     place = lax.axis_index("col").reshape(1)
     cot = cotangent.reshape(T, D)
     w_branch, w_gate = (in_weight[:, :DI], in_weight[:, DI:])
@@ -704,14 +692,13 @@
 
     before, act, raw_d, bc, step, log, tot, mv = call(
         first_kernel, [wide, low, square, square, square, square, square, message],
-        place, got, left, edge, right, w_branch, taps, row(conv_bias), w_step, w_bc, bias, rate,
+        place, got, w_branch, taps, row(conv_bias), w_step, w_bc, bias, rate,
         scratch=[pltpu.VMEM((R + 2, PITCH, DI), F32), opened], scalars=1,
     )
-    mv, edge_pair = lax.optimization_barrier((mv, in_pairs(edge)))
-    sv, edges = exchange(mv, "row", False, along_col(edge_pair))
+    sv, _ = exchange(mv, "row", False)
     s0, s1, later, gate_c = call(
         row_scan_kernel, [states, states, long, long],
-        place, got, edges, w_branch, taps, row(conv_bias), w_step, w_bc, bias, rate,
+        place, got, w_branch, taps, row(conv_bias), w_step, w_bc, bias, rate,
         scratch=[pltpu.VMEM((R + 2, 80, DI), F32)], scalars=1, flops=10**9,
     )
     (y,) = call(local_kernel, [wide], act, bc, step, log)
@@ -721,25 +708,27 @@
         scratch=[opened],
     )
     lv, pair = exchange(mv, "row", True, in_pairs(g))
+    lv, blocks = lax.optimization_barrier((lv, along_col(pair)))
     d_act, d_bc, d_step, d_log = call(
         back_kernel, [wide, square, square, square], act, bc, step, log, g, sv, s0, s1,
         scratch=[opened],
     )
     l0, l1 = call(
-        row_back_kernel, [states, states], place, along_col(pair), later, gate_c, scalars=1, flops=10**9
+        row_back_kernel, [states, states], place, blocks, later, gate_c, scalars=1, flops=10**9
     )
     gin_gate, gout = call(
         gate_grads_kernel, [((D, DI), F32), ((D, DI), F32)], own, d_gate, gated, cot, flops=10**7
     )
     gb, pack = call(
         last_kernel, [low, ((1024, 128), BF)],
-        place, got, left, edge, right, w_branch, taps, before, act, raw_d, bc, step, log, tot, g, sv, s0, s1, lv, l0, l1, d_act, d_bc,
+        place, got, w_branch, taps, before, act, raw_d, bc, step, log, tot, g, sv, s0, s1, lv, l0, l1, d_act, d_bc,
         d_step, d_log, skip, w_step, w_bc, bias, rate, gin_gate, gout, norms,
         scratch=[pltpu.VMEM((R + 2, PITCH, DI), F32), pltpu.VMEM((R + 2, PITCH, D), F32), opened, opened],
         scalars=1,
     )
     scale = float(T * lax.axis_size("row") * lax.axis_size("col")) ** (-0.5)
-    total, rim = reduced(pack, scale, with_rim(gb))
+    total = reduced(pack, scale)
+    rim = with_rim(gb)
     (d_tokens,) = call(
         out_kernel, [((T, D), BF)], *rim, taps, d_gate, w_branch, w_gate,
         scratch=[pltpu.VMEM((R + 2, PITCH, DI), F32)],

time: 226 us -> 194 us (0.86)
  the two profiles are of different devices: /device:TPU:1 before, /device:TPU:56 now
where the time goes in v5:
time: 194 us; the launch traced here: 193 us
  starting transfers between devices  111 us (57%)
  waiting for transfers between devices  26.2 us (14%)
  Pallas kernels  26 us (13%)
  blocking collectives  15.4 us (8%)
  local copies, waits for them, and re-layouts  12.6 us (6%)
    all_to_all x7, starting transfers between devices, all_to_all(): return lax.all_to_all(x, axis, 0, 0, tiled=True)  63.2 us
    ppermute x6, starting transfers between devices, neighbours(): return (lax.ppermute(last, axis, up), lax.ppermute(first, axis, down))  30.5 us
    pallas_call x14, Pallas kernels, call(): pl.pallas_call(kernel, out_shape=[jax.ShapeDtypeStruct(s, t) for s, t in...  26 us
    ppermute x4, starting transfers between devices, swapped(): lax.ppermute(x, 'col', [(i, i ^ step) for i in range(lax.axis_size('col'))])  17.3 us
    all_to_all x1, blocking collectives, all_to_all(): return lax.all_to_all(x, axis, 0, 0, tiled=True)  15.4 us
    all_to_all x7, waiting for transfers between devices, all_to_all(): return lax.all_to_all(x, axis, 0, 0, tiled=True)  11.8 us
    ppermute x6, waiting for transfers between devices, neighbours(): return (lax.ppermute(last, axis, up), lax.ppermute(first, axis, down))  11.3 us
    unnamed x33, local copies, waits for them, and re-layouts  7.81 us
  transfers between devices with their start and end apart: 17, of which 8 were waited for; matrix products, arithmetic and copies ran while one was open for 2% of the time, Pallas kernels for 6%

profile of v5, /device:TPU:56, one launch (start us, length us, event | category | flops | bytes accessed | tf_op | source)
XLA Modules:
  0.0 192.5 jit_solution(4129026059301351416)
XLA Ops:
  1.5 11.2 %collective-permute-start.1 = (bf16[8,96]{1,0:T(8,128)(2,1)S(1)}, bf16[8,96]{1,0:T(8,128)(2,1)S(1)}, u32[]{:S(2)}, u32[]{:S(2)}) collective-permute-start(bf16[8,96]{1,0:T(8,128)(2,1)S(1)} %slice.54), channel_id=1, source_target_pairs={{8,0},{16,8},{24,16},{32,24},{40,32},{48,40},{56,48},{64,56},{72,6... | collective-permute-start | bytes 4616 | tf_op jit(solution)/shard_map/ppermute | solution.py:613
  12.8 1.9 collective-permute-start
  15.6 4.2 %collective-permute-done = bf16[8,96]{1,0:T(8,128)(2,1)S(1)} collective-permute-done((bf16[8,96]{1,0:T(8,128)(2,1)S(1)}, bf16[8,96]{1,0:T(8,128)(2,1)S(1)}, u32[]{:S(2)}, u32[]{:S(2)}) %collective-permute-start) | collective-permute-done | bytes 1568 | tf_op jit(solution)/shard_map/ppermute | solution.py:613
  20.6 9.7 %all-to-all-start = ((bf16[8,144,96]{2,1,0:T(8,128)(2,1)}), bf16[8,144,96]{2,1,0:T(8,128)(2,1)S(1)}, u32[]{:S(2)}, u32[]{:S(2)}) async-start(bf16[8,144,96]{2,1,0:T(8,128)(2,1)} %broadcast_in_dim.3), calls=%async_computation | async-start | bytes 589824 | tf_op jit(solution)/shard_map/all_to_all | solution.py:625
  33.8 2.7 %all-to-all-done.got_ref = bf16[8,144,96]{2,1,0:T(8,128)(2,1)S(1)} async-done(((bf16[8,144,96]{2,1,0:T(8,128)(2,1)}), bf16[8,144,96]{2,1,0:T(8,128)(2,1)S(1)}, u32[]{:S(2)}, u32[]{:S(2)}) %all-to-all-start) | async-done | bytes 221216 | tf_op jit(solution)/shard_map/all_to_all | solution.py:625
  37.2 1.5 shard_map.211
  38.7 15.4 %all_to_all.40 = bf16[64,8,128]{2,1,0:T(8,128)(2,1)S(1)} all-to-all(bf16[64,8,128]{2,1,0:T(8,128)(2,1)S(1)} %bitcast.43), channel_id=1, replica_groups=mesh['row'=64,'col'=8] {'row'}, dimensions={0} | all-to-all | bytes 262144 | tf_op jit(solution)/shard_map/all_to_all | solution.py:625
  54.9 6.3 %all-to-all-start.2 = ((bf16[64,8,128]{2,1,0:T(8,128)(2,1)}), bf16[64,8,128]{2,1,0:T(8,128)(2,1)S(1)}, u32[]{:S(2)}, u32[]{:S(2)}) async-start(bf16[64,8,128]{2,1,0:T(8,128)(2,1)} %bitcast.7), calls=%async_computation.2 | async-start | bytes 262144 | tf_op jit(solution)/shard_map/all_to_all | solution.py:625
  62.2 6.1 %shard_map.214 = (f32[256,192]{1,0:T(8,128)S(1)}, f32[256,192]{1,0:T(8,128)S(1)}, f32[1024,128]{1,0:T(8,128)S(1)}, f32[1024,128]{1,0:T(8,128)S(1)}) custom-call(s32[1]{0:T(128)} %bitcast.me_ref, bf16[8,144,96]{2,1,0:T(8,128)(2,1)S(1)} %all-to-all-done.got_ref, bf16[96,192]{1,0:T(8,128)(2,1)S(1)} %get-tuple-element.101.wbr_ref, f32[16,192]{1,0:T(8,128)S(1)} %pad.15.cw_ref, ...), custom_call_target="tpu_custom_call" | custom-call | flops 1000000000 | bytes 1000000 | tf_op jit(solution)/shard_map/pallas_call | solution.py:598
  70.8 2.5 %shard_map.215 = (bf16[128,96]{1,0:T(8,128)(2,1)S(1)}, bf16[128,192]{1,0:T(8,128)(2,1)S(1)}, bf16[128,192]{1,0:T(8,128)(2,1)S(1)}, bf16[128,192]{1,0:T(8,128)(2,...) custom-call(f32[128,192]{1,0:T(8,128)S(1)} %shard_map.212.y_ref, bf16[128,192]{1,0:T(8,128)(2,1)S(1)} %get-tuple-element.54.act_ref, ...), custom_call_target="tpu_custom_call" | custom-call | flops 100000000 | bytes 1000000 | tf_op jit(solution)/shard_map/pallas_call | solution.py:598
  73.2 10.5 %all-to-all-start.3 = ((bf16[64,8,128]{2,1,0:T(8,128)(2,1)}), bf16[64,8,128]{2,1,0:T(8,128)(2,1)S(1)}, u32[]{:S(2)}, u32[]{:S(2)}) async-start(bf16[64,8,128]{2,1,0:T(8,128)(2,1)} %bitcast.12), calls=%async_computation.3 | async-start | bytes 262144 | tf_op jit(solution)/shard_map/all_to_all | solution.py:625
  83.8 7.5 %collective-permute-start.2 = (bf16[128,192]{1,0:T(8,128)(2,1)S(1)}, bf16[128,192]{1,0:T(8,128)(2,1)S(1)}, u32[]{:S(2)}, u32[]{:S(2)}) collective-permute-start(bf16[128,192]{1,0:T(8,128)(2,1)S(1)} %get-tuple-element.65.g_ref), channel_id=1, source_target_pairs={{0,1},{1,0},{2,3},{3,2},{4,5},{5,4},{6,7},{7,6},{8,9},{9,8},{10,11... | collective-permute-start | bytes 147464 | tf_op jit(solution)/shard_map/ppermute | solution.py:629
  91.3 2.5 %collective-permute-done.2 = bf16[128,192]{1,0:T(8,128)(2,1)S(1)} collective-permute-done((bf16[128,192]{1,0:T(8,128)(2,1)S(1)}, bf16[128,192]{1,0:T(8,128)(2,1)S(1)}, u32[]{:S(2)}, u32[]{:S(2)}) %collective-permute-start.2) | collective-permute-done | bytes 49184 | tf_op jit(solution)/shard_map/ppermute | solution.py:629
  94.8 11.3 %all-to-all-start.4 = ((bf16[64,8,128]{2,1,0:T(8,128)(2,1)}), bf16[64,8,128]{2,1,0:T(8,128)(2,1)S(1)}, u32[]{:S(2)}, u32[]{:S(2)}) async-start(bf16[64,8,128]{2,1,0:T(8,128)(2,1)} %bitcast.16), calls=%async_computation.4 | async-start | bytes 262144 | tf_op jit(solution)/shard_map/all_to_all | solution.py:625
  106.0 2.9 %collective-permute-start.5 = (bf16[2,128,192]{2,1,0:T(8,128)(2,1)S(1)}, bf16[2,128,192]{2,1,0:T(8,128)(2,1)S(1)}, u32[]{:S(2)}, u32[]{:S(2)}) collective-permute-start(bf16[2,128,192]{2,1,0:T(8,128)(2,1)S(1)} %pad_maximum_fusion.1), channel_id=1, source_target_pairs={{0,6},{1,7},{2,4},{3,5},{4,2},{5,3},{6,0},{7,1},{8,14},{9,15},{10,... | collective-permute-start | bytes 294920 | tf_op jit(solution)/shard_map/ppermute | solution.py:629
  109.0 3.3 %collective-permute-start.4 = (bf16[2,128,192]{2,1,0:T(8,128)(2,1)S(1)}, bf16[2,128,192]{2,1,0:T(8,128)(2,1)S(1)}, u32[]{:S(2)}, u32[]{:S(2)}) collective-permute-start(bf16[2,128,192]{2,1,0:T(8,128)(2,1)S(1)} %pad_maximum_fusion.1), channel_id=1, source_target_pairs={{0,4},{1,5},{2,6},{3,7},{4,0},{5,1},{6,2},{7,3},{8,12},{9,13},{10,... | collective-permute-start | bytes 294920 | tf_op jit(solution)/shard_map/ppermute | solution.py:629
  112.3 3.6 %collective-permute-start.3 = (bf16[2,128,192]{2,1,0:T(8,128)(2,1)S(1)}, bf16[2,128,192]{2,1,0:T(8,128)(2,1)S(1)}, u32[]{:S(2)}, u32[]{:S(2)}) collective-permute-start(bf16[2,128,192]{2,1,0:T(8,128)(2,1)S(1)} %pad_maximum_fusion.1), channel_id=1, source_target_pairs={{0,2},{1,3},{2,0},{3,1},{4,6},{5,7},{6,4},{7,5},{8,10},{9,11},{10,... | collective-permute-start | bytes 294920 | tf_op jit(solution)/shard_map/ppermute | solution.py:629
  116.1 3.3 %shard_map.218 = (f32[128,192]{1,0:T(8,128)S(1)}, f32[128,128]{1,0:T(8,128)S(1)}, f32[128,128]{1,0:T(8,128)S(1)}, f32[128,128]{1,0:T(8,128)S(1)}) custom-call(bf16[128,192]{1,0:T(8,128)(2,1)S(1)} %get-tuple-element.54.act_ref, f32[128,128]{1,0:T(8,128)S(1)} %get-tuple-element.55.bc_ref, f32[128,128]{1,0:T(8,128)S(1)} %get-tuple-element.56.step_ref, ...), custom_call_target="tpu_custom_call" | custom-call | flops 100000000 | bytes 1000000 | tf_op jit(solution)/shard_map/pallas_call | solution.py:598
  120.1 1.0 copy-done.5
  121.2 1.0 copy-done.7
  122.2 2.4 %shard_map.217 = (f32[256,192]{1,0:T(8,128)S(1)}, f32[256,192]{1,0:T(8,128)S(1)}) custom-call(s32[1]{0:T(128)} %bitcast.me_ref, bf16[8,128,192]{2,1,0:T(8,128)(2,1)S(1)} %pad_maximum_fusion.blocks_ref, f32[1024,128]{1,0:T(8,128)S(1)} %copy-done.5, f32[1024,128]{1,0:T(8,128)S(1)} %copy-done.7), custom_call_target="tpu_custom_call" | custom-call | flops 1000000000 | bytes 1000000 | tf_op jit(solution)/shard_map/pallas_call | solution.py:598
  124.6 5.0 %shard_map.220 = (bf16[128,192]{1,0:T(8,128)(2,1)S(1)}, bf16[1024,128]{1,0:T(8,128)(2,1)}) custom-call(s32[1]{0:T(128)} %bitcast.me_ref, bf16[8,144,96]{2,1,0:T(8,128)(2,1)S(1)} %all-to-all-done.got_ref, bf16[96,192]{1,0:T(8,128)(2,1)S(1)} %get-tuple-element.101.wbr_ref, f32[16,192]{1,0:T(8,128)S(1)} %pad.15.cw_ref, ...), custom_call_target="tpu_custom_call" | custom-call | flops 100000000 | bytes 1000000 | tf_op jit(solution)/shard_map/pallas_call | solution.py:598
  129.5 10.7 %all-to-all-start.5 = ((bf16[64,16,128]{2,1,0:T(8,128)(2,1)}), bf16[64,16,128]{2,1,0:T(8,128)(2,1)S(1)}, u32[]{:S(2)}, u32[]{:S(2)}) async-start(bf16[64,16,128]{2,1,0:T(8,128)(2,1)} %bitcast.21), calls=%async_computation.5 | async-start | bytes 524288 | tf_op jit(solution)/shard_map/all_to_all | solution.py:625
  140.3 2.1 %collective-permute-start.6 = (bf16[8,192]{1,0:T(8,128)(2,1)S(1)}, bf16[8,192]{1,0:T(8,128)(2,1)S(1)}, u32[]{:S(2)}, u32[]{:S(2)}) collective-permute-start(bf16[8,192]{1,0:T(8,128)(2,1)S(1)} %get-tuple-element.105), channel_id=1, source_target_pairs={{0,8},{8,16},{16,24},{24,32},{32,40},{40,48},{48,56},{56,64},{64,7... | collective-permute-start | bytes 9224 | tf_op jit(solution)/shard_map/ppermute | solution.py:613
  142.3 5.6 %collective-permute-start.7 = (bf16[8,192]{1,0:T(8,128)(2,1)S(1)}, bf16[8,192]{1,0:T(8,128)(2,1)S(1)}, u32[]{:S(2)}, u32[]{:S(2)}) collective-permute-start(bf16[8,192]{1,0:T(8,128)(2,1)S(1)} %get-tuple-element.104), channel_id=1, source_target_pairs={{8,0},{16,8},{24,16},{32,24},{40,32},{48,40},{56,48},{64,56},{72,6... | collective-permute-start | bytes 9224 | tf_op jit(solution)/shard_map/ppermute | solution.py:613
  148.0 3.8 %all-to-all-done.5.x_ref = bf16[64,16,128]{2,1,0:T(8,128)(2,1)S(1)} async-done(((bf16[64,16,128]{2,1,0:T(8,128)(2,1)}), bf16[64,16,128]{2,1,0:T(8,128)(2,1)S(1)}, u32[]{:S(2)}, u32[]{:S(2)}) %all-to-all-start.5) | async-done | bytes 262176 | tf_op jit(solution)/shard_map/all_to_all | solution.py:625
  152.4 8.4 %all-to-all-start.6 = ((f32[8,16,128]{2,1,0:T(8,128)}), f32[8,16,128]{2,1,0:T(8,128)S(1)}, u32[]{:S(2)}, u32[]{:S(2)}) async-start(f32[8,16,128]{2,1,0:T(8,128)} %shard_map.222), calls=%async_computation.6 | async-start | bytes 131072 | tf_op jit(solution)/shard_map/all_to_all | solution.py:625
  160.9 5.0 %all-to-all-done.6.x_ref = f32[8,16,128]{2,1,0:T(8,128)S(1)} async-done(((f32[8,16,128]{2,1,0:T(8,128)}), f32[8,16,128]{2,1,0:T(8,128)S(1)}, u32[]{:S(2)}, u32[]{:S(2)}) %all-to-all-start.6) | async-done | bytes 65568 | tf_op jit(solution)/shard_map/all_to_all | solution.py:625
  166.7 6.2 %all-to-all-start.7 = ((bf16[64,16,128]{2,1,0:T(8,128)(2,1)}), bf16[64,16,128]{2,1,0:T(8,128)(2,1)S(1)}, u32[]{:S(2)}, u32[]{:S(2)}) async-start(bf16[64,16,128]{2,1,0:T(8,128)(2,1)} %shard_map.223), calls=%async_computation.7 | async-start | bytes 524288 | tf_op jit(solution)/shard_map/all_to_all | solution.py:625
  173.0 7.1 %collective-permute-start.8 = (bf16[18,192]{1,0:T(8,128)(2,1)S(1)}, bf16[18,192]{1,0:T(8,128)(2,1)S(1)}, u32[]{:S(2)}, u32[]{:S(2)}) collective-permute-start(bf16[18,192]{1,0:T(8,128)(2,1)S(1)} %pad_maximum_fusion.4), channel_id=1, source_target_pairs={{0,1},{1,2},{2,3},{3,4},{4,5},{5,6},{6,7},{8,9},{9,10},{10,11},{11... | collective-permute-start | bytes 20744 | tf_op jit(solution)/shard_map/ppermute | solution.py:613
  180.1 2.6 %collective-permute-start.9 = (bf16[18,192]{1,0:T(8,128)(2,1)S(1)}, bf16[18,192]{1,0:T(8,128)(2,1)S(1)}, u32[]{:S(2)}, u32[]{:S(2)}) collective-permute-start(bf16[18,192]{1,0:T(8,128)(2,1)S(1)} %pad_maximum_fusion.5), channel_id=1, source_target_pairs={{1,0},{2,1},{3,2},{4,3},{5,4},{6,5},{7,6},{9,8},{10,9},{11,10},{12... | collective-permute-start | bytes 20744 | tf_op jit(solution)/shard_map/ppermute | solution.py:613
  183.5 7.0 %collective-permute-done.9.right_ref = bf16[18,192]{1,0:T(8,128)(2,1)S(1)} collective-permute-done((bf16[18,192]{1,0:T(8,128)(2,1)S(1)}, bf16[18,192]{1,0:T(8,128)(2,1)S(1)}, u32[]{:S(2)}, u32[]{:S(2)}) %collective-permute-start.9) | collective-permute-done | bytes 6944 | tf_op jit(solution)/shard_map/ppermute | solution.py:613
  (83 shorter events, 17.0 us)
Async XLA Ops:
  0.6 14.9 %copy-start.9 = (bf16[4,192,35]{1,0,2:T(4,128)(2,1)S(1)}, bf16[4,192,35]{1,0,2:T(4,128)(2,1)}, u32[]{:S(2)}) copy-start(bf16[4,192,35]{1,0,2:T(4,128)(2,1)} %param.16) | copy-start | bytes 161284
  1.5 14.0 %collective-permute-start.1 = (bf16[8,96]{1,0:T(8,128)(2,1)S(1)}, bf16[8,96]{1,0:T(8,128)(2,1)S(1)}, u32[]{:S(2)}, u32[]{:S(2)}) collective-permute-start(bf16[8,96]{1,0:T(8,128)(2,1)S(1)} %slice.54), channel_id=1, source_target_pairs={{8,0},{16,8},{24,16},{32,24},{40,32},{48,40},{56,48},{64,56},{72,6... | collective-permute-start | bytes 4616 | tf_op jit(solution)/shard_map/ppermute | solution.py:613
  12.8 7.0 %collective-permute-start = (bf16[8,96]{1,0:T(8,128)(2,1)S(1)}, bf16[8,96]{1,0:T(8,128)(2,1)S(1)}, u32[]{:S(2)}, u32[]{:S(2)}) collective-permute-start(bf16[8,96]{1,0:T(8,128)(2,1)S(1)} %slice.52), channel_id=1, source_target_pairs={{0,8},{8,16},{16,24},{24,32},{32,40},{40,48},{48,56},{56,64},{64,7... | collective-permute-start | bytes 4616 | tf_op jit(solution)/shard_map/ppermute | solution.py:613
  20.6 16.0 %all-to-all-start = ((bf16[8,144,96]{2,1,0:T(8,128)(2,1)}), bf16[8,144,96]{2,1,0:T(8,128)(2,1)S(1)}, u32[]{:S(2)}, u32[]{:S(2)}) async-start(bf16[8,144,96]{2,1,0:T(8,128)(2,1)} %broadcast_in_dim.3), calls=%async_computation | async-start | bytes 589824 | tf_op jit(solution)/shard_map/all_to_all | solution.py:625
  30.3 0.7 copy-start.11
  31.2 0.7 copy-start.13
  32.0 0.7 copy-start.14
  32.8 0.9 copy-start.8
  36.5 0.7 copy-start.1
  54.9 6.3 %copy-start.12 = (f32[4,192]{1,0:T(4,128)S(1)}, f32[4,192]{1,0:T(4,128)}, u32[]{:S(2)}) copy-start(f32[4,192]{1,0:T(4,128)} %param.19) | copy-start | bytes 9220
  54.9 6.4 %copy-start.10 = (bf16[16,768]{1,0:T(8,128)(2,1)S(1)}, bf16[16,768]{1,0:T(8,128)(2,1)}, u32[]{:S(2)}) copy-start(bf16[16,768]{1,0:T(8,128)(2,1)} %param.23) | copy-start | bytes 73732
  54.9 15.2 %all-to-all-start.2 = ((bf16[64,8,128]{2,1,0:T(8,128)(2,1)}), bf16[64,8,128]{2,1,0:T(8,128)(2,1)S(1)}, u32[]{:S(2)}, u32[]{:S(2)}) async-start(bf16[64,8,128]{2,1,0:T(8,128)(2,1)} %bitcast.7), calls=%async_computation.2 | async-start | bytes 262144 | tf_op jit(solution)/shard_map/all_to_all | solution.py:625
  62.2 7.9 %copy-start = (bf16[192,96]{1,0:T(8,128)(2,1)S(1)}, bf16[192,96]{1,0:T(8,128)(2,1)}, u32[]{:S(2)}) copy-start(bf16[192,96]{1,0:T(8,128)(2,1)} %ow_ref.1) | copy-start | bytes 110596
  62.2 7.9 %copy-start.3 = (f32[192]{0:T(256)S(1)}, f32[192]{0:T(256)}, u32[]{:S(2)}) copy-start(f32[192]{0:T(256)} %param.21) | copy-start | bytes 2308
  68.3 0.8 copy-start.4
  69.1 0.8 copy-start.6
  70.1 0.7 copy-start.2
  73.2 20.6 %all-to-all-start.3 = ((bf16[64,8,128]{2,1,0:T(8,128)(2,1)}), bf16[64,8,128]{2,1,0:T(8,128)(2,1)S(1)}, u32[]{:S(2)}, u32[]{:S(2)}) async-start(bf16[64,8,128]{2,1,0:T(8,128)(2,1)} %bitcast.12), calls=%async_computation.3 | async-start | bytes 262144 | tf_op jit(solution)/shard_map/all_to_all | solution.py:625
  83.8 10.1 %collective-permute-start.2 = (bf16[128,192]{1,0:T(8,128)(2,1)S(1)}, bf16[128,192]{1,0:T(8,128)(2,1)S(1)}, u32[]{:S(2)}, u32[]{:S(2)}) collective-permute-start(bf16[128,192]{1,0:T(8,128)(2,1)S(1)} %get-tuple-element.65.g_ref), channel_id=1, source_target_pairs={{0,1},{1,0},{2,3},{3,2},{4,5},{5,4},{6,7},{7,6},{8,9},{9,8},{10,11... | collective-permute-start | bytes 147464 | tf_op jit(solution)/shard_map/ppermute | solution.py:629
  94.8 25.3 %all-to-all-start.4 = ((bf16[64,8,128]{2,1,0:T(8,128)(2,1)}), bf16[64,8,128]{2,1,0:T(8,128)(2,1)S(1)}, u32[]{:S(2)}, u32[]{:S(2)}) async-start(bf16[64,8,128]{2,1,0:T(8,128)(2,1)} %bitcast.16), calls=%async_computation.4 | async-start | bytes 262144 | tf_op jit(solution)/shard_map/all_to_all | solution.py:625
  106.0 13.3 %collective-permute-start.5 = (bf16[2,128,192]{2,1,0:T(8,128)(2,1)S(1)}, bf16[2,128,192]{2,1,0:T(8,128)(2,1)S(1)}, u32[]{:S(2)}, u32[]{:S(2)}) collective-permute-start(bf16[2,128,192]{2,1,0:T(8,128)(2,1)S(1)} %pad_maximum_fusion.1), channel_id=1, source_target_pairs={{0,6},{1,7},{2,4},{3,5},{4,2},{5,3},{6,0},{7,1},{8,14},{9,15},{10,... | collective-permute-start | bytes 294920 | tf_op jit(solution)/shard_map/ppermute | solution.py:629
  109.0 10.4 %collective-permute-start.4 = (bf16[2,128,192]{2,1,0:T(8,128)(2,1)S(1)}, bf16[2,128,192]{2,1,0:T(8,128)(2,1)S(1)}, u32[]{:S(2)}, u32[]{:S(2)}) collective-permute-start(bf16[2,128,192]{2,1,0:T(8,128)(2,1)S(1)} %pad_maximum_fusion.1), channel_id=1, source_target_pairs={{0,4},{1,5},{2,6},{3,7},{4,0},{5,1},{6,2},{7,3},{8,12},{9,13},{10,... | collective-permute-start | bytes 294920 | tf_op jit(solution)/shard_map/ppermute | solution.py:629
  112.3 7.8 %collective-permute-start.3 = (bf16[2,128,192]{2,1,0:T(8,128)(2,1)S(1)}, bf16[2,128,192]{2,1,0:T(8,128)(2,1)S(1)}, u32[]{:S(2)}, u32[]{:S(2)}) collective-permute-start(bf16[2,128,192]{2,1,0:T(8,128)(2,1)S(1)} %pad_maximum_fusion.1), channel_id=1, source_target_pairs={{0,2},{1,3},{2,0},{3,1},{4,6},{5,7},{6,4},{7,5},{8,10},{9,11},{10,... | collective-permute-start | bytes 294920 | tf_op jit(solution)/shard_map/ppermute | solution.py:629
  120.1 1.0 copy-start.5
  121.2 1.0 copy-start.7
  129.5 22.2 %all-to-all-start.5 = ((bf16[64,16,128]{2,1,0:T(8,128)(2,1)}), bf16[64,16,128]{2,1,0:T(8,128)(2,1)S(1)}, u32[]{:S(2)}, u32[]{:S(2)}) async-start(bf16[64,16,128]{2,1,0:T(8,128)(2,1)} %bitcast.21), calls=%async_computation.5 | async-start | bytes 524288 | tf_op jit(solution)/shard_map/all_to_all | solution.py:625
  140.3 32.7 %collective-permute-start.6 = (bf16[8,192]{1,0:T(8,128)(2,1)S(1)}, bf16[8,192]{1,0:T(8,128)(2,1)S(1)}, u32[]{:S(2)}, u32[]{:S(2)}) collective-permute-start(bf16[8,192]{1,0:T(8,128)(2,1)S(1)} %get-tuple-element.105), channel_id=1, source_target_pairs={{0,8},{8,16},{16,24},{24,32},{32,40},{40,48},{48,56},{56,64},{64,7... | collective-permute-start | bytes 9224 | tf_op jit(solution)/shard_map/ppermute | solution.py:613
  142.3 30.6 %collective-permute-start.7 = (bf16[8,192]{1,0:T(8,128)(2,1)S(1)}, bf16[8,192]{1,0:T(8,128)(2,1)S(1)}, u32[]{:S(2)}, u32[]{:S(2)}) collective-permute-start(bf16[8,192]{1,0:T(8,128)(2,1)S(1)} %get-tuple-element.104), channel_id=1, source_target_pairs={{8,0},{16,8},{24,16},{32,24},{40,32},{48,40},{56,48},{64,56},{72,6... | collective-permute-start | bytes 9224 | tf_op jit(solution)/shard_map/ppermute | solution.py:613
  152.4 13.5 %all-to-all-start.6 = ((f32[8,16,128]{2,1,0:T(8,128)}), f32[8,16,128]{2,1,0:T(8,128)S(1)}, u32[]{:S(2)}, u32[]{:S(2)}) async-start(f32[8,16,128]{2,1,0:T(8,128)} %shard_map.222), calls=%async_computation.6 | async-start | bytes 131072 | tf_op jit(solution)/shard_map/all_to_all | solution.py:625
  166.7 24.9 %all-to-all-start.7 = ((bf16[64,16,128]{2,1,0:T(8,128)(2,1)}), bf16[64,16,128]{2,1,0:T(8,128)(2,1)S(1)}, u32[]{:S(2)}, u32[]{:S(2)}) async-start(bf16[64,16,128]{2,1,0:T(8,128)(2,1)} %shard_map.223), calls=%async_computation.7 | async-start | bytes 524288 | tf_op jit(solution)/shard_map/all_to_all | solution.py:625
  173.0 10.5 %collective-permute-start.8 = (bf16[18,192]{1,0:T(8,128)(2,1)S(1)}, bf16[18,192]{1,0:T(8,128)(2,1)S(1)}, u32[]{:S(2)}, u32[]{:S(2)}) collective-permute-start(bf16[18,192]{1,0:T(8,128)(2,1)S(1)} %pad_maximum_fusion.4), channel_id=1, source_target_pairs={{0,1},{1,2},{2,3},{3,4},{4,5},{5,6},{6,7},{8,9},{9,10},{10,11},{11... | collective-permute-start | bytes 20744 | tf_op jit(solution)/shard_map/ppermute | solution.py:613
  180.1 10.4 %collective-permute-start.9 = (bf16[18,192]{1,0:T(8,128)(2,1)S(1)}, bf16[18,192]{1,0:T(8,128)(2,1)S(1)}, u32[]{:S(2)}, u32[]{:S(2)}) collective-permute-start(bf16[18,192]{1,0:T(8,128)(2,1)S(1)} %pad_maximum_fusion.5), channel_id=1, source_target_pairs={{1,0},{2,1},{3,2},{4,3},{5,4},{6,5},{7,6},{9,8},{10,9},{11,10},{12... | collective-permute-start | bytes 20744 | tf_op jit(solution)/shard_map/ppermute | solution.py:613

commit v6 on v5

--- a/solution.py
+++ b/solution.py
@@ -15,6 +15,10 @@
 C = 8
 T = R * C
 PITCH = 24
+BIAS = slice(9, 10)
+GAIN = slice(10, 11)
+SHIFT = slice(11, 12)
+SKIP = slice(12, 13)
 
 F32 = jnp.float32
 BF = jnp.bfloat16
@@ -209,7 +213,7 @@
 
 
 def first_kernel(
-    me_ref, got_ref, wbr_ref, cw_ref, cb_ref, wd_ref, wbc_ref, sb_ref, ld_ref,
+    me_ref, got_ref, wbr_ref, cw_ref, wd_ref, wbc_ref, sb_ref, ld_ref,
     before_ref, act_ref, rawd_ref, bc_ref, step_ref, log_ref, tot_ref, mv_ref, pad_ref, wide_ref,
 ):
     fill_blocks(me_ref[0], got_ref, pad_ref, as_branch(wbr_ref))
@@ -218,7 +222,7 @@
         shifted = pad_ref[:, 7 + b : 7 + b + C, :]
         for a in range(3):
             total = total + cw_ref[3 * a + b : 3 * a + b + 1, :] * shifted[a : a + R]
-    before = total.reshape(T, DI) + cb_ref[...]
+    before = total.reshape(T, DI) + cw_ref[BIAS, :]
     act = (before * sigmoid(before)).astype(BF)
     before_ref[...] = before
     act_ref[...] = act
@@ -252,8 +256,8 @@
 
 
 def row_scan_kernel(
-    me_ref, got_ref, wbr_ref, cw_ref, cb_ref, wd_ref, wbc_ref, sb_ref, ld_ref,
-    s0_ref, s1_ref, later_ref, gate_ref, pad_ref,
+    me_ref, got_ref, wbr_ref, cw_ref, wd_ref, wbc_ref, sb_ref, ld_ref,
+    s0_ref, s1_ref, later_ref, pad_ref,
 ):
     nothing = jnp.zeros((R + 2, 8, DI), F32)
     pad_ref[:, 0:8, :] = nothing
@@ -286,32 +290,31 @@
             shifted = pad_ref[2 * group : 2 * group + 4, 7 + b : 71 + b, :]
             for a in range(3):
                 total = total + cw_ref[3 * a + b : 3 * a + b + 1, :] * shifted[a : a + 2]
-        wide = total.reshape(T, DI) + cb_ref[...]
+        wide = total.reshape(T, DI) + cw_ref[BIAS, :]
         act = (wide * sigmoid(wide)).astype(BF)
         wide = act.astype(F32)
         step = softplus(dot(act, wd_ref[...]) + sb_ref[...])
         bc = dot(act, wbc_ref[...])
         x = fine(reach, step * rate)
         w_in = jnp.exp(jnp.where(first, x[:T], x[T : 2 * T])) * step * valid_in
-        later_ref[group * T : group * T + T, :] = (
-            jnp.exp(jnp.where(first, x[2 * T : 3 * T], x[3 * T :])) * valid_out
+        later = jnp.exp(jnp.where(first, x[2 * T : 3 * T], x[3 * T :])) * valid_out
+        later_ref[group * T : group * T + T, :] = jnp.where(
+            iota((T, T), 1) < 64, shifted_gate(bc), pltpu.roll(later, 64, 1)
         )
-        gate_ref[group * T : group * T + T, :] = shifted_gate(bc)
         for k, ref in enumerate((s0_ref, s1_ref)):
             entry = ones(i == 16 * k + (ji & 15))
             spread = jnp.where(line, fine(bc, entry), 0.0)
             ref[32 * group : 32 * group + 32, :] = fine(spread, by_head(w_in, k) * wide, 0, 0)
 
 
-def row_back_kernel(me_ref, blocks_ref, later_ref, gate_ref, l0_ref, l1_ref):
+def row_back(me, blocks_ref, later_ref, out_refs):
     tj, j = (iota((T, 32), 0), iota((T, 32), 1))
     line = (tj >> 6) == (j >> 4)
     for group in range(R // 2):
-        part = slice(group * T, group * T + T)
-        g = row_pair(me_ref[0], blocks_ref, group)
-        later = later_ref[part, :]
-        gate = gate_ref[part, :]
-        for k, ref in enumerate((l0_ref, l1_ref)):
+        g = row_pair(me, blocks_ref, group)
+        gate = later_ref[group * T : group * T + T, :]
+        later = pltpu.roll(gate, 64, 1)
+        for k, ref in enumerate(out_refs):
             entry = ones(tj == 16 * k + (j & 15))
             spread = jnp.where(line, fine(gate, entry), 0.0)
             ref[32 * group : 32 * group + 32, :] = fine(spread, by_head(later, k) * g, 0, 0)
@@ -353,15 +356,16 @@
 
 
 def norm_kernel(
-    y_ref, act_ref, bc_ref, log_ref, tot_ref, sv_ref, s0_ref, s1_ref, skip_ref, tok_ref, wg_ref, gain_ref,
-    nb_ref, ow_ref, cot_ref,
+    y_ref, act_ref, bc_ref, log_ref, tot_ref, sv_ref, s0_ref, s1_ref, vec_ref, tok_ref, wg_ref, ow_ref,
+    cot_ref,
     out_ref, g_ref, dgate_ref, gated_ref, norms_ref, mv_ref, wide_ref,
 ):
     open_message(sv_ref, wide_ref)
     bc = bc_ref[...]
     out_gate = shifted_gate(bc)
     exp_log = jnp.exp(log_ref[...])
-    summed = y_ref[...] + skip_ref[...] * act_ref[...].astype(F32)
+    gain = vec_ref[GAIN, :]
+    summed = y_ref[...] + vec_ref[SKIP, :] * act_ref[...].astype(F32)
     for k in range(4):
         state = state_in(k, (s0_ref, s1_ref), wide_ref)
         summed = summed + carry(k, out_gate, exp_log, state)
@@ -370,7 +374,7 @@
     center = summed - jnp.mean(summed, axis=1, keepdims=True)
     inv = lax.rsqrt(jnp.mean(center * center, axis=1, keepdims=True) + 1e-5)
     unit = center * inv
-    normed = unit * gain_ref[...] + nb_ref[...]
+    normed = unit * gain + vec_ref[SHIFT, :]
     gated = (normed * gate * sig).astype(BF)
     gated_ref[...] = gated
     out_ref[...] = dot(gated, ow_ref[...]).astype(BF)
@@ -379,7 +383,7 @@
     dgate_ref[...] = (grad * normed * (sig * (1.0 + gate * (1.0 - sig)))).astype(BF)
     norms_ref[0:1, :] = jnp.sum(dnormed * unit, axis=0, keepdims=True)
     norms_ref[1:2, :] = jnp.sum(dnormed, axis=0, keepdims=True)
-    dunit = dnormed * gain_ref[...]
+    dunit = dnormed * gain
     g = inv * (
         dunit
         - jnp.mean(dunit, axis=1, keepdims=True)
@@ -396,7 +400,7 @@
 
 def back_kernel(
     act_ref, bc_ref, step_ref, log_ref, g_ref, sv_ref, s0_ref, s1_ref,
-    dact_ref, dbc_ref, dstep_ref, dlog_ref, wide_ref,
+    back_ref, wide_ref,
 ):
     open_message(sv_ref, wide_ref)
     bc = bc_ref[...]
@@ -438,31 +442,42 @@
         row_sums = row_sums + head_sum(carried * expg, k)
         d_out = d_out + gather_states(fine(expg, state, 1, 1), k)
     d_step = jnp.concatenate(step_rows + [jnp.zeros((T - 12, T), F32)], axis=0).T
-    dact_ref[...] = per_head(lambda h: fine(weights[h], g, 0, 0))
-    dbc_ref[...] = d_in + pltpu.roll(d_out, 64, 1)
-    dstep_ref[...] = d_step
-    dlog_ref[...] = row_sums - step * d_step
-
-
-def gate_grads_kernel(tok_ref, dgate_ref, gated_ref, cot_ref, gin_ref, gout_ref):
-    gin_ref[...] = dot(tok_ref[...], dgate_ref[...], 0, 0)
-    gout_ref[...] = dot(cot_ref[...], gated_ref[...], 0, 0)
+    back_ref[:, 0:192] = per_head(lambda h: fine(weights[h], g, 0, 0))
+    back_ref[:, 192:256] = jnp.zeros((T, 64), F32)
+    back_ref[:, 256:384] = d_in + pltpu.roll(d_out, 64, 1)
+    back_ref[:, 384:512] = jnp.where(lane1 < 64, d_step, pltpu.roll(row_sums - step * d_step, 64, 1))
+
+
+def gate_grads_kernel(
+    me_ref, got_ref, tok_ref, dgate_ref, gated_ref, cot_ref, side_ref, shifts_ref, near_ref
+):
+    fill_blocks(me_ref[0], got_ref, near_ref, lambda x: x.astype(F32))
+    for b in range(3):
+        near = near_ref[:, 7 + b : 7 + b + C, :]
+        for a in range(3):
+            i = 3 * a + b
+            shifts_ref[D * i : D * i + D, :] = near[a : a + R].reshape(T, D).T.astype(BF)
+    side_ref[:D, :] = dot(tok_ref[...], dgate_ref[...], 0, 0)
+    side_ref[D:, :] = dot(cot_ref[...], gated_ref[...], 0, 0)
 
 
 def last_kernel(
-    me_ref, got_ref, wbr_ref, cw_ref, before_ref, act_ref, rawd_ref, bc_ref, step_ref, log_ref, tot_ref, g_ref,
-    sv_ref, s0_ref, s1_ref, lv_ref, l0_ref, l1_ref, dact_ref, dbc_ref, dstep_ref, dlog_ref, skip_ref, wd_ref, wbc_ref,
-    sb_ref, ld_ref, gin_gate_ref, gout_ref, norms_ref,
-    gb_ref, pack_ref, pad_ref, tok_ref, early_ref, late_ref,
-):
+    me_ref, pad_ref, shifts_ref, vec_ref, before_ref, act_ref, rawd_ref, bc_ref, step_ref, log_ref, tot_ref, g_ref,
+    sv_ref, s0_ref, s1_ref, lv_ref, blocks_ref, later_ref, back_ref, wd_ref,
+    wbc_ref,
+    sb_ref, ld_ref, side_ref, norms_ref,
+    gb_ref, pack_ref, early_ref, late_ref, l0_ref, l1_ref,
+):
+    row_back(me_ref[0], blocks_ref, later_ref, (l0_ref, l1_ref))
     open_message(sv_ref, early_ref)
     open_message(lv_ref, late_ref)
     step, log, tot, bc = (step_ref[...], log_ref[...], tot_ref[...], bc_ref[...])
     act = act_ref[...]
     wide = act.astype(F32)
     g = g_ref[...].astype(F32)
-    d_act = dact_ref[...] + skip_ref[...] * g
-    d_bc = dbc_ref[...]
+    d_act = back_ref[:, 0:192] + vec_ref[SKIP, :] * g
+    d_bc = back_ref[:, 256:384]
+    d_mix = back_ref[:, 384:512]
     to_end = jnp.exp(tot - log)
     weight = to_end * step
     through = jnp.exp(tot)
@@ -477,9 +492,9 @@
         inner = inner + head_sum(wide * reach, k)
         d_bc = d_bc + gather_states(fine(wk * wide, later, 1, 1), k)
         cross = cross + fine(ones(on_line(k)), head_sum(later * earlier, k))
-    d_step = dstep_ref[...] + to_end * inner
+    d_step = d_mix + to_end * inner
     left = weight * inner
-    d_log = dlog_ref[...]
+    d_log = pltpu.roll(d_mix, 64, 1)
     parts = []
     for k in range(4):
         after = mask(k ^ 1)
@@ -500,19 +515,15 @@
     gb = (d_act * sig * (1.0 + before * (1.0 - sig))).astype(BF)
     gb_ref[...] = gb
     gbw = gb.astype(F32)
-    fill_blocks(me_ref[0], got_ref, pad_ref, as_branch(wbr_ref))
-    fill_blocks(me_ref[0], got_ref, tok_ref, lambda x: x.astype(F32))
+    product = dot(shifts_ref[...], gb)
     gin = jnp.zeros((D, DI), F32)
     conv_rows = [None] * 9
     for b in range(3):
         near = pad_ref[:, 7 + b : 7 + b + C, :]
-        near_tok = tok_ref[:, 7 + b : 7 + b + C, :]
         for a in range(3):
             i = 3 * a + b
             conv_rows[i] = jnp.sum(gbw * near[a : a + R].reshape(T, DI), axis=0, keepdims=True)
-            gin = gin + cw_ref[i : i + 1, :] * dot(
-                near_tok[a : a + R].reshape(T, D).astype(BF), gb, 0, 0
-            )
+            gin = gin + vec_ref[i : i + 1, :] * product[D * i : D * i + D]
     wide_row = lambda x: jnp.concatenate([x, jnp.zeros((1, DI - T), F32)], axis=1)
     small = jnp.concatenate(
         conv_rows
@@ -528,7 +539,7 @@
         axis=0,
     )
     both = [
-        gin, gin_gate_ref[...], gout_ref[...], small, dot(d_bc, act, 0, 0),
+        gin, side_ref[...], small, dot(d_bc, act, 0, 0),
         dot(d_raw, act, 0, 0)[:16],
     ]
     full = jnp.concatenate(both, axis=0)
@@ -668,7 +679,6 @@
     place = lax.axis_index("col").reshape(1)
     cot = cotangent.reshape(T, D)
     w_branch, w_gate = (in_weight[:, :DI], in_weight[:, DI:])
-    taps = jnp.pad(conv_weight.reshape(9, DI), ((0, 7), (0, 0)))
     by_channel = jnp.moveaxis(scan_weight, 1, 0)
     w_step = jnp.pad(by_channel[:, :, :HEADS].reshape(DI, 12), ((0, 0), (0, 116)))
     w_bc = jnp.concatenate(
@@ -681,7 +691,13 @@
     row = lambda x: x.reshape(1, -1)
     bias = jnp.pad(row(step_bias), ((0, 0), (0, 116)))
     rate = jnp.pad(row(log_decay), ((0, 0), (0, 116)))
-    skip = row(jnp.sum(skip_gain, axis=0))
+    vec = jnp.concatenate(
+        [
+            conv_weight.reshape(9, DI), row(conv_bias), row(norm_gain), row(norm_bias),
+            jnp.sum(skip_gain, axis=0, keepdims=True), jnp.zeros((3, DI), F32),
+        ],
+        axis=0,
+    )
     square = ((T, T), F32)
     wide = ((T, DI), F32)
     low = ((T, DI), BF)
@@ -690,47 +706,46 @@
     states = ((256, DI), F32)
     long = ((8 * T, T), F32)
 
-    before, act, raw_d, bc, step, log, tot, mv = call(
-        first_kernel, [wide, low, square, square, square, square, square, message],
-        place, got, w_branch, taps, row(conv_bias), w_step, w_bc, bias, rate,
-        scratch=[pltpu.VMEM((R + 2, PITCH, DI), F32), opened], scalars=1,
+    before, act, raw_d, bc, step, log, tot, mv, padded = call(
+        first_kernel,
+        [wide, low, square, square, square, square, square, message, ((R + 2, PITCH, DI), F32)],
+        place, got, w_branch, vec, w_step, w_bc, bias, rate, scratch=[opened], scalars=1,
     )
     sv, _ = exchange(mv, "row", False)
-    s0, s1, later, gate_c = call(
-        row_scan_kernel, [states, states, long, long],
-        place, got, w_branch, taps, row(conv_bias), w_step, w_bc, bias, rate,
+    s0, s1, later = call(
+        row_scan_kernel, [states, states, long],
+        place, got, w_branch, vec, w_step, w_bc, bias, rate,
         scratch=[pltpu.VMEM((R + 2, 80, DI), F32)], scalars=1, flops=10**9,
     )
     (y,) = call(local_kernel, [wide], act, bc, step, log)
     out, g, d_gate, gated, norms, mv = call(
         norm_kernel, [((T, D), BF), low, low, low, ((8, DI), F32), message],
-        y, act, bc, log, tot, sv, s0, s1, skip, own, w_gate, row(norm_gain), row(norm_bias), out_weight, cot,
+        y, act, bc, log, tot, sv, s0, s1, vec, own, w_gate, out_weight, cot,
         scratch=[opened],
     )
-    lv, pair = exchange(mv, "row", True, in_pairs(g))
+    back = call(
+        back_kernel, [((T, 512), F32)], act, bc, step, log, g, sv, s0, s1, scratch=[opened]
+    )
+    sides = call(
+        gate_grads_kernel, [((2 * D, DI), F32), ((9 * D, T), BF)],
+        place, got, own, d_gate, gated, cot,
+        scratch=[pltpu.VMEM((R + 2, PITCH, D), F32)], scalars=1, flops=10**7,
+    )
+    lv, (pair, back, sides) = exchange(mv, "row", True, (in_pairs(g), back, sides))
+    side, shifts = sides
     lv, blocks = lax.optimization_barrier((lv, along_col(pair)))
-    d_act, d_bc, d_step, d_log = call(
-        back_kernel, [wide, square, square, square], act, bc, step, log, g, sv, s0, s1,
-        scratch=[opened],
-    )
-    l0, l1 = call(
-        row_back_kernel, [states, states], place, blocks, later, gate_c, scalars=1, flops=10**9
-    )
-    gin_gate, gout = call(
-        gate_grads_kernel, [((D, DI), F32), ((D, DI), F32)], own, d_gate, gated, cot, flops=10**7
-    )
     gb, pack = call(
         last_kernel, [low, ((1024, 128), BF)],
-        place, got, w_branch, taps, before, act, raw_d, bc, step, log, tot, g, sv, s0, s1, lv, l0, l1, d_act, d_bc,
-        d_step, d_log, skip, w_step, w_bc, bias, rate, gin_gate, gout, norms,
-        scratch=[pltpu.VMEM((R + 2, PITCH, DI), F32), pltpu.VMEM((R + 2, PITCH, D), F32), opened, opened],
+        place, padded, shifts, vec, before, act, raw_d, bc, step, log, tot, g, sv, s0, s1, lv, blocks, later,
+        *back, w_step, w_bc, bias, rate, side, norms,
+        scratch=[opened, opened, pltpu.VMEM((256, DI), F32), pltpu.VMEM((256, DI), F32)],
         scalars=1,
     )
     scale = float(T * lax.axis_size("row") * lax.axis_size("col")) ** (-0.5)
     total = reduced(pack, scale)
     rim = with_rim(gb)
     (d_tokens,) = call(
-        out_kernel, [((T, D), BF)], *rim, taps, d_gate, w_branch, w_gate,
+        out_kernel, [((T, D), BF)], *rim, vec, d_gate, w_branch, w_gate,
         scratch=[pltpu.VMEM((R + 2, PITCH, DI), F32)],
     )
     row_shape = ((1, DI), F32)

time: 194 us -> 194 us (level)
  waiting for transfers between devices: 26.2 us -> 30.6 us
  starting transfers between devices: 111 us -> 107 us
    all_to_all x7, waiting for transfers between devices: 11.8 us -> 15.3 us  [all_to_all(): return lax.all_to_all(x, axis, 0, 0, tiled=True)]
    all_to_all x7, starting transfers between devices: 63.2 us -> 60.8 us  [all_to_all(): return lax.all_to_all(x, axis, 0, 0, tiled=True)]
    unnamed x33 -> x59, local copies, waits for them, and re-layouts: 7.81 us -> 6.43 us
    pallas_call x14 -> x13, Pallas kernels: 26 us -> 25.6 us  [call(): pl.pallas_call(kernel, out_shape=[jax.ShapeDtypeStruct(s, t) for s, t in...]
where the time goes in v6:
time: 194 us; the launch traced here: 193 us
  starting transfers between devices  107 us (55%)
  waiting for transfers between devices  30.6 us (16%)
  Pallas kernels  25.6 us (13%)
  blocking collectives  15.4 us (8%)
  local copies, waits for them, and re-layouts  11.3 us (6%)
    all_to_all x7, starting transfers between devices, all_to_all(): return lax.all_to_all(x, axis, 0, 0, tiled=True)  60.8 us
    ppermute x6, starting transfers between devices, neighbours(): return (lax.ppermute(last, axis, up), lax.ppermute(first, axis, down))  29.2 us
    pallas_call x13, Pallas kernels, call(): pl.pallas_call(kernel, out_shape=[jax.ShapeDtypeStruct(s, t) for s, t in...  25.6 us
    ppermute x4, starting transfers between devices, swapped(): lax.ppermute(x, 'col', [(i, i ^ step) for i in range(lax.axis_size('col'))])  17.3 us
    all_to_all x1, blocking collectives, all_to_all(): return lax.all_to_all(x, axis, 0, 0, tiled=True)  15.4 us
    all_to_all x7, waiting for transfers between devices, all_to_all(): return lax.all_to_all(x, axis, 0, 0, tiled=True)  15.3 us
    ppermute x6, waiting for transfers between devices, neighbours(): return (lax.ppermute(last, axis, up), lax.ppermute(first, axis, down))  11.3 us
    unnamed x59, local copies, waits for them, and re-layouts  6.43 us
  transfers between devices with their start and end apart: 17, of which 8 were waited for; matrix products, arithmetic and copies ran while one was open for 2% of the time, Pallas kernels for 6%

profile of v6, /device:TPU:56, one launch (start us, length us, event | category | flops | bytes accessed | tf_op | source)
XLA Modules:
  0.0 192.6 jit_solution(1864646610242555605)
XLA Ops:
  1.5 11.2 %collective-permute-start.1 = (bf16[8,96]{1,0:T(8,128)(2,1)S(1)}, bf16[8,96]{1,0:T(8,128)(2,1)S(1)}, u32[]{:S(2)}, u32[]{:S(2)}) collective-permute-start(bf16[8,96]{1,0:T(8,128)(2,1)S(1)} %slice.54), channel_id=1, source_target_pairs={{8,0},{16,8},{24,16},{32,24},{40,32},{48,40},{56,48},{64,56},{72,6... | collective-permute-start | bytes 4616 | tf_op jit(solution)/shard_map/ppermute | solution.py:624
  12.8 1.9 collective-permute-start
  15.6 4.2 %collective-permute-done = bf16[8,96]{1,0:T(8,128)(2,1)S(1)} collective-permute-done((bf16[8,96]{1,0:T(8,128)(2,1)S(1)}, bf16[8,96]{1,0:T(8,128)(2,1)S(1)}, u32[]{:S(2)}, u32[]{:S(2)}) %collective-permute-start) | collective-permute-done | bytes 1568 | tf_op jit(solution)/shard_map/ppermute | solution.py:624
  20.5 9.7 %all-to-all-start = ((bf16[8,144,96]{2,1,0:T(8,128)(2,1)}), bf16[8,144,96]{2,1,0:T(8,128)(2,1)S(1)}, u32[]{:S(2)}, u32[]{:S(2)}) async-start(bf16[8,144,96]{2,1,0:T(8,128)(2,1)} %broadcast_in_dim.9), calls=%async_computation | async-start | bytes 589824 | tf_op jit(solution)/shard_map/all_to_all | solution.py:636
  33.3 3.2 %all-to-all-done.got_ref = bf16[8,144,96]{2,1,0:T(8,128)(2,1)S(1)} async-done(((bf16[8,144,96]{2,1,0:T(8,128)(2,1)}), bf16[8,144,96]{2,1,0:T(8,128)(2,1)S(1)}, u32[]{:S(2)}, u32[]{:S(2)}) %all-to-all-start) | async-done | bytes 221216 | tf_op jit(solution)/shard_map/all_to_all | solution.py:636
  36.5 1.5 shard_map.211
  38.6 15.4 %all_to_all.40 = bf16[64,8,128]{2,1,0:T(8,128)(2,1)S(1)} all-to-all(bf16[64,8,128]{2,1,0:T(8,128)(2,1)S(1)} %bitcast.43), channel_id=1, replica_groups=mesh['row'=64,'col'=8] {'row'}, dimensions={0} | all-to-all | bytes 262144 | tf_op jit(solution)/shard_map/all_to_all | solution.py:636
  54.9 6.3 %all-to-all-start.2 = ((bf16[64,8,128]{2,1,0:T(8,128)(2,1)}), bf16[64,8,128]{2,1,0:T(8,128)(2,1)S(1)}, u32[]{:S(2)}, u32[]{:S(2)}) async-start(bf16[64,8,128]{2,1,0:T(8,128)(2,1)} %bitcast.10), calls=%async_computation.2 | async-start | bytes 262144 | tf_op jit(solution)/shard_map/all_to_all | solution.py:636
  62.1 6.1 %shard_map.214 = (f32[256,192]{1,0:T(8,128)S(1)}, f32[256,192]{1,0:T(8,128)S(1)}, f32[1024,128]{1,0:T(8,128)S(1)}) custom-call(s32[1]{0:T(128)} %bitcast.me_ref, bf16[8,144,96]{2,1,0:T(8,128)(2,1)S(1)} %all-to-all-done.got_ref, bf16[96,192]{1,0:T(8,128)(2,1)S(1)} %get-tuple-element.95.wbr_ref, f32[16,192]{1,0:T(8,128)S(1)} %concatenate.19.cw_ref.vec_ref, ...), custom_call_target="tpu_custom_call" | custom-call | flops 1000000000 | bytes 1000000 | tf_op jit(solution)/shard_map/pallas_call | solution.py:609
  68.2 1.8 all-to-all-done.2
  70.0 2.5 %shard_map.215 = (bf16[128,96]{1,0:T(8,128)(2,1)S(1)}, bf16[128,192]{1,0:T(8,128)(2,1)S(1)}, bf16[128,192]{1,0:T(8,128)(2,1)S(1)}, bf16[128,192]{1,0:T(8,128)(2,...) custom-call(f32[128,192]{1,0:T(8,128)S(1)} %shard_map.212.y_ref, bf16[128,192]{1,0:T(8,128)(2,1)S(1)} %get-tuple-element.51.act_ref, ...), custom_call_target="tpu_custom_call" | custom-call | flops 100000000 | bytes 1000000 | tf_op jit(solution)/shard_map/pallas_call | solution.py:609
  73.1 8.9 %all-to-all-start.3 = ((bf16[64,8,128]{2,1,0:T(8,128)(2,1)}), bf16[64,8,128]{2,1,0:T(8,128)(2,1)S(1)}, u32[]{:S(2)}, u32[]{:S(2)}) async-start(bf16[64,8,128]{2,1,0:T(8,128)(2,1)} %bitcast.12), calls=%async_computation.3 | async-start | bytes 262144 | tf_op jit(solution)/shard_map/all_to_all | solution.py:636
  82.0 7.5 %collective-permute-start.2 = (bf16[128,192]{1,0:T(8,128)(2,1)S(1)}, bf16[128,192]{1,0:T(8,128)(2,1)S(1)}, u32[]{:S(2)}, u32[]{:S(2)}) collective-permute-start(bf16[128,192]{1,0:T(8,128)(2,1)S(1)} %get-tuple-element.62.g_ref), channel_id=1, source_target_pairs={{0,1},{1,0},{2,3},{3,2},{4,5},{5,4},{6,7},{7,6},{8,9},{9,8},{10,11... | collective-permute-start | bytes 147464 | tf_op jit(solution)/shard_map/ppermute | solution.py:640
  89.8 3.3 %shard_map.216.back_ref = f32[128,512]{1,0:T(8,128)S(1)} custom-call(bf16[128,192]{1,0:T(8,128)(2,1)S(1)} %get-tuple-element.51.act_ref, f32[128,128]{1,0:T(8,128)S(1)} %get-tuple-element.52.bc_ref, f32[128,128]{1,0:T(8,128)S(1)} %get-tuple-element.53.step_ref, f32[128,128]{1,0:T(8,128)S(1)} %get-tuple-element.54.log_ref, ...), custom_call_target="tpu_custom_call" | custom-call | flops 100000000 | bytes 1000000 | tf_op jit(solution)/shard_map/pallas_call | solution.py:609
  94.0 10.7 %all-to-all-start.4 = ((bf16[64,8,128]{2,1,0:T(8,128)(2,1)}), bf16[64,8,128]{2,1,0:T(8,128)(2,1)S(1)}, u32[]{:S(2)}, u32[]{:S(2)}) async-start(bf16[64,8,128]{2,1,0:T(8,128)(2,1)} %bitcast.16), calls=%async_computation.4 | async-start | bytes 262144 | tf_op jit(solution)/shard_map/all_to_all | solution.py:636
  104.7 2.8 %collective-permute-start.5 = (bf16[2,128,192]{2,1,0:T(8,128)(2,1)S(1)}, bf16[2,128,192]{2,1,0:T(8,128)(2,1)S(1)}, u32[]{:S(2)}, u32[]{:S(2)}) collective-permute-start(bf16[2,128,192]{2,1,0:T(8,128)(2,1)S(1)} %pad_maximum_fusion.1), channel_id=1, source_target_pairs={{0,6},{1,7},{2,4},{3,5},{4,2},{5,3},{6,0},{7,1},{8,14},{9,15},{10,... | collective-permute-start | bytes 294920 | tf_op jit(solution)/shard_map/ppermute | solution.py:640
  107.5 3.2 %collective-permute-start.4 = (bf16[2,128,192]{2,1,0:T(8,128)(2,1)S(1)}, bf16[2,128,192]{2,1,0:T(8,128)(2,1)S(1)}, u32[]{:S(2)}, u32[]{:S(2)}) collective-permute-start(bf16[2,128,192]{2,1,0:T(8,128)(2,1)S(1)} %pad_maximum_fusion.1), channel_id=1, source_target_pairs={{0,4},{1,5},{2,6},{3,7},{4,0},{5,1},{6,2},{7,3},{8,12},{9,13},{10,... | collective-permute-start | bytes 294920 | tf_op jit(solution)/shard_map/ppermute | solution.py:640
  110.7 3.8 %collective-permute-start.3 = (bf16[2,128,192]{2,1,0:T(8,128)(2,1)S(1)}, bf16[2,128,192]{2,1,0:T(8,128)(2,1)S(1)}, u32[]{:S(2)}, u32[]{:S(2)}) collective-permute-start(bf16[2,128,192]{2,1,0:T(8,128)(2,1)S(1)} %pad_maximum_fusion.1), channel_id=1, source_target_pairs={{0,2},{1,3},{2,0},{3,1},{4,6},{5,7},{6,4},{7,5},{8,10},{9,11},{10,... | collective-permute-start | bytes 294920 | tf_op jit(solution)/shard_map/ppermute | solution.py:640
  114.6 2.1 %collective-permute-done.4 = bf16[2,128,192]{2,1,0:T(8,128)(2,1)S(1)} collective-permute-done((bf16[2,128,192]{2,1,0:T(8,128)(2,1)S(1)}, bf16[2,128,192]{2,1,0:T(8,128)(2,1)S(1)}, u32[]{:S(2)}, u32[]{:S(2)}) %collective-permute-start.4) | collective-permute-done | bytes 98336 | tf_op jit(solution)/shard_map/ppermute | solution.py:640
  116.7 2.0 %collective-permute-done.3 = bf16[2,128,192]{2,1,0:T(8,128)(2,1)S(1)} collective-permute-done((bf16[2,128,192]{2,1,0:T(8,128)(2,1)S(1)}, bf16[2,128,192]{2,1,0:T(8,128)(2,1)S(1)}, u32[]{:S(2)}, u32[]{:S(2)}) %collective-permute-start.3) | collective-permute-done | bytes 98336 | tf_op jit(solution)/shard_map/ppermute | solution.py:640
  118.7 1.0 pad_maximum_fusion.blocks_ref
  122.1 6.9 %shard_map.219 = (bf16[128,192]{1,0:T(8,128)(2,1)S(1)}, bf16[1024,128]{1,0:T(8,128)(2,1)}) custom-call(s32[1]{0:T(128)} %bitcast.me_ref, f32[18,24,192]{2,1,0:T(8,128)S(1)} %get-tuple-element.60.pad_ref, bf16[864,128]{1,0:T(8,128)(2,1)S(1)} %get-tuple-element.67.shifts_ref, f32[16,192]{1,0:T(8,128)S(1)} %concatenate.19.cw_ref.vec_ref, ...), custom_call_target="tpu_custom_call" | custom-call | flops 100000000 | bytes 1000000 | tf_op jit(solution)/shard_map/pallas_call | solution.py:609
  129.7 10.9 %all-to-all-start.5 = ((bf16[64,16,128]{2,1,0:T(8,128)(2,1)}), bf16[64,16,128]{2,1,0:T(8,128)(2,1)S(1)}, u32[]{:S(2)}, u32[]{:S(2)}) async-start(bf16[64,16,128]{2,1,0:T(8,128)(2,1)} %bitcast.21), calls=%async_computation.5 | async-start | bytes 524288 | tf_op jit(solution)/shard_map/all_to_all | solution.py:636
  140.6 4.3 %collective-permute-start.7 = (bf16[8,192]{1,0:T(8,128)(2,1)S(1)}, bf16[8,192]{1,0:T(8,128)(2,1)S(1)}, u32[]{:S(2)}, u32[]{:S(2)}) collective-permute-start(bf16[8,192]{1,0:T(8,128)(2,1)S(1)} %get-tuple-element.98), channel_id=1, source_target_pairs={{8,0},{16,8},{24,16},{32,24},{40,32},{48,40},{56,48},{64,56},{72,6... | collective-permute-start | bytes 9224 | tf_op jit(solution)/shard_map/ppermute | solution.py:624
  144.9 1.9 collective-permute-start.6
  146.8 5.2 %all-to-all-done.5.x_ref = bf16[64,16,128]{2,1,0:T(8,128)(2,1)S(1)} async-done(((bf16[64,16,128]{2,1,0:T(8,128)(2,1)}), bf16[64,16,128]{2,1,0:T(8,128)(2,1)S(1)}, u32[]{:S(2)}, u32[]{:S(2)}) %all-to-all-start.5) | async-done | bytes 262176 | tf_op jit(solution)/shard_map/all_to_all | solution.py:636
  152.7 8.0 %all-to-all-start.6 = ((f32[8,16,128]{2,1,0:T(8,128)}), f32[8,16,128]{2,1,0:T(8,128)S(1)}, u32[]{:S(2)}, u32[]{:S(2)}) async-start(f32[8,16,128]{2,1,0:T(8,128)} %shard_map.221), calls=%async_computation.6 | async-start | bytes 131072 | tf_op jit(solution)/shard_map/all_to_all | solution.py:636
  160.8 5.0 %all-to-all-done.6.x_ref = f32[8,16,128]{2,1,0:T(8,128)S(1)} async-done(((f32[8,16,128]{2,1,0:T(8,128)}), f32[8,16,128]{2,1,0:T(8,128)S(1)}, u32[]{:S(2)}, u32[]{:S(2)}) %all-to-all-start.6) | async-done | bytes 65568 | tf_op jit(solution)/shard_map/all_to_all | solution.py:636
  166.6 6.3 %all-to-all-start.7 = ((bf16[64,16,128]{2,1,0:T(8,128)(2,1)}), bf16[64,16,128]{2,1,0:T(8,128)(2,1)S(1)}, u32[]{:S(2)}, u32[]{:S(2)}) async-start(bf16[64,16,128]{2,1,0:T(8,128)(2,1)} %shard_map.222), calls=%async_computation.7 | async-start | bytes 524288 | tf_op jit(solution)/shard_map/all_to_all | solution.py:636
  173.0 7.2 %collective-permute-start.8 = (bf16[18,192]{1,0:T(8,128)(2,1)S(1)}, bf16[18,192]{1,0:T(8,128)(2,1)S(1)}, u32[]{:S(2)}, u32[]{:S(2)}) collective-permute-start(bf16[18,192]{1,0:T(8,128)(2,1)S(1)} %pad_maximum_fusion.4), channel_id=1, source_target_pairs={{0,1},{1,2},{2,3},{3,4},{4,5},{5,6},{6,7},{8,9},{9,10},{10,11},{11... | collective-permute-start | bytes 20744 | tf_op jit(solution)/shard_map/ppermute | solution.py:624
  180.2 2.6 %collective-permute-start.9 = (bf16[18,192]{1,0:T(8,128)(2,1)S(1)}, bf16[18,192]{1,0:T(8,128)(2,1)S(1)}, u32[]{:S(2)}, u32[]{:S(2)}) collective-permute-start(bf16[18,192]{1,0:T(8,128)(2,1)S(1)} %pad_maximum_fusion.5), channel_id=1, source_target_pairs={{1,0},{2,1},{3,2},{4,3},{5,4},{6,5},{7,6},{9,8},{10,9},{11,10},{12... | collective-permute-start | bytes 20744 | tf_op jit(solution)/shard_map/ppermute | solution.py:624
  183.6 7.0 %collective-permute-done.9.right_ref = bf16[18,192]{1,0:T(8,128)(2,1)S(1)} collective-permute-done((bf16[18,192]{1,0:T(8,128)(2,1)S(1)}, bf16[18,192]{1,0:T(8,128)(2,1)S(1)}, u32[]{:S(2)}, u32[]{:S(2)}) %collective-permute-start.9) | collective-permute-done | bytes 6944 | tf_op jit(solution)/shard_map/ppermute | solution.py:624
  (109 shorter events, 16.9 us)
Async XLA Ops:
  0.6 14.9 %copy-start.19 = (bf16[4,192,35]{1,0,2:T(4,128)(2,1)S(1)}, bf16[4,192,35]{1,0,2:T(4,128)(2,1)}, u32[]{:S(2)}) copy-start(bf16[4,192,35]{1,0,2:T(4,128)(2,1)} %param.16) | copy-start | bytes 161284
  1.5 14.0 %collective-permute-start.1 = (bf16[8,96]{1,0:T(8,128)(2,1)S(1)}, bf16[8,96]{1,0:T(8,128)(2,1)S(1)}, u32[]{:S(2)}, u32[]{:S(2)}) collective-permute-start(bf16[8,96]{1,0:T(8,128)(2,1)S(1)} %slice.54), channel_id=1, source_target_pairs={{8,0},{16,8},{24,16},{32,24},{40,32},{48,40},{56,48},{64,56},{72,6... | collective-permute-start | bytes 4616 | tf_op jit(solution)/shard_map/ppermute | solution.py:624
  12.8 7.0 %collective-permute-start = (bf16[8,96]{1,0:T(8,128)(2,1)S(1)}, bf16[8,96]{1,0:T(8,128)(2,1)S(1)}, u32[]{:S(2)}, u32[]{:S(2)}) collective-permute-start(bf16[8,96]{1,0:T(8,128)(2,1)S(1)} %slice.52), channel_id=1, source_target_pairs={{0,8},{8,16},{16,24},{24,32},{32,40},{40,48},{48,56},{56,64},{64,7... | collective-permute-start | bytes 4616 | tf_op jit(solution)/shard_map/ppermute | solution.py:624
  20.5 16.0 %all-to-all-start = ((bf16[8,144,96]{2,1,0:T(8,128)(2,1)}), bf16[8,144,96]{2,1,0:T(8,128)(2,1)S(1)}, u32[]{:S(2)}, u32[]{:S(2)}) async-start(bf16[8,144,96]{2,1,0:T(8,128)(2,1)} %broadcast_in_dim.9), calls=%async_computation | async-start | bytes 589824 | tf_op jit(solution)/shard_map/all_to_all | solution.py:636
  31.1 31.0 %copy-start.13 = (f32[1,128]{1,0:T(1,128)}, f32[1,128]{1,0:T(1,128)S(1)}, u32[]{:S(2)}) copy-start(f32[1,128]{1,0:T(1,128)S(1)} %pad.12.sb_ref) | copy-start | bytes 1540
  31.1 30.9 %copy-start.15 = (f32[1,128]{1,0:T(1,128)}, f32[1,128]{1,0:T(1,128)S(1)}, u32[]{:S(2)}) copy-start(f32[1,128]{1,0:T(1,128)S(1)} %pad.13.ld_ref) | copy-start | bytes 1540
  32.3 0.9 copy-start.18
  33.3 28.8 %copy-start = (bf16[96,192]{1,0:T(8,128)(2,1)}, bf16[96,192]{1,0:T(8,128)(2,1)S(1)}, u32[]{:S(2)}) copy-start(bf16[96,192]{1,0:T(8,128)(2,1)S(1)} %get-tuple-element.95.wbr_ref) | copy-start | bytes 110596
  38.6 15.4 %copy-start.2 = (f32[128,192]{1,0:T(8,128)}, f32[128,192]{1,0:T(8,128)S(1)}, u32[]{:S(2)}) copy-start(f32[128,192]{1,0:T(8,128)S(1)} %get-tuple-element.68.before_ref) | copy-start | bytes 294916
  54.9 6.3 %copy-start.20 = (bf16[16,768]{1,0:T(8,128)(2,1)S(1)}, bf16[16,768]{1,0:T(8,128)(2,1)}, u32[]{:S(2)}) copy-start(bf16[16,768]{1,0:T(8,128)(2,1)} %param.23) | copy-start | bytes 73732
  54.9 15.2 %all-to-all-start.2 = ((bf16[64,8,128]{2,1,0:T(8,128)(2,1)}), bf16[64,8,128]{2,1,0:T(8,128)(2,1)S(1)}, u32[]{:S(2)}, u32[]{:S(2)}) async-start(bf16[64,8,128]{2,1,0:T(8,128)(2,1)} %bitcast.10), calls=%async_computation.2 | async-start | bytes 262144 | tf_op jit(solution)/shard_map/all_to_all | solution.py:636
  62.1 7.9 %copy-start.8 = (bf16[192,96]{1,0:T(8,128)(2,1)S(1)}, bf16[192,96]{1,0:T(8,128)(2,1)}, u32[]{:S(2)}) copy-start(bf16[192,96]{1,0:T(8,128)(2,1)} %ow_ref.1) | copy-start | bytes 110596
  72.5 17.1 %copy-start.6 = (bf16[128,192]{1,0:T(8,128)(2,1)}, bf16[128,192]{1,0:T(8,128)(2,1)S(1)}, u32[]{:S(2)}) copy-start(bf16[128,192]{1,0:T(8,128)(2,1)S(1)} %get-tuple-element.63.dgate_ref) | copy-start | bytes 147460
  73.1 20.0 %all-to-all-start.3 = ((bf16[64,8,128]{2,1,0:T(8,128)(2,1)}), bf16[64,8,128]{2,1,0:T(8,128)(2,1)S(1)}, u32[]{:S(2)}, u32[]{:S(2)}) async-start(bf16[64,8,128]{2,1,0:T(8,128)(2,1)} %bitcast.12), calls=%async_computation.3 | async-start | bytes 262144 | tf_op jit(solution)/shard_map/all_to_all | solution.py:636
  82.0 11.0 %collective-permute-start.2 = (bf16[128,192]{1,0:T(8,128)(2,1)S(1)}, bf16[128,192]{1,0:T(8,128)(2,1)S(1)}, u32[]{:S(2)}, u32[]{:S(2)}) collective-permute-start(bf16[128,192]{1,0:T(8,128)(2,1)S(1)} %get-tuple-element.62.g_ref), channel_id=1, source_target_pairs={{0,1},{1,0},{2,3},{3,2},{4,5},{5,4},{6,7},{7,6},{8,9},{9,8},{10,11... | collective-permute-start | bytes 147464 | tf_op jit(solution)/shard_map/ppermute | solution.py:640
  93.1 23.6 %copy-start.17 = (bf16[2,128,192]{2,1,0:T(8,128)(2,1)}, bf16[2,128,192]{2,1,0:T(8,128)(2,1)S(1)}, u32[]{:S(2)}) copy-start(bf16[2,128,192]{2,1,0:T(8,128)(2,1)S(1)} %pad_maximum_fusion.1) | copy-start | bytes 294916
  94.0 25.7 %all-to-all-start.4 = ((bf16[64,8,128]{2,1,0:T(8,128)(2,1)}), bf16[64,8,128]{2,1,0:T(8,128)(2,1)S(1)}, u32[]{:S(2)}, u32[]{:S(2)}) async-start(bf16[64,8,128]{2,1,0:T(8,128)(2,1)} %bitcast.16), calls=%async_computation.4 | async-start | bytes 262144 | tf_op jit(solution)/shard_map/all_to_all | solution.py:636
  104.7 9.8 %collective-permute-start.5 = (bf16[2,128,192]{2,1,0:T(8,128)(2,1)S(1)}, bf16[2,128,192]{2,1,0:T(8,128)(2,1)S(1)}, u32[]{:S(2)}, u32[]{:S(2)}) collective-permute-start(bf16[2,128,192]{2,1,0:T(8,128)(2,1)S(1)} %pad_maximum_fusion.1), channel_id=1, source_target_pairs={{0,6},{1,7},{2,4},{3,5},{4,2},{5,3},{6,0},{7,1},{8,14},{9,15},{10,... | collective-permute-start | bytes 294920 | tf_op jit(solution)/shard_map/ppermute | solution.py:640
  107.5 9.2 %collective-permute-start.4 = (bf16[2,128,192]{2,1,0:T(8,128)(2,1)S(1)}, bf16[2,128,192]{2,1,0:T(8,128)(2,1)S(1)}, u32[]{:S(2)}, u32[]{:S(2)}) collective-permute-start(bf16[2,128,192]{2,1,0:T(8,128)(2,1)S(1)} %pad_maximum_fusion.1), channel_id=1, source_target_pairs={{0,4},{1,5},{2,6},{3,7},{4,0},{5,1},{6,2},{7,3},{8,12},{9,13},{10,... | collective-permute-start | bytes 294920 | tf_op jit(solution)/shard_map/ppermute | solution.py:640
  110.7 7.9 %collective-permute-start.3 = (bf16[2,128,192]{2,1,0:T(8,128)(2,1)S(1)}, bf16[2,128,192]{2,1,0:T(8,128)(2,1)S(1)}, u32[]{:S(2)}, u32[]{:S(2)}) collective-permute-start(bf16[2,128,192]{2,1,0:T(8,128)(2,1)S(1)} %pad_maximum_fusion.1), channel_id=1, source_target_pairs={{0,2},{1,3},{2,0},{3,1},{4,6},{5,7},{6,4},{7,5},{8,10},{9,11},{10,... | collective-permute-start | bytes 294920 | tf_op jit(solution)/shard_map/ppermute | solution.py:640
  120.4 0.9 copy-start.3
  129.7 10.9 %copy-start.12 = (bf16[128,192]{1,0:T(8,128)(2,1)S(1)}, bf16[128,192]{1,0:T(8,128)(2,1)}, u32[]{:S(2)}) copy-start(bf16[128,192]{1,0:T(8,128)(2,1)} %copy-done.11) | copy-start | bytes 147460
  129.7 22.3 %all-to-all-start.5 = ((bf16[64,16,128]{2,1,0:T(8,128)(2,1)}), bf16[64,16,128]{2,1,0:T(8,128)(2,1)S(1)}, u32[]{:S(2)}, u32[]{:S(2)}) async-start(bf16[64,16,128]{2,1,0:T(8,128)(2,1)} %bitcast.21), calls=%async_computation.5 | async-start | bytes 524288 | tf_op jit(solution)/shard_map/all_to_all | solution.py:636
  140.6 32.3 %collective-permute-start.7 = (bf16[8,192]{1,0:T(8,128)(2,1)S(1)}, bf16[8,192]{1,0:T(8,128)(2,1)S(1)}, u32[]{:S(2)}, u32[]{:S(2)}) collective-permute-start(bf16[8,192]{1,0:T(8,128)(2,1)S(1)} %get-tuple-element.98), channel_id=1, source_target_pairs={{8,0},{16,8},{24,16},{32,24},{40,32},{48,40},{56,48},{64,56},{72,6... | collective-permute-start | bytes 9224 | tf_op jit(solution)/shard_map/ppermute | solution.py:624
  144.9 28.0 %collective-permute-start.6 = (bf16[8,192]{1,0:T(8,128)(2,1)S(1)}, bf16[8,192]{1,0:T(8,128)(2,1)S(1)}, u32[]{:S(2)}, u32[]{:S(2)}) collective-permute-start(bf16[8,192]{1,0:T(8,128)(2,1)S(1)} %get-tuple-element.99), channel_id=1, source_target_pairs={{0,8},{8,16},{16,24},{24,32},{32,40},{40,48},{48,56},{56,64},{64,7... | collective-permute-start | bytes 9224 | tf_op jit(solution)/shard_map/ppermute | solution.py:624
  152.7 13.1 %all-to-all-start.6 = ((f32[8,16,128]{2,1,0:T(8,128)}), f32[8,16,128]{2,1,0:T(8,128)S(1)}, u32[]{:S(2)}, u32[]{:S(2)}) async-start(f32[8,16,128]{2,1,0:T(8,128)} %shard_map.221), calls=%async_computation.6 | async-start | bytes 131072 | tf_op jit(solution)/shard_map/all_to_all | solution.py:636
  166.6 16.3 %copy-start.10 = (bf16[128,96]{1,0:T(8,128)(2,1)S(1)}, bf16[128,96]{1,0:T(8,128)(2,1)}, u32[]{:S(2)}) copy-start(bf16[128,96]{1,0:T(8,128)(2,1)} %copy-done.9) | copy-start | bytes 73732
  166.6 25.2 %all-to-all-start.7 = ((bf16[64,16,128]{2,1,0:T(8,128)(2,1)}), bf16[64,16,128]{2,1,0:T(8,128)(2,1)S(1)}, u32[]{:S(2)}, u32[]{:S(2)}) async-start(bf16[64,16,128]{2,1,0:T(8,128)(2,1)} %shard_map.222), calls=%async_computation.7 | async-start | bytes 524288 | tf_op jit(solution)/shard_map/all_to_all | solution.py:636
  172.9 17.8 %copy-start.7 = (bf16[128,192]{1,0:T(8,128)(2,1)S(1)}, bf16[128,192]{1,0:T(8,128)(2,1)}, u32[]{:S(2)}) copy-start(bf16[128,192]{1,0:T(8,128)(2,1)} %copy-done.6) | copy-start | bytes 147460
  173.0 17.7 %copy-start.1 = (bf16[96,192]{1,0:T(8,128)(2,1)S(1)}, bf16[96,192]{1,0:T(8,128)(2,1)}, u32[]{:S(2)}) copy-start(bf16[96,192]{1,0:T(8,128)(2,1)} %copy-done) | copy-start | bytes 110596
  173.0 10.6 %collective-permute-start.8 = (bf16[18,192]{1,0:T(8,128)(2,1)S(1)}, bf16[18,192]{1,0:T(8,128)(2,1)S(1)}, u32[]{:S(2)}, u32[]{:S(2)}) collective-permute-start(bf16[18,192]{1,0:T(8,128)(2,1)S(1)} %pad_maximum_fusion.4), channel_id=1, source_target_pairs={{0,1},{1,2},{2,3},{3,4},{4,5},{5,6},{6,7},{8,9},{9,10},{10,11},{11... | collective-permute-start | bytes 20744 | tf_op jit(solution)/shard_map/ppermute | solution.py:624
  180.2 10.4 %collective-permute-start.9 = (bf16[18,192]{1,0:T(8,128)(2,1)S(1)}, bf16[18,192]{1,0:T(8,128)(2,1)S(1)}, u32[]{:S(2)}, u32[]{:S(2)}) collective-permute-start(bf16[18,192]{1,0:T(8,128)(2,1)S(1)} %pad_maximum_fusion.5), channel_id=1, source_target_pairs={{1,0},{2,1},{3,2},{4,3},{5,4},{6,5},{7,6},{9,8},{10,9},{11,10},{12... | collective-permute-start | bytes 20744 | tf_op jit(solution)/shard_map/ppermute | solution.py:624
  (13 other events, 9.2 us)

commit v7 on v6

--- a/solution.py
+++ b/solution.py
@@ -19,6 +19,8 @@
 GAIN = slice(10, 11)
 SHIFT = slice(11, 12)
 SKIP = slice(12, 13)
+STEP_BIAS = slice(13, 14)
+RATE = slice(14, 15)
 
 F32 = jnp.float32
 BF = jnp.bfloat16
@@ -213,8 +215,8 @@
 
 
 def first_kernel(
-    me_ref, got_ref, wbr_ref, cw_ref, wd_ref, wbc_ref, sb_ref, ld_ref,
-    before_ref, act_ref, rawd_ref, bc_ref, step_ref, log_ref, tot_ref, mv_ref, pad_ref, wide_ref,
+    me_ref, got_ref, wbr_ref, cw_ref, wd_ref, wbc_ref,
+    act_ref, bc_ref, step_ref, log_ref, tot_ref, mv_ref, pad_ref, wide_ref,
 ):
     fill_blocks(me_ref[0], got_ref, pad_ref, as_branch(wbr_ref))
     total = jnp.zeros((R, C, DI), F32)
@@ -224,16 +226,14 @@
             total = total + cw_ref[3 * a + b : 3 * a + b + 1, :] * shifted[a : a + R]
     before = total.reshape(T, DI) + cw_ref[BIAS, :]
     act = (before * sigmoid(before)).astype(BF)
-    before_ref[...] = before
     act_ref[...] = act
     raw_d = dot(act, wd_ref[...])
     bc = dot(act, wbc_ref[...])
-    step = softplus(raw_d + sb_ref[...])
-    log_step = step * -jnp.exp(ld_ref[...])
+    step = softplus(raw_d + cw_ref[STEP_BIAS, :T])
+    log_step = step * -jnp.exp(cw_ref[RATE, :T])
     log = pick_lanes([fine(ones(mask(k)), log_step) for k in range(4)])
     rows, cols = (fine(ones(same_line(v)), log_step) for v in (False, True))
     tot = pick_lanes([rows, rows, cols, cols])
-    rawd_ref[...] = raw_d
     bc_ref[...] = bc
     step_ref[...] = step
     log_ref[...] = log
@@ -256,7 +256,7 @@
 
 
 def row_scan_kernel(
-    me_ref, got_ref, wbr_ref, cw_ref, wd_ref, wbc_ref, sb_ref, ld_ref,
+    me_ref, got_ref, wbr_ref, cw_ref, wd_ref, wbc_ref,
     s0_ref, s1_ref, later_ref, pad_ref,
 ):
     nothing = jnp.zeros((R + 2, 8, DI), F32)
@@ -283,7 +283,7 @@
     tj, j = (iota((T, 32), 0), iota((T, 32), 1))
     line = (tj >> 6) == (j >> 4)
     i, ji = (iota((T, 32), 0), iota((T, 32), 1))
-    rate = -jnp.exp(ld_ref[...])
+    rate = -jnp.exp(cw_ref[RATE, :T])
     for group in range(R // 2):
         total = jnp.zeros((2, 64, DI), F32)
         for b in range(3):
@@ -293,7 +293,7 @@
         wide = total.reshape(T, DI) + cw_ref[BIAS, :]
         act = (wide * sigmoid(wide)).astype(BF)
         wide = act.astype(F32)
-        step = softplus(dot(act, wd_ref[...]) + sb_ref[...])
+        step = softplus(dot(act, wd_ref[...]) + cw_ref[STEP_BIAS, :T])
         bc = dot(act, wbc_ref[...])
         x = fine(reach, step * rate)
         w_in = jnp.exp(jnp.where(first, x[:T], x[T : 2 * T])) * step * valid_in
@@ -462,12 +462,13 @@
 
 
 def last_kernel(
-    me_ref, pad_ref, shifts_ref, vec_ref, before_ref, act_ref, rawd_ref, bc_ref, step_ref, log_ref, tot_ref, g_ref,
-    sv_ref, s0_ref, s1_ref, lv_ref, blocks_ref, later_ref, back_ref, wd_ref,
-    wbc_ref,
-    sb_ref, ld_ref, side_ref, norms_ref,
-    gb_ref, pack_ref, early_ref, late_ref, l0_ref, l1_ref,
-):
+    me_ref, pad_ref, shifts_ref, vec_ref, act_ref, bc_ref, step_ref, log_ref, tot_ref, g_ref,
+    sv_ref, s0_ref, s1_ref, lv_ref, p0_ref, p1_ref, p2_ref, p3_ref, later_ref, back_ref, wd_ref,
+    wbc_ref, side_ref, norms_ref,
+    gb_ref, pack_ref, early_ref, late_ref, l0_ref, l1_ref, blocks_ref,
+):
+    for i, pair_ref in enumerate((p0_ref, p1_ref, p2_ref, p3_ref)):
+        blocks_ref[2 * i : 2 * i + 2] = pair_ref[...]
     row_back(me_ref[0], blocks_ref, later_ref, (l0_ref, l1_ref))
     open_message(sv_ref, early_ref)
     open_message(lv_ref, late_ref)
@@ -501,29 +502,30 @@
         rest = same_line(k >= 2) & jnp.logical_not(after)
         parts.append(fine(ones(after), d_log) + fine(ones(rest), left))
     d_log_step = pick_lanes(parts) + cross * through
-    rate = -jnp.exp(ld_ref[...])
+    rate = -jnp.exp(vec_ref[RATE, :T])
     d_rate = jnp.sum(d_log_step * step, axis=0, keepdims=True) * rate
-    d_raw = (d_step + rate * d_log_step) * sigmoid(rawd_ref[...] + sb_ref[...])
+    small = step * (1.0 - 0.5 * step + step * step / 6.0)
+    d_raw = (d_step + rate * d_log_step) * jnp.where(step < 0.01, small, 1.0 - jnp.exp(-step))
     live = iota((T, T), 1) < 12
     d_raw = jnp.where(live, d_raw, 0.0)
     d_bias = jnp.sum(d_raw, axis=0, keepdims=True)
     d_raw = d_raw.astype(BF)
     d_bc = d_bc.astype(BF)
     d_act = d_act + dot(d_raw, wd_ref[...], 1, 1) + dot(d_bc, wbc_ref[...], 1, 1)
-    before = before_ref[...]
+    near = [pad_ref[:, 7 + b : 7 + b + C, :] for b in range(3)]
+    near = [near[i % 3][i // 3 : i // 3 + R].reshape(T, DI) for i in range(9)]
+    before = jnp.zeros((T, DI), F32) + vec_ref[BIAS, :]
+    for i in range(9):
+        before = before + vec_ref[i : i + 1, :] * near[i]
     sig = sigmoid(before)
     gb = (d_act * sig * (1.0 + before * (1.0 - sig))).astype(BF)
     gb_ref[...] = gb
     gbw = gb.astype(F32)
     product = dot(shifts_ref[...], gb)
     gin = jnp.zeros((D, DI), F32)
-    conv_rows = [None] * 9
-    for b in range(3):
-        near = pad_ref[:, 7 + b : 7 + b + C, :]
-        for a in range(3):
-            i = 3 * a + b
-            conv_rows[i] = jnp.sum(gbw * near[a : a + R].reshape(T, DI), axis=0, keepdims=True)
-            gin = gin + vec_ref[i : i + 1, :] * product[D * i : D * i + D]
+    conv_rows = [jnp.sum(gbw * near[i], axis=0, keepdims=True) for i in range(9)]
+    for i in range(9):
+        gin = gin + vec_ref[i : i + 1, :] * product[D * i : D * i + D]
     wide_row = lambda x: jnp.concatenate([x, jnp.zeros((1, DI - T), F32)], axis=1)
     small = jnp.concatenate(
         conv_rows
@@ -645,8 +647,7 @@
 
 
 def along_col(pair):
-    others = [swapped(pair, step) for step in range(2, lax.axis_size("col"), 2)]
-    return jnp.concatenate([pair] + others, axis=0)
+    return [pair] + [swapped(pair, step) for step in range(2, lax.axis_size("col"), 2)]
 
 
 def exchange(message, axis, backward, meanwhile=()):
@@ -658,14 +659,15 @@
     return all_to_all(states.reshape(chunks), axis).reshape(512, 128), meanwhile
 
 
-def reduced(pack, scale):
+def reduced(pack, scale, later):
     rows, cols = (lax.axis_size("row"), lax.axis_size("col"))
     chunk = pack.shape[0] // rows
     got = all_to_all(pack.reshape(rows, chunk, 128), "row")
     (part,) = call(partial(sum_kernel, 1.0), [((cols, chunk, 128), F32)], got, flops=10**7)
+    part, later = lax.optimization_barrier((part, later))
     got = all_to_all(part, "col")
     (part,) = call(partial(sum_kernel, scale), [((rows, chunk, 128), BF)], got, flops=10**7)
-    return all_to_all(part, "row").reshape(pack.shape)
+    return all_to_all(part, "row").reshape(pack.shape), later
 
 
 def local(
@@ -689,12 +691,12 @@
         axis=1,
     )
     row = lambda x: x.reshape(1, -1)
-    bias = jnp.pad(row(step_bias), ((0, 0), (0, 116)))
-    rate = jnp.pad(row(log_decay), ((0, 0), (0, 116)))
+    bias = jnp.pad(row(step_bias), ((0, 0), (0, DI - 12)))
+    rate = jnp.pad(row(log_decay), ((0, 0), (0, DI - 12)))
     vec = jnp.concatenate(
         [
             conv_weight.reshape(9, DI), row(conv_bias), row(norm_gain), row(norm_bias),
-            jnp.sum(skip_gain, axis=0, keepdims=True), jnp.zeros((3, DI), F32),
+            jnp.sum(skip_gain, axis=0, keepdims=True), bias, rate, jnp.zeros((1, DI), F32),
         ],
         axis=0,
     )
@@ -706,15 +708,15 @@
     states = ((256, DI), F32)
     long = ((8 * T, T), F32)
 
-    before, act, raw_d, bc, step, log, tot, mv, padded = call(
+    act, bc, step, log, tot, mv, padded = call(
         first_kernel,
-        [wide, low, square, square, square, square, square, message, ((R + 2, PITCH, DI), F32)],
-        place, got, w_branch, vec, w_step, w_bc, bias, rate, scratch=[opened], scalars=1,
+        [low, square, square, square, square, message, ((R + 2, PITCH, DI), F32)],
+        place, got, w_branch, vec, w_step, w_bc, scratch=[opened], scalars=1,
     )
     sv, _ = exchange(mv, "row", False)
     s0, s1, later = call(
         row_scan_kernel, [states, states, long],
-        place, got, w_branch, vec, w_step, w_bc, bias, rate,
+        place, got, w_branch, vec, w_step, w_bc,
         scratch=[pltpu.VMEM((R + 2, 80, DI), F32)], scalars=1, flops=10**9,
     )
     (y,) = call(local_kernel, [wide], act, bc, step, log)
@@ -736,13 +738,14 @@
     lv, blocks = lax.optimization_barrier((lv, along_col(pair)))
     gb, pack = call(
         last_kernel, [low, ((1024, 128), BF)],
-        place, padded, shifts, vec, before, act, raw_d, bc, step, log, tot, g, sv, s0, s1, lv, blocks, later,
-        *back, w_step, w_bc, bias, rate, side, norms,
-        scratch=[opened, opened, pltpu.VMEM((256, DI), F32), pltpu.VMEM((256, DI), F32)],
+        place, padded, shifts, vec, act, bc, step, log, tot, g, sv, s0, s1, lv, *blocks, later,
+        *back, w_step, w_bc, side, norms,
+        scratch=[opened, opened, pltpu.VMEM((256, DI), F32), pltpu.VMEM((256, DI), F32)]
+        + [pltpu.VMEM((8, T, DI), BF)],
         scalars=1,
     )
     scale = float(T * lax.axis_size("row") * lax.axis_size("col")) ** (-0.5)
-    total = reduced(pack, scale)
+    total, gb = reduced(pack, scale, gb)
     rim = with_rim(gb)
     (d_tokens,) = call(
         out_kernel, [((T, D), BF)], *rim, vec, d_gate, w_branch, w_gate,

time: 194 us -> 190 us (0.979)
  blocking collectives: 15.4 us -> 37.4 us
  starting transfers between devices: 107 us -> 95.6 us
  waiting for transfers between devices: 30.6 us -> 20 us
  local copies, waits for them, and re-layouts: 11.3 us -> 9.17 us
    all_to_all x1 -> x2, blocking collectives: 15.4 us -> 37.4 us  [all_to_all(): return lax.all_to_all(x, axis, 0, 0, tiled=True)]
    all_to_all x7 -> x6, starting transfers between devices: 60.8 us -> 51.2 us  [all_to_all(): return lax.all_to_all(x, axis, 0, 0, tiled=True)]
    all_to_all x7 -> x6, waiting for transfers between devices: 15.3 us -> 5.8 us  [all_to_all(): return lax.all_to_all(x, axis, 0, 0, tiled=True)]
    unnamed x59 -> x41, local copies, waits for them, and re-layouts: 6.43 us -> 4.32 us
    ppermute x6, starting transfers between devices: 29.2 us -> 27.1 us  [neighbours(): return (lax.ppermute(last, axis, up), lax.ppermute(first, axis, down))]
  transfers between devices with their start and end apart: 17 -> 16, of which waited for: 8 -> 7; matrix products, arithmetic and copies ran while one was open for 2% -> 2% of each run, Pallas kernels for 6% -> 6%
where the time goes in v7:
time: 190 us; the launch traced here: 189 us
  starting transfers between devices  95.6 us (50%)
  blocking collectives  37.4 us (20%)
  Pallas kernels  25 us (13%)
  waiting for transfers between devices  20 us (11%)
  local copies, waits for them, and re-layouts  9.17 us (5%)
    all_to_all x6, starting transfers between devices, all_to_all(): return lax.all_to_all(x, axis, 0, 0, tiled=True)  51.2 us
    all_to_all x2, blocking collectives, all_to_all(): return lax.all_to_all(x, axis, 0, 0, tiled=True)  37.4 us
    ppermute x6, starting transfers between devices, neighbours(): return (lax.ppermute(last, axis, up), lax.ppermute(first, axis, down))  27.1 us
    pallas_call x13, Pallas kernels, call(): pl.pallas_call(kernel, out_shape=[jax.ShapeDtypeStruct(s, t) for s, t in...  25 us
    ppermute x4, starting transfers between devices, swapped(): lax.ppermute(x, 'col', [(i, i ^ step) for i in range(lax.axis_size('col'))])  17.3 us
    ppermute x6, waiting for transfers between devices, neighbours(): return (lax.ppermute(last, axis, up), lax.ppermute(first, axis, down))  10.1 us
    all_to_all x6, waiting for transfers between devices, all_to_all(): return lax.all_to_all(x, axis, 0, 0, tiled=True)  5.8 us
    unnamed x41, local copies, waits for them, and re-layouts  4.32 us
  transfers between devices with their start and end apart: 16, of which 7 were waited for; matrix products, arithmetic and copies ran while one was open for 2% of the time, Pallas kernels for 6%

profile of v7, /device:TPU:56, one launch (start us, length us, event | category | flops | bytes accessed | tf_op | source)
XLA Modules:
  0.0 188.5 jit_solution(5627398357532567424)
XLA Ops:
  1.5 11.2 %collective-permute-start.1 = (bf16[8,96]{1,0:T(8,128)(2,1)S(1)}, bf16[8,96]{1,0:T(8,128)(2,1)S(1)}, u32[]{:S(2)}, u32[]{:S(2)}) collective-permute-start(bf16[8,96]{1,0:T(8,128)(2,1)S(1)} %slice.54), channel_id=1, source_target_pairs={{8,0},{16,8},{24,16},{32,24},{40,32},{48,40},{56,48},{64,56},{72,6... | collective-permute-start | bytes 4616 | tf_op jit(solution)/shard_map/ppermute | solution.py:626
  12.8 1.9 %collective-permute-start = (bf16[8,96]{1,0:T(8,128)(2,1)S(1)}, bf16[8,96]{1,0:T(8,128)(2,1)S(1)}, u32[]{:S(2)}, u32[]{:S(2)}) collective-permute-start(bf16[8,96]{1,0:T(8,128)(2,1)S(1)} %slice.52), channel_id=1, source_target_pairs={{0,8},{8,16},{16,24},{24,32},{32,40},{40,48},{48,56},{56,64},{64,7... | collective-permute-start | bytes 4616 | tf_op jit(solution)/shard_map/ppermute | solution.py:626
  15.6 4.2 %collective-permute-done = bf16[8,96]{1,0:T(8,128)(2,1)S(1)} collective-permute-done((bf16[8,96]{1,0:T(8,128)(2,1)S(1)}, bf16[8,96]{1,0:T(8,128)(2,1)S(1)}, u32[]{:S(2)}, u32[]{:S(2)}) %collective-permute-start) | collective-permute-done | bytes 1568 | tf_op jit(solution)/shard_map/ppermute | solution.py:626
  20.6 9.7 %all-to-all-start = ((bf16[8,144,96]{2,1,0:T(8,128)(2,1)}), bf16[8,144,96]{2,1,0:T(8,128)(2,1)S(1)}, u32[]{:S(2)}, u32[]{:S(2)}) async-start(bf16[8,144,96]{2,1,0:T(8,128)(2,1)} %broadcast_in_dim.9), calls=%async_computation | async-start | bytes 589824 | tf_op jit(solution)/shard_map/all_to_all | solution.py:638
  33.3 3.2 %all-to-all-done.got_ref = bf16[8,144,96]{2,1,0:T(8,128)(2,1)S(1)} async-done(((bf16[8,144,96]{2,1,0:T(8,128)(2,1)}), bf16[8,144,96]{2,1,0:T(8,128)(2,1)S(1)}, u32[]{:S(2)}, u32[]{:S(2)}) %all-to-all-start) | async-done | bytes 221216 | tf_op jit(solution)/shard_map/all_to_all | solution.py:638
  36.5 1.5 shard_map.211
  38.0 15.4 %all_to_all.40 = bf16[64,8,128]{2,1,0:T(8,128)(2,1)S(1)} all-to-all(bf16[64,8,128]{2,1,0:T(8,128)(2,1)S(1)} %bitcast.44), channel_id=1, replica_groups=mesh['row'=64,'col'=8] {'row'}, dimensions={0} | all-to-all | bytes 262144 | tf_op jit(solution)/shard_map/all_to_all | solution.py:638
  54.3 6.3 %all-to-all-start.2 = ((bf16[64,8,128]{2,1,0:T(8,128)(2,1)}), bf16[64,8,128]{2,1,0:T(8,128)(2,1)S(1)}, u32[]{:S(2)}, u32[]{:S(2)}) async-start(bf16[64,8,128]{2,1,0:T(8,128)(2,1)} %bitcast.10), calls=%async_computation.2 | async-start | bytes 262144 | tf_op jit(solution)/shard_map/all_to_all | solution.py:638
  61.5 6.1 %shard_map.214 = (f32[256,192]{1,0:T(8,128)S(1)}, f32[256,192]{1,0:T(8,128)S(1)}, f32[1024,128]{1,0:T(8,128)S(1)}) custom-call(s32[1]{0:T(128)} %bitcast.me_ref, bf16[8,144,96]{2,1,0:T(8,128)(2,1)S(1)} %all-to-all-done.got_ref, bf16[96,192]{1,0:T(8,128)(2,1)S(1)} %get-tuple-element.101.wbr_ref, f32[16,192]{1,0:T(8,128)S(1)} %concatenate.16.cw_ref.vec_ref, ...), custom_call_target="tpu_custom_call" | custom-call | flops 1000000000 | bytes 1000000 | tf_op jit(solution)/shard_map/pallas_call | solution.py:611
  67.6 1.9 all-to-all-done.2
  69.5 2.5 %shard_map.215 = (bf16[128,96]{1,0:T(8,128)(2,1)S(1)}, bf16[128,192]{1,0:T(8,128)(2,1)S(1)}, bf16[128,192]{1,0:T(8,128)(2,1)S(1)}, bf16[128,192]{1,0:T(8,128)(2,...) custom-call(f32[128,192]{1,0:T(8,128)S(1)} %shard_map.212.y_ref, bf16[128,192]{1,0:T(8,128)(2,1)S(1)} %get-tuple-element.54.act_ref, ...), custom_call_target="tpu_custom_call" | custom-call | flops 100000000 | bytes 1000000 | tf_op jit(solution)/shard_map/pallas_call | solution.py:611
  72.5 8.9 %all-to-all-start.3 = ((bf16[64,8,128]{2,1,0:T(8,128)(2,1)}), bf16[64,8,128]{2,1,0:T(8,128)(2,1)S(1)}, u32[]{:S(2)}, u32[]{:S(2)}) async-start(bf16[64,8,128]{2,1,0:T(8,128)(2,1)} %bitcast.12), calls=%async_computation.3 | async-start | bytes 262144 | tf_op jit(solution)/shard_map/all_to_all | solution.py:638
  81.4 7.5 %collective-permute-start.2 = (bf16[128,192]{1,0:T(8,128)(2,1)S(1)}, bf16[128,192]{1,0:T(8,128)(2,1)S(1)}, u32[]{:S(2)}, u32[]{:S(2)}) collective-permute-start(bf16[128,192]{1,0:T(8,128)(2,1)S(1)} %get-tuple-element.65.g_ref), channel_id=1, source_target_pairs={{0,1},{1,0},{2,3},{3,2},{4,5},{5,4},{6,7},{7,6},{8,9},{9,8},{10,11... | collective-permute-start | bytes 147464 | tf_op jit(solution)/shard_map/ppermute | solution.py:642
  89.2 3.3 %shard_map.216.back_ref = f32[128,512]{1,0:T(8,128)S(1)} custom-call(bf16[128,192]{1,0:T(8,128)(2,1)S(1)} %get-tuple-element.54.act_ref, f32[128,128]{1,0:T(8,128)S(1)} %get-tuple-element.55.bc_ref, f32[128,128]{1,0:T(8,128)S(1)} %get-tuple-element.56.step_ref, f32[128,128]{1,0:T(8,128)S(1)} %get-tuple-element.57.log_ref, ...), custom_call_target="tpu_custom_call" | custom-call | flops 100000000 | bytes 1000000 | tf_op jit(solution)/shard_map/pallas_call | solution.py:611
  92.5 0.9 shard_map.218
  93.4 10.7 %all-to-all-start.4 = ((bf16[64,8,128]{2,1,0:T(8,128)(2,1)}), bf16[64,8,128]{2,1,0:T(8,128)(2,1)S(1)}, u32[]{:S(2)}, u32[]{:S(2)}) async-start(bf16[64,8,128]{2,1,0:T(8,128)(2,1)} %bitcast.16), calls=%async_computation.4 | async-start | bytes 262144 | tf_op jit(solution)/shard_map/all_to_all | solution.py:638
  104.1 2.8 %collective-permute-start.5 = (bf16[2,128,192]{2,1,0:T(8,128)(2,1)S(1)}, bf16[2,128,192]{2,1,0:T(8,128)(2,1)S(1)}, u32[]{:S(2)}, u32[]{:S(2)}) collective-permute-start(bf16[2,128,192]{2,1,0:T(8,128)(2,1)S(1)} %pad_maximum_fusion.p0_ref), channel_id=1, source_target_pairs={{0,6},{1,7},{2,4},{3,5},{4,2},{5,3},{6,0},{7,1},{8,14},{9,15},{10,... | collective-permute-start | bytes 294920 | tf_op jit(solution)/shard_map/ppermute | solution.py:642
  106.9 3.2 %collective-permute-start.4 = (bf16[2,128,192]{2,1,0:T(8,128)(2,1)S(1)}, bf16[2,128,192]{2,1,0:T(8,128)(2,1)S(1)}, u32[]{:S(2)}, u32[]{:S(2)}) collective-permute-start(bf16[2,128,192]{2,1,0:T(8,128)(2,1)S(1)} %pad_maximum_fusion.p0_ref), channel_id=1, source_target_pairs={{0,4},{1,5},{2,6},{3,7},{4,0},{5,1},{6,2},{7,3},{8,12},{9,13},{10,... | collective-permute-start | bytes 294920 | tf_op jit(solution)/shard_map/ppermute | solution.py:642
  110.1 3.8 %collective-permute-start.3 = (bf16[2,128,192]{2,1,0:T(8,128)(2,1)S(1)}, bf16[2,128,192]{2,1,0:T(8,128)(2,1)S(1)}, u32[]{:S(2)}, u32[]{:S(2)}) collective-permute-start(bf16[2,128,192]{2,1,0:T(8,128)(2,1)S(1)} %pad_maximum_fusion.p0_ref), channel_id=1, source_target_pairs={{0,2},{1,3},{2,0},{3,1},{4,6},{5,7},{6,4},{7,5},{8,10},{9,11},{10,... | collective-permute-start | bytes 294920 | tf_op jit(solution)/shard_map/ppermute | solution.py:642
  114.0 2.1 %collective-permute-done.4.p2_ref = bf16[2,128,192]{2,1,0:T(8,128)(2,1)S(1)} collective-permute-done((bf16[2,128,192]{2,1,0:T(8,128)(2,1)S(1)}, bf16[2,128,192]{2,1,0:T(8,128)(2,1)S(1)}, u32[]{:S(2)}, u32[]{:S(2)}) %collective-permute-start.4) | collective-permute-done | bytes 98336 | tf_op jit(solution)/shard_map/ppermute | solution.py:642
  116.1 2.0 %collective-permute-done.3.p1_ref = bf16[2,128,192]{2,1,0:T(8,128)(2,1)S(1)} collective-permute-done((bf16[2,128,192]{2,1,0:T(8,128)(2,1)S(1)}, bf16[2,128,192]{2,1,0:T(8,128)(2,1)S(1)}, u32[]{:S(2)}, u32[]{:S(2)}) %collective-permute-start.3) | collective-permute-done | bytes 98336 | tf_op jit(solution)/shard_map/ppermute | solution.py:642
  118.7 0.9 copy-done.1
  119.6 6.3 %shard_map.219 = (bf16[128,192]{1,0:T(8,128)(2,1)S(1)}, bf16[1024,128]{1,0:T(8,128)(2,1)S(1)}) custom-call(s32[1]{0:T(128)} %bitcast.me_ref, f32[18,24,192]{2,1,0:T(8,128)S(1)} %get-tuple-element.63.pad_ref, bf16[864,128]{1,0:T(8,128)(2,1)S(1)} %get-tuple-element.70.shifts_ref, f32[16,192]{1,0:T(8,128)S(1)} %concatenate.16.cw_ref.vec_ref, ...), custom_call_target="tpu_custom_call" | custom-call | flops 100000000 | bytes 1000000 | tf_op jit(solution)/shard_map/pallas_call | solution.py:611
  125.9 22.0 %all_to_all.41.x_ref = bf16[64,16,128]{2,1,0:T(8,128)(2,1)S(1)} all-to-all(bf16[64,16,128]{2,1,0:T(8,128)(2,1)S(1)} %bitcast.43), channel_id=1, replica_groups=mesh['row'=64,'col'=8] {'row'}, dimensions={0} | all-to-all | bytes 524288 | tf_op jit(solution)/shard_map/all_to_all | solution.py:638
  148.6 8.1 %all-to-all-start.6 = ((f32[8,16,128]{2,1,0:T(8,128)}), f32[8,16,128]{2,1,0:T(8,128)S(1)}, u32[]{:S(2)}, u32[]{:S(2)}) async-start(f32[8,16,128]{2,1,0:T(8,128)} %shard_map.220), calls=%async_computation.6 | async-start | bytes 131072 | tf_op jit(solution)/shard_map/all_to_all | solution.py:638
  156.8 2.1 %collective-permute-start.7 = (bf16[8,192]{1,0:T(8,128)(2,1)S(1)}, bf16[8,192]{1,0:T(8,128)(2,1)S(1)}, u32[]{:S(2)}, u32[]{:S(2)}) collective-permute-start(bf16[8,192]{1,0:T(8,128)(2,1)S(1)} %get-tuple-element.104), channel_id=1, source_target_pairs={{8,0},{16,8},{24,16},{32,24},{40,32},{48,40},{56,48},{64,56},{72,6... | collective-permute-start | bytes 9224 | tf_op jit(solution)/shard_map/ppermute | solution.py:626
  158.9 2.2 %collective-permute-start.6 = (bf16[8,192]{1,0:T(8,128)(2,1)S(1)}, bf16[8,192]{1,0:T(8,128)(2,1)S(1)}, u32[]{:S(2)}, u32[]{:S(2)}) collective-permute-start(bf16[8,192]{1,0:T(8,128)(2,1)S(1)} %get-tuple-element.105), channel_id=1, source_target_pairs={{0,8},{8,16},{16,24},{24,32},{32,40},{40,48},{48,56},{56,64},{64,7... | collective-permute-start | bytes 9224 | tf_op jit(solution)/shard_map/ppermute | solution.py:626
  162.6 7.4 %all-to-all-start.7 = ((bf16[64,16,128]{2,1,0:T(8,128)(2,1)}), bf16[64,16,128]{2,1,0:T(8,128)(2,1)S(1)}, u32[]{:S(2)}, u32[]{:S(2)}) async-start(bf16[64,16,128]{2,1,0:T(8,128)(2,1)} %shard_map.222), calls=%async_computation.7 | async-start | bytes 524288 | tf_op jit(solution)/shard_map/all_to_all | solution.py:638
  170.1 6.0 %collective-permute-start.8 = (bf16[18,192]{1,0:T(8,128)(2,1)S(1)}, bf16[18,192]{1,0:T(8,128)(2,1)S(1)}, u32[]{:S(2)}, u32[]{:S(2)}) collective-permute-start(bf16[18,192]{1,0:T(8,128)(2,1)S(1)} %pad_maximum_fusion.3), channel_id=1, source_target_pairs={{0,1},{1,2},{2,3},{3,4},{4,5},{5,6},{6,7},{8,9},{9,10},{10,11},{11... | collective-permute-start | bytes 20744 | tf_op jit(solution)/shard_map/ppermute | solution.py:626
  176.2 3.7 %collective-permute-start.9 = (bf16[18,192]{1,0:T(8,128)(2,1)S(1)}, bf16[18,192]{1,0:T(8,128)(2,1)S(1)}, u32[]{:S(2)}, u32[]{:S(2)}) collective-permute-start(bf16[18,192]{1,0:T(8,128)(2,1)S(1)} %pad_maximum_fusion.4), channel_id=1, source_target_pairs={{1,0},{2,1},{3,2},{4,3},{5,4},{6,5},{7,6},{9,8},{10,9},{11,10},{12... | collective-permute-start | bytes 20744 | tf_op jit(solution)/shard_map/ppermute | solution.py:626
  180.6 5.9 %collective-permute-done.9.right_ref = bf16[18,192]{1,0:T(8,128)(2,1)S(1)} collective-permute-done((bf16[18,192]{1,0:T(8,128)(2,1)S(1)}, bf16[18,192]{1,0:T(8,128)(2,1)S(1)}, u32[]{:S(2)}, u32[]{:S(2)}) %collective-permute-start.9) | collective-permute-done | bytes 6944 | tf_op jit(solution)/shard_map/ppermute | solution.py:626
  187.6 0.9 shard_map.223
  (89 shorter events, 12.8 us)
Async XLA Ops:
  0.6 14.9 %copy-start.10 = (bf16[4,192,35]{1,0,2:T(4,128)(2,1)S(1)}, bf16[4,192,35]{1,0,2:T(4,128)(2,1)}, u32[]{:S(2)}) copy-start(bf16[4,192,35]{1,0,2:T(4,128)(2,1)} %param.16) | copy-start | bytes 161284
  1.5 14.0 %collective-permute-start.1 = (bf16[8,96]{1,0:T(8,128)(2,1)S(1)}, bf16[8,96]{1,0:T(8,128)(2,1)S(1)}, u32[]{:S(2)}, u32[]{:S(2)}) collective-permute-start(bf16[8,96]{1,0:T(8,128)(2,1)S(1)} %slice.54), channel_id=1, source_target_pairs={{8,0},{16,8},{24,16},{32,24},{40,32},{48,40},{56,48},{64,56},{72,6... | collective-permute-start | bytes 4616 | tf_op jit(solution)/shard_map/ppermute | solution.py:626
  12.8 7.0 %collective-permute-start = (bf16[8,96]{1,0:T(8,128)(2,1)S(1)}, bf16[8,96]{1,0:T(8,128)(2,1)S(1)}, u32[]{:S(2)}, u32[]{:S(2)}) collective-permute-start(bf16[8,96]{1,0:T(8,128)(2,1)S(1)} %slice.52), channel_id=1, source_target_pairs={{0,8},{8,16},{16,24},{24,32},{32,40},{40,48},{48,56},{56,64},{64,7... | collective-permute-start | bytes 4616 | tf_op jit(solution)/shard_map/ppermute | solution.py:626
  20.6 16.0 %all-to-all-start = ((bf16[8,144,96]{2,1,0:T(8,128)(2,1)}), bf16[8,144,96]{2,1,0:T(8,128)(2,1)S(1)}, u32[]{:S(2)}, u32[]{:S(2)}) async-start(bf16[8,144,96]{2,1,0:T(8,128)(2,1)} %broadcast_in_dim.9), calls=%async_computation | async-start | bytes 589824 | tf_op jit(solution)/shard_map/all_to_all | solution.py:638
  30.3 0.7 copy-start.14
  30.3 0.8 copy-start.15
  30.3 0.8 copy-start.13
  30.3 0.9 copy-start.12
  31.6 0.7 copy-start.17
  31.6 0.7 copy-start.18
  32.3 0.9 copy-start.9
  54.3 6.3 %copy-start.11 = (bf16[16,768]{1,0:T(8,128)(2,1)S(1)}, bf16[16,768]{1,0:T(8,128)(2,1)}, u32[]{:S(2)}) copy-start(bf16[16,768]{1,0:T(8,128)(2,1)} %param.23) | copy-start | bytes 73732
  54.3 15.2 %all-to-all-start.2 = ((bf16[64,8,128]{2,1,0:T(8,128)(2,1)}), bf16[64,8,128]{2,1,0:T(8,128)(2,1)S(1)}, u32[]{:S(2)}, u32[]{:S(2)}) async-start(bf16[64,8,128]{2,1,0:T(8,128)(2,1)} %bitcast.10), calls=%async_computation.2 | async-start | bytes 262144 | tf_op jit(solution)/shard_map/all_to_all | solution.py:638
  61.5 8.0 %copy-start.4 = (bf16[192,96]{1,0:T(8,128)(2,1)S(1)}, bf16[192,96]{1,0:T(8,128)(2,1)}, u32[]{:S(2)}) copy-start(bf16[192,96]{1,0:T(8,128)(2,1)} %ow_ref.1) | copy-start | bytes 110596
  72.5 16.4 %copy-start.2 = (bf16[128,192]{1,0:T(8,128)(2,1)}, bf16[128,192]{1,0:T(8,128)(2,1)S(1)}, u32[]{:S(2)}) copy-start(bf16[128,192]{1,0:T(8,128)(2,1)S(1)} %get-tuple-element.66.dgate_ref) | copy-start | bytes 147460
  72.5 20.0 %all-to-all-start.3 = ((bf16[64,8,128]{2,1,0:T(8,128)(2,1)}), bf16[64,8,128]{2,1,0:T(8,128)(2,1)S(1)}, u32[]{:S(2)}, u32[]{:S(2)}) async-start(bf16[64,8,128]{2,1,0:T(8,128)(2,1)} %bitcast.12), calls=%async_computation.3 | async-start | bytes 262144 | tf_op jit(solution)/shard_map/all_to_all | solution.py:638
  81.4 11.0 %collective-permute-start.2 = (bf16[128,192]{1,0:T(8,128)(2,1)S(1)}, bf16[128,192]{1,0:T(8,128)(2,1)S(1)}, u32[]{:S(2)}, u32[]{:S(2)}) collective-permute-start(bf16[128,192]{1,0:T(8,128)(2,1)S(1)} %get-tuple-element.65.g_ref), channel_id=1, source_target_pairs={{0,1},{1,0},{2,3},{3,2},{4,5},{5,4},{6,7},{7,6},{8,9},{9,8},{10,11... | collective-permute-start | bytes 147464 | tf_op jit(solution)/shard_map/ppermute | solution.py:642
  93.4 25.4 %all-to-all-start.4 = ((bf16[64,8,128]{2,1,0:T(8,128)(2,1)}), bf16[64,8,128]{2,1,0:T(8,128)(2,1)S(1)}, u32[]{:S(2)}, u32[]{:S(2)}) async-start(bf16[64,8,128]{2,1,0:T(8,128)(2,1)} %bitcast.16), calls=%async_computation.4 | async-start | bytes 262144 | tf_op jit(solution)/shard_map/all_to_all | solution.py:638
  104.1 9.8 %collective-permute-start.5 = (bf16[2,128,192]{2,1,0:T(8,128)(2,1)S(1)}, bf16[2,128,192]{2,1,0:T(8,128)(2,1)S(1)}, u32[]{:S(2)}, u32[]{:S(2)}) collective-permute-start(bf16[2,128,192]{2,1,0:T(8,128)(2,1)S(1)} %pad_maximum_fusion.p0_ref), channel_id=1, source_target_pairs={{0,6},{1,7},{2,4},{3,5},{4,2},{5,3},{6,0},{7,1},{8,14},{9,15},{10,... | collective-permute-start | bytes 294920 | tf_op jit(solution)/shard_map/ppermute | solution.py:642
  106.9 9.2 %collective-permute-start.4 = (bf16[2,128,192]{2,1,0:T(8,128)(2,1)S(1)}, bf16[2,128,192]{2,1,0:T(8,128)(2,1)S(1)}, u32[]{:S(2)}, u32[]{:S(2)}) collective-permute-start(bf16[2,128,192]{2,1,0:T(8,128)(2,1)S(1)} %pad_maximum_fusion.p0_ref), channel_id=1, source_target_pairs={{0,4},{1,5},{2,6},{3,7},{4,0},{5,1},{6,2},{7,3},{8,12},{9,13},{10,... | collective-permute-start | bytes 294920 | tf_op jit(solution)/shard_map/ppermute | solution.py:642
  110.1 7.9 %collective-permute-start.3 = (bf16[2,128,192]{2,1,0:T(8,128)(2,1)S(1)}, bf16[2,128,192]{2,1,0:T(8,128)(2,1)S(1)}, u32[]{:S(2)}, u32[]{:S(2)}) collective-permute-start(bf16[2,128,192]{2,1,0:T(8,128)(2,1)S(1)} %pad_maximum_fusion.p0_ref), channel_id=1, source_target_pairs={{0,2},{1,3},{2,0},{3,1},{4,6},{5,7},{6,4},{7,5},{8,10},{9,11},{10,... | collective-permute-start | bytes 294920 | tf_op jit(solution)/shard_map/ppermute | solution.py:642
  118.7 0.9 copy-start.1
  125.9 22.7 %copy-start.7 = (bf16[128,192]{1,0:T(8,128)(2,1)}, bf16[128,192]{1,0:T(8,128)(2,1)S(1)}, u32[]{:S(2)}) copy-start(bf16[128,192]{1,0:T(8,128)(2,1)S(1)} %get-tuple-element.84.own_ref) | copy-start | bytes 147460
  148.6 12.5 %copy-start.8 = (bf16[128,192]{1,0:T(8,128)(2,1)S(1)}, bf16[128,192]{1,0:T(8,128)(2,1)}, u32[]{:S(2)}) copy-start(bf16[128,192]{1,0:T(8,128)(2,1)} %copy-done.7) | copy-start | bytes 147460
  148.6 13.2 %all-to-all-start.6 = ((f32[8,16,128]{2,1,0:T(8,128)}), f32[8,16,128]{2,1,0:T(8,128)S(1)}, u32[]{:S(2)}, u32[]{:S(2)}) async-start(f32[8,16,128]{2,1,0:T(8,128)} %shard_map.220), calls=%async_computation.6 | async-start | bytes 131072 | tf_op jit(solution)/shard_map/all_to_all | solution.py:638
  156.8 13.3 %collective-permute-start.7 = (bf16[8,192]{1,0:T(8,128)(2,1)S(1)}, bf16[8,192]{1,0:T(8,128)(2,1)S(1)}, u32[]{:S(2)}, u32[]{:S(2)}) collective-permute-start(bf16[8,192]{1,0:T(8,128)(2,1)S(1)} %get-tuple-element.104), channel_id=1, source_target_pairs={{8,0},{16,8},{24,16},{32,24},{40,32},{48,40},{56,48},{64,56},{72,6... | collective-permute-start | bytes 9224 | tf_op jit(solution)/shard_map/ppermute | solution.py:626
  158.9 11.2 %collective-permute-start.6 = (bf16[8,192]{1,0:T(8,128)(2,1)S(1)}, bf16[8,192]{1,0:T(8,128)(2,1)S(1)}, u32[]{:S(2)}, u32[]{:S(2)}) collective-permute-start(bf16[8,192]{1,0:T(8,128)(2,1)S(1)} %get-tuple-element.105), channel_id=1, source_target_pairs={{0,8},{8,16},{16,24},{24,32},{32,40},{40,48},{48,56},{56,64},{64,7... | collective-permute-start | bytes 9224 | tf_op jit(solution)/shard_map/ppermute | solution.py:626
  162.6 17.3 %copy-start.6 = (bf16[128,96]{1,0:T(8,128)(2,1)S(1)}, bf16[128,96]{1,0:T(8,128)(2,1)}, u32[]{:S(2)}) copy-start(bf16[128,96]{1,0:T(8,128)(2,1)} %copy-done.5) | copy-start | bytes 73732
  162.6 25.0 %all-to-all-start.7 = ((bf16[64,16,128]{2,1,0:T(8,128)(2,1)}), bf16[64,16,128]{2,1,0:T(8,128)(2,1)S(1)}, u32[]{:S(2)}, u32[]{:S(2)}) async-start(bf16[64,16,128]{2,1,0:T(8,128)(2,1)} %shard_map.222), calls=%async_computation.7 | async-start | bytes 524288 | tf_op jit(solution)/shard_map/all_to_all | solution.py:638
  170.0 16.5 %copy-start.3 = (bf16[128,192]{1,0:T(8,128)(2,1)S(1)}, bf16[128,192]{1,0:T(8,128)(2,1)}, u32[]{:S(2)}) copy-start(bf16[128,192]{1,0:T(8,128)(2,1)} %copy-done.2) | copy-start | bytes 147460
  170.1 10.5 %collective-permute-start.8 = (bf16[18,192]{1,0:T(8,128)(2,1)S(1)}, bf16[18,192]{1,0:T(8,128)(2,1)S(1)}, u32[]{:S(2)}, u32[]{:S(2)}) collective-permute-start(bf16[18,192]{1,0:T(8,128)(2,1)S(1)} %pad_maximum_fusion.3), channel_id=1, source_target_pairs={{0,1},{1,2},{2,3},{3,4},{4,5},{5,6},{6,7},{8,9},{9,10},{10,11},{11... | collective-permute-start | bytes 20744 | tf_op jit(solution)/shard_map/ppermute | solution.py:626
  176.2 10.4 %collective-permute-start.9 = (bf16[18,192]{1,0:T(8,128)(2,1)S(1)}, bf16[18,192]{1,0:T(8,128)(2,1)S(1)}, u32[]{:S(2)}, u32[]{:S(2)}) collective-permute-start(bf16[18,192]{1,0:T(8,128)(2,1)S(1)} %pad_maximum_fusion.4), channel_id=1, source_target_pairs={{1,0},{2,1},{3,2},{4,3},{5,4},{6,5},{7,6},{9,8},{10,9},{11,10},{12... | collective-permute-start | bytes 20744 | tf_op jit(solution)/shard_map/ppermute | solution.py:626
  (3 other events, 1.9 us)

commit v8 on v7

--- a/solution.py
+++ b/solution.py
@@ -663,7 +663,7 @@
     rows, cols = (lax.axis_size("row"), lax.axis_size("col"))
     chunk = pack.shape[0] // rows
     got = all_to_all(pack.reshape(rows, chunk, 128), "row")
-    (part,) = call(partial(sum_kernel, 1.0), [((cols, chunk, 128), F32)], got, flops=10**7)
+    (part,) = call(partial(sum_kernel, 1.0), [((cols, chunk, 128), BF)], got, flops=10**7)
     part, later = lax.optimization_barrier((part, later))
     got = all_to_all(part, "col")
     (part,) = call(partial(sum_kernel, scale), [((rows, chunk, 128), BF)], got, flops=10**7)

time: 190 us -> 190 us (level)
  no operation moved by 1% of the time
where the time goes in v8:
time: 190 us; the launch traced here: 188 us
  starting transfers between devices  95.8 us (50%)
  blocking collectives  37.4 us (20%)
  Pallas kernels  25 us (13%)
  waiting for transfers between devices  19.8 us (10%)
  local copies, waits for them, and re-layouts  9.17 us (5%)
    all_to_all x6, starting transfers between devices, all_to_all(): return lax.all_to_all(x, axis, 0, 0, tiled=True)  51.3 us
    all_to_all x2, blocking collectives, all_to_all(): return lax.all_to_all(x, axis, 0, 0, tiled=True)  37.4 us
    ppermute x6, starting transfers between devices, neighbours(): return (lax.ppermute(last, axis, up), lax.ppermute(first, axis, down))  27.1 us
    pallas_call x13, Pallas kernels, call(): pl.pallas_call(kernel, out_shape=[jax.ShapeDtypeStruct(s, t) for s, t in...  25 us
    ppermute x4, starting transfers between devices, swapped(): lax.ppermute(x, 'col', [(i, i ^ step) for i in range(lax.axis_size('col'))])  17.3 us
    ppermute x6, waiting for transfers between devices, neighbours(): return (lax.ppermute(last, axis, up), lax.ppermute(first, axis, down))  10 us
    all_to_all x6, waiting for transfers between devices, all_to_all(): return lax.all_to_all(x, axis, 0, 0, tiled=True)  5.62 us
    unnamed x41, local copies, waits for them, and re-layouts  4.32 us
  transfers between devices with their start and end apart: 16, of which 7 were waited for; matrix products, arithmetic and copies ran while one was open for 2% of the time, Pallas kernels for 6%

profile of v8, /device:TPU:56, one launch (start us, length us, event | category | flops | bytes accessed | tf_op | source)
XLA Modules:
  0.0 188.4 jit_solution(1590025782648422915)
XLA Ops:
  1.5 11.2 %collective-permute-start.1 = (bf16[8,96]{1,0:T(8,128)(2,1)S(1)}, bf16[8,96]{1,0:T(8,128)(2,1)S(1)}, u32[]{:S(2)}, u32[]{:S(2)}) collective-permute-start(bf16[8,96]{1,0:T(8,128)(2,1)S(1)} %slice.54), channel_id=1, source_target_pairs={{8,0},{16,8},{24,16},{32,24},{40,32},{48,40},{56,48},{64,56},{72,6... | collective-permute-start | bytes 4616 | tf_op jit(solution)/shard_map/ppermute | solution.py:626
  12.8 1.9 %collective-permute-start = (bf16[8,96]{1,0:T(8,128)(2,1)S(1)}, bf16[8,96]{1,0:T(8,128)(2,1)S(1)}, u32[]{:S(2)}, u32[]{:S(2)}) collective-permute-start(bf16[8,96]{1,0:T(8,128)(2,1)S(1)} %slice.52), channel_id=1, source_target_pairs={{0,8},{8,16},{16,24},{24,32},{32,40},{40,48},{48,56},{56,64},{64,7... | collective-permute-start | bytes 4616 | tf_op jit(solution)/shard_map/ppermute | solution.py:626
  15.6 4.2 %collective-permute-done = bf16[8,96]{1,0:T(8,128)(2,1)S(1)} collective-permute-done((bf16[8,96]{1,0:T(8,128)(2,1)S(1)}, bf16[8,96]{1,0:T(8,128)(2,1)S(1)}, u32[]{:S(2)}, u32[]{:S(2)}) %collective-permute-start) | collective-permute-done | bytes 1568 | tf_op jit(solution)/shard_map/ppermute | solution.py:626
  20.6 9.7 %all-to-all-start = ((bf16[8,144,96]{2,1,0:T(8,128)(2,1)}), bf16[8,144,96]{2,1,0:T(8,128)(2,1)S(1)}, u32[]{:S(2)}, u32[]{:S(2)}) async-start(bf16[8,144,96]{2,1,0:T(8,128)(2,1)} %broadcast_in_dim.9), calls=%async_computation | async-start | bytes 589824 | tf_op jit(solution)/shard_map/all_to_all | solution.py:638
  33.3 3.2 %all-to-all-done.got_ref = bf16[8,144,96]{2,1,0:T(8,128)(2,1)S(1)} async-done(((bf16[8,144,96]{2,1,0:T(8,128)(2,1)}), bf16[8,144,96]{2,1,0:T(8,128)(2,1)S(1)}, u32[]{:S(2)}, u32[]{:S(2)}) %all-to-all-start) | async-done | bytes 221216 | tf_op jit(solution)/shard_map/all_to_all | solution.py:638
  36.5 1.5 shard_map.211
  38.0 15.4 %all_to_all.40 = bf16[64,8,128]{2,1,0:T(8,128)(2,1)S(1)} all-to-all(bf16[64,8,128]{2,1,0:T(8,128)(2,1)S(1)} %bitcast.44), channel_id=1, replica_groups=mesh['row'=64,'col'=8] {'row'}, dimensions={0} | all-to-all | bytes 262144 | tf_op jit(solution)/shard_map/all_to_all | solution.py:638
  54.3 6.3 %all-to-all-start.2 = ((bf16[64,8,128]{2,1,0:T(8,128)(2,1)}), bf16[64,8,128]{2,1,0:T(8,128)(2,1)S(1)}, u32[]{:S(2)}, u32[]{:S(2)}) async-start(bf16[64,8,128]{2,1,0:T(8,128)(2,1)} %bitcast.10), calls=%async_computation.2 | async-start | bytes 262144 | tf_op jit(solution)/shard_map/all_to_all | solution.py:638
  61.5 6.1 %shard_map.214 = (f32[256,192]{1,0:T(8,128)S(1)}, f32[256,192]{1,0:T(8,128)S(1)}, f32[1024,128]{1,0:T(8,128)S(1)}) custom-call(s32[1]{0:T(128)} %bitcast.me_ref, bf16[8,144,96]{2,1,0:T(8,128)(2,1)S(1)} %all-to-all-done.got_ref, bf16[96,192]{1,0:T(8,128)(2,1)S(1)} %get-tuple-element.101.wbr_ref, f32[16,192]{1,0:T(8,128)S(1)} %concatenate.16.cw_ref.vec_ref, ...), custom_call_target="tpu_custom_call" | custom-call | flops 1000000000 | bytes 1000000 | tf_op jit(solution)/shard_map/pallas_call | solution.py:611
  67.6 1.9 all-to-all-done.2
  69.5 2.5 %shard_map.215 = (bf16[128,96]{1,0:T(8,128)(2,1)S(1)}, bf16[128,192]{1,0:T(8,128)(2,1)S(1)}, bf16[128,192]{1,0:T(8,128)(2,1)S(1)}, bf16[128,192]{1,0:T(8,128)(2,...) custom-call(f32[128,192]{1,0:T(8,128)S(1)} %shard_map.212.y_ref, bf16[128,192]{1,0:T(8,128)(2,1)S(1)} %get-tuple-element.54.act_ref, ...), custom_call_target="tpu_custom_call" | custom-call | flops 100000000 | bytes 1000000 | tf_op jit(solution)/shard_map/pallas_call | solution.py:611
  72.5 8.9 %all-to-all-start.3 = ((bf16[64,8,128]{2,1,0:T(8,128)(2,1)}), bf16[64,8,128]{2,1,0:T(8,128)(2,1)S(1)}, u32[]{:S(2)}, u32[]{:S(2)}) async-start(bf16[64,8,128]{2,1,0:T(8,128)(2,1)} %bitcast.12), calls=%async_computation.3 | async-start | bytes 262144 | tf_op jit(solution)/shard_map/all_to_all | solution.py:638
  81.4 7.5 %collective-permute-start.2 = (bf16[128,192]{1,0:T(8,128)(2,1)S(1)}, bf16[128,192]{1,0:T(8,128)(2,1)S(1)}, u32[]{:S(2)}, u32[]{:S(2)}) collective-permute-start(bf16[128,192]{1,0:T(8,128)(2,1)S(1)} %get-tuple-element.65.g_ref), channel_id=1, source_target_pairs={{0,1},{1,0},{2,3},{3,2},{4,5},{5,4},{6,7},{7,6},{8,9},{9,8},{10,11... | collective-permute-start | bytes 147464 | tf_op jit(solution)/shard_map/ppermute | solution.py:642
  89.2 3.3 %shard_map.216.back_ref = f32[128,512]{1,0:T(8,128)S(1)} custom-call(bf16[128,192]{1,0:T(8,128)(2,1)S(1)} %get-tuple-element.54.act_ref, f32[128,128]{1,0:T(8,128)S(1)} %get-tuple-element.55.bc_ref, f32[128,128]{1,0:T(8,128)S(1)} %get-tuple-element.56.step_ref, f32[128,128]{1,0:T(8,128)S(1)} %get-tuple-element.57.log_ref, ...), custom_call_target="tpu_custom_call" | custom-call | flops 100000000 | bytes 1000000 | tf_op jit(solution)/shard_map/pallas_call | solution.py:611
  92.5 0.9 shard_map.218
  93.4 10.7 %all-to-all-start.4 = ((bf16[64,8,128]{2,1,0:T(8,128)(2,1)}), bf16[64,8,128]{2,1,0:T(8,128)(2,1)S(1)}, u32[]{:S(2)}, u32[]{:S(2)}) async-start(bf16[64,8,128]{2,1,0:T(8,128)(2,1)} %bitcast.16), calls=%async_computation.4 | async-start | bytes 262144 | tf_op jit(solution)/shard_map/all_to_all | solution.py:638
  104.1 2.8 %collective-permute-start.5 = (bf16[2,128,192]{2,1,0:T(8,128)(2,1)S(1)}, bf16[2,128,192]{2,1,0:T(8,128)(2,1)S(1)}, u32[]{:S(2)}, u32[]{:S(2)}) collective-permute-start(bf16[2,128,192]{2,1,0:T(8,128)(2,1)S(1)} %pad_maximum_fusion.p0_ref), channel_id=1, source_target_pairs={{0,6},{1,7},{2,4},{3,5},{4,2},{5,3},{6,0},{7,1},{8,14},{9,15},{10,... | collective-permute-start | bytes 294920 | tf_op jit(solution)/shard_map/ppermute | solution.py:642
  106.9 3.2 %collective-permute-start.4 = (bf16[2,128,192]{2,1,0:T(8,128)(2,1)S(1)}, bf16[2,128,192]{2,1,0:T(8,128)(2,1)S(1)}, u32[]{:S(2)}, u32[]{:S(2)}) collective-permute-start(bf16[2,128,192]{2,1,0:T(8,128)(2,1)S(1)} %pad_maximum_fusion.p0_ref), channel_id=1, source_target_pairs={{0,4},{1,5},{2,6},{3,7},{4,0},{5,1},{6,2},{7,3},{8,12},{9,13},{10,... | collective-permute-start | bytes 294920 | tf_op jit(solution)/shard_map/ppermute | solution.py:642
  110.1 3.8 %collective-permute-start.3 = (bf16[2,128,192]{2,1,0:T(8,128)(2,1)S(1)}, bf16[2,128,192]{2,1,0:T(8,128)(2,1)S(1)}, u32[]{:S(2)}, u32[]{:S(2)}) collective-permute-start(bf16[2,128,192]{2,1,0:T(8,128)(2,1)S(1)} %pad_maximum_fusion.p0_ref), channel_id=1, source_target_pairs={{0,2},{1,3},{2,0},{3,1},{4,6},{5,7},{6,4},{7,5},{8,10},{9,11},{10,... | collective-permute-start | bytes 294920 | tf_op jit(solution)/shard_map/ppermute | solution.py:642
  114.0 2.1 %collective-permute-done.4.p2_ref = bf16[2,128,192]{2,1,0:T(8,128)(2,1)S(1)} collective-permute-done((bf16[2,128,192]{2,1,0:T(8,128)(2,1)S(1)}, bf16[2,128,192]{2,1,0:T(8,128)(2,1)S(1)}, u32[]{:S(2)}, u32[]{:S(2)}) %collective-permute-start.4) | collective-permute-done | bytes 98336 | tf_op jit(solution)/shard_map/ppermute | solution.py:642
  116.1 2.0 %collective-permute-done.3.p1_ref = bf16[2,128,192]{2,1,0:T(8,128)(2,1)S(1)} collective-permute-done((bf16[2,128,192]{2,1,0:T(8,128)(2,1)S(1)}, bf16[2,128,192]{2,1,0:T(8,128)(2,1)S(1)}, u32[]{:S(2)}, u32[]{:S(2)}) %collective-permute-start.3) | collective-permute-done | bytes 98336 | tf_op jit(solution)/shard_map/ppermute | solution.py:642
  118.7 0.9 copy-done.1
  119.6 6.3 %shard_map.219 = (bf16[128,192]{1,0:T(8,128)(2,1)S(1)}, bf16[1024,128]{1,0:T(8,128)(2,1)S(1)}) custom-call(s32[1]{0:T(128)} %bitcast.me_ref, f32[18,24,192]{2,1,0:T(8,128)S(1)} %get-tuple-element.63.pad_ref, bf16[864,128]{1,0:T(8,128)(2,1)S(1)} %get-tuple-element.70.shifts_ref, f32[16,192]{1,0:T(8,128)S(1)} %concatenate.16.cw_ref.vec_ref, ...), custom_call_target="tpu_custom_call" | custom-call | flops 100000000 | bytes 1000000 | tf_op jit(solution)/shard_map/pallas_call | solution.py:611
  125.9 22.0 %all_to_all.41.x_ref = bf16[64,16,128]{2,1,0:T(8,128)(2,1)S(1)} all-to-all(bf16[64,16,128]{2,1,0:T(8,128)(2,1)S(1)} %bitcast.43), channel_id=1, replica_groups=mesh['row'=64,'col'=8] {'row'}, dimensions={0} | all-to-all | bytes 524288 | tf_op jit(solution)/shard_map/all_to_all | solution.py:638
  148.6 8.1 %all-to-all-start.6 = ((bf16[8,16,128]{2,1,0:T(8,128)(2,1)}), bf16[8,16,128]{2,1,0:T(8,128)(2,1)S(1)}, u32[]{:S(2)}, u32[]{:S(2)}) async-start(bf16[8,16,128]{2,1,0:T(8,128)(2,1)} %shard_map.220), calls=%async_computation.6 | async-start | bytes 65536 | tf_op jit(solution)/shard_map/all_to_all | solution.py:638
  156.8 2.1 %collective-permute-start.7 = (bf16[8,192]{1,0:T(8,128)(2,1)S(1)}, bf16[8,192]{1,0:T(8,128)(2,1)S(1)}, u32[]{:S(2)}, u32[]{:S(2)}) collective-permute-start(bf16[8,192]{1,0:T(8,128)(2,1)S(1)} %get-tuple-element.104), channel_id=1, source_target_pairs={{8,0},{16,8},{24,16},{32,24},{40,32},{48,40},{56,48},{64,56},{72,6... | collective-permute-start | bytes 9224 | tf_op jit(solution)/shard_map/ppermute | solution.py:626
  158.9 2.2 %collective-permute-start.6 = (bf16[8,192]{1,0:T(8,128)(2,1)S(1)}, bf16[8,192]{1,0:T(8,128)(2,1)S(1)}, u32[]{:S(2)}, u32[]{:S(2)}) collective-permute-start(bf16[8,192]{1,0:T(8,128)(2,1)S(1)} %get-tuple-element.105), channel_id=1, source_target_pairs={{0,8},{8,16},{16,24},{24,32},{32,40},{40,48},{48,56},{56,64},{64,7... | collective-permute-start | bytes 9224 | tf_op jit(solution)/shard_map/ppermute | solution.py:626
  162.4 7.6 %all-to-all-start.7 = ((bf16[64,16,128]{2,1,0:T(8,128)(2,1)}), bf16[64,16,128]{2,1,0:T(8,128)(2,1)S(1)}, u32[]{:S(2)}, u32[]{:S(2)}) async-start(bf16[64,16,128]{2,1,0:T(8,128)(2,1)} %shard_map.222), calls=%async_computation.7 | async-start | bytes 524288 | tf_op jit(solution)/shard_map/all_to_all | solution.py:638
  170.1 5.9 %collective-permute-start.8 = (bf16[18,192]{1,0:T(8,128)(2,1)S(1)}, bf16[18,192]{1,0:T(8,128)(2,1)S(1)}, u32[]{:S(2)}, u32[]{:S(2)}) collective-permute-start(bf16[18,192]{1,0:T(8,128)(2,1)S(1)} %pad_maximum_fusion.3), channel_id=1, source_target_pairs={{0,1},{1,2},{2,3},{3,4},{4,5},{5,6},{6,7},{8,9},{9,10},{10,11},{11... | collective-permute-start | bytes 20744 | tf_op jit(solution)/shard_map/ppermute | solution.py:626
  176.0 3.8 %collective-permute-start.9 = (bf16[18,192]{1,0:T(8,128)(2,1)S(1)}, bf16[18,192]{1,0:T(8,128)(2,1)S(1)}, u32[]{:S(2)}, u32[]{:S(2)}) collective-permute-start(bf16[18,192]{1,0:T(8,128)(2,1)S(1)} %pad_maximum_fusion.4), channel_id=1, source_target_pairs={{1,0},{2,1},{3,2},{4,3},{5,4},{6,5},{7,6},{9,8},{10,9},{11,10},{12... | collective-permute-start | bytes 20744 | tf_op jit(solution)/shard_map/ppermute | solution.py:626
  180.6 5.8 %collective-permute-done.9.right_ref = bf16[18,192]{1,0:T(8,128)(2,1)S(1)} collective-permute-done((bf16[18,192]{1,0:T(8,128)(2,1)S(1)}, bf16[18,192]{1,0:T(8,128)(2,1)S(1)}, u32[]{:S(2)}, u32[]{:S(2)}) %collective-permute-start.9) | collective-permute-done | bytes 6944 | tf_op jit(solution)/shard_map/ppermute | solution.py:626
  187.5 0.9 shard_map.223
  (89 shorter events, 12.6 us)
Async XLA Ops:
  0.6 14.9 %copy-start.10 = (bf16[4,192,35]{1,0,2:T(4,128)(2,1)S(1)}, bf16[4,192,35]{1,0,2:T(4,128)(2,1)}, u32[]{:S(2)}) copy-start(bf16[4,192,35]{1,0,2:T(4,128)(2,1)} %param.16) | copy-start | bytes 161284
  1.5 14.0 %collective-permute-start.1 = (bf16[8,96]{1,0:T(8,128)(2,1)S(1)}, bf16[8,96]{1,0:T(8,128)(2,1)S(1)}, u32[]{:S(2)}, u32[]{:S(2)}) collective-permute-start(bf16[8,96]{1,0:T(8,128)(2,1)S(1)} %slice.54), channel_id=1, source_target_pairs={{8,0},{16,8},{24,16},{32,24},{40,32},{48,40},{56,48},{64,56},{72,6... | collective-permute-start | bytes 4616 | tf_op jit(solution)/shard_map/ppermute | solution.py:626
  12.8 7.0 %collective-permute-start = (bf16[8,96]{1,0:T(8,128)(2,1)S(1)}, bf16[8,96]{1,0:T(8,128)(2,1)S(1)}, u32[]{:S(2)}, u32[]{:S(2)}) collective-permute-start(bf16[8,96]{1,0:T(8,128)(2,1)S(1)} %slice.52), channel_id=1, source_target_pairs={{0,8},{8,16},{16,24},{24,32},{32,40},{40,48},{48,56},{56,64},{64,7... | collective-permute-start | bytes 4616 | tf_op jit(solution)/shard_map/ppermute | solution.py:626
  20.6 16.0 %all-to-all-start = ((bf16[8,144,96]{2,1,0:T(8,128)(2,1)}), bf16[8,144,96]{2,1,0:T(8,128)(2,1)S(1)}, u32[]{:S(2)}, u32[]{:S(2)}) async-start(bf16[8,144,96]{2,1,0:T(8,128)(2,1)} %broadcast_in_dim.9), calls=%async_computation | async-start | bytes 589824 | tf_op jit(solution)/shard_map/all_to_all | solution.py:638
  30.3 0.7 copy-start.14
  30.3 0.8 copy-start.15
  30.3 0.8 copy-start.13
  30.3 0.9 copy-start.12
  31.6 0.7 copy-start.17
  31.6 0.7 copy-start.18
  32.3 0.9 copy-start.9
  54.3 6.3 %copy-start.11 = (bf16[16,768]{1,0:T(8,128)(2,1)S(1)}, bf16[16,768]{1,0:T(8,128)(2,1)}, u32[]{:S(2)}) copy-start(bf16[16,768]{1,0:T(8,128)(2,1)} %param.23) | copy-start | bytes 73732
  54.3 15.2 %all-to-all-start.2 = ((bf16[64,8,128]{2,1,0:T(8,128)(2,1)}), bf16[64,8,128]{2,1,0:T(8,128)(2,1)S(1)}, u32[]{:S(2)}, u32[]{:S(2)}) async-start(bf16[64,8,128]{2,1,0:T(8,128)(2,1)} %bitcast.10), calls=%async_computation.2 | async-start | bytes 262144 | tf_op jit(solution)/shard_map/all_to_all | solution.py:638
  61.5 8.0 %copy-start.4 = (bf16[192,96]{1,0:T(8,128)(2,1)S(1)}, bf16[192,96]{1,0:T(8,128)(2,1)}, u32[]{:S(2)}) copy-start(bf16[192,96]{1,0:T(8,128)(2,1)} %ow_ref.1) | copy-start | bytes 110596
  72.5 16.4 %copy-start.2 = (bf16[128,192]{1,0:T(8,128)(2,1)}, bf16[128,192]{1,0:T(8,128)(2,1)S(1)}, u32[]{:S(2)}) copy-start(bf16[128,192]{1,0:T(8,128)(2,1)S(1)} %get-tuple-element.66.dgate_ref) | copy-start | bytes 147460
  72.5 20.0 %all-to-all-start.3 = ((bf16[64,8,128]{2,1,0:T(8,128)(2,1)}), bf16[64,8,128]{2,1,0:T(8,128)(2,1)S(1)}, u32[]{:S(2)}, u32[]{:S(2)}) async-start(bf16[64,8,128]{2,1,0:T(8,128)(2,1)} %bitcast.12), calls=%async_computation.3 | async-start | bytes 262144 | tf_op jit(solution)/shard_map/all_to_all | solution.py:638
  81.4 11.0 %collective-permute-start.2 = (bf16[128,192]{1,0:T(8,128)(2,1)S(1)}, bf16[128,192]{1,0:T(8,128)(2,1)S(1)}, u32[]{:S(2)}, u32[]{:S(2)}) collective-permute-start(bf16[128,192]{1,0:T(8,128)(2,1)S(1)} %get-tuple-element.65.g_ref), channel_id=1, source_target_pairs={{0,1},{1,0},{2,3},{3,2},{4,5},{5,4},{6,7},{7,6},{8,9},{9,8},{10,11... | collective-permute-start | bytes 147464 | tf_op jit(solution)/shard_map/ppermute | solution.py:642
  93.4 25.4 %all-to-all-start.4 = ((bf16[64,8,128]{2,1,0:T(8,128)(2,1)}), bf16[64,8,128]{2,1,0:T(8,128)(2,1)S(1)}, u32[]{:S(2)}, u32[]{:S(2)}) async-start(bf16[64,8,128]{2,1,0:T(8,128)(2,1)} %bitcast.16), calls=%async_computation.4 | async-start | bytes 262144 | tf_op jit(solution)/shard_map/all_to_all | solution.py:638
  104.1 9.8 %collective-permute-start.5 = (bf16[2,128,192]{2,1,0:T(8,128)(2,1)S(1)}, bf16[2,128,192]{2,1,0:T(8,128)(2,1)S(1)}, u32[]{:S(2)}, u32[]{:S(2)}) collective-permute-start(bf16[2,128,192]{2,1,0:T(8,128)(2,1)S(1)} %pad_maximum_fusion.p0_ref), channel_id=1, source_target_pairs={{0,6},{1,7},{2,4},{3,5},{4,2},{5,3},{6,0},{7,1},{8,14},{9,15},{10,... | collective-permute-start | bytes 294920 | tf_op jit(solution)/shard_map/ppermute | solution.py:642
  106.9 9.2 %collective-permute-start.4 = (bf16[2,128,192]{2,1,0:T(8,128)(2,1)S(1)}, bf16[2,128,192]{2,1,0:T(8,128)(2,1)S(1)}, u32[]{:S(2)}, u32[]{:S(2)}) collective-permute-start(bf16[2,128,192]{2,1,0:T(8,128)(2,1)S(1)} %pad_maximum_fusion.p0_ref), channel_id=1, source_target_pairs={{0,4},{1,5},{2,6},{3,7},{4,0},{5,1},{6,2},{7,3},{8,12},{9,13},{10,... | collective-permute-start | bytes 294920 | tf_op jit(solution)/shard_map/ppermute | solution.py:642
  110.1 7.9 %collective-permute-start.3 = (bf16[2,128,192]{2,1,0:T(8,128)(2,1)S(1)}, bf16[2,128,192]{2,1,0:T(8,128)(2,1)S(1)}, u32[]{:S(2)}, u32[]{:S(2)}) collective-permute-start(bf16[2,128,192]{2,1,0:T(8,128)(2,1)S(1)} %pad_maximum_fusion.p0_ref), channel_id=1, source_target_pairs={{0,2},{1,3},{2,0},{3,1},{4,6},{5,7},{6,4},{7,5},{8,10},{9,11},{10,... | collective-permute-start | bytes 294920 | tf_op jit(solution)/shard_map/ppermute | solution.py:642
  118.7 0.9 copy-start.1
  125.9 22.7 %copy-start.7 = (bf16[128,192]{1,0:T(8,128)(2,1)}, bf16[128,192]{1,0:T(8,128)(2,1)S(1)}, u32[]{:S(2)}) copy-start(bf16[128,192]{1,0:T(8,128)(2,1)S(1)} %get-tuple-element.84.own_ref) | copy-start | bytes 147460
  148.6 12.5 %copy-start.8 = (bf16[128,192]{1,0:T(8,128)(2,1)S(1)}, bf16[128,192]{1,0:T(8,128)(2,1)}, u32[]{:S(2)}) copy-start(bf16[128,192]{1,0:T(8,128)(2,1)} %copy-done.7) | copy-start | bytes 147460
  148.6 13.1 %all-to-all-start.6 = ((bf16[8,16,128]{2,1,0:T(8,128)(2,1)}), bf16[8,16,128]{2,1,0:T(8,128)(2,1)S(1)}, u32[]{:S(2)}, u32[]{:S(2)}) async-start(bf16[8,16,128]{2,1,0:T(8,128)(2,1)} %shard_map.220), calls=%async_computation.6 | async-start | bytes 65536 | tf_op jit(solution)/shard_map/all_to_all | solution.py:638
  156.8 13.3 %collective-permute-start.7 = (bf16[8,192]{1,0:T(8,128)(2,1)S(1)}, bf16[8,192]{1,0:T(8,128)(2,1)S(1)}, u32[]{:S(2)}, u32[]{:S(2)}) collective-permute-start(bf16[8,192]{1,0:T(8,128)(2,1)S(1)} %get-tuple-element.104), channel_id=1, source_target_pairs={{8,0},{16,8},{24,16},{32,24},{40,32},{48,40},{56,48},{64,56},{72,6... | collective-permute-start | bytes 9224 | tf_op jit(solution)/shard_map/ppermute | solution.py:626
  158.9 11.2 %collective-permute-start.6 = (bf16[8,192]{1,0:T(8,128)(2,1)S(1)}, bf16[8,192]{1,0:T(8,128)(2,1)S(1)}, u32[]{:S(2)}, u32[]{:S(2)}) collective-permute-start(bf16[8,192]{1,0:T(8,128)(2,1)S(1)} %get-tuple-element.105), channel_id=1, source_target_pairs={{0,8},{8,16},{16,24},{24,32},{32,40},{40,48},{48,56},{56,64},{64,7... | collective-permute-start | bytes 9224 | tf_op jit(solution)/shard_map/ppermute | solution.py:626
  162.4 17.5 %copy-start.6 = (bf16[128,96]{1,0:T(8,128)(2,1)S(1)}, bf16[128,96]{1,0:T(8,128)(2,1)}, u32[]{:S(2)}) copy-start(bf16[128,96]{1,0:T(8,128)(2,1)} %copy-done.5) | copy-start | bytes 73732
  162.4 25.1 %all-to-all-start.7 = ((bf16[64,16,128]{2,1,0:T(8,128)(2,1)}), bf16[64,16,128]{2,1,0:T(8,128)(2,1)S(1)}, u32[]{:S(2)}, u32[]{:S(2)}) async-start(bf16[64,16,128]{2,1,0:T(8,128)(2,1)} %shard_map.222), calls=%async_computation.7 | async-start | bytes 524288 | tf_op jit(solution)/shard_map/all_to_all | solution.py:638
  170.0 16.4 %copy-start.3 = (bf16[128,192]{1,0:T(8,128)(2,1)S(1)}, bf16[128,192]{1,0:T(8,128)(2,1)}, u32[]{:S(2)}) copy-start(bf16[128,192]{1,0:T(8,128)(2,1)} %copy-done.2) | copy-start | bytes 147460
  170.1 10.5 %collective-permute-start.8 = (bf16[18,192]{1,0:T(8,128)(2,1)S(1)}, bf16[18,192]{1,0:T(8,128)(2,1)S(1)}, u32[]{:S(2)}, u32[]{:S(2)}) collective-permute-start(bf16[18,192]{1,0:T(8,128)(2,1)S(1)} %pad_maximum_fusion.3), channel_id=1, source_target_pairs={{0,1},{1,2},{2,3},{3,4},{4,5},{5,6},{6,7},{8,9},{9,10},{10,11},{11... | collective-permute-start | bytes 20744 | tf_op jit(solution)/shard_map/ppermute | solution.py:626
  176.0 10.4 %collective-permute-start.9 = (bf16[18,192]{1,0:T(8,128)(2,1)S(1)}, bf16[18,192]{1,0:T(8,128)(2,1)S(1)}, u32[]{:S(2)}, u32[]{:S(2)}) collective-permute-start(bf16[18,192]{1,0:T(8,128)(2,1)S(1)} %pad_maximum_fusion.4), channel_id=1, source_target_pairs={{1,0},{2,1},{3,2},{4,3},{5,4},{6,5},{7,6},{9,8},{10,9},{11,10},{12... | collective-permute-start | bytes 20744 | tf_op jit(solution)/shard_map/ppermute | solution.py:626
  (3 other events, 1.9 us)
